TPU v7x, 32 devices: a whole 2x2x4 slice. The times are simulated.
32 devices in a mesh: seq: 16 (over z, y, core), head: 2 (over x).
Axes of the slice: x: 2, y: 2, z: 4, core: 2. Of those that a mesh axis runs over, the one named last changes fastest.
Arguments:
- prefill_input: bfloat16 [4096, 8192], P('seq', 'head'), may hold values from -6 to 6
- prefill_step: float32 [4096, 128], P('seq', 'head'), may hold values from 0 to 4096, as said below
- write_proj: bfloat16 [4096, 1024], P('seq', 'head'), may hold values from -2.5 to 2.5
- read_proj: bfloat16 [4096, 1024], P('seq', 'head'), may hold values from -0.5 to 0.5
- decay_rate: float32 [128], P('head'), may hold values from 0 to 1, as said below
- skip_gain: float32 [128], P('head'), may hold values from 0.5 to 2
- resident_state: bfloat16 [16, 128, 64, 128], P('seq', 'head'), may hold values from -6 to 6
- owner_slot: int32 [16], replicated, may hold values from 0 to 15, each once
- draft_ids: int32 [16, 8], replicated, may hold values from 0 to 15
- accepted_len: int32 [16], replicated, may hold values from 0 to 8
- draft_input: bfloat16 [256, 8192], P('seq', 'head'), may hold values from -6 to 6
- draft_gate: bfloat16 [256, 8192], P('seq', 'head'), may hold values from -6 to 6
- draft_write: bfloat16 [256, 1024], P('seq', 'head'), may hold values from -2.5 to 2.5
- draft_read: bfloat16 [256, 1024], P('seq', 'head'), may hold values from -0.5 to 0.5
- draft_step: float32 [256, 128], P('seq', 'head'), may hold values from 0.05 to 1
- norm_gain: float32 [8192], P('head'), may hold values from 0.5 to 1.5
- out_weight: bfloat16 [8192, 8192], P('head', 'seq'), may hold values from -0.0625 to 0.0625
Outputs:
- prefill_out: bfloat16 [4096, 8192], P('seq', 'head')
- new_state: bfloat16 [16, 128, 64, 128], P('seq', 'head')
- verify_out: bfloat16 [128, 8192], P('head', 'seq')
- prompt_state: bfloat16 [128, 8192], P('head', 'seq')
Inputs may be any that keep to these rules, and one draw needn't show every extreme that they name: owner_slot holds every slot once. `decay_rate`: positive. `prefill_step`: positive.
All inputs are finite; a program needn't handle non-finite values.
Results may differ from a plain program's by a relative error of at most 0.005.
Values may be sent and summed in bfloat16 or wider, within the bound.
No kernel may reach another device: no remote copies, remote signals or barrier semaphores. Data moves between devices by JAX's collectives and lax.ppermute only.
A program may use at most 128 MiB of HBM per device.

v0:
```python
import functools

import jax
import jax.numpy as jnp
from jax import lax
from jax.experimental import pallas as pl
from jax.experimental.pallas import tpu as pltpu
from jax.sharding import PartitionSpec as P

HEAD_DIM = 64
STATE_SIZE = 128
BLOCK_LEN = 256
DRAFTS = 8
EPSILON = 1e-05
EXTRA = 32
UP_ROWS = STATE_SIZE + EXTRA
READ_AT = STATE_SIZE + 16
LOG_AT = STATE_SIZE + 24
DOWN_ROWS = STATE_SIZE + 16

F32 = jnp.float32
BF16 = jnp.bfloat16


def tree_stages(count):
    factors, rest = [], count
    if rest > 1:
        factors.append(2)
        rest //= 2
    inner = 1
    while inner * inner * 4 <= rest:
        inner *= 2
    factors += [inner, rest // inner]
    stages, stride = [], 1
    for factor in factors:
        stages.append((factor, stride))
        stride *= factor
    assert stride == count
    return stages


def swap(value, axis, stage, offset):
    count, stride = lax.axis_size(axis), stage[1]
    return lax.ppermute(value, axis, [(k, k ^ (offset * stride)) for k in range(count)])


def place_of(stage):
    factor, stride = stage
    return lax.rem(lax.div(lax.axis_index("seq"), stride), factor)


def dot(a, b, dims=((1,), (0,))):
    return lax.dot_general(a, b, (dims, ((), ())), preferred_element_type=F32)


def split(value, parts):
    found = []
    for _ in range(parts):
        part = value.astype(BF16).astype(F32)
        found.append(part)
        value = value - part
    return found


def head_mask(rows, heads, lanes, lane0):
    row = lax.broadcasted_iota(jnp.int32, (rows, lanes), 0) & (heads - 1)
    head = lax.shift_right_logical(lax.broadcasted_iota(jnp.int32, (rows, lanes), 1) + lane0, 6)
    return jnp.where(row == head, 1.0, 0.0).astype(BF16)


def window(start, size):
    return pl.ds(pl.multiple_of(start, size), size)


def ordered(kernel, count):
    return lambda *refs: kernel(*refs[count:])


ANYWHERE = pl.BlockSpec(memory_space=pl.ANY)
WHOLE = pl.BlockSpec(memory_space=pltpu.VMEM)
IN_HBM = pl.BlockSpec(memory_space=pltpu.HBM)


def call(
    kernel, name, outs, args, specs=None, out_specs=None, grid=(), after=(), scratch=(), alias=None,
    flops=0, exps=0, moved=None, vmem=32,
):
    if specs is None:
        specs = [WHOLE] * len(args)
    if out_specs is None:
        out_specs = [WHOLE] * len(outs)
    if moved is None:
        moved = sum(a.size * a.dtype.itemsize for a in (*args, *outs))
    first = len(after)
    return pl.pallas_call(
        ordered(kernel, first),
        name=name,
        grid=grid,
        out_shape=outs,
        in_specs=[ANYWHERE] * first + specs,
        out_specs=out_specs,
        scratch_shapes=list(scratch),
        input_output_aliases={first + k: v for k, v in (alias or {}).items()},
        compiler_params=pltpu.CompilerParams(vmem_limit_bytes=vmem * 1024 * 1024),
        cost_estimate=pl.CostEstimate(flops=flops, bytes_accessed=moved, transcendentals=exps),
    )(*after, *args)


def in_hbm(value):
    return pltpu.with_memory_space_constraint(value, pltpu.HBM)


def shape(dims, dtype):
    return jax.ShapeDtypeStruct(dims, dtype)


def open_kernel(stage, count, passed, *refs):
    sources, rest = refs[:count], refs[count:]
    outs, scratch = rest[: 14 + passed], rest[14 + passed :]
    outs, later = outs[:14], list(outs[14:])
    sent_ref, run_ref, runt_ref, stept_ref, reach_ref, end_ref, skip_out = outs[:7]
    q1_ref, q2_ref, vread_ref, vwrite_ref, tail_ref, owner_out, extra_ref = outs[7:]
    sems, held = scratch[0], [*scratch[1:], *later]
    fetches = [
        pltpu.make_async_copy(source, target, sems.at[k])
        for k, (source, target) in enumerate(zip(sources, held))
    ]
    for fetch in fetches:
        fetch.start()
    early = count - passed
    for fetch in fetches[:early]:
        fetch.wait()
    turned_ref, rate_ref, skip_ref, owner_ref, ids_ref, kept_ref = held[:6]
    din_ref, dgate_ref, dwrite_ref, dread_ref, dstep_ref, write_ref, x_ref = held[6:13]
    heads, span = turned_ref.shape
    lanes = x_ref.shape[1]
    groups = write_ref.shape[1] // STATE_SIZE
    per_group = heads // groups
    wide = per_group * HEAD_DIM
    here = lax.axis_index("seq")
    place = place_of(stage)
    owner_out[...] = jnp.zeros(owner_out.shape, jnp.int32) + owner_ref[0]

    step_rows = turned_ref[...]
    stept_ref[...] = step_rows
    pad = (-heads) % 128
    if pad:
        step_rows = jnp.concatenate([step_rows, jnp.zeros((pad, span), F32)], axis=0)
    step = step_rows.T[:, :heads]
    log_decay = -step * rate_ref[...]
    lower = lax.broadcasted_iota(jnp.int32, (span, span), 0) >= lax.broadcasted_iota(
        jnp.int32, (span, span), 1
    )
    lower = jnp.where(lower, 1.0, 0.0).astype(BF16)
    running = sum(dot(lower, part.astype(BF16)) for part in split(log_decay, 3))
    total = running[span - 1 : span, :]
    to_end = jnp.exp(total - running) * step
    wide_run = running
    if pad:
        wide_run = jnp.concatenate([running, jnp.zeros((span, pad), F32)], axis=1)
    runt_ref[...] = wide_run.T[:heads]
    for g in range(groups):
        run_ref[g] = running[:, g * per_group : (g + 1) * per_group]
    reach_ref[...] = jnp.concatenate(split(jnp.exp(running), 2), axis=1).astype(BF16)
    end_ref[...] = jnp.concatenate(split(to_end, 2), axis=1).astype(BF16)

    slots = owner_ref.shape[0]
    request = lax.fori_loop(
        0, slots, lambda r, found: jnp.where(owner_ref[r] == here, r, found), jnp.int32(0)
    )
    kept = kept_ref[request]
    candidates = din_ref.shape[0]
    row = lax.broadcasted_iota(jnp.int32, (DRAFTS, candidates), 0)
    col = lax.broadcasted_iota(jnp.int32, (DRAFTS, candidates), 1)
    pick = jnp.zeros((DRAFTS, candidates), F32)
    for i in range(DRAFTS):
        pick = jnp.where((row == i) & (col == ids_ref[i, request]), 1.0, pick)
    pick = pick.astype(BF16)
    vin = dot(pick, din_ref[...])
    vgate = dot(pick, dgate_ref[...])
    vwrite = dot(pick, dwrite_ref[...]).astype(BF16)
    vread = dot(pick, dread_ref[...]).astype(BF16)
    vwrite_ref[...] = vwrite
    vread_ref[...] = vread
    vstep = sum(dot(pick, part.astype(BF16)) for part in split(dstep_ref[...], 3))
    vlog = -vstep * rate_ref[...]
    index = lax.broadcasted_iota(jnp.int32, (DRAFTS, heads), 0)
    acc = jnp.zeros((1, heads), F32)
    vrun = jnp.zeros((DRAFTS, heads), F32)
    reach = jnp.zeros((1, heads), F32)
    for i in range(DRAFTS):
        acc = acc + vlog[i : i + 1]
        vrun = jnp.where(index == i, acc, vrun)
        reach = jnp.where(i < kept, acc, reach)
    others = jnp.where(index == 0, total, jnp.where(index == 1, skip_ref[...], reach))
    stacked = split(jnp.concatenate([vrun, vstep, others], axis=0), 3)
    stacked = jnp.concatenate(stacked, axis=0).astype(BF16)
    row = lax.broadcasted_iota(jnp.int32, (DRAFTS, wide), 0)
    is_owner = owner_ref[0] == here
    for g in range(groups):
        at = slice(g * wide, (g + 1) * wide)
        spread = dot(stacked, head_mask(heads, heads, wide, g * wide))
        spread = spread[0:24] + spread[24:48] + spread[48:72]
        vrun_l, vstep_l = spread[0:8], spread[8:16]
        total_l, skip_l, reach_l = spread[16:17], spread[17:18], spread[18:19]
        skip_out[:, at] = skip_l
        vin_g = vin[:, at]
        vr = vread[:, g * STATE_SIZE : (g + 1) * STATE_SIZE]
        vw = vwrite[:, g * STATE_SIZE : (g + 1) * STATE_SIZE]
        scores = dot(vr, vw, ((1,), (1,)))
        direct = skip_l * vin_g
        for j in range(DRAFTS):
            decay = jnp.exp(jnp.where(row >= j, vrun_l - vrun_l[j : j + 1], -jnp.inf))
            direct = direct + decay * scores[:, j : j + 1] * (vstep_l[j : j + 1] * vin_g[j : j + 1])
        gate = vgate[:, at]
        gate = gate / (1.0 + jnp.exp(-gate))
        q1 = direct * gate
        q2 = jnp.exp(vrun_l) * gate
        q1_ref[:, at] = q1
        q2_ref[:, at] = q2
        live = jnp.exp(jnp.where(row < kept, reach_l - vrun_l, -jnp.inf)) * vstep_l * vin_g
        keep_l = jnp.concatenate(
            split(jnp.exp(reach_l), 3) + [jnp.zeros((5, wide), F32)], axis=0
        )
        tail_ref[:, at] = jnp.concatenate(split(live, 3) + [keep_l], axis=0).astype(BF16)
        read_l = jnp.concatenate([vr.astype(F32)] * (wide // STATE_SIZE), axis=1)
        mine = jnp.concatenate([q1, q2, read_l], axis=0)
        mine = jnp.where(is_owner, mine, 0.0)
        logs = jnp.concatenate(split(total_l, 3) + [jnp.zeros((5, wide), F32)], axis=0)
        extra_ref[:, at] = jnp.concatenate([mine, logs], axis=0).astype(BF16)

    for fetch in fetches[early : early + 2]:
        fetch.wait()
    fill_message(place ^ 1, end_ref, x_ref, write_ref, extra_ref, sent_ref)
    for fetch in fetches[early + 2 :]:
        fetch.wait()


def fill_message(side, end_ref, x_ref, write_ref, extra_ref, out_ref):
    heads = end_ref.shape[1] // 2
    half = out_ref.shape[1]
    wide = 2 * half // (write_ref.shape[1] // STATE_SIZE)
    chunk = min(wide, half)
    start = side * half
    out_ref[STATE_SIZE:, :] = extra_ref[:, window(start, half)]
    for at in range(0, half, chunk):
        lane0 = start + at
        group = lax.div(lane0, wide)
        scale = dot(end_ref[...], head_mask(2 * heads, heads, chunk, lane0))
        weighted = (x_ref[:, window(lane0, chunk)].astype(F32) * scale).astype(BF16)
        writes = write_ref[:, window(group * STATE_SIZE, STATE_SIZE)]
        writes = writes.astype(F32).T.astype(BF16)
        out_ref[:STATE_SIZE, at : at + chunk] = dot(writes, weighted).astype(BF16)


def own_kernel(stage, end_ref, x_ref, write_ref, extra_ref, out_ref):
    fill_message(place_of(stage), end_ref, x_ref, write_ref, extra_ref, out_ref)


def logs_of(block):
    return block[0:1].astype(F32) + block[1:2].astype(F32) + block[2:3].astype(F32)


def weights_of(logs, place, target):
    spots = [place ^ k for k in range(len(logs))]
    found = []
    for k, spot in enumerate(spots):
        between = jnp.zeros_like(logs[0])
        for other, log in zip(spots, logs):
            if other is not spot:
                between = between + jnp.where((spot < other) & (other < target), log, 0.0)
        found.append(jnp.where(spot < target, jnp.exp(between), 0.0))
    return found


def carry_of(logs, place, target):
    ahead = jnp.zeros_like(logs[0])
    for k, log in enumerate(logs):
        ahead = ahead + jnp.where((place ^ k) < target, log, 0.0)
    return jnp.exp(ahead)


def up_kernel(stage, following, count, *refs):
    parts, outs = refs[:count], refs[count:]
    place, target = place_of(stage), place_of(following)
    width = outs[0].shape[1]
    chunk = min(256, width)
    order = list(range(1, len(outs))) + [0]
    for k in order:
        for at in range(0, width, chunk):
            start = at if len(outs) == 1 else (target ^ k) * width + at
            at_in = window(start, chunk)
            logs = [logs_of(part[LOG_AT:UP_ROWS, at_in]) for part in parts]
            scale = weights_of(logs, place, count)
            state = sum(
                w * part[:STATE_SIZE, at_in].astype(F32) for w, part in zip(scale, parts)
            )
            outs[k][:STATE_SIZE, at : at + chunk] = state.astype(BF16)
            mine = sum(part[STATE_SIZE:UP_ROWS, at_in].astype(F32) for part in parts)
            total = jnp.concatenate(
                split(sum(logs), 3) + [jnp.zeros((5, chunk), F32)], axis=0
            )
            outs[k][STATE_SIZE:, at : at + chunk] = jnp.concatenate(
                [mine[:24], total], axis=0
            ).astype(BF16)


def top_kernel(stage, count, *refs):
    parts, outs, prompt_ref = refs[:count], refs[count:-1], refs[-1]
    place = place_of(stage)
    width = prompt_ref.shape[1]
    logs = [logs_of(part[LOG_AT:UP_ROWS, :]) for part in parts]
    states = [part[:STATE_SIZE, :].astype(F32) for part in parts]
    final = sum(w * s for w, s in zip(weights_of(logs, place, count), states)).astype(BF16)
    prompt_ref[...] = final
    mine = sum(part[STATE_SIZE:LOG_AT, :].astype(F32) for part in parts)
    reads = mine[16:24, :STATE_SIZE].astype(BF16)
    gated = mine[0:8] + mine[8:16] * dot(reads, final)
    gated = jnp.concatenate(split(gated, 2), axis=0).astype(BF16)
    for k in list(range(1, len(outs))) + [0]:
        scale = weights_of(logs, place, place ^ k)
        outs[k][:STATE_SIZE, :] = sum(w * s for w, s in zip(scale, states)).astype(BF16)
        outs[k][STATE_SIZE:, :] = gated


def down_kernel(stage, above, above_count, count, targets, handed, *refs):
    pieces, parts = refs[:above_count], refs[above_count : above_count + count]
    outs = refs[above_count + count :]
    if handed:
        outs[-1][...] = outs[0][...]
        outs = outs[1:-1]
    place, source = place_of(stage), place_of(above)
    width = pieces[0].shape[1]
    chunk = min(256, width)
    for k, out_ref in zip(targets, outs):
        for piece in range(above_count):
            for at in range(0, width, chunk):
                start = at if above_count == 1 else (source ^ piece) * width + at
                at_out = window(start, chunk)
                block = pieces[piece][:, at : at + chunk]
                logs = [logs_of(part[LOG_AT:UP_ROWS, at_out]) for part in parts]
                state = carry_of(logs, place, place ^ k) * block[:STATE_SIZE].astype(F32)
                for w, part in zip(weights_of(logs, place, place ^ k), parts):
                    state = state + w * part[:STATE_SIZE, at_out].astype(F32)
                out_ref[:STATE_SIZE, at_out] = state.astype(BF16)
                out_ref[STATE_SIZE:, at_out] = block[STATE_SIZE:]


def intra_kernel(group, run_ref, runt_ref, stept_ref, skip_ref, x_ref, write_ref, read_ref, *refs):
    fetch = None
    out_ref = refs[0]
    if len(refs) > 1:
        source_ref, out_ref, held_ref, sem = refs
        fetch = pltpu.make_async_copy(source_ref, held_ref, sem)
        fetch.start()
    span, heads = run_ref.shape[1:]
    mid = span // 2
    states = slice(group * STATE_SIZE, (group + 1) * STATE_SIZE)
    scores = dot(read_ref[:, states], write_ref[:, states], ((1,), (1,)))
    row = lax.broadcasted_iota(jnp.int32, (mid, mid), 0)
    causal = row >= lax.broadcasted_iota(jnp.int32, (mid, mid), 1)
    running = run_ref[group]
    low, high = slice(0, mid), slice(mid, span)
    for pair in range(heads // 2):
        found = []
        for k in (2 * pair, 2 * pair + 1):
            h = group * heads + k
            x = x_ref[:, h * HEAD_DIM : (h + 1) * HEAD_DIM]
            t_run, j_run = running[:, k : k + 1], runt_ref[h : h + 1, :]
            step = stept_ref[h : h + 1, :]

            def mixed(rows, cols, masked):
                gap = t_run[rows] - j_run[:, cols]
                if masked:
                    gap = jnp.where(causal, gap, -jnp.inf)
                return (scores[rows, cols] * jnp.exp(gap) * step[:, cols]).astype(BF16)

            top = dot(mixed(low, low, True), x[low])
            bottom = dot(mixed(high, low, False), x[low]) + dot(mixed(high, high, True), x[high])
            found.append(jnp.concatenate([top, bottom], axis=0))
        at = slice(pair * 2 * HEAD_DIM, (pair + 1) * 2 * HEAD_DIM)
        lanes = slice((group * heads + 2 * pair) * HEAD_DIM, (group * heads + 2 * pair + 2) * HEAD_DIM)
        both = jnp.concatenate(found, axis=1)
        out_ref[:, at] = both + skip_ref[:, lanes] * x_ref[:, lanes].astype(F32)
    if fetch is not None:
        fetch.wait()


def intra(group, run, runt, stept, skip, x, write, read, after, wanted=()):
    span, per_group = run.shape[1:]
    wide = per_group * HEAD_DIM
    return call(
        functools.partial(intra_kernel, group),
        "intra",
        [shape((span, wide), F32)] + [shape(value.shape, value.dtype) for value in wanted],
        (run, runt, stept, skip, x, write, read, *map(in_hbm, wanted)),
        specs=[WHOLE] * 7 + [IN_HBM] * len(wanted),
        scratch=[pltpu.SemaphoreType.DMA] * len(wanted),
        after=after,
        flops=per_group * span * span * HEAD_DIM * 2,
        moved=wide * span * 6,
        exps=per_group * span * span * 3 // 4,
    )


def finish_kernel(stage, offset, reach_ref, read_ref, entering_ref, *refs):
    base_refs, (out_ref, token_ref, held_ref, sems) = refs[:-4], refs[-4:]
    if offset:
        base_refs = base_refs[:-1]
    token_ref[...] = jnp.zeros_like(token_ref)
    side = place_of(stage) ^ offset
    heads = reach_ref.shape[1] // 2
    half = held_ref.shape[1]
    wide = 2 * half // len(base_refs)
    chunk = half // sems.shape[0]
    copies = []
    for k, at in enumerate(range(0, half, chunk)):
        found = []
        for lane0 in (at, half + at):
            group = lane0 // wide
            found.append(
                (
                    read_ref[:, group * STATE_SIZE : (group + 1) * STATE_SIZE],
                    base_refs[group][:, lane0 % wide : lane0 % wide + chunk],
                )
            )
        reads, base = (jnp.where(side == 0, a, b) for a, b in zip(*found))
        lane0 = side * half + at
        inter = dot(reads, entering_ref[:STATE_SIZE, at : at + chunk])
        inter = inter * dot(reach_ref[...], head_mask(2 * heads, heads, chunk, lane0))
        held_ref[:, at : at + chunk] = (inter + base).astype(BF16)
        copies.append(
            pltpu.make_async_copy(
                held_ref.at[:, at : at + chunk], out_ref.at[:, window(lane0, chunk)], sems.at[k]
            )
        )
        copies[-1].start()
    for copy in copies:
        copy.wait()


def finish(stage, offset, reach, read, entering, bases, out, after):
    span, half = read.shape[0], entering.shape[1]
    chunk = min(512, half)
    args = [reach, read, entering, *bases]
    specs = [WHOLE] * len(args)
    if offset:
        args.append(out)
        specs.append(IN_HBM)
    return call(
        functools.partial(finish_kernel, stage, offset),
        "finish",
        [shape((span, 2 * half), BF16), shape((8, 128), F32)],
        args,
        specs=specs,
        out_specs=[IN_HBM, WHOLE],
        after=after,
        alias={len(args) - 1: 0} if offset else None,
        scratch=[pltpu.VMEM((span, half), BF16), pltpu.SemaphoreType.DMA((half // chunk,))],
        moved=1,
    )


def resident_kernel(state_ref, vread_ref, q1_ref, q2_ref, gain_ref, out_ref):
    groups = vread_ref.shape[1] // STATE_SIZE
    wide = state_ref.shape[0] // groups
    for g in range(groups):
        at = slice(g * wide, (g + 1) * wide)
        reads = vread_ref[:, g * STATE_SIZE : (g + 1) * STATE_SIZE]
        drawn = dot(reads, state_ref[at, :], ((1,), (1,)))
        gated = q1_ref[:, at] + q2_ref[:, at] * drawn
        out_ref[:, at] = normed(gated, gain_ref[:, at]).astype(BF16)


def normed(gated, gain):
    mean_square = jnp.mean(gated * gated, axis=1, keepdims=True)
    return gated * lax.rsqrt(mean_square + EPSILON) * gain


def resident_hidden(state, vread, q1, q2, gain, after):
    lanes = state.shape[0]
    return call(
        resident_kernel,
        "resident_hidden",
        [shape((DRAFTS, lanes), BF16)],
        (state, vread, q1, q2, gain),
        after=after,
        flops=2 * DRAFTS * lanes * STATE_SIZE,
    )[0]


def hand_on(value, after):
    def copy(value_ref, out_ref):
        out_ref[...] = value_ref[...]

    return call(copy, "hand_on", [shape(value.shape, value.dtype)], [value], after=after)[0]


def join_kernel(axis, *refs):
    out_ref = refs[-1]
    for k, ref in enumerate(refs[:-1]):
        size = ref.shape[axis]
        at = slice(k * size, (k + 1) * size)
        if axis == 0:
            out_ref[at, :] = ref[...]
        else:
            out_ref[:, at] = ref[...]


def join(parts, axis, after=()):
    dims = list(parts[0].shape)
    dims[axis] *= len(parts)
    return call(
        functools.partial(join_kernel, axis), "join", [shape(tuple(dims), parts[0].dtype)], parts, after=after, moved=1
    )[0]


def project_kernel(stages, head_count, *refs):
    owner_ref, own_rows, got_rows, own_ref, got_ref, gain_ref, weight_ref = refs[:7]
    outs = refs[7 : 7 + head_count]
    gated_ref, left_ref, total_ref = refs[7 + head_count :]
    here, head = lax.axis_index("seq"), lax.axis_index("head")
    place = place_of(stages[0])
    half = own_ref.shape[1]
    lanes = weight_ref.shape[0]
    wide = min(1024, lanes)
    rows = own_rows.shape[0]
    for k, ref in enumerate((own_ref, got_ref)):
        both = ref[STATE_SIZE:, :].astype(F32)
        gated_ref[:, window((place ^ k) * half, half)] = both[0:8] + both[8:16]
    left_ref[0:rows, :] = own_rows[...]
    left_ref[rows : 2 * rows, :] = got_rows[...]
    for lane0 in range(0, lanes, wide):
        at = slice(lane0, lane0 + wide)
        hidden = normed(gated_ref[:, at], gain_ref[:, at])
        hidden = jnp.concatenate([hidden, jnp.zeros_like(hidden)], axis=0)
        left_ref[2 * rows :, at] = hidden.astype(BF16)
    total_ref[...] = dot(left_ref[...], weight_ref[...])

    per_head = 2 * rows // DRAFTS // head_count
    offsets = [0]
    for factor, stride in reversed(stages):
        offsets = [a + k * stride for k in range(factor) for a in offsets]
    owner = owner_ref[...]
    tail = total_ref[2 * rows : 2 * rows + DRAFTS, :]
    for k in range(head_count):
        first = (head ^ k) * per_head
        for slot in range(per_head):
            at = slice(slot * DRAFTS, (slot + 1) * DRAFTS)
            offset = here ^ (first + slot)
            block = jnp.int32(0)
            for position, value in enumerate(offsets):
                block = jnp.where(offset == value, position, block)
            drawn = total_ref[window(block * DRAFTS, DRAFTS), :]
            outs[k][at, :] = jnp.where(owner == first + slot, tail, drawn)


def project(stages, owner, own_rows, got_rows, own, got, gain, weight, head_count, after):
    lanes, cols = weight.shape
    rows = 2 * own_rows.shape[0]
    return call(
        functools.partial(project_kernel, stages, head_count),
        "project",
        [shape((rows // head_count, cols), F32)] * head_count,
        (owner, own_rows, got_rows, own, got, gain, weight),
        after=after,
        scratch=[
            pltpu.VMEM((DRAFTS, lanes), F32),
            pltpu.VMEM((rows + 16, lanes), BF16),
            pltpu.VMEM((rows + 16, cols), F32),
        ],
        moved=1,
    )


def states_kernel(stage, scattered, offset, *refs):
    owner_ref, resident_ref, prompt_ref, tail_ref, vwrite_ref = refs[:5]
    here = lax.axis_index("seq")
    side = place_of(stage) ^ offset
    if offset:
        other_ref, _, new_ref, slice_ref, turned_ref, held_ref, sems = refs[5:]
    else:
        share_refs, (new_ref, turned_ref, verify_ref, held_ref, sems) = refs[5:-5], refs[-5:]
        verify_ref[...] = sum(ref[...] for ref in share_refs).astype(BF16)
    half = prompt_ref.shape[1]
    wide = 2 * half // (vwrite_ref.shape[1] // STATE_SIZE)
    blocks = [0]
    for factor, stride in scattered:
        blocks = [a | (k * stride) for k in range(factor) for a in blocks]
    width = half // len(blocks)
    chunk = half // sems.shape[0]
    is_owner = owner_ref[0:1, :STATE_SIZE] == here
    row = lax.broadcasted_iota(jnp.int32, (32, STATE_SIZE), 0)
    ones = jnp.where((row >= 24) & (row < 27), 1.0, 0.0)
    copies = []
    for part in range(sems.shape[0]):
        rows = slice(part * chunk, (part + 1) * chunk)
        for lane in range(part * chunk, (part + 1) * chunk, width):
            spot, size, rest = 0, half, lane
            for factor, stride in scattered:
                size = size // factor
                spot |= rest // size * stride
                rest %= size
            apart = (spot ^ here) & sum((factor - 1) * stride for factor, stride in scattered)
            position = jnp.int32(0)
            for place, value in enumerate(blocks):
                position = jnp.where(apart == value, place, position)
            found = prompt_ref[:, window(position * width, width)]
            turned_ref[lane : lane + width, :] = found.astype(F32).T
        groups = [start // wide for start in (part * chunk, half + part * chunk)]
        low, high = (vwrite_ref[:, g * STATE_SIZE : (g + 1) * STATE_SIZE] for g in groups)
        writes = jnp.where(side == 0, low, high).astype(F32)
        writes = jnp.concatenate([writes, writes, writes, jnp.zeros_like(writes)], axis=0)
        right = jnp.concatenate([writes, ones], axis=1).astype(BF16)
        at = window(side * half + part * chunk, chunk)
        left = tail_ref[:, at].astype(F32).T.astype(BF16)
        both = dot(left, right)
        start = jnp.where(is_owner, turned_ref[rows, :], resident_ref[at, :].astype(F32))
        held_ref[rows, :] = (start * both[:, STATE_SIZE:] + both[:, :STATE_SIZE]).astype(BF16)
        copies.append(pltpu.make_async_copy(held_ref.at[rows, :], new_ref.at[at, :], sems.at[part]))
        copies[-1].start()
    if offset:
        per_slice = slice_ref.shape[1] // STATE_SIZE
        heads = slice_ref.shape[0] // 2
        for k in range(per_slice):
            row = pl.ds(here * per_slice + k, heads, stride=HEAD_DIM)
            got, own = turned_ref[row, :], other_ref[row, :]
            low, high = jnp.where(side == 0, got, own), jnp.where(side == 0, own, got)
            at = slice(k * STATE_SIZE, (k + 1) * STATE_SIZE)
            slice_ref[:, at] = jnp.concatenate([low, high], axis=0).astype(BF16)
    for copy in copies:
        copy.wait()


def states(stage, scattered, owner, resident, prompts, tail, vwrite, shares, seq_count):
    lanes = resident.shape[0]
    half = lanes // 2
    chunk = min(512, half)
    args = [owner, resident, prompts[0], tail, vwrite, *shares]
    scratch = [pltpu.VMEM((half, STATE_SIZE), BF16), pltpu.SemaphoreType.DMA((half // chunk,))]
    new, turned, verify = call(
        functools.partial(states_kernel, stage, scattered, 0),
        "states",
        [
            shape((lanes, STATE_SIZE), BF16),
            shape((half, STATE_SIZE), F32),
            shape(shares[0].shape, BF16),
        ],
        args,
        out_specs=[IN_HBM, WHOLE, WHOLE],
        scratch=scratch,
        flops=lanes * STATE_SIZE * 64,
        moved=lanes * STATE_SIZE * 3,
    )
    args = [owner, resident, prompts[1], tail, vwrite, turned, new]
    new, sliced = call(
        functools.partial(states_kernel, stage, scattered, 1),
        "states",
        [
            shape((lanes, STATE_SIZE), BF16),
            shape((lanes // HEAD_DIM, HEAD_DIM // seq_count * STATE_SIZE), BF16),
        ],
        args,
        specs=[WHOLE] * 6 + [IN_HBM],
        out_specs=[IN_HBM, WHOLE],
        alias={6: 0},
        scratch=[pltpu.VMEM((half, STATE_SIZE), F32)] + scratch,
        flops=lanes * STATE_SIZE * 64,
        moved=lanes * STATE_SIZE * 3,
    )
    return new, verify, sliced


def on_device(
    prefill_input,
    prefill_step,
    write_proj,
    read_proj,
    decay_rate,
    skip_gain,
    resident_state,
    owner_slot,
    draft_ids,
    accepted_len,
    draft_input,
    draft_gate,
    draft_write,
    draft_read,
    draft_step,
    norm_gain,
    out_weight,
):
    span, lanes = prefill_input.shape
    assert span == BLOCK_LEN
    heads = decay_rate.shape[0]
    groups = write_proj.shape[1] // STATE_SIZE
    per_group = heads // groups
    half = lanes // 2
    seq_count, head_count = lax.axis_size("seq"), lax.axis_size("head")
    stages = tree_stages(seq_count)
    core, line, last = stages
    slots = owner_slot.shape[0]
    assert core[0] == 2 and slots == seq_count
    rate, skip, gain = decay_rate[None], skip_gain[None], norm_gain[None]
    resident = resident_state.reshape(lanes, STATE_SIZE)

    inputs = (
        prefill_step.T, rate, skip, owner_slot, draft_ids.T, accepted_len, draft_input, draft_gate,
        draft_write, draft_read, draft_step, write_proj, prefill_input, read_proj, resident, gain,
    )
    passed = 5
    inputs = [in_hbm(value) for value in inputs]
    opened = call(
        functools.partial(open_kernel, core, len(inputs), passed),
        "open_block",
        [
            shape((UP_ROWS, half), BF16),
            shape((groups, span, per_group), F32),
            shape((heads, span), F32),
            shape((heads, span), F32),
            shape((span, 2 * heads), BF16),
            shape((span, 2 * heads), BF16),
            shape((1, lanes), F32),
            shape((DRAFTS, lanes), F32),
            shape((DRAFTS, lanes), F32),
            shape((DRAFTS, groups * STATE_SIZE), BF16),
            shape((DRAFTS, groups * STATE_SIZE), BF16),
            shape((32, lanes), BF16),
            shape((DRAFTS, out_weight.shape[1]), jnp.int32),
            shape((EXTRA, lanes), BF16),
        ]
        + [shape(value.shape, value.dtype) for value in inputs[-passed:]],
        inputs,
        specs=[IN_HBM] * len(inputs),
        scratch=[pltpu.SemaphoreType.DMA((len(inputs),))]
        + [
            (pltpu.SMEM if value.dtype == jnp.int32 else pltpu.VMEM)(value.shape, value.dtype)
            for value in inputs[:-passed]
        ],
        flops=2 * span * lanes * STATE_SIZE * 2,
    )
    sent, run, runt, stept, reach, end, skip_lanes, q1, q2, vread, vwrite, tail, owner, extra = opened[:14]
    writes, x, reads, resident, gain = opened[14:]
    received = swap(sent, "seq", core, 1)
    (own,) = call(
        functools.partial(own_kernel, core),
        "own_message",
        [shape((UP_ROWS, half), BF16)],
        (end, x, writes, extra),
        flops=span * lanes * STATE_SIZE * 2,
    )
    core_parts = [own, received]
    hidden = resident_hidden(resident, vread, q1, q2, gain, [own])

    bases, fetched = [], []

    def fill(after):
        if len(bases) < groups:
            wanted = [] if bases else [out_weight]
            base, *found = intra(
                len(bases), run, runt, stept, skip_lanes, x, writes, reads, after, wanted
            )
            bases.append(base)
            fetched.extend(found)
        return bases[-1:]

    def exchange(parts, stage):
        got = {k: swap(parts[k], "seq", stage, k) for k in range(stage[0] - 1, 0, -1)}
        return [parts[0]] + [got[k] for k in range(1, stage[0])]

    line_width = half // line[0]
    split_last = line_width % (last[0] * 128) == 0
    last_width = line_width // last[0] if split_last else line_width
    outs = call(
        functools.partial(up_kernel, core, line, 2),
        "up_line",
        [shape((UP_ROWS, line_width), BF16)] * line[0],
        core_parts,
        after=[hidden],
        flops=half * UP_ROWS * 4,
    )
    line_parts = exchange(outs, line)
    hiddens = exchange([hand_on(hidden, [outs[-1]])] * last[0], last)
    filled = fill([outs[-1]])
    hidden = join(hiddens, 0)
    outs = call(
        functools.partial(up_kernel, line, last, line[0]),
        "up_last",
        [shape((UP_ROWS, last_width), BF16)] * (last[0] if split_last else 1),
        line_parts,
        after=filled + [hidden],
        flops=line_width * UP_ROWS * 4,
    )
    last_parts = exchange(outs if split_last else outs * last[0], last)
    hiddens = exchange([hand_on(hidden, [outs[-1]])] * line[0], line)
    filled = fill([outs[-1]])
    *outs, prompt = call(
        functools.partial(top_kernel, last, last[0]),
        "top",
        [shape((DOWN_ROWS, last_width), BF16)] * (last[0] if split_last else 1)
        + [shape((STATE_SIZE, last_width), BF16)],
        last_parts,
        after=filled,
        flops=last_width * UP_ROWS * 16,
    )

    pieces = exchange(outs, last) if split_last else outs
    hidden = join(hiddens, 0, [outs[-1]])
    filled = fill([outs[-1], hidden])
    prompt = join(exchange([prompt] * line[0], line), 1)
    *outs, prompt = call(
        functools.partial(down_kernel, line, last, len(pieces), line[0], range(line[0]), True),
        "down_line",
        [shape((DOWN_ROWS, line_width), BF16)] * line[0] + [shape(prompt.shape, BF16)],
        [*pieces, *line_parts, prompt],
        after=filled,
        flops=line_width * UP_ROWS * 8,
    )
    pieces = exchange(outs, line)
    filled = fill([outs[-1]])
    scattered = [line, last] if split_last else [line]
    prompts = exchange([prompt] * last[0], last) if split_last else [prompt]
    def down_core(target, after):
        return call(
            functools.partial(down_kernel, core, line, line[0], 2, (target,), False),
            "down_core",
            [shape((DOWN_ROWS, half), BF16)],
            pieces + core_parts,
            after=after,
            moved=1,
        )[0]

    sent = down_core(1, filled + [prompts[k] for k in (1, last[0] - 1) if split_last])
    entering = [down_core(0, [sent]), swap(sent, "seq", core, 1)]
    while len(bases) < groups:
        fill([])

    prefill_out, token = finish(core, 0, reach, reads, entering[0], bases, None, entering[:1])
    shares = project(
        stages, owner, hidden, swap(hidden, "seq", core, 1), *entering, gain, fetched[0], head_count, [token]
    )
    prefill_out, token = finish(
        core, 1, reach, reads, entering[1], bases, prefill_out, [shares[0], token]
    )
    shares = [shares[0]] + [swap(shares[k], "head", (head_count, 1), k) for k in range(1, head_count)]

    prompt = join(prompts, 1, [token, *shares[1:]])
    prompts = exchange([prompt] * 2, core)
    new_state, verify_out, state_slice = states(
        core, scattered, owner, resident, prompts, tail, vwrite, shares, seq_count
    )
    return (
        prefill_out,
        new_state.reshape(1, heads, HEAD_DIM, STATE_SIZE),
        verify_out,
        state_slice,
    )


def solution(mesh):
    return jax.shard_map(
        on_device,
        mesh=mesh,
        in_specs=(
            P("seq", "head"),
            P("seq", "head"),
            P("seq", "head"),
            P("seq", "head"),
            P("head"),
            P("head"),
            P("seq", "head", None, None),
            P(),
            P(),
            P(),
            P("seq", "head"),
            P("seq", "head"),
            P("seq", "head"),
            P("seq", "head"),
            P("seq", "head"),
            P("head"),
            P("head", "seq"),
        ),
        out_specs=(
            P("seq", "head"),
            P("seq", "head", None, None),
            P("head", "seq"),
            P("head", "seq"),
        ),
        check_vma=False,
    )
```

profile of v0, /device:TPU:0, one launch (start us, length us, event | category | flops | bytes accessed | tf_op | source)
XLA Modules:
  0.0 64.3 jit_solution(2151852675178018551)
XLA Ops:
  0.6 3.7 %open_block.1 = (bf16[160,2048]{1,0:T(8,128)(2,1)S(1)}, f32[4,256,16]{2,1,0:T(8,128)S(1)}, f32[64,256]{1,0:T(8,128)S(1)}, f32[64,256]{1,0:T(8,128)S(1)}, bf16[25...) custom-call(f32[64,256]{1,0:T(8,128)} %bitcast.9, ...), custom_call_target="tpu_custom_call" | custom-call | flops 536870912 | bytes 9557120 | tf_op jit(solution)/shard_map/open_block/pallas_call | solution.py:95
  6.9 3.0 %collective-permute-start.4 = (bf16[160,1024]{1,0:T(8,128)(2,1)S(1)}, bf16[160,1024]{1,0:T(8,128)(2,1)S(1)}, u32[]{:S(2)}, u32[]{:S(2)}) collective-permute-start(bf16[160,1024]{1,0:T(8,128)(2,1)S(1)} %get-tuple-element.60.refs_0_), channel_id=1, source_target_pairs={{0,4},{2,6},{4,0},{6,2},{8,12},{10,14},{12,8},{14,10},{16,20},{18,... | collective-permute-start | bytes 983048 | tf_op jit(solution)/shard_map/ppermute | solution.py:44
  9.8 1.6 %collective-permute-start.1 = (bf16[8,4096]{1,0:T(8,128)(2,1)S(1)}, bf16[8,4096]{1,0:T(8,128)(2,1)S(1)}, u32[]{:S(2)}, u32[]{:S(2)}) collective-permute-start(bf16[8,4096]{1,0:T(8,128)(2,1)S(1)} %hand_on.2.refs_0_), channel_id=1, source_target_pairs={{0,8},{2,10},{4,12},{6,14},{8,0},{10,2},{12,4},{14,6},{16,24},{18,... | collective-permute-start | bytes 196616 | tf_op jit(solution)/shard_map/ppermute | solution.py:44
  11.4 2.6 %collective-permute-start.2 = (bf16[8,4096]{1,0:T(8,128)(2,1)S(1)}, bf16[8,4096]{1,0:T(8,128)(2,1)S(1)}, u32[]{:S(2)}, u32[]{:S(2)}) collective-permute-start(bf16[8,4096]{1,0:T(8,128)(2,1)S(1)} %hand_on.2.refs_0_), channel_id=1, source_target_pairs={{0,16},{2,18},{4,20},{6,22},{8,24},{10,26},{12,28},{14,30},{16,0},... | collective-permute-start | bytes 196616 | tf_op jit(solution)/shard_map/ppermute | solution.py:44
  14.2 3.6 %intra.4 = (f32[256,1024]{1,0:T(8,128)S(1)}, bf16[4096,512]{1,0:T(8,128)(2,1)S(1)}) custom-call(bf16[160,1024]{1,0:T(8,128)(2,1)S(1)} %get-tuple-element.60.refs_0_, f32[4,256,16]{2,1,0:T(8,128)S(1)} %get-tuple-element.61.refs_1_.refs_2_, f32[64,256]{1,0:T(8,128)S(1)} %get-tuple-element.62.refs_2_.refs_3_, f32[64,256]{1,0:T(8,128)S(1)} %get-tuple-element.63.refs_3_.refs_4_, ...), custom_call_target="tpu_custom_call" | custom-call | flops 134217728 | bytes 1572864 | tf_op jit(solution)/shard_map/intra/pallas_call | solution.py:95
  18.7 1.4 %collective-permute-done.3.refs_3_ = bf16[8,4096]{1,0:T(8,128)(2,1)S(1)} collective-permute-done((bf16[8,4096]{1,0:T(8,128)(2,1)S(1)}, bf16[8,4096]{1,0:T(8,128)(2,1)S(1)}, u32[]{:S(2)}, u32[]{:S(2)}) %collective-permute-start.3) | collective-permute-done | bytes 65568 | tf_op jit(solution)/shard_map/ppermute | solution.py:44
  21.4 2.6 %collective-permute-start.6 = (bf16[160,256]{1,0:T(8,128)(2,1)S(1)}, bf16[160,256]{1,0:T(8,128)(2,1)S(1)}, u32[]{:S(2)}, u32[]{:S(2)}) collective-permute-start(bf16[160,256]{1,0:T(8,128)(2,1)S(1)} %get-tuple-element.71), channel_id=1, source_target_pairs={{0,16},{2,18},{4,20},{6,22},{8,24},{10,26},{12,28},{14,30},{16,0},... | collective-permute-start | bytes 245768 | tf_op jit(solution)/shard_map/ppermute | solution.py:44
  24.0 1.3 %collective-permute-start.7 = (bf16[160,256]{1,0:T(8,128)(2,1)S(1)}, bf16[160,256]{1,0:T(8,128)(2,1)S(1)}, u32[]{:S(2)}, u32[]{:S(2)}) collective-permute-start(bf16[160,256]{1,0:T(8,128)(2,1)S(1)} %get-tuple-element.68.refs_0_), channel_id=1, source_target_pairs={{0,24},{2,26},{4,28},{6,30},{8,16},{10,18},{12,20},{14,22},{16,8},... | collective-permute-start | bytes 245768 | tf_op jit(solution)/shard_map/ppermute | solution.py:44
  25.3 1.7 %intra.5.refs_0_.refs_5_.refs_6_ = f32[256,1024]{1,0:T(8,128)S(1)} custom-call(bf16[160,256]{1,0:T(8,128)(2,1)S(1)} %get-tuple-element.68.refs_0_, f32[4,256,16]{2,1,0:T(8,128)S(1)} %get-tuple-element.61.refs_1_.refs_2_, f32[64,256]{1,0:T(8,128)S(1)} %get-tuple-element.62.refs_2_.refs_3_, f32[64,256]{1,0:T(8,128)S(1)} %get-tuple-element.63.refs_3_.refs_4_, ...), custom_call_target="tpu_custom_call" | custom-call | flops 134217728 | bytes 1572864 | tf_op jit(solution)/shard_map/intra/pallas_call | solution.py:95
  27.0 1.9 %collective-permute-done.6.refs_3_ = bf16[160,256]{1,0:T(8,128)(2,1)S(1)} collective-permute-done((bf16[160,256]{1,0:T(8,128)(2,1)S(1)}, bf16[160,256]{1,0:T(8,128)(2,1)S(1)}, u32[]{:S(2)}, u32[]{:S(2)}) %collective-permute-start.6) | collective-permute-done | bytes 81952 | tf_op jit(solution)/shard_map/ppermute | solution.py:44
  28.9 1.4 %collective-permute-done.7.refs_4_ = bf16[160,256]{1,0:T(8,128)(2,1)S(1)} collective-permute-done((bf16[160,256]{1,0:T(8,128)(2,1)S(1)}, bf16[160,256]{1,0:T(8,128)(2,1)S(1)}, u32[]{:S(2)}, u32[]{:S(2)}) %collective-permute-start.7) | collective-permute-done | bytes 81952 | tf_op jit(solution)/shard_map/ppermute | solution.py:44
  31.5 2.4 %collective-permute-start.10 = (bf16[144,256]{1,0:T(8,128)(2,1)S(1)}, bf16[144,256]{1,0:T(8,128)(2,1)S(1)}, u32[]{:S(2)}, u32[]{:S(2)}) collective-permute-start(bf16[144,256]{1,0:T(8,128)(2,1)S(1)} %get-tuple-element.75), channel_id=1, source_target_pairs={{0,16},{2,18},{4,20},{6,22},{8,24},{10,26},{12,28},{14,30},{16,0},... | collective-permute-start | bytes 221192 | tf_op jit(solution)/shard_map/ppermute | solution.py:44
  35.1 1.7 %intra.6.refs_0_.refs_6_.refs_7_ = f32[256,1024]{1,0:T(8,128)S(1)} custom-call(bf16[144,256]{1,0:T(8,128)(2,1)S(1)} %get-tuple-element.72.refs_0_, bf16[64,4096]{1,0:T(8,128)(2,1)S(1)} %join.5.refs_1_.refs_2_, f32[4,256,16]{2,1,0:T(8,128)S(1)} %get-tuple-element.61.refs_1_.refs_2_, f32[64,256]{1,0:T(8,128)S(1)} %get-tuple-element.62.refs_2_.refs_3_, ...), custom_call_target="tpu_custom_call" | custom-call | flops 134217728 | bytes 1572864 | tf_op jit(solution)/shard_map/intra/pallas_call | solution.py:95
  37.3 2.8 %collective-permute-done.11.refs_4_ = bf16[144,256]{1,0:T(8,128)(2,1)S(1)} collective-permute-done((bf16[144,256]{1,0:T(8,128)(2,1)S(1)}, bf16[144,256]{1,0:T(8,128)(2,1)S(1)}, u32[]{:S(2)}, u32[]{:S(2)}) %collective-permute-start.11) | collective-permute-done | bytes 73760 | tf_op jit(solution)/shard_map/ppermute | solution.py:44
  41.8 2.2 %collective-permute-start.14 = (bf16[128,512]{1,0:T(8,128)(2,1)S(1)}, bf16[128,512]{1,0:T(8,128)(2,1)S(1)}, u32[]{:S(2)}, u32[]{:S(2)}) collective-permute-start(bf16[128,512]{1,0:T(8,128)(2,1)S(1)} %get-tuple-element.78.refs_2_), channel_id=1, source_target_pairs={{0,24},{2,26},{4,28},{6,30},{8,16},{10,18},{12,20},{14,22},{16,8},... | collective-permute-start | bytes 393224 | tf_op jit(solution)/shard_map/ppermute | solution.py:44
  44.0 1.7 %intra.7.refs_0_.refs_7_.refs_8_ = f32[256,1024]{1,0:T(8,128)S(1)} custom-call(bf16[144,1024]{1,0:T(8,128)(2,1)S(1)} %get-tuple-element.77.refs_0_, f32[4,256,16]{2,1,0:T(8,128)S(1)} %get-tuple-element.61.refs_1_.refs_2_, f32[64,256]{1,0:T(8,128)S(1)} %get-tuple-element.62.refs_2_.refs_3_, f32[64,256]{1,0:T(8,128)S(1)} %get-tuple-element.63.refs_3_.refs_4_, ...), custom_call_target="tpu_custom_call" | custom-call | flops 134217728 | bytes 1572864 | tf_op jit(solution)/shard_map/intra/pallas_call | solution.py:95
  46.7 1.9 %collective-permute-done.14.refs_2_.refs_5_ = bf16[128,512]{1,0:T(8,128)(2,1)S(1)} collective-permute-done((bf16[128,512]{1,0:T(8,128)(2,1)S(1)}, bf16[128,512]{1,0:T(8,128)(2,1)S(1)}, u32[]{:S(2)}, u32[]{:S(2)}) %collective-permute-start.14) | collective-permute-done | bytes 131104 | tf_op jit(solution)/shard_map/ppermute | solution.py:44
  49.6 2.1 %collective-permute-start.19 = (bf16[128,512]{1,0:T(8,128)(2,1)S(1)}, bf16[128,512]{1,0:T(8,128)(2,1)S(1)}, u32[]{:S(2)}, u32[]{:S(2)}) collective-permute-start(bf16[128,512]{1,0:T(8,128)(2,1)S(1)} %get-tuple-element.78.refs_2_), channel_id=1, source_target_pairs={{0,16},{2,18},{4,20},{6,22},{8,24},{10,26},{12,28},{14,30},{16,0},... | collective-permute-start | bytes 393224 | tf_op jit(solution)/shard_map/ppermute | solution.py:44
  52.2 1.6 %finish.2 = (bf16[256,4096]{1,0:T(8,128)(2,1)}, f32[8,128]{1,0:T(8,128)S(1)}) custom-call(bf16[144,2048]{1,0:T(8,128)(2,1)S(1)} %down_core.3.refs_0_.refs_3_.refs_4_, bf16[256,128]{1,0:T(8,128)(2,1)S(1)} %get-tuple-element.80.refs_1_.refs_2_, bf16[256,512]{1,0:T(8,128)(2,1)S(1)} %get-tuple-element.65.refs_7_.refs_8_.refs_2_.refs_3_, ...), custom_call_target="tpu_custom_call" | custom-call | bytes 1 | tf_op jit(solution)/shard_map/finish/pallas_call | solution.py:95
  56.0 1.6 %finish.3 = (bf16[256,4096]{1,0:T(8,128)(2,1)}, f32[8,128]{1,0:T(8,128)S(1)}) custom-call(f32[64,512]{1,0:T(8,128)S(1)} %get-tuple-element.84.refs_0_.refs_5_, f32[8,128]{1,0:T(8,128)S(1)} %get-tuple-element.81.refs_0_.refs_1_, bf16[256,128]{1,0:T(8,128)(2,1)S(1)} %get-tuple-element.80.refs_1_.refs_2_, ...), custom_call_target="tpu_custom_call", output_to_operand_aliasing={{0}: (9, {})} | custom-call | bytes 1 | tf_op jit(solution)/shard_map/finish/pallas_call | solution.py:95
  57.6 1.2 %collective-permute-done.19.refs_4_ = bf16[128,512]{1,0:T(8,128)(2,1)S(1)} collective-permute-done((bf16[128,512]{1,0:T(8,128)(2,1)S(1)}, bf16[128,512]{1,0:T(8,128)(2,1)S(1)}, u32[]{:S(2)}, u32[]{:S(2)}) %collective-permute-start.19) | collective-permute-done | bytes 131104 | tf_op jit(solution)/shard_map/ppermute | solution.py:44
  58.8 1.4 %collective-permute-done.18.refs_1_.refs_6_ = f32[64,512]{1,0:T(8,128)S(1)} collective-permute-done((f32[64,512]{1,0:T(8,128)S(1)}, f32[64,512]{1,0:T(8,128)S(1)}, u32[]{:S(2)}, u32[]{:S(2)}) %collective-permute-start.18) | collective-permute-done | bytes 131104 | tf_op jit(solution)/shard_map/ppermute | solution.py:44
  60.3 1.9 %states.2 = (bf16[4096,128]{1,0:T(8,128)(2,1)}, f32[2048,128]{1,0:T(8,128)S(1)}, bf16[64,512]{1,0:T(8,128)(2,1)}) custom-call(s32[8,512]{1,0:T(8,128)S(1)} %get-tuple-element.82.refs_1_.refs_0_, bf16[4096,128]{1,0:T(8,128)(2,1)S(1)} %get-tuple-element.54.refs_1_, bf16[128,2048]{1,0:T(8,128)(2,1)S(1)} %join.7.refs_2_, ...), custom_call_target="tpu_custom_call" | custom-call | flops 33554432 | bytes 1572864 | tf_op jit(solution)/shard_map/states/pallas_call | solution.py:95
  62.2 1.9 %states.3 = (bf16[4096,128]{1,0:T(8,128)(2,1)}, bf16[64,512]{1,0:T(8,128)(2,1)}) custom-call(s32[8,512]{1,0:T(8,128)S(1)} %get-tuple-element.82.refs_1_.refs_0_, bf16[4096,128]{1,0:T(8,128)(2,1)S(1)} %get-tuple-element.54.refs_1_, bf16[128,2048]{1,0:T(8,128)(2,1)S(1)} %collective-permute-done.20.refs_2_, ...), custom_call_target="tpu_custom_call", output_to_operand_aliasing={{0}: (6, {})} | custom-call | flops 33554432 | bytes 1572864 | tf_op jit(solution)/shard_map/states/pallas_call | solution.py:95
  (42 shorter events, 14.1 us)
Async XLA Ops:
  4.3 2.2 %collective-permute-start = (bf16[160,2048]{1,0:T(8,128)(2,1)S(1)}, bf16[160,2048]{1,0:T(8,128)(2,1)S(1)}, u32[]{:S(2)}, u32[]{:S(2)}) collective-permute-start(bf16[160,2048]{1,0:T(8,128)(2,1)S(1)} %get-tuple-element.59), channel_id=1, source_target_pairs={{0,2},{2,0},{4,6},{6,4},{8,10},{10,8},{12,14},{14,12},{16,18},{18,... | collective-permute-start | bytes 1966088 | tf_op jit(solution)/shard_map/ppermute | solution.py:44
  6.9 13.2 %collective-permute-start.4 = (bf16[160,1024]{1,0:T(8,128)(2,1)S(1)}, bf16[160,1024]{1,0:T(8,128)(2,1)S(1)}, u32[]{:S(2)}, u32[]{:S(2)}) collective-permute-start(bf16[160,1024]{1,0:T(8,128)(2,1)S(1)} %get-tuple-element.60.refs_0_), channel_id=1, source_target_pairs={{0,4},{2,6},{4,0},{6,2},{8,12},{10,14},{12,8},{14,10},{16,20},{18,... | collective-permute-start | bytes 983048 | tf_op jit(solution)/shard_map/ppermute | solution.py:44
  9.8 8.0 %collective-permute-start.1 = (bf16[8,4096]{1,0:T(8,128)(2,1)S(1)}, bf16[8,4096]{1,0:T(8,128)(2,1)S(1)}, u32[]{:S(2)}, u32[]{:S(2)}) collective-permute-start(bf16[8,4096]{1,0:T(8,128)(2,1)S(1)} %hand_on.2.refs_0_), channel_id=1, source_target_pairs={{0,8},{2,10},{4,12},{6,14},{8,0},{10,2},{12,4},{14,6},{16,24},{18,... | collective-permute-start | bytes 196616 | tf_op jit(solution)/shard_map/ppermute | solution.py:44
  11.4 7.3 %collective-permute-start.2 = (bf16[8,4096]{1,0:T(8,128)(2,1)S(1)}, bf16[8,4096]{1,0:T(8,128)(2,1)S(1)}, u32[]{:S(2)}, u32[]{:S(2)}) collective-permute-start(bf16[8,4096]{1,0:T(8,128)(2,1)S(1)} %hand_on.2.refs_0_), channel_id=1, source_target_pairs={{0,16},{2,18},{4,20},{6,22},{8,24},{10,26},{12,28},{14,30},{16,0},... | collective-permute-start | bytes 196616 | tf_op jit(solution)/shard_map/ppermute | solution.py:44
  14.0 6.1 %collective-permute-start.3 = (bf16[8,4096]{1,0:T(8,128)(2,1)S(1)}, bf16[8,4096]{1,0:T(8,128)(2,1)S(1)}, u32[]{:S(2)}, u32[]{:S(2)}) collective-permute-start(bf16[8,4096]{1,0:T(8,128)(2,1)S(1)} %hand_on.2.refs_0_), channel_id=1, source_target_pairs={{0,24},{2,26},{4,28},{6,30},{8,16},{10,18},{12,20},{14,22},{16,8},... | collective-permute-start | bytes 196616 | tf_op jit(solution)/shard_map/ppermute | solution.py:44
  20.3 14.7 %collective-permute-start.8 = (bf16[32,4096]{1,0:T(8,128)(2,1)S(1)}, bf16[32,4096]{1,0:T(8,128)(2,1)S(1)}, u32[]{:S(2)}, u32[]{:S(2)}) collective-permute-start(bf16[32,4096]{1,0:T(8,128)(2,1)S(1)} %hand_on.3.refs_1_), channel_id=1, source_target_pairs={{0,4},{2,6},{4,0},{6,2},{8,12},{10,14},{12,8},{14,10},{16,20},{18,... | collective-permute-start | bytes 786440 | tf_op jit(solution)/shard_map/ppermute | solution.py:44
  20.9 6.1 %collective-permute-start.5 = (bf16[160,256]{1,0:T(8,128)(2,1)S(1)}, bf16[160,256]{1,0:T(8,128)(2,1)S(1)}, u32[]{:S(2)}, u32[]{:S(2)}) collective-permute-start(bf16[160,256]{1,0:T(8,128)(2,1)S(1)} %get-tuple-element.70), channel_id=1, source_target_pairs={{0,8},{2,10},{4,12},{6,14},{8,0},{10,2},{12,4},{14,6},{16,24},{18,... | collective-permute-start | bytes 245768 | tf_op jit(solution)/shard_map/ppermute | solution.py:44
  21.4 7.5 %collective-permute-start.6 = (bf16[160,256]{1,0:T(8,128)(2,1)S(1)}, bf16[160,256]{1,0:T(8,128)(2,1)S(1)}, u32[]{:S(2)}, u32[]{:S(2)}) collective-permute-start(bf16[160,256]{1,0:T(8,128)(2,1)S(1)} %get-tuple-element.71), channel_id=1, source_target_pairs={{0,16},{2,18},{4,20},{6,22},{8,24},{10,26},{12,28},{14,30},{16,0},... | collective-permute-start | bytes 245768 | tf_op jit(solution)/shard_map/ppermute | solution.py:44
  24.0 6.3 %collective-permute-start.7 = (bf16[160,256]{1,0:T(8,128)(2,1)S(1)}, bf16[160,256]{1,0:T(8,128)(2,1)S(1)}, u32[]{:S(2)}, u32[]{:S(2)}) collective-permute-start(bf16[160,256]{1,0:T(8,128)(2,1)S(1)} %get-tuple-element.68.refs_0_), channel_id=1, source_target_pairs={{0,24},{2,26},{4,28},{6,30},{8,16},{10,18},{12,20},{14,22},{16,8},... | collective-permute-start | bytes 245768 | tf_op jit(solution)/shard_map/ppermute | solution.py:44
  30.7 4.4 %collective-permute-start.12 = (bf16[128,256]{1,0:T(8,128)(2,1)S(1)}, bf16[128,256]{1,0:T(8,128)(2,1)S(1)}, u32[]{:S(2)}, u32[]{:S(2)}) collective-permute-start(bf16[128,256]{1,0:T(8,128)(2,1)S(1)} %get-tuple-element.76.refs_0_), channel_id=1, source_target_pairs={{0,4},{2,6},{4,0},{6,2},{8,12},{10,14},{12,8},{14,10},{16,20},{18,... | collective-permute-start | bytes 196616 | tf_op jit(solution)/shard_map/ppermute | solution.py:44
  31.5 5.8 %collective-permute-start.10 = (bf16[144,256]{1,0:T(8,128)(2,1)S(1)}, bf16[144,256]{1,0:T(8,128)(2,1)S(1)}, u32[]{:S(2)}, u32[]{:S(2)}) collective-permute-start(bf16[144,256]{1,0:T(8,128)(2,1)S(1)} %get-tuple-element.75), channel_id=1, source_target_pairs={{0,16},{2,18},{4,20},{6,22},{8,24},{10,26},{12,28},{14,30},{16,0},... | collective-permute-start | bytes 221192 | tf_op jit(solution)/shard_map/ppermute | solution.py:44
  33.8 6.3 %collective-permute-start.11 = (bf16[144,256]{1,0:T(8,128)(2,1)S(1)}, bf16[144,256]{1,0:T(8,128)(2,1)S(1)}, u32[]{:S(2)}, u32[]{:S(2)}) collective-permute-start(bf16[144,256]{1,0:T(8,128)(2,1)S(1)} %get-tuple-element.72.refs_0_), channel_id=1, source_target_pairs={{0,24},{2,26},{4,28},{6,30},{8,16},{10,18},{12,20},{14,22},{16,8},... | collective-permute-start | bytes 221192 | tf_op jit(solution)/shard_map/ppermute | solution.py:44
  35.0 5.4 %collective-permute-start.9 = (bf16[144,256]{1,0:T(8,128)(2,1)S(1)}, bf16[144,256]{1,0:T(8,128)(2,1)S(1)}, u32[]{:S(2)}, u32[]{:S(2)}) collective-permute-start(bf16[144,256]{1,0:T(8,128)(2,1)S(1)} %get-tuple-element.74), channel_id=1, source_target_pairs={{0,8},{2,10},{4,12},{6,14},{8,0},{10,2},{12,4},{14,6},{16,24},{18,... | collective-permute-start | bytes 221192 | tf_op jit(solution)/shard_map/ppermute | solution.py:44
  40.8 7.9 %collective-permute-start.15 = (bf16[144,1024]{1,0:T(8,128)(2,1)S(1)}, bf16[144,1024]{1,0:T(8,128)(2,1)S(1)}, u32[]{:S(2)}, u32[]{:S(2)}) collective-permute-start(bf16[144,1024]{1,0:T(8,128)(2,1)S(1)} %get-tuple-element.77.refs_0_), channel_id=1, source_target_pairs={{0,4},{2,6},{4,0},{6,2},{8,12},{10,14},{12,8},{14,10},{16,20},{18,... | collective-permute-start | bytes 884744 | tf_op jit(solution)/shard_map/ppermute | solution.py:44
  41.8 5.0 %collective-permute-start.13 = (bf16[128,512]{1,0:T(8,128)(2,1)S(1)}, bf16[128,512]{1,0:T(8,128)(2,1)S(1)}, u32[]{:S(2)}, u32[]{:S(2)}) collective-permute-start(bf16[128,512]{1,0:T(8,128)(2,1)S(1)} %get-tuple-element.78.refs_2_), channel_id=1, source_target_pairs={{0,8},{2,10},{4,12},{6,14},{8,0},{10,2},{12,4},{14,6},{16,24},{18,... | collective-permute-start | bytes 393224 | tf_op jit(solution)/shard_map/ppermute | solution.py:44
  41.8 6.9 %collective-permute-start.14 = (bf16[128,512]{1,0:T(8,128)(2,1)S(1)}, bf16[128,512]{1,0:T(8,128)(2,1)S(1)}, u32[]{:S(2)}, u32[]{:S(2)}) collective-permute-start(bf16[128,512]{1,0:T(8,128)(2,1)S(1)} %get-tuple-element.78.refs_2_), channel_id=1, source_target_pairs={{0,24},{2,26},{4,28},{6,30},{8,16},{10,18},{12,20},{14,22},{16,8},... | collective-permute-start | bytes 393224 | tf_op jit(solution)/shard_map/ppermute | solution.py:44
  49.0 4.7 %collective-permute-start.17 = (bf16[144,2048]{1,0:T(8,128)(2,1)S(1)}, bf16[144,2048]{1,0:T(8,128)(2,1)S(1)}, u32[]{:S(2)}, u32[]{:S(2)}) collective-permute-start(bf16[144,2048]{1,0:T(8,128)(2,1)S(1)} %down_core.2.refs_0_), channel_id=1, source_target_pairs={{0,2},{2,0},{4,6},{6,4},{8,10},{10,8},{12,14},{14,12},{16,18},{18,... | collective-permute-start | bytes 1769480 | tf_op jit(solution)/shard_map/ppermute | solution.py:44
  49.1 4.6 %collective-permute-start.16 = (bf16[64,4096]{1,0:T(8,128)(2,1)S(1)}, bf16[64,4096]{1,0:T(8,128)(2,1)S(1)}, u32[]{:S(2)}, u32[]{:S(2)}) collective-permute-start(bf16[64,4096]{1,0:T(8,128)(2,1)S(1)} %join.5.refs_1_.refs_2_), channel_id=1, source_target_pairs={{0,2},{2,0},{4,6},{6,4},{8,10},{10,8},{12,14},{14,12},{16,18},{18,... | collective-permute-start | bytes 1572872 | tf_op jit(solution)/shard_map/ppermute | solution.py:44
  49.6 9.2 %collective-permute-start.19 = (bf16[128,512]{1,0:T(8,128)(2,1)S(1)}, bf16[128,512]{1,0:T(8,128)(2,1)S(1)}, u32[]{:S(2)}, u32[]{:S(2)}) collective-permute-start(bf16[128,512]{1,0:T(8,128)(2,1)S(1)} %get-tuple-element.78.refs_2_), channel_id=1, source_target_pairs={{0,16},{2,18},{4,20},{6,22},{8,24},{10,26},{12,28},{14,30},{16,0},... | collective-permute-start | bytes 393224 | tf_op jit(solution)/shard_map/ppermute | solution.py:44
  54.9 5.3 %collective-permute-start.18 = (f32[64,512]{1,0:T(8,128)S(1)}, f32[64,512]{1,0:T(8,128)S(1)}, u32[]{:S(2)}, u32[]{:S(2)}) collective-permute-start(f32[64,512]{1,0:T(8,128)S(1)} %get-tuple-element.88), channel_id=1, source_target_pairs={{0,1},{1,0},{2,3},{3,2},{4,5},{5,4},{6,7},{7,6},{8,9},{9,8},{10,11... | collective-permute-start | bytes 393224 | tf_op jit(solution)/shard_map/ppermute | solution.py:44
  60.2 2.0 %collective-permute-start.20 = (bf16[128,2048]{1,0:T(8,128)(2,1)S(1)}, bf16[128,2048]{1,0:T(8,128)(2,1)S(1)}, u32[]{:S(2)}, u32[]{:S(2)}) collective-permute-start(bf16[128,2048]{1,0:T(8,128)(2,1)S(1)} %join.7.refs_2_), channel_id=1, source_target_pairs={{0,2},{2,0},{4,6},{6,4},{8,10},{10,8},{12,14},{14,12},{16,18},{18,... | collective-permute-start | bytes 1572872 | tf_op jit(solution)/shard_map/ppermute | solution.py:44
where the time goes:
time: 64.5 us; the launch traced here: 64.3 us
  starting transfers between devices  24.4 us (38%)
  Pallas kernels  23.7 us (37%)
  waiting for transfers between devices  15.2 us (24%)
  between operations  1.02 us (2%)
    ppermute x21, starting transfers between devices, swap(): lax.ppermute(value, axis, [(k, k ^ offset * stride) for k in range(count)])  24.4 us
    pallas_call x24, Pallas kernels, call(): pl.pallas_call(ordered(kernel, first), name=name, grid=grid, out_shape=ou...  23.7 us
    ppermute x21, waiting for transfers between devices, swap(): lax.ppermute(value, axis, [(k, k ^ offset * stride) for k in range(count)])  15.2 us
  transfers between devices with their start and end apart: 21, of which 12 were waited for; matrix products, arithmetic and copies ran while one was open for 0% of the time, Pallas kernels for 26%

commit v1 on v0

--- a/solution.py
+++ b/solution.py
@@ -116,10 +116,9 @@
 
 def open_kernel(stage, count, passed, *refs):
     sources, rest = refs[:count], refs[count:]
-    outs, scratch = rest[: 14 + passed], rest[14 + passed :]
-    outs, later = outs[:14], list(outs[14:])
-    sent_ref, run_ref, runt_ref, stept_ref, reach_ref, end_ref, skip_out = outs[:7]
-    q1_ref, q2_ref, vread_ref, vwrite_ref, tail_ref, owner_out, extra_ref = outs[7:]
+    outs, scratch = rest[: 9 + passed], rest[9 + passed :]
+    outs, later = outs[:9], list(outs[9:])
+    sent_ref, run_ref, runt_ref, stept_ref, reach_ref, end_ref, pick_ref, kept_out, owner_out = outs
     sems, held = scratch[0], [*scratch[1:], *later]
     fetches = [
         pltpu.make_async_copy(source, target, sems.at[k])
@@ -130,16 +129,12 @@
     early = count - passed
     for fetch in fetches[:early]:
         fetch.wait()
-    turned_ref, rate_ref, skip_ref, owner_ref, ids_ref, kept_ref = held[:6]
-    din_ref, dgate_ref, dwrite_ref, dread_ref, dstep_ref, write_ref, x_ref = held[6:13]
+    turned_ref, rate_ref, owner_ref, ids_ref, kept_ref, write_ref, x_ref = held[:7]
     heads, span = turned_ref.shape
-    lanes = x_ref.shape[1]
     groups = write_ref.shape[1] // STATE_SIZE
     per_group = heads // groups
-    wide = per_group * HEAD_DIM
     here = lax.axis_index("seq")
     place = place_of(stage)
-    owner_out[...] = jnp.zeros(owner_out.shape, jnp.int32) + owner_ref[0]
 
     step_rows = turned_ref[...]
     stept_ref[...] = step_rows
@@ -153,8 +148,13 @@
     )
     lower = jnp.where(lower, 1.0, 0.0).astype(BF16)
     running = sum(dot(lower, part.astype(BF16)) for part in split(log_decay, 3))
-    total = running[span - 1 : span, :]
-    to_end = jnp.exp(total - running) * step
+    to_end = jnp.exp(running[span - 1 : span, :] - running) * step
+    end_ref[...] = jnp.concatenate(split(to_end, 2), axis=1).astype(BF16)
+
+    for fetch in fetches[early : early + 2]:
+        fetch.wait()
+    fill_message(place ^ 1, end_ref, x_ref, write_ref, sent_ref)
+
     wide_run = running
     if pad:
         wide_run = jnp.concatenate([running, jnp.zeros((span, pad), F32)], axis=1)
@@ -162,20 +162,53 @@
     for g in range(groups):
         run_ref[g] = running[:, g * per_group : (g + 1) * per_group]
     reach_ref[...] = jnp.concatenate(split(jnp.exp(running), 2), axis=1).astype(BF16)
-    end_ref[...] = jnp.concatenate(split(to_end, 2), axis=1).astype(BF16)
 
     slots = owner_ref.shape[0]
     request = lax.fori_loop(
         0, slots, lambda r, found: jnp.where(owner_ref[r] == here, r, found), jnp.int32(0)
     )
-    kept = kept_ref[request]
-    candidates = din_ref.shape[0]
-    row = lax.broadcasted_iota(jnp.int32, (DRAFTS, candidates), 0)
-    col = lax.broadcasted_iota(jnp.int32, (DRAFTS, candidates), 1)
-    pick = jnp.zeros((DRAFTS, candidates), F32)
+    row = lax.broadcasted_iota(jnp.int32, pick_ref.shape, 0)
+    col = lax.broadcasted_iota(jnp.int32, pick_ref.shape, 1)
+    pick = jnp.zeros(pick_ref.shape, F32)
     for i in range(DRAFTS):
         pick = jnp.where((row == i) & (col == ids_ref[i, request]), 1.0, pick)
-    pick = pick.astype(BF16)
+    pick_ref[...] = pick
+    kept_out[...] = jnp.zeros(kept_out.shape, jnp.int32) + kept_ref[request]
+    owner_out[...] = jnp.zeros(owner_out.shape, jnp.int32) + owner_ref[0]
+    for fetch in fetches[early + 2 :]:
+        fetch.wait()
+
+
+def draft_kernel(
+    stage,
+    pick_ref,
+    kept_ref,
+    owner_ref,
+    runt_ref,
+    rate_ref,
+    skip_ref,
+    din_ref,
+    dgate_ref,
+    dwrite_ref,
+    dread_ref,
+    dstep_ref,
+    own_ref,
+    sent_ref,
+    skip_out,
+    q1_ref,
+    q2_ref,
+    vread_ref,
+    vwrite_ref,
+    tail_ref,
+    extra_ref,
+):
+    heads, span = runt_ref.shape
+    lanes = din_ref.shape[1]
+    groups = dwrite_ref.shape[1] // STATE_SIZE
+    wide = lanes // groups
+    here = lax.axis_index("seq")
+    place = place_of(stage)
+    pick = pick_ref[...].astype(BF16)
     vin = dot(pick, din_ref[...])
     vgate = dot(pick, dgate_ref[...])
     vwrite = dot(pick, dwrite_ref[...]).astype(BF16)
@@ -185,18 +218,24 @@
     vstep = sum(dot(pick, part.astype(BF16)) for part in split(dstep_ref[...], 3))
     vlog = -vstep * rate_ref[...]
     index = lax.broadcasted_iota(jnp.int32, (DRAFTS, heads), 0)
+    kept_heads = kept_ref[:, :1]
     acc = jnp.zeros((1, heads), F32)
     vrun = jnp.zeros((DRAFTS, heads), F32)
     reach = jnp.zeros((1, heads), F32)
     for i in range(DRAFTS):
         acc = acc + vlog[i : i + 1]
         vrun = jnp.where(index == i, acc, vrun)
-        reach = jnp.where(i < kept, acc, reach)
+        reach = jnp.where(i < kept_heads[0:1], acc, reach)
+    total = runt_ref[:, span - 128 :]
+    if heads < 128:
+        total = jnp.concatenate([total, jnp.zeros((128 - heads, 128), F32)], axis=0)
+    total = total.T[127:128, :heads]
     others = jnp.where(index == 0, total, jnp.where(index == 1, skip_ref[...], reach))
     stacked = split(jnp.concatenate([vrun, vstep, others], axis=0), 3)
     stacked = jnp.concatenate(stacked, axis=0).astype(BF16)
     row = lax.broadcasted_iota(jnp.int32, (DRAFTS, wide), 0)
-    is_owner = owner_ref[0] == here
+    kept = kept_ref[:, :1]
+    is_owner = owner_ref[0:1, :1] == here
     for g in range(groups):
         at = slice(g * wide, (g + 1) * wide)
         spread = dot(stacked, head_mask(heads, heads, wide, g * wide))
@@ -228,21 +267,17 @@
         mine = jnp.where(is_owner, mine, 0.0)
         logs = jnp.concatenate(split(total_l, 3) + [jnp.zeros((5, wide), F32)], axis=0)
         extra_ref[:, at] = jnp.concatenate([mine, logs], axis=0).astype(BF16)
-
-    for fetch in fetches[early : early + 2]:
-        fetch.wait()
-    fill_message(place ^ 1, end_ref, x_ref, write_ref, extra_ref, sent_ref)
-    for fetch in fetches[early + 2 :]:
-        fetch.wait()
-
-
-def fill_message(side, end_ref, x_ref, write_ref, extra_ref, out_ref):
+    half = lanes // 2
+    own_ref[...] = extra_ref[:, window(place * half, half)]
+    sent_ref[...] = extra_ref[:, window((place ^ 1) * half, half)]
+
+
+def fill_message(side, end_ref, x_ref, write_ref, out_ref):
     heads = end_ref.shape[1] // 2
     half = out_ref.shape[1]
     wide = 2 * half // (write_ref.shape[1] // STATE_SIZE)
     chunk = min(wide, half)
     start = side * half
-    out_ref[STATE_SIZE:, :] = extra_ref[:, window(start, half)]
     for at in range(0, half, chunk):
         lane0 = start + at
         group = lax.div(lane0, wide)
@@ -250,15 +285,34 @@
         weighted = (x_ref[:, window(lane0, chunk)].astype(F32) * scale).astype(BF16)
         writes = write_ref[:, window(group * STATE_SIZE, STATE_SIZE)]
         writes = writes.astype(F32).T.astype(BF16)
-        out_ref[:STATE_SIZE, at : at + chunk] = dot(writes, weighted).astype(BF16)
-
-
-def own_kernel(stage, end_ref, x_ref, write_ref, extra_ref, out_ref):
-    fill_message(place_of(stage), end_ref, x_ref, write_ref, extra_ref, out_ref)
-
-
-def logs_of(block):
-    return block[0:1].astype(F32) + block[1:2].astype(F32) + block[2:3].astype(F32)
+        out_ref[:, at : at + chunk] = dot(writes, weighted).astype(BF16)
+
+
+def own_kernel(stage, end_ref, x_ref, write_ref, out_ref):
+    fill_message(place_of(stage), end_ref, x_ref, write_ref, out_ref)
+
+
+def state_of(part, at):
+    return part[0][:STATE_SIZE, at].astype(F32)
+
+
+def extra_of(part, at):
+    return (part[1][:, at] if part[2] else part[0][STATE_SIZE:UP_ROWS, at]).astype(F32)
+
+
+def logs_of(part, at):
+    found = extra_of(part, at)[LOG_AT - STATE_SIZE :]
+    return found[0:1] + found[1:2] + found[2:3]
+
+
+def turned(parts):
+    return [parts[0], *parts[:0:-1]]
+
+
+def paired(refs, apart):
+    if apart:
+        return [(refs[k], refs[k + 1], True) for k in range(0, len(refs), 2)]
+    return [(ref, None, False) for ref in refs]
 
 
 def weights_of(logs, place, target):
@@ -280,8 +334,9 @@
     return jnp.exp(ahead)
 
 
-def up_kernel(stage, following, count, *refs):
-    parts, outs = refs[:count], refs[count:]
+def up_kernel(stage, following, count, apart, *refs):
+    taken = 2 * count if apart else count
+    parts, outs = paired(refs[:taken], apart), refs[taken:]
     place, target = place_of(stage), place_of(following)
     width = outs[0].shape[1]
     chunk = min(256, width)
@@ -290,13 +345,11 @@
         for at in range(0, width, chunk):
             start = at if len(outs) == 1 else (target ^ k) * width + at
             at_in = window(start, chunk)
-            logs = [logs_of(part[LOG_AT:UP_ROWS, at_in]) for part in parts]
+            logs = [logs_of(part, at_in) for part in parts]
             scale = weights_of(logs, place, count)
-            state = sum(
-                w * part[:STATE_SIZE, at_in].astype(F32) for w, part in zip(scale, parts)
-            )
+            state = sum(w * state_of(part, at_in) for w, part in zip(scale, parts))
             outs[k][:STATE_SIZE, at : at + chunk] = state.astype(BF16)
-            mine = sum(part[STATE_SIZE:UP_ROWS, at_in].astype(F32) for part in parts)
+            mine = sum(extra_of(part, at_in) for part in parts)
             total = jnp.concatenate(
                 split(sum(logs), 3) + [jnp.zeros((5, chunk), F32)], axis=0
             )
@@ -306,14 +359,15 @@
 
 
 def top_kernel(stage, count, *refs):
-    parts, outs, prompt_ref = refs[:count], refs[count:-1], refs[-1]
+    parts, outs, prompt_ref = paired(turned(refs[:count]), False), refs[count:-1], refs[-1]
+    whole = slice(None)
     place = place_of(stage)
     width = prompt_ref.shape[1]
-    logs = [logs_of(part[LOG_AT:UP_ROWS, :]) for part in parts]
-    states = [part[:STATE_SIZE, :].astype(F32) for part in parts]
+    logs = [logs_of(part, whole) for part in parts]
+    states = [state_of(part, whole) for part in parts]
     final = sum(w * s for w, s in zip(weights_of(logs, place, count), states)).astype(BF16)
     prompt_ref[...] = final
-    mine = sum(part[STATE_SIZE:LOG_AT, :].astype(F32) for part in parts)
+    mine = sum(extra_of(part, whole) for part in parts)
     reads = mine[16:24, :STATE_SIZE].astype(BF16)
     gated = mine[0:8] + mine[8:16] * dot(reads, final)
     gated = jnp.concatenate(split(gated, 2), axis=0).astype(BF16)
@@ -323,9 +377,10 @@
         outs[k][STATE_SIZE:, :] = gated
 
 
-def down_kernel(stage, above, above_count, count, targets, handed, *refs):
-    pieces, parts = refs[:above_count], refs[above_count : above_count + count]
-    outs = refs[above_count + count :]
+def down_kernel(stage, above, above_count, count, apart, targets, handed, *refs):
+    end = above_count + (2 * count if apart else count)
+    pieces, outs = turned(refs[:above_count]), refs[end:]
+    parts = paired(refs[above_count:end], apart)
     if handed:
         outs[-1][...] = outs[0][...]
         outs = outs[1:-1]
@@ -338,10 +393,10 @@
                 start = at if above_count == 1 else (source ^ piece) * width + at
                 at_out = window(start, chunk)
                 block = pieces[piece][:, at : at + chunk]
-                logs = [logs_of(part[LOG_AT:UP_ROWS, at_out]) for part in parts]
+                logs = [logs_of(part, at_out) for part in parts]
                 state = carry_of(logs, place, place ^ k) * block[:STATE_SIZE].astype(F32)
                 for w, part in zip(weights_of(logs, place, place ^ k), parts):
-                    state = state + w * part[:STATE_SIZE, at_out].astype(F32)
+                    state = state + w * state_of(part, at_out)
                 out_ref[:STATE_SIZE, at_out] = state.astype(BF16)
                 out_ref[STATE_SIZE:, at_out] = block[STATE_SIZE:]
 
@@ -552,7 +607,8 @@
             for position, value in enumerate(offsets):
                 block = jnp.where(offset == value, position, block)
             drawn = total_ref[window(block * DRAFTS, DRAFTS), :]
-            outs[k][at, :] = jnp.where(owner == first + slot, tail, drawn)
+            drawn = jnp.where(owner == first + slot, tail, drawn)
+            outs[k][at, :] = drawn.astype(outs[k].dtype)
 
 
 def project(stages, owner, own_rows, got_rows, own, got, gain, weight, head_count, after):
@@ -561,7 +617,7 @@
     return call(
         functools.partial(project_kernel, stages, head_count),
         "project",
-        [shape((rows // head_count, cols), F32)] * head_count,
+        [shape((rows // head_count, cols), BF16 if k else F32) for k in range(head_count)],
         (owner, own_rows, got_rows, own, got, gain, weight),
         after=after,
         scratch=[
@@ -581,7 +637,7 @@
         other_ref, _, new_ref, slice_ref, turned_ref, held_ref, sems = refs[5:]
     else:
         share_refs, (new_ref, turned_ref, verify_ref, held_ref, sems) = refs[5:-5], refs[-5:]
-        verify_ref[...] = sum(ref[...] for ref in share_refs).astype(BF16)
+        verify_ref[...] = sum(ref[...].astype(F32) for ref in share_refs).astype(BF16)
     half = prompt_ref.shape[1]
     wide = 2 * half // (vwrite_ref.shape[1] // STATE_SIZE)
     blocks = [0]
@@ -704,30 +760,28 @@
     rate, skip, gain = decay_rate[None], skip_gain[None], norm_gain[None]
     resident = resident_state.reshape(lanes, STATE_SIZE)
 
-    inputs = (
-        prefill_step.T, rate, skip, owner_slot, draft_ids.T, accepted_len, draft_input, draft_gate,
-        draft_write, draft_read, draft_step, write_proj, prefill_input, read_proj, resident, gain,
-    )
-    passed = 5
-    inputs = [in_hbm(value) for value in inputs]
+    inputs = [
+        in_hbm(value)
+        for value in (
+            prefill_step.T, rate, owner_slot, draft_ids.T, accepted_len, write_proj, prefill_input,
+            draft_input, draft_gate, draft_write, draft_read, draft_step, skip, rate, read_proj, resident,
+            gain,
+        )
+    ]
+    passed = 12
     opened = call(
         functools.partial(open_kernel, core, len(inputs), passed),
         "open_block",
         [
-            shape((UP_ROWS, half), BF16),
+            shape((STATE_SIZE, half), BF16),
             shape((groups, span, per_group), F32),
             shape((heads, span), F32),
             shape((heads, span), F32),
             shape((span, 2 * heads), BF16),
             shape((span, 2 * heads), BF16),
-            shape((1, lanes), F32),
-            shape((DRAFTS, lanes), F32),
-            shape((DRAFTS, lanes), F32),
-            shape((DRAFTS, groups * STATE_SIZE), BF16),
-            shape((DRAFTS, groups * STATE_SIZE), BF16),
-            shape((32, lanes), BF16),
+            shape((DRAFTS, draft_input.shape[0]), F32),
+            shape((DRAFTS, 128), jnp.int32),
             shape((DRAFTS, out_weight.shape[1]), jnp.int32),
-            shape((EXTRA, lanes), BF16),
         ]
         + [shape(value.shape, value.dtype) for value in inputs[-passed:]],
         inputs,
@@ -737,19 +791,39 @@
             (pltpu.SMEM if value.dtype == jnp.int32 else pltpu.VMEM)(value.shape, value.dtype)
             for value in inputs[:-passed]
         ],
-        flops=2 * span * lanes * STATE_SIZE * 2,
-    )
-    sent, run, runt, stept, reach, end, skip_lanes, q1, q2, vread, vwrite, tail, owner, extra = opened[:14]
-    writes, x, reads, resident, gain = opened[14:]
+        flops=span * lanes * STATE_SIZE * 2,
+    )
+    sent, run, runt, stept, reach, end, pick, kept, owner = opened[:9]
+    writes, x, din, dgate, dwrite, dread, dstep, skip, rate, reads, resident, gain = opened[9:]
     received = swap(sent, "seq", core, 1)
+    own_extra, sent_extra, skip_lanes, q1, q2, vread, vwrite, tail = call(
+        functools.partial(draft_kernel, core),
+        "draft_rows",
+        [
+            shape((EXTRA, half), BF16),
+            shape((EXTRA, half), BF16),
+            shape((1, lanes), F32),
+            shape((DRAFTS, lanes), F32),
+            shape((DRAFTS, lanes), F32),
+            shape((DRAFTS, groups * STATE_SIZE), BF16),
+            shape((DRAFTS, groups * STATE_SIZE), BF16),
+            shape((32, lanes), BF16),
+        ],
+        (pick, kept, owner, runt, rate, skip, din, dgate, dwrite, dread, dstep),
+        after=[sent],
+        scratch=[pltpu.VMEM((EXTRA, lanes), BF16)],
+        flops=DRAFTS * lanes * 100,
+    )
+    received_extra = swap(sent_extra, "seq", core, 1)
     (own,) = call(
         functools.partial(own_kernel, core),
         "own_message",
-        [shape((UP_ROWS, half), BF16)],
-        (end, x, writes, extra),
-        flops=span * lanes * STATE_SIZE * 2,
-    )
-    core_parts = [own, received]
+        [shape((STATE_SIZE, half), BF16)],
+        (end, x, writes),
+        after=[sent_extra],
+        flops=span * lanes * STATE_SIZE,
+    )
+    core_parts = [own, own_extra, received, received_extra]
     hidden = resident_hidden(resident, vread, q1, q2, gain, [own])
 
     bases, fetched = [], []
@@ -765,14 +839,14 @@
         return bases[-1:]
 
     def exchange(parts, stage):
-        got = {k: swap(parts[k], "seq", stage, k) for k in range(stage[0] - 1, 0, -1)}
+        got = {k: swap(parts[k], "seq", stage, k) for k in range(1, stage[0])}
         return [parts[0]] + [got[k] for k in range(1, stage[0])]
 
     line_width = half // line[0]
     split_last = line_width % (last[0] * 128) == 0
     last_width = line_width // last[0] if split_last else line_width
     outs = call(
-        functools.partial(up_kernel, core, line, 2),
+        functools.partial(up_kernel, core, line, 2, True),
         "up_line",
         [shape((UP_ROWS, line_width), BF16)] * line[0],
         core_parts,
@@ -782,50 +856,51 @@
     line_parts = exchange(outs, line)
     hiddens = exchange([hand_on(hidden, [outs[-1]])] * last[0], last)
     filled = fill([outs[-1]])
-    hidden = join(hiddens, 0)
     outs = call(
-        functools.partial(up_kernel, line, last, line[0]),
+        functools.partial(up_kernel, line, last, line[0], False),
         "up_last",
         [shape((UP_ROWS, last_width), BF16)] * (last[0] if split_last else 1),
         line_parts,
-        after=filled + [hidden],
+        after=filled + hiddens[2:],
         flops=line_width * UP_ROWS * 4,
     )
     last_parts = exchange(outs if split_last else outs * last[0], last)
-    hiddens = exchange([hand_on(hidden, [outs[-1]])] * line[0], line)
     filled = fill([outs[-1]])
     *outs, prompt = call(
         functools.partial(top_kernel, last, last[0]),
         "top",
         [shape((DOWN_ROWS, last_width), BF16)] * (last[0] if split_last else 1)
         + [shape((STATE_SIZE, last_width), BF16)],
-        last_parts,
+        turned(last_parts),
         after=filled,
         flops=last_width * UP_ROWS * 16,
     )
 
     pieces = exchange(outs, last) if split_last else outs
     hidden = join(hiddens, 0, [outs[-1]])
-    filled = fill([outs[-1], hidden])
-    prompt = join(exchange([prompt] * line[0], line), 1)
-    *outs, prompt = call(
-        functools.partial(down_kernel, line, last, len(pieces), line[0], range(line[0]), True),
+    hiddens = exchange([hidden] * line[0], line)
+    filled = fill([outs[-1]])
+    prompts = exchange([prompt] * line[0], line)
+    outs = call(
+        functools.partial(down_kernel, line, last, len(pieces), line[0], False, range(line[0]), False),
         "down_line",
-        [shape((DOWN_ROWS, line_width), BF16)] * line[0] + [shape(prompt.shape, BF16)],
-        [*pieces, *line_parts, prompt],
-        after=filled,
+        [shape((DOWN_ROWS, line_width), BF16)] * line[0],
+        [*turned(pieces), *line_parts],
+        after=filled + prompts[1:] + hiddens[1:],
         flops=line_width * UP_ROWS * 8,
     )
     pieces = exchange(outs, line)
     filled = fill([outs[-1]])
     scattered = [line, last] if split_last else [line]
+    hidden = join(hiddens, 0, [outs[-1]])
+    prompt = join(prompts, 1, [outs[-1]])
     prompts = exchange([prompt] * last[0], last) if split_last else [prompt]
     def down_core(target, after):
         return call(
-            functools.partial(down_kernel, core, line, line[0], 2, (target,), False),
+            functools.partial(down_kernel, core, line, line[0], 2, True, (target,), False),
             "down_core",
             [shape((DOWN_ROWS, half), BF16)],
-            pieces + core_parts,
+            turned(pieces) + core_parts,
             after=after,
             moved=1,
         )[0]

time: 64.5 us -> 62.7 us (0.972)
  waiting for transfers between devices: 15.2 us -> 14.4 us
  starting transfers between devices: 24.4 us -> 23.7 us
    ppermute x21 -> x22, waiting for transfers between devices: 15.2 us -> 14.4 us  [swap(): lax.ppermute(value, axis, [(k, k ^ offset * stride) for k in range(count)])]
    ppermute x21 -> x22, starting transfers between devices: 24.4 us -> 23.7 us  [swap(): lax.ppermute(value, axis, [(k, k ^ offset * stride) for k in range(count)])]
  transfers between devices with their start and end apart: 21 -> 22, of which waited for: 12 -> 9; matrix products, arithmetic and copies ran while one was open for 0% -> 0% of each run, Pallas kernels for 26% -> 28%
where the time goes in v1:
time: 62.7 us; the launch traced here: 62.6 us
  starting transfers between devices  23.7 us (38%)
  Pallas kernels  23.5 us (37%)
  waiting for transfers between devices  14.4 us (23%)
  between operations  0.85 us (1%)
    ppermute x22, starting transfers between devices, swap(): lax.ppermute(value, axis, [(k, k ^ offset * stride) for k in range(count)])  23.7 us
    pallas_call x24, Pallas kernels, call(): pl.pallas_call(ordered(kernel, first), name=name, grid=grid, out_shape=ou...  23.5 us
    ppermute x22, waiting for transfers between devices, swap(): lax.ppermute(value, axis, [(k, k ^ offset * stride) for k in range(count)])  14.4 us
  transfers between devices with their start and end apart: 22, of which 9 were waited for; matrix products, arithmetic and copies ran while one was open for 0% of the time, Pallas kernels for 28%

profile of v1, /device:TPU:0, one launch (start us, length us, event | category | flops | bytes accessed | tf_op | source)
XLA Modules:
  0.0 62.6 jit_solution(4553493302488591134)
XLA Ops:
  0.6 2.9 %open_block.1 = (bf16[128,2048]{1,0:T(8,128)(2,1)S(1)}, f32[4,256,16]{2,1,0:T(8,128)S(1)}, f32[64,256]{1,0:T(8,128)S(1)}, f32[64,256]{1,0:T(8,128)S(1)}, bf16[25...) custom-call(f32[64,256]{1,0:T(8,128)} %bitcast.9, ...), custom_call_target="tpu_custom_call" | custom-call | flops 268435456 | bytes 8911232 | tf_op jit(solution)/shard_map/open_block/pallas_call | solution.py:95
  6.8 3.0 %collective-permute-start.4 = (bf16[160,1024]{1,0:T(8,128)(2,1)S(1)}, bf16[160,1024]{1,0:T(8,128)(2,1)S(1)}, u32[]{:S(2)}, u32[]{:S(2)}) collective-permute-start(bf16[160,1024]{1,0:T(8,128)(2,1)S(1)} %get-tuple-element.81.refs_0_), channel_id=1, source_target_pairs={{0,4},{2,6},{4,0},{6,2},{8,12},{10,14},{12,8},{14,10},{16,20},{18,... | collective-permute-start | bytes 983048 | tf_op jit(solution)/shard_map/ppermute | solution.py:44
  9.8 3.6 %collective-permute-start.3 = (bf16[8,4096]{1,0:T(8,128)(2,1)S(1)}, bf16[8,4096]{1,0:T(8,128)(2,1)S(1)}, u32[]{:S(2)}, u32[]{:S(2)}) collective-permute-start(bf16[8,4096]{1,0:T(8,128)(2,1)S(1)} %hand_on.1.refs_1_), channel_id=1, source_target_pairs={{0,24},{2,26},{4,28},{6,30},{8,16},{10,18},{12,20},{14,22},{16,8},... | collective-permute-start | bytes 196616 | tf_op jit(solution)/shard_map/ppermute | solution.py:44
  13.4 3.6 %intra.4 = (f32[256,1024]{1,0:T(8,128)S(1)}, bf16[4096,512]{1,0:T(8,128)(2,1)S(1)}) custom-call(bf16[160,1024]{1,0:T(8,128)(2,1)S(1)} %get-tuple-element.81.refs_0_, f32[4,256,16]{2,1,0:T(8,128)S(1)} %get-tuple-element.82.refs_1_, f32[64,256]{1,0:T(8,128)S(1)} %get-tuple-element.63.refs_4_.refs_2_, f32[64,256]{1,0:T(8,128)S(1)} %get-tuple-element.83.refs_3_, ...), custom_call_target="tpu_custom_call" | custom-call | flops 134217728 | bytes 1572864 | tf_op jit(solution)/shard_map/intra/pallas_call | solution.py:95
  17.0 1.9 %collective-permute-done.2.refs_1_.refs_3_ = bf16[8,4096]{1,0:T(8,128)(2,1)S(1)} collective-permute-done((bf16[8,4096]{1,0:T(8,128)(2,1)S(1)}, bf16[8,4096]{1,0:T(8,128)(2,1)S(1)}, u32[]{:S(2)}, u32[]{:S(2)}) %collective-permute-start.2) | collective-permute-done | bytes 65568 | tf_op jit(solution)/shard_map/ppermute | solution.py:44
  19.1 1.7 %collective-permute-start.6 = (bf16[160,256]{1,0:T(8,128)(2,1)S(1)}, bf16[160,256]{1,0:T(8,128)(2,1)S(1)}, u32[]{:S(2)}, u32[]{:S(2)}) collective-permute-start(bf16[160,256]{1,0:T(8,128)(2,1)S(1)} %get-tuple-element.90), channel_id=1, source_target_pairs={{0,16},{2,18},{4,20},{6,22},{8,24},{10,26},{12,28},{14,30},{16,0},... | collective-permute-start | bytes 245768 | tf_op jit(solution)/shard_map/ppermute | solution.py:44
  20.7 1.7 %collective-permute-start.7 = (bf16[160,256]{1,0:T(8,128)(2,1)S(1)}, bf16[160,256]{1,0:T(8,128)(2,1)S(1)}, u32[]{:S(2)}, u32[]{:S(2)}) collective-permute-start(bf16[160,256]{1,0:T(8,128)(2,1)S(1)} %get-tuple-element.91), channel_id=1, source_target_pairs={{0,8},{2,10},{4,12},{6,14},{8,0},{10,2},{12,4},{14,6},{16,24},{18,... | collective-permute-start | bytes 245768 | tf_op jit(solution)/shard_map/ppermute | solution.py:44
  23.5 1.6 %intra.5.refs_0_.refs_5_.refs_6_ = f32[256,1024]{1,0:T(8,128)S(1)} custom-call(bf16[160,256]{1,0:T(8,128)(2,1)S(1)} %get-tuple-element.88.refs_0_, f32[4,256,16]{2,1,0:T(8,128)S(1)} %get-tuple-element.82.refs_1_, f32[64,256]{1,0:T(8,128)S(1)} %get-tuple-element.63.refs_4_.refs_2_, f32[64,256]{1,0:T(8,128)S(1)} %get-tuple-element.83.refs_3_, ...), custom_call_target="tpu_custom_call" | custom-call | flops 134217728 | bytes 1572864 | tf_op jit(solution)/shard_map/intra/pallas_call | solution.py:95
  25.2 1.9 %collective-permute-done.6.refs_3_ = bf16[160,256]{1,0:T(8,128)(2,1)S(1)} collective-permute-done((bf16[160,256]{1,0:T(8,128)(2,1)S(1)}, bf16[160,256]{1,0:T(8,128)(2,1)S(1)}, u32[]{:S(2)}, u32[]{:S(2)}) %collective-permute-start.6) | collective-permute-done | bytes 81952 | tf_op jit(solution)/shard_map/ppermute | solution.py:44
  27.2 1.6 %collective-permute-done.5.refs_2_ = bf16[160,256]{1,0:T(8,128)(2,1)S(1)} collective-permute-done((bf16[160,256]{1,0:T(8,128)(2,1)S(1)}, bf16[160,256]{1,0:T(8,128)(2,1)S(1)}, u32[]{:S(2)}, u32[]{:S(2)}) %collective-permute-start.5) | collective-permute-done | bytes 81952 | tf_op jit(solution)/shard_map/ppermute | solution.py:44
  29.2 1.3 %collective-permute-start.10 = (bf16[32,4096]{1,0:T(8,128)(2,1)S(1)}, bf16[32,4096]{1,0:T(8,128)(2,1)S(1)}, u32[]{:S(2)}, u32[]{:S(2)}) collective-permute-start(bf16[32,4096]{1,0:T(8,128)(2,1)S(1)} %join.4.refs_1_), channel_id=1, source_target_pairs={{0,4},{2,6},{4,0},{6,2},{8,12},{10,14},{12,8},{14,10},{16,20},{18,... | collective-permute-start | bytes 786440 | tf_op jit(solution)/shard_map/ppermute | solution.py:44
  30.5 1.9 %collective-permute-start.12 = (bf16[144,256]{1,0:T(8,128)(2,1)S(1)}, bf16[144,256]{1,0:T(8,128)(2,1)S(1)}, u32[]{:S(2)}, u32[]{:S(2)}) collective-permute-start(bf16[144,256]{1,0:T(8,128)(2,1)S(1)} %get-tuple-element.95), channel_id=1, source_target_pairs={{0,16},{2,18},{4,20},{6,22},{8,24},{10,26},{12,28},{14,30},{16,0},... | collective-permute-start | bytes 221192 | tf_op jit(solution)/shard_map/ppermute | solution.py:44
  33.4 1.5 %collective-permute-start.11 = (bf16[144,256]{1,0:T(8,128)(2,1)S(1)}, bf16[144,256]{1,0:T(8,128)(2,1)S(1)}, u32[]{:S(2)}, u32[]{:S(2)}) collective-permute-start(bf16[144,256]{1,0:T(8,128)(2,1)S(1)} %get-tuple-element.92.refs_0_), channel_id=1, source_target_pairs={{0,24},{2,26},{4,28},{6,30},{8,16},{10,18},{12,20},{14,22},{16,8},... | collective-permute-start | bytes 221192 | tf_op jit(solution)/shard_map/ppermute | solution.py:44
  35.7 1.6 %intra.6.refs_0_.refs_6_.refs_7_ = f32[256,1024]{1,0:T(8,128)S(1)} custom-call(bf16[144,256]{1,0:T(8,128)(2,1)S(1)} %get-tuple-element.92.refs_0_, f32[4,256,16]{2,1,0:T(8,128)S(1)} %get-tuple-element.82.refs_1_, f32[64,256]{1,0:T(8,128)S(1)} %get-tuple-element.63.refs_4_.refs_2_, f32[64,256]{1,0:T(8,128)S(1)} %get-tuple-element.83.refs_3_, ...), custom_call_target="tpu_custom_call" | custom-call | flops 134217728 | bytes 1572864 | tf_op jit(solution)/shard_map/intra/pallas_call | solution.py:95
  37.3 1.8 %collective-permute-done.8.refs_1_.refs_2_ = bf16[128,256]{1,0:T(8,128)(2,1)S(1)} collective-permute-done((bf16[128,256]{1,0:T(8,128)(2,1)S(1)}, bf16[128,256]{1,0:T(8,128)(2,1)S(1)}, u32[]{:S(2)}, u32[]{:S(2)}) %collective-permute-start.8) | collective-permute-done | bytes 65568 | tf_op jit(solution)/shard_map/ppermute | solution.py:44
  40.5 2.0 %collective-permute-start.15 = (bf16[128,512]{1,0:T(8,128)(2,1)S(1)}, bf16[128,512]{1,0:T(8,128)(2,1)S(1)}, u32[]{:S(2)}, u32[]{:S(2)}) collective-permute-start(bf16[128,512]{1,0:T(8,128)(2,1)S(1)} %join.5.refs_2_), channel_id=1, source_target_pairs={{0,24},{2,26},{4,28},{6,30},{8,16},{10,18},{12,20},{14,22},{16,8},... | collective-permute-start | bytes 393224 | tf_op jit(solution)/shard_map/ppermute | solution.py:44
  42.5 1.6 %intra.7.refs_0_.refs_7_.refs_8_ = f32[256,1024]{1,0:T(8,128)S(1)} custom-call(bf16[144,1024]{1,0:T(8,128)(2,1)S(1)} %get-tuple-element.97.refs_0_, f32[4,256,16]{2,1,0:T(8,128)S(1)} %get-tuple-element.82.refs_1_, f32[64,256]{1,0:T(8,128)S(1)} %get-tuple-element.63.refs_4_.refs_2_, f32[64,256]{1,0:T(8,128)S(1)} %get-tuple-element.83.refs_3_, ...), custom_call_target="tpu_custom_call" | custom-call | flops 134217728 | bytes 1572864 | tf_op jit(solution)/shard_map/intra/pallas_call | solution.py:95
  44.2 3.3 %collective-permute-done.15.refs_2_.refs_5_ = bf16[128,512]{1,0:T(8,128)(2,1)S(1)} collective-permute-done((bf16[128,512]{1,0:T(8,128)(2,1)S(1)}, bf16[128,512]{1,0:T(8,128)(2,1)S(1)}, u32[]{:S(2)}, u32[]{:S(2)}) %collective-permute-start.15) | collective-permute-done | bytes 131104 | tf_op jit(solution)/shard_map/ppermute | solution.py:44
  50.8 1.6 %finish.2 = (bf16[256,4096]{1,0:T(8,128)(2,1)}, f32[8,128]{1,0:T(8,128)S(1)}) custom-call(bf16[144,2048]{1,0:T(8,128)(2,1)S(1)} %down_core.3.refs_0_.refs_3_.refs_4_, bf16[256,128]{1,0:T(8,128)(2,1)S(1)} %get-tuple-element.99.refs_1_.refs_2_, bf16[256,512]{1,0:T(8,128)(2,1)S(1)} %get-tuple-element.85.refs_7_.refs_2_.refs_3_, ...), custom_call_target="tpu_custom_call" | custom-call | bytes 1 | tf_op jit(solution)/shard_map/finish/pallas_call | solution.py:95
  53.3 1.6 %collective-permute-start.19 = (bf16[64,512]{1,0:T(8,128)(2,1)S(1)}, bf16[64,512]{1,0:T(8,128)(2,1)S(1)}, u32[]{:S(2)}, u32[]{:S(2)}) collective-permute-start(bf16[64,512]{1,0:T(8,128)(2,1)S(1)} %get-tuple-element.106), channel_id=1, source_target_pairs={{0,1},{1,0},{2,3},{3,2},{4,5},{5,4},{6,7},{7,6},{8,9},{9,8},{10,11... | collective-permute-start | bytes 196616 | tf_op jit(solution)/shard_map/ppermute | solution.py:44
  54.9 1.6 %finish.3 = (bf16[256,4096]{1,0:T(8,128)(2,1)}, f32[8,128]{1,0:T(8,128)S(1)}) custom-call(f32[64,512]{1,0:T(8,128)S(1)} %get-tuple-element.102.refs_0_.refs_5_, f32[8,128]{1,0:T(8,128)S(1)} %get-tuple-element.100.refs_0_.refs_1_, bf16[256,128]{1,0:T(8,128)(2,1)S(1)} %get-tuple-element.99.refs_1_.refs_2_, ...), custom_call_target="tpu_custom_call", output_to_operand_aliasing={{0}: (9, {})} | custom-call | bytes 1 | tf_op jit(solution)/shard_map/finish/pallas_call | solution.py:95
  56.5 2.1 %collective-permute-done.20.refs_4_ = bf16[128,512]{1,0:T(8,128)(2,1)S(1)} collective-permute-done((bf16[128,512]{1,0:T(8,128)(2,1)S(1)}, bf16[128,512]{1,0:T(8,128)(2,1)S(1)}, u32[]{:S(2)}, u32[]{:S(2)}) %collective-permute-start.20) | collective-permute-done | bytes 131104 | tf_op jit(solution)/shard_map/ppermute | solution.py:44
  58.7 1.9 %states.2 = (bf16[4096,128]{1,0:T(8,128)(2,1)}, f32[2048,128]{1,0:T(8,128)S(1)}, bf16[64,512]{1,0:T(8,128)(2,1)}) custom-call(s32[8,512]{1,0:T(8,128)S(1)} %get-tuple-element.62.refs_3_.refs_1_.refs_0_, bf16[4096,128]{1,0:T(8,128)(2,1)S(1)} %get-tuple-element.75.refs_1_, bf16[128,2048]{1,0:T(8,128)(2,1)S(1)} %join.7.refs_2_, ...), custom_call_target="tpu_custom_call" | custom-call | flops 33554432 | bytes 1572864 | tf_op jit(solution)/shard_map/states/pallas_call | solution.py:95
  60.6 1.9 %states.3 = (bf16[4096,128]{1,0:T(8,128)(2,1)}, bf16[64,512]{1,0:T(8,128)(2,1)}) custom-call(s32[8,512]{1,0:T(8,128)S(1)} %get-tuple-element.62.refs_3_.refs_1_.refs_0_, bf16[4096,128]{1,0:T(8,128)(2,1)S(1)} %get-tuple-element.75.refs_1_, bf16[128,2048]{1,0:T(8,128)(2,1)S(1)} %collective-permute-done.21.refs_2_, ...), custom_call_target="tpu_custom_call", output_to_operand_aliasing={{0}: (6, {})} | custom-call | flops 33554432 | bytes 1572864 | tf_op jit(solution)/shard_map/states/pallas_call | solution.py:95
  (44 shorter events, 12.3 us)
Async XLA Ops:
  3.5 2.9 %collective-permute-start = (bf16[128,2048]{1,0:T(8,128)(2,1)S(1)}, bf16[128,2048]{1,0:T(8,128)(2,1)S(1)}, u32[]{:S(2)}, u32[]{:S(2)}) collective-permute-start(bf16[128,2048]{1,0:T(8,128)(2,1)S(1)} %get-tuple-element.59.refs_0_), channel_id=1, source_target_pairs={{0,2},{2,0},{4,6},{6,4},{8,10},{10,8},{12,14},{14,12},{16,18},{18,... | collective-permute-start | bytes 1572872 | tf_op jit(solution)/shard_map/ppermute | solution.py:44
  5.0 1.4 %collective-permute-start.1 = (bf16[32,2048]{1,0:T(8,128)(2,1)S(1)}, bf16[32,2048]{1,0:T(8,128)(2,1)S(1)}, u32[]{:S(2)}, u32[]{:S(2)}) collective-permute-start(bf16[32,2048]{1,0:T(8,128)(2,1)S(1)} %get-tuple-element.71.refs_0_), channel_id=1, source_target_pairs={{0,2},{2,0},{4,6},{6,4},{8,10},{10,8},{12,14},{14,12},{16,18},{18,... | collective-permute-start | bytes 393224 | tf_op jit(solution)/shard_map/ppermute | solution.py:44
  6.8 12.2 %collective-permute-start.4 = (bf16[160,1024]{1,0:T(8,128)(2,1)S(1)}, bf16[160,1024]{1,0:T(8,128)(2,1)S(1)}, u32[]{:S(2)}, u32[]{:S(2)}) collective-permute-start(bf16[160,1024]{1,0:T(8,128)(2,1)S(1)} %get-tuple-element.81.refs_0_), channel_id=1, source_target_pairs={{0,4},{2,6},{4,0},{6,2},{8,12},{10,14},{12,8},{14,10},{16,20},{18,... | collective-permute-start | bytes 983048 | tf_op jit(solution)/shard_map/ppermute | solution.py:44
  9.8 7.2 %collective-permute-start.3 = (bf16[8,4096]{1,0:T(8,128)(2,1)S(1)}, bf16[8,4096]{1,0:T(8,128)(2,1)S(1)}, u32[]{:S(2)}, u32[]{:S(2)}) collective-permute-start(bf16[8,4096]{1,0:T(8,128)(2,1)S(1)} %hand_on.1.refs_1_), channel_id=1, source_target_pairs={{0,24},{2,26},{4,28},{6,30},{8,16},{10,18},{12,20},{14,22},{16,8},... | collective-permute-start | bytes 196616 | tf_op jit(solution)/shard_map/ppermute | solution.py:44
  13.4 5.5 %collective-permute-start.2 = (bf16[8,4096]{1,0:T(8,128)(2,1)S(1)}, bf16[8,4096]{1,0:T(8,128)(2,1)S(1)}, u32[]{:S(2)}, u32[]{:S(2)}) collective-permute-start(bf16[8,4096]{1,0:T(8,128)(2,1)S(1)} %hand_on.1.refs_1_), channel_id=1, source_target_pairs={{0,16},{2,18},{4,20},{6,22},{8,24},{10,26},{12,28},{14,30},{16,0},... | collective-permute-start | bytes 196616 | tf_op jit(solution)/shard_map/ppermute | solution.py:44
  19.1 8.0 %collective-permute-start.6 = (bf16[160,256]{1,0:T(8,128)(2,1)S(1)}, bf16[160,256]{1,0:T(8,128)(2,1)S(1)}, u32[]{:S(2)}, u32[]{:S(2)}) collective-permute-start(bf16[160,256]{1,0:T(8,128)(2,1)S(1)} %get-tuple-element.90), channel_id=1, source_target_pairs={{0,16},{2,18},{4,20},{6,22},{8,24},{10,26},{12,28},{14,30},{16,0},... | collective-permute-start | bytes 245768 | tf_op jit(solution)/shard_map/ppermute | solution.py:44
  20.7 6.4 %collective-permute-start.7 = (bf16[160,256]{1,0:T(8,128)(2,1)S(1)}, bf16[160,256]{1,0:T(8,128)(2,1)S(1)}, u32[]{:S(2)}, u32[]{:S(2)}) collective-permute-start(bf16[160,256]{1,0:T(8,128)(2,1)S(1)} %get-tuple-element.91), channel_id=1, source_target_pairs={{0,8},{2,10},{4,12},{6,14},{8,0},{10,2},{12,4},{14,6},{16,24},{18,... | collective-permute-start | bytes 245768 | tf_op jit(solution)/shard_map/ppermute | solution.py:44
  22.4 6.4 %collective-permute-start.5 = (bf16[160,256]{1,0:T(8,128)(2,1)S(1)}, bf16[160,256]{1,0:T(8,128)(2,1)S(1)}, u32[]{:S(2)}, u32[]{:S(2)}) collective-permute-start(bf16[160,256]{1,0:T(8,128)(2,1)S(1)} %get-tuple-element.88.refs_0_), channel_id=1, source_target_pairs={{0,24},{2,26},{4,28},{6,30},{8,16},{10,18},{12,20},{14,22},{16,8},... | collective-permute-start | bytes 245768 | tf_op jit(solution)/shard_map/ppermute | solution.py:44
  23.5 5.6 %collective-permute-start.9 = (bf16[8,4096]{1,0:T(8,128)(2,1)S(1)}, bf16[8,4096]{1,0:T(8,128)(2,1)S(1)}, u32[]{:S(2)}, u32[]{:S(2)}) collective-permute-start(bf16[8,4096]{1,0:T(8,128)(2,1)S(1)} %hand_on.1.refs_1_), channel_id=1, source_target_pairs={{0,8},{2,10},{4,12},{6,14},{8,0},{10,2},{12,4},{14,6},{16,24},{18,... | collective-permute-start | bytes 196616 | tf_op jit(solution)/shard_map/ppermute | solution.py:44
  29.2 10.3 %collective-permute-start.10 = (bf16[32,4096]{1,0:T(8,128)(2,1)S(1)}, bf16[32,4096]{1,0:T(8,128)(2,1)S(1)}, u32[]{:S(2)}, u32[]{:S(2)}) collective-permute-start(bf16[32,4096]{1,0:T(8,128)(2,1)S(1)} %join.4.refs_1_), channel_id=1, source_target_pairs={{0,4},{2,6},{4,0},{6,2},{8,12},{10,14},{12,8},{14,10},{16,20},{18,... | collective-permute-start | bytes 786440 | tf_op jit(solution)/shard_map/ppermute | solution.py:44
  30.5 8.7 %collective-permute-start.12 = (bf16[144,256]{1,0:T(8,128)(2,1)S(1)}, bf16[144,256]{1,0:T(8,128)(2,1)S(1)}, u32[]{:S(2)}, u32[]{:S(2)}) collective-permute-start(bf16[144,256]{1,0:T(8,128)(2,1)S(1)} %get-tuple-element.95), channel_id=1, source_target_pairs={{0,16},{2,18},{4,20},{6,22},{8,24},{10,26},{12,28},{14,30},{16,0},... | collective-permute-start | bytes 221192 | tf_op jit(solution)/shard_map/ppermute | solution.py:44
  32.4 6.8 %collective-permute-start.13 = (bf16[144,256]{1,0:T(8,128)(2,1)S(1)}, bf16[144,256]{1,0:T(8,128)(2,1)S(1)}, u32[]{:S(2)}, u32[]{:S(2)}) collective-permute-start(bf16[144,256]{1,0:T(8,128)(2,1)S(1)} %get-tuple-element.96), channel_id=1, source_target_pairs={{0,8},{2,10},{4,12},{6,14},{8,0},{10,2},{12,4},{14,6},{16,24},{18,... | collective-permute-start | bytes 221192 | tf_op jit(solution)/shard_map/ppermute | solution.py:44
  33.4 6.2 %collective-permute-start.11 = (bf16[144,256]{1,0:T(8,128)(2,1)S(1)}, bf16[144,256]{1,0:T(8,128)(2,1)S(1)}, u32[]{:S(2)}, u32[]{:S(2)}) collective-permute-start(bf16[144,256]{1,0:T(8,128)(2,1)S(1)} %get-tuple-element.92.refs_0_), channel_id=1, source_target_pairs={{0,24},{2,26},{4,28},{6,30},{8,16},{10,18},{12,20},{14,22},{16,8},... | collective-permute-start | bytes 221192 | tf_op jit(solution)/shard_map/ppermute | solution.py:44
  34.9 4.3 %collective-permute-start.8 = (bf16[128,256]{1,0:T(8,128)(2,1)S(1)}, bf16[128,256]{1,0:T(8,128)(2,1)S(1)}, u32[]{:S(2)}, u32[]{:S(2)}) collective-permute-start(bf16[128,256]{1,0:T(8,128)(2,1)S(1)} %get-tuple-element.93.refs_1_), channel_id=1, source_target_pairs={{0,4},{2,6},{4,0},{6,2},{8,12},{10,14},{12,8},{14,10},{16,20},{18,... | collective-permute-start | bytes 196616 | tf_op jit(solution)/shard_map/ppermute | solution.py:44
  39.9 8.9 %collective-permute-start.16 = (bf16[144,1024]{1,0:T(8,128)(2,1)S(1)}, bf16[144,1024]{1,0:T(8,128)(2,1)S(1)}, u32[]{:S(2)}, u32[]{:S(2)}) collective-permute-start(bf16[144,1024]{1,0:T(8,128)(2,1)S(1)} %get-tuple-element.97.refs_0_), channel_id=1, source_target_pairs={{0,4},{2,6},{4,0},{6,2},{8,12},{10,14},{12,8},{14,10},{16,20},{18,... | collective-permute-start | bytes 884744 | tf_op jit(solution)/shard_map/ppermute | solution.py:44
  40.5 6.9 %collective-permute-start.15 = (bf16[128,512]{1,0:T(8,128)(2,1)S(1)}, bf16[128,512]{1,0:T(8,128)(2,1)S(1)}, u32[]{:S(2)}, u32[]{:S(2)}) collective-permute-start(bf16[128,512]{1,0:T(8,128)(2,1)S(1)} %join.5.refs_2_), channel_id=1, source_target_pairs={{0,24},{2,26},{4,28},{6,30},{8,16},{10,18},{12,20},{14,22},{16,8},... | collective-permute-start | bytes 393224 | tf_op jit(solution)/shard_map/ppermute | solution.py:44
  42.5 6.2 %collective-permute-start.14 = (bf16[128,512]{1,0:T(8,128)(2,1)S(1)}, bf16[128,512]{1,0:T(8,128)(2,1)S(1)}, u32[]{:S(2)}, u32[]{:S(2)}) collective-permute-start(bf16[128,512]{1,0:T(8,128)(2,1)S(1)} %join.5.refs_2_), channel_id=1, source_target_pairs={{0,8},{2,10},{4,12},{6,14},{8,0},{10,2},{12,4},{14,6},{16,24},{18,... | collective-permute-start | bytes 393224 | tf_op jit(solution)/shard_map/ppermute | solution.py:44
  49.1 3.2 %collective-permute-start.18 = (bf16[144,2048]{1,0:T(8,128)(2,1)S(1)}, bf16[144,2048]{1,0:T(8,128)(2,1)S(1)}, u32[]{:S(2)}, u32[]{:S(2)}) collective-permute-start(bf16[144,2048]{1,0:T(8,128)(2,1)S(1)} %down_core.2.refs_0_), channel_id=1, source_target_pairs={{0,2},{2,0},{4,6},{6,4},{8,10},{10,8},{12,14},{14,12},{16,18},{18,... | collective-permute-start | bytes 1769480 | tf_op jit(solution)/shard_map/ppermute | solution.py:44
  49.3 3.1 %collective-permute-start.17 = (bf16[64,4096]{1,0:T(8,128)(2,1)S(1)}, bf16[64,4096]{1,0:T(8,128)(2,1)S(1)}, u32[]{:S(2)}, u32[]{:S(2)}) collective-permute-start(bf16[64,4096]{1,0:T(8,128)(2,1)S(1)} %join.6.refs_2_), channel_id=1, source_target_pairs={{0,2},{2,0},{4,6},{6,4},{8,10},{10,8},{12,14},{14,12},{16,18},{18,... | collective-permute-start | bytes 1572872 | tf_op jit(solution)/shard_map/ppermute | solution.py:44
  49.8 8.8 %collective-permute-start.20 = (bf16[128,512]{1,0:T(8,128)(2,1)S(1)}, bf16[128,512]{1,0:T(8,128)(2,1)S(1)}, u32[]{:S(2)}, u32[]{:S(2)}) collective-permute-start(bf16[128,512]{1,0:T(8,128)(2,1)S(1)} %join.5.refs_2_), channel_id=1, source_target_pairs={{0,16},{2,18},{4,20},{6,22},{8,24},{10,26},{12,28},{14,30},{16,0},... | collective-permute-start | bytes 393224 | tf_op jit(solution)/shard_map/ppermute | solution.py:44
  53.3 5.3 %collective-permute-start.19 = (bf16[64,512]{1,0:T(8,128)(2,1)S(1)}, bf16[64,512]{1,0:T(8,128)(2,1)S(1)}, u32[]{:S(2)}, u32[]{:S(2)}) collective-permute-start(bf16[64,512]{1,0:T(8,128)(2,1)S(1)} %get-tuple-element.106), channel_id=1, source_target_pairs={{0,1},{1,0},{2,3},{3,2},{4,5},{5,4},{6,7},{7,6},{8,9},{9,8},{10,11... | collective-permute-start | bytes 196616 | tf_op jit(solution)/shard_map/ppermute | solution.py:44
  58.6 2.0 %collective-permute-start.21 = (bf16[128,2048]{1,0:T(8,128)(2,1)S(1)}, bf16[128,2048]{1,0:T(8,128)(2,1)S(1)}, u32[]{:S(2)}, u32[]{:S(2)}) collective-permute-start(bf16[128,2048]{1,0:T(8,128)(2,1)S(1)} %join.7.refs_2_), channel_id=1, source_target_pairs={{0,2},{2,0},{4,6},{6,4},{8,10},{10,8},{12,14},{14,12},{16,18},{18,... | collective-permute-start | bytes 1572872 | tf_op jit(solution)/shard_map/ppermute | solution.py:44

commit v2 on v1

--- a/solution.py
+++ b/solution.py
@@ -42,6 +42,24 @@
 def swap(value, axis, stage, offset):
     count, stride = lax.axis_size(axis), stage[1]
     return lax.ppermute(value, axis, [(k, k ^ (offset * stride)) for k in range(count)])
+
+
+def shift(value, axis, stage, step):
+    count, (factor, stride) = lax.axis_size(axis), stage
+    pairs = [
+        (k, k + step * stride) for k in range(count) if 0 <= k // stride % factor + step < factor
+    ]
+    return lax.ppermute(value, axis, pairs)
+
+
+def chain(value, stage):
+    before, after = [], []
+    up = down = value
+    for _ in range(1, stage[0]):
+        up, down = shift(up, "seq", stage, 1), shift(down, "seq", stage, -1)
+        before.append(up)
+        after.append(down)
+    return before, after
 
 
 def place_of(stage):
@@ -387,6 +405,7 @@
     place, source = place_of(stage), place_of(above)
     width = pieces[0].shape[1]
     chunk = min(256, width)
+    gated_ref = outs[1] if apart and len(outs) > 1 else None
     for k, out_ref in zip(targets, outs):
         for piece in range(above_count):
             for at in range(0, width, chunk):
@@ -398,7 +417,10 @@
                 for w, part in zip(weights_of(logs, place, place ^ k), parts):
                     state = state + w * state_of(part, at_out)
                 out_ref[:STATE_SIZE, at_out] = state.astype(BF16)
-                out_ref[STATE_SIZE:, at_out] = block[STATE_SIZE:]
+                if gated_ref is not None:
+                    gated_ref[:, at_out] = block[STATE_SIZE:]
+                elif out_ref.shape[0] > STATE_SIZE:
+                    out_ref[STATE_SIZE:, at_out] = block[STATE_SIZE:]
 
 
 def intra_kernel(group, run_ref, runt_ref, stept_ref, skip_ref, x_ref, write_ref, read_ref, *refs):
@@ -406,7 +428,10 @@
     out_ref = refs[0]
     if len(refs) > 1:
         source_ref, out_ref, held_ref, sem = refs
-        fetch = pltpu.make_async_copy(source_ref, held_ref, sem)
+        wanted = held_ref.shape[0]
+        fetch = pltpu.make_async_copy(
+            source_ref.at[group * wanted : (group + 1) * wanted, :], held_ref, sem
+        )
         fetch.start()
     span, heads = run_ref.shape[1:]
     mid = span // 2
@@ -441,16 +466,16 @@
         fetch.wait()
 
 
-def intra(group, run, runt, stept, skip, x, write, read, after, wanted=()):
+def intra(group, run, runt, stept, skip, x, write, read, weight, after):
     span, per_group = run.shape[1:]
     wide = per_group * HEAD_DIM
     return call(
         functools.partial(intra_kernel, group),
         "intra",
-        [shape((span, wide), F32)] + [shape(value.shape, value.dtype) for value in wanted],
-        (run, runt, stept, skip, x, write, read, *map(in_hbm, wanted)),
-        specs=[WHOLE] * 7 + [IN_HBM] * len(wanted),
-        scratch=[pltpu.SemaphoreType.DMA] * len(wanted),
+        [shape((span, wide), F32), shape((wide, weight.shape[1]), weight.dtype)],
+        (run, runt, stept, skip, x, write, read, in_hbm(weight)),
+        specs=[WHOLE] * 7 + [IN_HBM],
+        scratch=[pltpu.SemaphoreType.DMA],
         after=after,
         flops=per_group * span * span * HEAD_DIM * 2,
         moved=wide * span * 6,
@@ -458,60 +483,43 @@
     )
 
 
-def finish_kernel(stage, offset, reach_ref, read_ref, entering_ref, *refs):
+def finish_kernel(stage, reach_ref, read_ref, own_ref, got_ref, *refs):
     base_refs, (out_ref, token_ref, held_ref, sems) = refs[:-4], refs[-4:]
-    if offset:
-        base_refs = base_refs[:-1]
     token_ref[...] = jnp.zeros_like(token_ref)
-    side = place_of(stage) ^ offset
+    place = place_of(stage)
     heads = reach_ref.shape[1] // 2
-    half = held_ref.shape[1]
-    wide = 2 * half // len(base_refs)
-    chunk = half // sems.shape[0]
+    lanes = held_ref.shape[1]
+    wide = lanes // len(base_refs)
+    half = lanes // 2
+    chunk = lanes // sems.shape[0]
     copies = []
-    for k, at in enumerate(range(0, half, chunk)):
-        found = []
-        for lane0 in (at, half + at):
-            group = lane0 // wide
-            found.append(
-                (
-                    read_ref[:, group * STATE_SIZE : (group + 1) * STATE_SIZE],
-                    base_refs[group][:, lane0 % wide : lane0 % wide + chunk],
-                )
-            )
-        reads, base = (jnp.where(side == 0, a, b) for a, b in zip(*found))
-        lane0 = side * half + at
-        inter = dot(reads, entering_ref[:STATE_SIZE, at : at + chunk])
+    for k, lane0 in enumerate(range(0, lanes, chunk)):
+        group, at = lane0 // wide, lane0 % half
+        at_in, at_out = slice(at, at + chunk), slice(lane0, lane0 + chunk)
+        entering = jnp.where(place == lane0 // half, own_ref[:, at_in], got_ref[:, at_in])
+        inter = dot(read_ref[:, group * STATE_SIZE : (group + 1) * STATE_SIZE], entering)
         inter = inter * dot(reach_ref[...], head_mask(2 * heads, heads, chunk, lane0))
-        held_ref[:, at : at + chunk] = (inter + base).astype(BF16)
+        base = base_refs[group][:, lane0 % wide : lane0 % wide + chunk]
+        held_ref[:, at_out] = (inter + base).astype(BF16)
         copies.append(
-            pltpu.make_async_copy(
-                held_ref.at[:, at : at + chunk], out_ref.at[:, window(lane0, chunk)], sems.at[k]
-            )
+            pltpu.make_async_copy(held_ref.at[:, at_out], out_ref.at[:, at_out], sems.at[k])
         )
         copies[-1].start()
     for copy in copies:
         copy.wait()
 
 
-def finish(stage, offset, reach, read, entering, bases, out, after):
-    span, half = read.shape[0], entering.shape[1]
-    chunk = min(512, half)
-    args = [reach, read, entering, *bases]
-    specs = [WHOLE] * len(args)
-    if offset:
-        args.append(out)
-        specs.append(IN_HBM)
+def finish(stage, reach, read, own, got, bases):
+    span = read.shape[0]
+    lanes = 2 * own.shape[1]
+    chunk = min(512, own.shape[1])
     return call(
-        functools.partial(finish_kernel, stage, offset),
+        functools.partial(finish_kernel, stage),
         "finish",
-        [shape((span, 2 * half), BF16), shape((8, 128), F32)],
-        args,
-        specs=specs,
+        [shape((span, lanes), BF16), shape((8, 128), F32)],
+        (reach, read, own, got, *bases),
         out_specs=[IN_HBM, WHOLE],
-        after=after,
-        alias={len(args) - 1: 0} if offset else None,
-        scratch=[pltpu.VMEM((span, half), BF16), pltpu.SemaphoreType.DMA((half // chunk,))],
+        scratch=[pltpu.VMEM((span, lanes), BF16), pltpu.SemaphoreType.DMA((lanes // chunk,))],
         moved=1,
     )
 
@@ -551,6 +559,49 @@
     return call(copy, "hand_on", [shape(value.shape, value.dtype)], [value], after=after)[0]
 
 
+def line_up_kernel(stage, axis, *refs):
+    refs, out_ref = refs[:-1], refs[-1]
+    place = place_of(stage)
+    size = refs[0].shape[1]
+    others = (len(refs) - 1) // 2
+
+    def put(ref, spot):
+        if axis == 0:
+            out_ref[spot] = ref[...]
+        else:
+            out_ref[:, window(spot * size, size)] = ref[...]
+
+    put(refs[0], place)
+    for k in range(1, others + 1):
+        pl.when(place - k >= 0)(functools.partial(put, refs[k], place - k))
+        pl.when(place + k < stage[0])(functools.partial(put, refs[others + k], place + k))
+
+
+def line_up(stage, axis, own, chained, after=()):
+    if axis == 0:
+        dims = (stage[0], *own.shape)
+    else:
+        dims = (own.shape[0], stage[0] * own.shape[1])
+    return call(
+        functools.partial(line_up_kernel, stage, axis),
+        "line_up",
+        [shape(dims, own.dtype)],
+        (own, *chained[0], *chained[1]),
+        after=after,
+        moved=1,
+    )[0]
+
+
+def stack_kernel(*refs):
+    for k, ref in enumerate(refs[:-1]):
+        refs[-1][k] = ref[...]
+
+
+def stack(parts, after=()):
+    dims = (len(parts), *parts[0].shape)
+    return call(stack_kernel, "stack", [shape(dims, parts[0].dtype)], parts, after=after, moved=1)[0]
+
+
 def join_kernel(axis, *refs):
     out_ref = refs[-1]
     for k, ref in enumerate(refs[:-1]):
@@ -570,56 +621,59 @@
     )[0]
 
 
-def project_kernel(stages, head_count, *refs):
-    owner_ref, own_rows, got_rows, own_ref, got_ref, gain_ref, weight_ref = refs[:7]
-    outs = refs[7 : 7 + head_count]
-    gated_ref, left_ref, total_ref = refs[7 + head_count :]
-    here, head = lax.axis_index("seq"), lax.axis_index("head")
-    place = place_of(stages[0])
+def project_kernel(stages, head_count, pieces, *refs):
+    owner_ref, own_rows, got_rows, own_ref, got_ref, gain_ref = refs[:6]
+    weight_refs, refs = refs[6 : 6 + pieces], refs[6 + pieces :]
+    outs, (gated_ref, left_ref, total_ref) = refs[:head_count], refs[head_count:]
+    head = lax.axis_index("head")
+    core, line, last = stages
+    place = place_of(core)
     half = own_ref.shape[1]
-    lanes = weight_ref.shape[0]
-    wide = min(1024, lanes)
-    rows = own_rows.shape[0]
+    lanes = 2 * half
+    wide = lanes // pieces
     for k, ref in enumerate((own_ref, got_ref)):
-        both = ref[STATE_SIZE:, :].astype(F32)
+        both = ref[...].astype(F32)
         gated_ref[:, window((place ^ k) * half, half)] = both[0:8] + both[8:16]
-    left_ref[0:rows, :] = own_rows[...]
-    left_ref[rows : 2 * rows, :] = got_rows[...]
-    for lane0 in range(0, lanes, wide):
-        at = slice(lane0, lane0 + wide)
+    row = 0
+    for ref in (own_rows, got_rows):
+        for k in range(line[0]):
+            for z in range(last[0]):
+                left_ref[row : row + DRAFTS, :] = ref[k, z]
+                row += DRAFTS
+    norm = min(1024, lanes)
+    for lane0 in range(0, lanes, norm):
+        at = slice(lane0, lane0 + norm)
         hidden = normed(gated_ref[:, at], gain_ref[:, at])
         hidden = jnp.concatenate([hidden, jnp.zeros_like(hidden)], axis=0)
-        left_ref[2 * rows :, at] = hidden.astype(BF16)
-    total_ref[...] = dot(left_ref[...], weight_ref[...])
-
-    per_head = 2 * rows // DRAFTS // head_count
-    offsets = [0]
-    for factor, stride in reversed(stages):
-        offsets = [a + k * stride for k in range(factor) for a in offsets]
+        left_ref[row:, at] = hidden.astype(BF16)
+    total_ref[...] = sum(
+        dot(left_ref[:, k * wide : (k + 1) * wide], ref[...]) for k, ref in enumerate(weight_refs)
+    )
+
+    per_head = row // DRAFTS // head_count
     owner = owner_ref[...]
-    tail = total_ref[2 * rows : 2 * rows + DRAFTS, :]
-    for k in range(head_count):
+    tail = total_ref[row : row + DRAFTS, :]
+    for k in list(range(1, head_count)) + [0]:
         first = (head ^ k) * per_head
         for slot in range(per_head):
             at = slice(slot * DRAFTS, (slot + 1) * DRAFTS)
-            offset = here ^ (first + slot)
-            block = jnp.int32(0)
-            for position, value in enumerate(offsets):
-                block = jnp.where(offset == value, position, block)
+            spot = first + slot
+            block = (lax.rem(spot, 2) ^ place) * line[0]
+            block = block + (lax.rem(lax.div(spot, line[1]), line[0]) ^ place_of(line))
+            block = block * last[0] + lax.div(spot, last[1])
             drawn = total_ref[window(block * DRAFTS, DRAFTS), :]
-            drawn = jnp.where(owner == first + slot, tail, drawn)
+            drawn = jnp.where(owner == spot, tail, drawn)
             outs[k][at, :] = drawn.astype(outs[k].dtype)
 
 
-def project(stages, owner, own_rows, got_rows, own, got, gain, weight, head_count, after):
-    lanes, cols = weight.shape
-    rows = 2 * own_rows.shape[0]
+def project(stages, owner, own_rows, got_rows, own, got, gain, weights, head_count):
+    lanes, cols = gain.shape[1], weights[0].shape[1]
+    rows = 2 * own_rows.size // lanes
     return call(
-        functools.partial(project_kernel, stages, head_count),
+        functools.partial(project_kernel, stages, head_count, len(weights)),
         "project",
         [shape((rows // head_count, cols), BF16 if k else F32) for k in range(head_count)],
-        (owner, own_rows, got_rows, own, got, gain, weight),
-        after=after,
+        (owner, own_rows, got_rows, own, got, gain, *weights),
         scratch=[
             pltpu.VMEM((DRAFTS, lanes), F32),
             pltpu.VMEM((rows + 16, lanes), BF16),
@@ -640,40 +694,35 @@
         verify_ref[...] = sum(ref[...].astype(F32) for ref in share_refs).astype(BF16)
     half = prompt_ref.shape[1]
     wide = 2 * half // (vwrite_ref.shape[1] // STATE_SIZE)
-    blocks = [0]
-    for factor, stride in scattered:
-        blocks = [a | (k * stride) for k in range(factor) for a in blocks]
-    width = half // len(blocks)
+    width = half
+    for factor, _ in scattered:
+        width //= factor
     chunk = half // sems.shape[0]
     is_owner = owner_ref[0:1, :STATE_SIZE] == here
     row = lax.broadcasted_iota(jnp.int32, (32, STATE_SIZE), 0)
     ones = jnp.where((row >= 24) & (row < 27), 1.0, 0.0)
     copies = []
-    for part in range(sems.shape[0]):
-        rows = slice(part * chunk, (part + 1) * chunk)
-        for lane in range(part * chunk, (part + 1) * chunk, width):
-            spot, size, rest = 0, half, lane
-            for factor, stride in scattered:
-                size = size // factor
-                spot |= rest // size * stride
-                rest %= size
-            apart = (spot ^ here) & sum((factor - 1) * stride for factor, stride in scattered)
-            position = jnp.int32(0)
-            for place, value in enumerate(blocks):
-                position = jnp.where(apart == value, place, position)
+    for step in range(sems.shape[0]):
+        rows = slice(step * chunk, (step + 1) * chunk)
+        for lane in range(step * chunk, (step + 1) * chunk, width):
+            line = scattered[0]
+            part = half // line[0]
+            position = (lane // part) ^ place_of(line)
+            if len(scattered) > 1:
+                position = lane % part // width * line[0] + position
             found = prompt_ref[:, window(position * width, width)]
             turned_ref[lane : lane + width, :] = found.astype(F32).T
-        groups = [start // wide for start in (part * chunk, half + part * chunk)]
+        groups = [start // wide for start in (step * chunk, half + step * chunk)]
         low, high = (vwrite_ref[:, g * STATE_SIZE : (g + 1) * STATE_SIZE] for g in groups)
         writes = jnp.where(side == 0, low, high).astype(F32)
         writes = jnp.concatenate([writes, writes, writes, jnp.zeros_like(writes)], axis=0)
         right = jnp.concatenate([writes, ones], axis=1).astype(BF16)
-        at = window(side * half + part * chunk, chunk)
+        at = window(side * half + step * chunk, chunk)
         left = tail_ref[:, at].astype(F32).T.astype(BF16)
         both = dot(left, right)
         start = jnp.where(is_owner, turned_ref[rows, :], resident_ref[at, :].astype(F32))
         held_ref[rows, :] = (start * both[:, STATE_SIZE:] + both[:, :STATE_SIZE]).astype(BF16)
-        copies.append(pltpu.make_async_copy(held_ref.at[rows, :], new_ref.at[at, :], sems.at[part]))
+        copies.append(pltpu.make_async_copy(held_ref.at[rows, :], new_ref.at[at, :], sems.at[step]))
         copies[-1].start()
     if offset:
         per_slice = slice_ref.shape[1] // STATE_SIZE
@@ -830,12 +879,11 @@
 
     def fill(after):
         if len(bases) < groups:
-            wanted = [] if bases else [out_weight]
-            base, *found = intra(
-                len(bases), run, runt, stept, skip_lanes, x, writes, reads, after, wanted
+            base, weight = intra(
+                len(bases), run, runt, stept, skip_lanes, x, writes, reads, out_weight, after
             )
             bases.append(base)
-            fetched.extend(found)
+            fetched.append(weight)
         return bases[-1:]
 
     def exchange(parts, stage):
@@ -854,14 +902,16 @@
         flops=half * UP_ROWS * 4,
     )
     line_parts = exchange(outs, line)
-    hiddens = exchange([hand_on(hidden, [outs[-1]])] * last[0], last)
+    hidden = hand_on(hidden, [outs[-1]])
+    hiddens = chain(hidden, last)
     filled = fill([outs[-1]])
+    arrived = [side[k] for side in hiddens for k in range(len(side) - 1)]
     outs = call(
         functools.partial(up_kernel, line, last, line[0], False),
         "up_last",
         [shape((UP_ROWS, last_width), BF16)] * (last[0] if split_last else 1),
         line_parts,
-        after=filled + hiddens[2:],
+        after=filled + arrived,
         flops=line_width * UP_ROWS * 4,
     )
     last_parts = exchange(outs if split_last else outs * last[0], last)
@@ -877,7 +927,7 @@
     )
 
     pieces = exchange(outs, last) if split_last else outs
-    hidden = join(hiddens, 0, [outs[-1]])
+    hidden = line_up(last, 0, hidden, hiddens, [outs[-1]])
     hiddens = exchange([hidden] * line[0], line)
     filled = fill([outs[-1]])
     prompts = exchange([prompt] * line[0], line)
@@ -890,36 +940,37 @@
         flops=line_width * UP_ROWS * 8,
     )
     pieces = exchange(outs, line)
-    filled = fill([outs[-1]])
+    hidden = stack(hiddens, [outs[-1]])
+    hiddens = [hidden, swap(hidden, "seq", core, 1)]
     scattered = [line, last] if split_last else [line]
-    hidden = join(hiddens, 0, [outs[-1]])
     prompt = join(prompts, 1, [outs[-1]])
-    prompts = exchange([prompt] * last[0], last) if split_last else [prompt]
+    filled = fill([outs[-1]]) + hiddens[1:]
+    if split_last:
+        prompts = chain(prompt, last)
+        filled += [side[k] for side in prompts for k in range(len(side) - 1)]
+
     def down_core(target, after):
         return call(
             functools.partial(down_kernel, core, line, line[0], 2, True, (target,), False),
             "down_core",
-            [shape((DOWN_ROWS, half), BF16)],
+            [shape((STATE_SIZE, half), BF16)] + [shape((16, half), BF16)] * target,
             turned(pieces) + core_parts,
             after=after,
             moved=1,
-        )[0]
-
-    sent = down_core(1, filled + [prompts[k] for k in (1, last[0] - 1) if split_last])
-    entering = [down_core(0, [sent]), swap(sent, "seq", core, 1)]
+        )
+
+    sent, gated = down_core(1, filled)
+    received_gated, received = swap(gated, "seq", core, 1), swap(sent, "seq", core, 1)
     while len(bases) < groups:
         fill([])
 
-    prefill_out, token = finish(core, 0, reach, reads, entering[0], bases, None, entering[:1])
-    shares = project(
-        stages, owner, hidden, swap(hidden, "seq", core, 1), *entering, gain, fetched[0], head_count, [token]
-    )
-    prefill_out, token = finish(
-        core, 1, reach, reads, entering[1], bases, prefill_out, [shares[0], token]
-    )
+    shares = project(stages, owner, *hiddens, gated, received_gated, gain, fetched, head_count)
+    (entering,) = down_core(0, shares[:1])
+    prefill_out, token = finish(core, reach, reads, entering, received, bases)
     shares = [shares[0]] + [swap(shares[k], "head", (head_count, 1), k) for k in range(1, head_count)]
 
-    prompt = join(prompts, 1, [token, *shares[1:]])
+    if split_last:
+        prompt = line_up(last, 1, prompt, prompts, [token, *shares[1:]])
     prompts = exchange([prompt] * 2, core)
     new_state, verify_out, state_slice = states(
         core, scattered, owner, resident, prompts, tail, vwrite, shares, seq_count

time: 62.7 us -> 82.8 us (1.32)
  starting transfers between devices: 23.7 us -> 53.4 us
  waiting for transfers between devices: 14.4 us -> 3.02 us
  Pallas kernels: 23.5 us -> 24.6 us
    ppermute x0 -> x12, starting transfers between devices: none -> 34.9 us  [shift(): return lax.ppermute(value, axis, pairs)]
    ppermute x22 -> x17, waiting for transfers between devices: 14.4 us -> 0.8 us  [swap(): lax.ppermute(value, axis, [(k, k ^ offset * stride) for k in range(count)])]
    ppermute x22 -> x17, starting transfers between devices: 23.7 us -> 18.5 us  [swap(): lax.ppermute(value, axis, [(k, k ^ offset * stride) for k in range(count)])]
    ppermute x0 -> x12, waiting for transfers between devices: none -> 2.22 us  [shift(): return lax.ppermute(value, axis, pairs)]
    pallas_call x24 -> x23, Pallas kernels: 23.5 us -> 24.6 us  [call(): pl.pallas_call(ordered(kernel, first), name=name, grid=grid, out_shape=ou...]
  transfers between devices with their start and end apart: 22 -> 29, of which waited for: 9 -> 5; matrix products, arithmetic and copies ran while one was open for 0% -> 0% of each run, Pallas kernels for 28% -> 22%
where the time goes in v2:
time: 82.8 us; the launch traced here: 82.2 us
  starting transfers between devices  53.4 us (64%)
  Pallas kernels  24.6 us (30%)
  waiting for transfers between devices  3.02 us (4%)
  between operations  1.25 us (2%)
    ppermute x12, starting transfers between devices, shift(): return lax.ppermute(value, axis, pairs)  34.9 us
    pallas_call x23, Pallas kernels, call(): pl.pallas_call(ordered(kernel, first), name=name, grid=grid, out_shape=ou...  24.6 us
    ppermute x17, starting transfers between devices, swap(): lax.ppermute(value, axis, [(k, k ^ offset * stride) for k in range(count)])  18.5 us
    ppermute x12, waiting for transfers between devices, shift(): return lax.ppermute(value, axis, pairs)  2.22 us
  transfers between devices with their start and end apart: 29, of which 5 were waited for; matrix products, arithmetic and copies ran while one was open for 0% of the time, Pallas kernels for 22%

profile of v2, /device:TPU:0, one launch (start us, length us, event | category | flops | bytes accessed | tf_op | source)
XLA Modules:
  0.0 82.2 jit_solution(12072153840423028536)
XLA Ops:
  0.6 2.9 %open_block.1 = (bf16[128,2048]{1,0:T(8,128)(2,1)S(1)}, f32[4,256,16]{2,1,0:T(8,128)S(1)}, f32[64,256]{1,0:T(8,128)S(1)}, f32[64,256]{1,0:T(8,128)S(1)}, bf16[25...) custom-call(f32[64,256]{1,0:T(8,128)} %bitcast.9, ...), custom_call_target="tpu_custom_call" | custom-call | flops 268435456 | bytes 8911232 | tf_op jit(solution)/shard_map/open_block/pallas_call | solution.py:113
  6.8 3.0 %collective-permute-start.6 = (bf16[160,1024]{1,0:T(8,128)(2,1)S(1)}, bf16[160,1024]{1,0:T(8,128)(2,1)S(1)}, u32[]{:S(2)}, u32[]{:S(2)}) collective-permute-start(bf16[160,1024]{1,0:T(8,128)(2,1)S(1)} %get-tuple-element.89.refs_0_), channel_id=1, source_target_pairs={{0,4},{2,6},{4,0},{6,2},{8,12},{10,14},{12,8},{14,10},{16,20},{18,... | collective-permute-start | bytes 983048 | tf_op jit(solution)/shard_map/ppermute | solution.py:44
  11.1 4.5 %collective-permute-start.2 = (bf16[8,4096]{1,0:T(8,128)(2,1)S(1)}, bf16[8,4096]{1,0:T(8,128)(2,1)S(1)}, u32[]{:S(2)}, u32[]{:S(2)}) collective-permute-start(bf16[8,4096]{1,0:T(8,128)(2,1)S(1)} %hand_on.1.refs_1_), channel_id=1, source_target_pairs={{0,8},{2,10},{4,12},{6,14},{8,16},{10,18},{12,20},{14,22},{16,24},... | collective-permute-start | bytes 196616 | tf_op jit(solution)/shard_map/ppermute | solution.py:52
  15.9 1.3 %collective-permute-start.5 = (bf16[8,4096]{1,0:T(8,128)(2,1)S(1)}, bf16[8,4096]{1,0:T(8,128)(2,1)S(1)}, u32[]{:S(2)}, u32[]{:S(2)}) collective-permute-start(bf16[8,4096]{1,0:T(8,128)(2,1)S(1)} %collective-permute-done.4.refs_3_.refs_5_), channel_id=1, source_target_pairs={{8,0},{10,2},{12,4},{14,6},{16,8},{18,10},{20,12},{22,14},{24,16},... | collective-permute-start | bytes 196616 | tf_op jit(solution)/shard_map/ppermute | solution.py:52
  17.5 4.3 %collective-permute-start.3 = (bf16[8,4096]{1,0:T(8,128)(2,1)S(1)}, bf16[8,4096]{1,0:T(8,128)(2,1)S(1)}, u32[]{:S(2)}, u32[]{:S(2)}) collective-permute-start(bf16[8,4096]{1,0:T(8,128)(2,1)S(1)} %collective-permute-done.2.refs_1_.refs_2_), channel_id=1, source_target_pairs={{0,8},{2,10},{4,12},{6,14},{8,16},{10,18},{12,20},{14,22},{16,24},... | collective-permute-start | bytes 196616 | tf_op jit(solution)/shard_map/ppermute | solution.py:52
  21.8 2.7 %intra.4 = (f32[256,1024]{1,0:T(8,128)S(1)}, bf16[1024,512]{1,0:T(8,128)(2,1)S(1)}) custom-call(bf16[160,1024]{1,0:T(8,128)(2,1)S(1)} %get-tuple-element.89.refs_0_, f32[4,256,16]{2,1,0:T(8,128)S(1)} %get-tuple-element.90.refs_1_, f32[64,256]{1,0:T(8,128)S(1)} %get-tuple-element.71.refs_4_.refs_2_, f32[64,256]{1,0:T(8,128)S(1)} %get-tuple-element.91.refs_3_, ...), custom_call_target="tpu_custom_call" | custom-call | flops 134217728 | bytes 1572864 | tf_op jit(solution)/shard_map/intra/pallas_call | solution.py:113
  24.7 2.7 %collective-permute-start.8 = (bf16[160,256]{1,0:T(8,128)(2,1)S(1)}, bf16[160,256]{1,0:T(8,128)(2,1)S(1)}, u32[]{:S(2)}, u32[]{:S(2)}) collective-permute-start(bf16[160,256]{1,0:T(8,128)(2,1)S(1)} %get-tuple-element.98), channel_id=1, source_target_pairs={{0,16},{2,18},{4,20},{6,22},{8,24},{10,26},{12,28},{14,30},{16,0},... | collective-permute-start | bytes 245768 | tf_op jit(solution)/shard_map/ppermute | solution.py:44
  27.3 1.5 %collective-permute-start.9 = (bf16[160,256]{1,0:T(8,128)(2,1)S(1)}, bf16[160,256]{1,0:T(8,128)(2,1)S(1)}, u32[]{:S(2)}, u32[]{:S(2)}) collective-permute-start(bf16[160,256]{1,0:T(8,128)(2,1)S(1)} %get-tuple-element.99), channel_id=1, source_target_pairs={{0,8},{2,10},{4,12},{6,14},{8,0},{10,2},{12,4},{14,6},{16,24},{18,... | collective-permute-start | bytes 245768 | tf_op jit(solution)/shard_map/ppermute | solution.py:44
  30.4 4.5 %collective-permute-start.11 = (bf16[8,4096]{1,0:T(8,128)(2,1)S(1)}, bf16[8,4096]{1,0:T(8,128)(2,1)S(1)}, u32[]{:S(2)}, u32[]{:S(2)}) collective-permute-start(bf16[8,4096]{1,0:T(8,128)(2,1)S(1)} %collective-permute-done.3.refs_2_.refs_3_), channel_id=1, source_target_pairs={{0,8},{2,10},{4,12},{6,14},{8,16},{10,18},{12,20},{14,22},{16,24},... | collective-permute-start | bytes 196616 | tf_op jit(solution)/shard_map/ppermute | solution.py:52
  35.0 2.7 %intra.5 = (f32[256,1024]{1,0:T(8,128)S(1)}, bf16[1024,512]{1,0:T(8,128)(2,1)S(1)}) custom-call(bf16[160,256]{1,0:T(8,128)(2,1)S(1)} %get-tuple-element.95.refs_0_, f32[4,256,16]{2,1,0:T(8,128)S(1)} %get-tuple-element.90.refs_1_, f32[64,256]{1,0:T(8,128)S(1)} %get-tuple-element.71.refs_4_.refs_2_, f32[64,256]{1,0:T(8,128)S(1)} %get-tuple-element.91.refs_3_, ...), custom_call_target="tpu_custom_call" | custom-call | flops 134217728 | bytes 1572864 | tf_op jit(solution)/shard_map/intra/pallas_call | solution.py:113
  38.4 2.0 %collective-permute-start.15 = (bf16[144,256]{1,0:T(8,128)(2,1)S(1)}, bf16[144,256]{1,0:T(8,128)(2,1)S(1)}, u32[]{:S(2)}, u32[]{:S(2)}) collective-permute-start(bf16[144,256]{1,0:T(8,128)(2,1)S(1)} %get-tuple-element.104), channel_id=1, source_target_pairs={{0,16},{2,18},{4,20},{6,22},{8,24},{10,26},{12,28},{14,30},{16,0},... | collective-permute-start | bytes 221192 | tf_op jit(solution)/shard_map/ppermute | solution.py:44
  42.8 1.8 %collective-permute-start.10 = (bf16[128,256]{1,0:T(8,128)(2,1)S(1)}, bf16[128,256]{1,0:T(8,128)(2,1)S(1)}, u32[]{:S(2)}, u32[]{:S(2)}) collective-permute-start(bf16[128,256]{1,0:T(8,128)(2,1)S(1)} %get-tuple-element.102.refs_1_), channel_id=1, source_target_pairs={{0,4},{2,6},{4,0},{6,2},{8,12},{10,14},{12,8},{14,10},{16,20},{18,... | collective-permute-start | bytes 196616 | tf_op jit(solution)/shard_map/ppermute | solution.py:44
  44.6 2.7 %intra.6 = (f32[256,1024]{1,0:T(8,128)S(1)}, bf16[1024,512]{1,0:T(8,128)(2,1)S(1)}) custom-call(bf16[144,256]{1,0:T(8,128)(2,1)S(1)} %get-tuple-element.100.refs_0_, f32[4,256,16]{2,1,0:T(8,128)S(1)} %get-tuple-element.90.refs_1_, f32[64,256]{1,0:T(8,128)S(1)} %get-tuple-element.71.refs_4_.refs_2_, f32[64,256]{1,0:T(8,128)S(1)} %get-tuple-element.91.refs_3_, ...), custom_call_target="tpu_custom_call" | custom-call | flops 134217728 | bytes 1572864 | tf_op jit(solution)/shard_map/intra/pallas_call | solution.py:113
  48.2 1.6 %collective-permute-start.22 = (bf16[144,1024]{1,0:T(8,128)(2,1)S(1)}, bf16[144,1024]{1,0:T(8,128)(2,1)S(1)}, u32[]{:S(2)}, u32[]{:S(2)}) collective-permute-start(bf16[144,1024]{1,0:T(8,128)(2,1)S(1)} %get-tuple-element.106.refs_0_), channel_id=1, source_target_pairs={{0,4},{2,6},{4,0},{6,2},{8,12},{10,14},{12,8},{14,10},{16,20},{18,... | collective-permute-start | bytes 884744 | tf_op jit(solution)/shard_map/ppermute | solution.py:44
  49.8 1.3 %collective-permute-start.20 = (bf16[128,512]{1,0:T(8,128)(2,1)S(1)}, bf16[128,512]{1,0:T(8,128)(2,1)S(1)}, u32[]{:S(2)}, u32[]{:S(2)}) collective-permute-start(bf16[128,512]{1,0:T(8,128)(2,1)S(1)} %join.1.refs_2_), channel_id=1, source_target_pairs={{8,0},{10,2},{12,4},{14,6},{16,8},{18,10},{20,12},{22,14},{24,16},... | collective-permute-start | bytes 393224 | tf_op jit(solution)/shard_map/ppermute | solution.py:52
  51.1 4.6 %collective-permute-start.18 = (bf16[128,512]{1,0:T(8,128)(2,1)S(1)}, bf16[128,512]{1,0:T(8,128)(2,1)S(1)}, u32[]{:S(2)}, u32[]{:S(2)}) collective-permute-start(bf16[128,512]{1,0:T(8,128)(2,1)S(1)} %join.1.refs_2_), channel_id=1, source_target_pairs={{0,8},{2,10},{4,12},{6,14},{8,16},{10,18},{12,20},{14,22},{16,24},... | collective-permute-start | bytes 393224 | tf_op jit(solution)/shard_map/ppermute | solution.py:52
  55.6 1.6 %collective-permute-done.20.refs_4_.refs_6_ = bf16[128,512]{1,0:T(8,128)(2,1)S(1)} collective-permute-done((bf16[128,512]{1,0:T(8,128)(2,1)S(1)}, bf16[128,512]{1,0:T(8,128)(2,1)S(1)}, u32[]{:S(2)}, u32[]{:S(2)}) %collective-permute-start.20) | collective-permute-done | bytes 131104 | tf_op jit(solution)/shard_map/ppermute | solution.py:52
  58.5 4.7 %collective-permute-start.19 = (bf16[128,512]{1,0:T(8,128)(2,1)S(1)}, bf16[128,512]{1,0:T(8,128)(2,1)S(1)}, u32[]{:S(2)}, u32[]{:S(2)}) collective-permute-start(bf16[128,512]{1,0:T(8,128)(2,1)S(1)} %collective-permute-done.18.refs_2_.refs_3_), channel_id=1, source_target_pairs={{0,8},{2,10},{4,12},{6,14},{8,16},{10,18},{12,20},{14,22},{16,24},... | collective-permute-start | bytes 393224 | tf_op jit(solution)/shard_map/ppermute | solution.py:52
  63.3 2.7 %intra.7 = (f32[256,1024]{1,0:T(8,128)S(1)}, bf16[1024,512]{1,0:T(8,128)(2,1)S(1)}) custom-call(bf16[144,1024]{1,0:T(8,128)(2,1)S(1)} %get-tuple-element.106.refs_0_, f32[4,256,16]{2,1,0:T(8,128)S(1)} %get-tuple-element.90.refs_1_, f32[64,256]{1,0:T(8,128)S(1)} %get-tuple-element.71.refs_4_.refs_2_, f32[64,256]{1,0:T(8,128)S(1)} %get-tuple-element.91.refs_3_, ...), custom_call_target="tpu_custom_call" | custom-call | flops 134217728 | bytes 1572864 | tf_op jit(solution)/shard_map/intra/pallas_call | solution.py:113
  68.3 4.6 %collective-permute-start.26 = (bf16[128,512]{1,0:T(8,128)(2,1)S(1)}, bf16[128,512]{1,0:T(8,128)(2,1)S(1)}, u32[]{:S(2)}, u32[]{:S(2)}) collective-permute-start(bf16[128,512]{1,0:T(8,128)(2,1)S(1)} %collective-permute-done.19.refs_3_.refs_4_), channel_id=1, source_target_pairs={{0,8},{2,10},{4,12},{6,14},{8,16},{10,18},{12,20},{14,22},{16,24},... | collective-permute-start | bytes 393224 | tf_op jit(solution)/shard_map/ppermute | solution.py:52
  73.8 1.6 %collective-permute-start.25 = (bf16[64,512]{1,0:T(8,128)(2,1)S(1)}, bf16[64,512]{1,0:T(8,128)(2,1)S(1)}, u32[]{:S(2)}, u32[]{:S(2)}) collective-permute-start(bf16[64,512]{1,0:T(8,128)(2,1)S(1)} %get-tuple-element.118), channel_id=1, source_target_pairs={{0,1},{1,0},{2,3},{3,2},{4,5},{5,4},{6,7},{7,6},{8,9},{9,8},{10,11... | collective-permute-start | bytes 196616 | tf_op jit(solution)/shard_map/ppermute | solution.py:44
  75.7 2.0 %finish.1 = (bf16[256,4096]{1,0:T(8,128)(2,1)}, f32[8,128]{1,0:T(8,128)S(1)}) custom-call(bf16[256,128]{1,0:T(8,128)(2,1)S(1)} %get-tuple-element.65.refs_0_, bf16[256,512]{1,0:T(8,128)(2,1)S(1)} %get-tuple-element.66.refs_7_.refs_1_, bf16[128,2048]{1,0:T(8,128)(2,1)S(1)} %down_core.3.refs_2_, bf16[128,2048]{1,0:T(8,128)(2,1)S(1)} %collective-permute-done.24.refs_3_, ...), custom_call_target="tpu_custom_call" | custom-call | bytes 1 | tf_op jit(solution)/shard_map/finish/pallas_call | solution.py:113
  78.3 1.9 %states.2 = (bf16[4096,128]{1,0:T(8,128)(2,1)}, f32[2048,128]{1,0:T(8,128)S(1)}, bf16[64,512]{1,0:T(8,128)(2,1)}) custom-call(s32[8,512]{1,0:T(8,128)S(1)} %get-tuple-element.67.refs_3_.refs_0_, bf16[4096,128]{1,0:T(8,128)(2,1)S(1)} %get-tuple-element.83.refs_1_, bf16[128,2048]{1,0:T(8,128)(2,1)S(1)} %line_up.3.refs_2_, ...), custom_call_target="tpu_custom_call" | custom-call | flops 33554432 | bytes 1572864 | tf_op jit(solution)/shard_map/states/pallas_call | solution.py:113
  80.2 1.9 %states.3 = (bf16[4096,128]{1,0:T(8,128)(2,1)}, bf16[64,512]{1,0:T(8,128)(2,1)}) custom-call(s32[8,512]{1,0:T(8,128)S(1)} %get-tuple-element.67.refs_3_.refs_0_, bf16[4096,128]{1,0:T(8,128)(2,1)S(1)} %get-tuple-element.83.refs_1_, bf16[128,2048]{1,0:T(8,128)(2,1)S(1)} %collective-permute-done.28.refs_2_, ...), custom_call_target="tpu_custom_call", output_to_operand_aliasing={{0}: (6, {})} | custom-call | flops 33554432 | bytes 1572864 | tf_op jit(solution)/shard_map/states/pallas_call | solution.py:113
  (57 shorter events, 16.1 us)
Async XLA Ops:
  6.8 17.7 %collective-permute-start.6 = (bf16[160,1024]{1,0:T(8,128)(2,1)S(1)}, bf16[160,1024]{1,0:T(8,128)(2,1)S(1)}, u32[]{:S(2)}, u32[]{:S(2)}) collective-permute-start(bf16[160,1024]{1,0:T(8,128)(2,1)S(1)} %get-tuple-element.89.refs_0_), channel_id=1, source_target_pairs={{0,4},{2,6},{4,0},{6,2},{8,12},{10,14},{12,8},{14,10},{16,20},{18,... | collective-permute-start | bytes 983048 | tf_op jit(solution)/shard_map/ppermute | solution.py:44
  9.8 6.1 %collective-permute-start.4 = (bf16[8,4096]{1,0:T(8,128)(2,1)S(1)}, bf16[8,4096]{1,0:T(8,128)(2,1)S(1)}, u32[]{:S(2)}, u32[]{:S(2)}) collective-permute-start(bf16[8,4096]{1,0:T(8,128)(2,1)S(1)} %hand_on.1.refs_1_), channel_id=1, source_target_pairs={{8,0},{10,2},{12,4},{14,6},{16,8},{18,10},{20,12},{22,14},{24,16},... | collective-permute-start | bytes 196616 | tf_op jit(solution)/shard_map/ppermute | solution.py:52
  11.1 6.4 %collective-permute-start.2 = (bf16[8,4096]{1,0:T(8,128)(2,1)S(1)}, bf16[8,4096]{1,0:T(8,128)(2,1)S(1)}, u32[]{:S(2)}, u32[]{:S(2)}) collective-permute-start(bf16[8,4096]{1,0:T(8,128)(2,1)S(1)} %hand_on.1.refs_1_), channel_id=1, source_target_pairs={{0,8},{2,10},{4,12},{6,14},{8,16},{10,18},{12,20},{14,22},{16,24},... | collective-permute-start | bytes 196616 | tf_op jit(solution)/shard_map/ppermute | solution.py:52
  15.9 8.5 %collective-permute-start.5 = (bf16[8,4096]{1,0:T(8,128)(2,1)S(1)}, bf16[8,4096]{1,0:T(8,128)(2,1)S(1)}, u32[]{:S(2)}, u32[]{:S(2)}) collective-permute-start(bf16[8,4096]{1,0:T(8,128)(2,1)S(1)} %collective-permute-done.4.refs_3_.refs_5_), channel_id=1, source_target_pairs={{8,0},{10,2},{12,4},{14,6},{16,8},{18,10},{20,12},{22,14},{24,16},... | collective-permute-start | bytes 196616 | tf_op jit(solution)/shard_map/ppermute | solution.py:52
  17.5 7.0 %collective-permute-start.3 = (bf16[8,4096]{1,0:T(8,128)(2,1)S(1)}, bf16[8,4096]{1,0:T(8,128)(2,1)S(1)}, u32[]{:S(2)}, u32[]{:S(2)}) collective-permute-start(bf16[8,4096]{1,0:T(8,128)(2,1)S(1)} %collective-permute-done.2.refs_1_.refs_2_), channel_id=1, source_target_pairs={{0,8},{2,10},{4,12},{6,14},{8,16},{10,18},{12,20},{14,22},{16,24},... | collective-permute-start | bytes 196616 | tf_op jit(solution)/shard_map/ppermute | solution.py:52
  24.7 13.0 %collective-permute-start.8 = (bf16[160,256]{1,0:T(8,128)(2,1)S(1)}, bf16[160,256]{1,0:T(8,128)(2,1)S(1)}, u32[]{:S(2)}, u32[]{:S(2)}) collective-permute-start(bf16[160,256]{1,0:T(8,128)(2,1)S(1)} %get-tuple-element.98), channel_id=1, source_target_pairs={{0,16},{2,18},{4,20},{6,22},{8,24},{10,26},{12,28},{14,30},{16,0},... | collective-permute-start | bytes 245768 | tf_op jit(solution)/shard_map/ppermute | solution.py:44
  27.3 10.3 %collective-permute-start.9 = (bf16[160,256]{1,0:T(8,128)(2,1)S(1)}, bf16[160,256]{1,0:T(8,128)(2,1)S(1)}, u32[]{:S(2)}, u32[]{:S(2)}) collective-permute-start(bf16[160,256]{1,0:T(8,128)(2,1)S(1)} %get-tuple-element.99), channel_id=1, source_target_pairs={{0,8},{2,10},{4,12},{6,14},{8,0},{10,2},{12,4},{14,6},{16,24},{18,... | collective-permute-start | bytes 245768 | tf_op jit(solution)/shard_map/ppermute | solution.py:44
  28.9 8.8 %collective-permute-start.7 = (bf16[160,256]{1,0:T(8,128)(2,1)S(1)}, bf16[160,256]{1,0:T(8,128)(2,1)S(1)}, u32[]{:S(2)}, u32[]{:S(2)}) collective-permute-start(bf16[160,256]{1,0:T(8,128)(2,1)S(1)} %get-tuple-element.95.refs_0_), channel_id=1, source_target_pairs={{0,24},{2,26},{4,28},{6,30},{8,16},{10,18},{12,20},{14,22},{16,8},... | collective-permute-start | bytes 245768 | tf_op jit(solution)/shard_map/ppermute | solution.py:44
  29.1 8.9 %collective-permute-start.12 = (bf16[8,4096]{1,0:T(8,128)(2,1)S(1)}, bf16[8,4096]{1,0:T(8,128)(2,1)S(1)}, u32[]{:S(2)}, u32[]{:S(2)}) collective-permute-start(bf16[8,4096]{1,0:T(8,128)(2,1)S(1)} %collective-permute-done.5.refs_4_.refs_6_), channel_id=1, source_target_pairs={{8,0},{10,2},{12,4},{14,6},{16,8},{18,10},{20,12},{22,14},{24,16},... | collective-permute-start | bytes 196616 | tf_op jit(solution)/shard_map/ppermute | solution.py:52
  30.4 7.6 %collective-permute-start.11 = (bf16[8,4096]{1,0:T(8,128)(2,1)S(1)}, bf16[8,4096]{1,0:T(8,128)(2,1)S(1)}, u32[]{:S(2)}, u32[]{:S(2)}) collective-permute-start(bf16[8,4096]{1,0:T(8,128)(2,1)S(1)} %collective-permute-done.3.refs_2_.refs_3_), channel_id=1, source_target_pairs={{0,8},{2,10},{4,12},{6,14},{8,16},{10,18},{12,20},{14,22},{16,24},... | collective-permute-start | bytes 196616 | tf_op jit(solution)/shard_map/ppermute | solution.py:52
  38.1 9.6 %collective-permute-start.13 = (bf16[4,8,4096]{2,1,0:T(8,128)(2,1)S(1)}, bf16[4,8,4096]{2,1,0:T(8,128)(2,1)S(1)}, u32[]{:S(2)}, u32[]{:S(2)}) collective-permute-start(bf16[4,8,4096]{2,1,0:T(8,128)(2,1)S(1)} %line_up.2.refs_1_), channel_id=1, source_target_pairs={{0,4},{2,6},{4,0},{6,2},{8,12},{10,14},{12,8},{14,10},{16,20},{18,... | collective-permute-start | bytes 786440 | tf_op jit(solution)/shard_map/ppermute | solution.py:44
  38.4 8.8 %collective-permute-start.15 = (bf16[144,256]{1,0:T(8,128)(2,1)S(1)}, bf16[144,256]{1,0:T(8,128)(2,1)S(1)}, u32[]{:S(2)}, u32[]{:S(2)}) collective-permute-start(bf16[144,256]{1,0:T(8,128)(2,1)S(1)} %get-tuple-element.104), channel_id=1, source_target_pairs={{0,16},{2,18},{4,20},{6,22},{8,24},{10,26},{12,28},{14,30},{16,0},... | collective-permute-start | bytes 221192 | tf_op jit(solution)/shard_map/ppermute | solution.py:44
  40.4 6.9 %collective-permute-start.16 = (bf16[144,256]{1,0:T(8,128)(2,1)S(1)}, bf16[144,256]{1,0:T(8,128)(2,1)S(1)}, u32[]{:S(2)}, u32[]{:S(2)}) collective-permute-start(bf16[144,256]{1,0:T(8,128)(2,1)S(1)} %get-tuple-element.105), channel_id=1, source_target_pairs={{0,8},{2,10},{4,12},{6,14},{8,0},{10,2},{12,4},{14,6},{16,24},{18,... | collective-permute-start | bytes 221192 | tf_op jit(solution)/shard_map/ppermute | solution.py:44
  41.5 6.2 %collective-permute-start.14 = (bf16[144,256]{1,0:T(8,128)(2,1)S(1)}, bf16[144,256]{1,0:T(8,128)(2,1)S(1)}, u32[]{:S(2)}, u32[]{:S(2)}) collective-permute-start(bf16[144,256]{1,0:T(8,128)(2,1)S(1)} %get-tuple-element.100.refs_0_), channel_id=1, source_target_pairs={{0,24},{2,26},{4,28},{6,30},{8,16},{10,18},{12,20},{14,22},{16,8},... | collective-permute-start | bytes 221192 | tf_op jit(solution)/shard_map/ppermute | solution.py:44
  48.1 17.9 %collective-permute-start.17 = (bf16[2,4,8,4096]{3,2,1,0:T(8,128)(2,1)S(1)}, bf16[2,4,8,4096]{3,2,1,0:T(8,128)(2,1)S(1)}, u32[]{:S(2)}, u32[]{:S(2)}) collective-permute-start(bf16[2,4,8,4096]{3,2,1,0:T(8,128)(2,1)S(1)} %stack.1.refs_1_), channel_id=1, source_target_pairs={{0,2},{2,0},{4,6},{6,4},{8,10},{10,8},{12,14},{14,12},{16,18},{18,... | collective-permute-start | bytes 1572872 | tf_op jit(solution)/shard_map/ppermute | solution.py:44
  48.2 17.8 %collective-permute-start.22 = (bf16[144,1024]{1,0:T(8,128)(2,1)S(1)}, bf16[144,1024]{1,0:T(8,128)(2,1)S(1)}, u32[]{:S(2)}, u32[]{:S(2)}) collective-permute-start(bf16[144,1024]{1,0:T(8,128)(2,1)S(1)} %get-tuple-element.106.refs_0_), channel_id=1, source_target_pairs={{0,4},{2,6},{4,0},{6,2},{8,12},{10,14},{12,8},{14,10},{16,20},{18,... | collective-permute-start | bytes 884744 | tf_op jit(solution)/shard_map/ppermute | solution.py:44
  49.8 7.5 %collective-permute-start.20 = (bf16[128,512]{1,0:T(8,128)(2,1)S(1)}, bf16[128,512]{1,0:T(8,128)(2,1)S(1)}, u32[]{:S(2)}, u32[]{:S(2)}) collective-permute-start(bf16[128,512]{1,0:T(8,128)(2,1)S(1)} %join.1.refs_2_), channel_id=1, source_target_pairs={{8,0},{10,2},{12,4},{14,6},{16,8},{18,10},{20,12},{22,14},{24,16},... | collective-permute-start | bytes 393224 | tf_op jit(solution)/shard_map/ppermute | solution.py:52
  51.1 7.5 %collective-permute-start.18 = (bf16[128,512]{1,0:T(8,128)(2,1)S(1)}, bf16[128,512]{1,0:T(8,128)(2,1)S(1)}, u32[]{:S(2)}, u32[]{:S(2)}) collective-permute-start(bf16[128,512]{1,0:T(8,128)(2,1)S(1)} %join.1.refs_2_), channel_id=1, source_target_pairs={{0,8},{2,10},{4,12},{6,14},{8,16},{10,18},{12,20},{14,22},{16,24},... | collective-permute-start | bytes 393224 | tf_op jit(solution)/shard_map/ppermute | solution.py:52
  57.2 8.7 %collective-permute-start.21 = (bf16[128,512]{1,0:T(8,128)(2,1)S(1)}, bf16[128,512]{1,0:T(8,128)(2,1)S(1)}, u32[]{:S(2)}, u32[]{:S(2)}) collective-permute-start(bf16[128,512]{1,0:T(8,128)(2,1)S(1)} %collective-permute-done.20.refs_4_.refs_6_), channel_id=1, source_target_pairs={{8,0},{10,2},{12,4},{14,6},{16,8},{18,10},{20,12},{22,14},{24,16},... | collective-permute-start | bytes 393224 | tf_op jit(solution)/shard_map/ppermute | solution.py:52
  58.5 7.4 %collective-permute-start.19 = (bf16[128,512]{1,0:T(8,128)(2,1)S(1)}, bf16[128,512]{1,0:T(8,128)(2,1)S(1)}, u32[]{:S(2)}, u32[]{:S(2)}) collective-permute-start(bf16[128,512]{1,0:T(8,128)(2,1)S(1)} %collective-permute-done.18.refs_2_.refs_3_), channel_id=1, source_target_pairs={{0,8},{2,10},{4,12},{6,14},{8,16},{10,18},{12,20},{14,22},{16,24},... | collective-permute-start | bytes 393224 | tf_op jit(solution)/shard_map/ppermute | solution.py:52
  66.4 9.3 %collective-permute-start.24 = (bf16[128,2048]{1,0:T(8,128)(2,1)S(1)}, bf16[128,2048]{1,0:T(8,128)(2,1)S(1)}, u32[]{:S(2)}, u32[]{:S(2)}) collective-permute-start(bf16[128,2048]{1,0:T(8,128)(2,1)S(1)} %get-tuple-element.115), channel_id=1, source_target_pairs={{0,2},{2,0},{4,6},{6,4},{8,10},{10,8},{12,14},{14,12},{16,18},{18,... | collective-permute-start | bytes 1572872 | tf_op jit(solution)/shard_map/ppermute | solution.py:44
  66.5 6.4 %collective-permute-start.23 = (bf16[16,2048]{1,0:T(8,128)(2,1)S(1)}, bf16[16,2048]{1,0:T(8,128)(2,1)S(1)}, u32[]{:S(2)}, u32[]{:S(2)}) collective-permute-start(bf16[16,2048]{1,0:T(8,128)(2,1)S(1)} %get-tuple-element.109.refs_3_), channel_id=1, source_target_pairs={{0,2},{2,0},{4,6},{6,4},{8,10},{10,8},{12,14},{14,12},{16,18},{18,... | collective-permute-start | bytes 196616 | tf_op jit(solution)/shard_map/ppermute | solution.py:44
  67.0 10.8 %collective-permute-start.27 = (bf16[128,512]{1,0:T(8,128)(2,1)S(1)}, bf16[128,512]{1,0:T(8,128)(2,1)S(1)}, u32[]{:S(2)}, u32[]{:S(2)}) collective-permute-start(bf16[128,512]{1,0:T(8,128)(2,1)S(1)} %collective-permute-done.21.refs_5_.refs_7_), channel_id=1, source_target_pairs={{8,0},{10,2},{12,4},{14,6},{16,8},{18,10},{20,12},{22,14},{24,16},... | collective-permute-start | bytes 393224 | tf_op jit(solution)/shard_map/ppermute | solution.py:52
  68.3 9.5 %collective-permute-start.26 = (bf16[128,512]{1,0:T(8,128)(2,1)S(1)}, bf16[128,512]{1,0:T(8,128)(2,1)S(1)}, u32[]{:S(2)}, u32[]{:S(2)}) collective-permute-start(bf16[128,512]{1,0:T(8,128)(2,1)S(1)} %collective-permute-done.19.refs_3_.refs_4_), channel_id=1, source_target_pairs={{0,8},{2,10},{4,12},{6,14},{8,16},{10,18},{12,20},{14,22},{16,24},... | collective-permute-start | bytes 393224 | tf_op jit(solution)/shard_map/ppermute | solution.py:52
  (5 other events, 15.1 us)

commit v3 on v1

--- a/solution.py
+++ b/solution.py
@@ -387,6 +387,7 @@
     place, source = place_of(stage), place_of(above)
     width = pieces[0].shape[1]
     chunk = min(256, width)
+    gated_ref = outs[1] if apart and len(outs) > 1 else None
     for k, out_ref in zip(targets, outs):
         for piece in range(above_count):
             for at in range(0, width, chunk):
@@ -398,7 +399,10 @@
                 for w, part in zip(weights_of(logs, place, place ^ k), parts):
                     state = state + w * state_of(part, at_out)
                 out_ref[:STATE_SIZE, at_out] = state.astype(BF16)
-                out_ref[STATE_SIZE:, at_out] = block[STATE_SIZE:]
+                if gated_ref is not None:
+                    gated_ref[:, at_out] = block[STATE_SIZE:]
+                elif out_ref.shape[0] > STATE_SIZE:
+                    out_ref[STATE_SIZE:, at_out] = block[STATE_SIZE:]
 
 
 def intra_kernel(group, run_ref, runt_ref, stept_ref, skip_ref, x_ref, write_ref, read_ref, *refs):
@@ -458,60 +462,43 @@
     )
 
 
-def finish_kernel(stage, offset, reach_ref, read_ref, entering_ref, *refs):
+def finish_kernel(stage, reach_ref, read_ref, own_ref, got_ref, *refs):
     base_refs, (out_ref, token_ref, held_ref, sems) = refs[:-4], refs[-4:]
-    if offset:
-        base_refs = base_refs[:-1]
     token_ref[...] = jnp.zeros_like(token_ref)
-    side = place_of(stage) ^ offset
+    place = place_of(stage)
     heads = reach_ref.shape[1] // 2
-    half = held_ref.shape[1]
-    wide = 2 * half // len(base_refs)
-    chunk = half // sems.shape[0]
+    lanes = held_ref.shape[1]
+    wide = lanes // len(base_refs)
+    half = lanes // 2
+    chunk = lanes // sems.shape[0]
     copies = []
-    for k, at in enumerate(range(0, half, chunk)):
-        found = []
-        for lane0 in (at, half + at):
-            group = lane0 // wide
-            found.append(
-                (
-                    read_ref[:, group * STATE_SIZE : (group + 1) * STATE_SIZE],
-                    base_refs[group][:, lane0 % wide : lane0 % wide + chunk],
-                )
-            )
-        reads, base = (jnp.where(side == 0, a, b) for a, b in zip(*found))
-        lane0 = side * half + at
-        inter = dot(reads, entering_ref[:STATE_SIZE, at : at + chunk])
+    for k, lane0 in enumerate(range(0, lanes, chunk)):
+        group, at = lane0 // wide, lane0 % half
+        at_in, at_out = slice(at, at + chunk), slice(lane0, lane0 + chunk)
+        entering = jnp.where(place == lane0 // half, own_ref[:, at_in], got_ref[:, at_in])
+        inter = dot(read_ref[:, group * STATE_SIZE : (group + 1) * STATE_SIZE], entering)
         inter = inter * dot(reach_ref[...], head_mask(2 * heads, heads, chunk, lane0))
-        held_ref[:, at : at + chunk] = (inter + base).astype(BF16)
+        base = base_refs[group][:, lane0 % wide : lane0 % wide + chunk]
+        held_ref[:, at_out] = (inter + base).astype(BF16)
         copies.append(
-            pltpu.make_async_copy(
-                held_ref.at[:, at : at + chunk], out_ref.at[:, window(lane0, chunk)], sems.at[k]
-            )
+            pltpu.make_async_copy(held_ref.at[:, at_out], out_ref.at[:, at_out], sems.at[k])
         )
         copies[-1].start()
     for copy in copies:
         copy.wait()
 
 
-def finish(stage, offset, reach, read, entering, bases, out, after):
-    span, half = read.shape[0], entering.shape[1]
-    chunk = min(512, half)
-    args = [reach, read, entering, *bases]
-    specs = [WHOLE] * len(args)
-    if offset:
-        args.append(out)
-        specs.append(IN_HBM)
+def finish(stage, reach, read, own, got, bases):
+    span = read.shape[0]
+    lanes = 2 * own.shape[1]
+    chunk = min(512, own.shape[1])
     return call(
-        functools.partial(finish_kernel, stage, offset),
+        functools.partial(finish_kernel, stage),
         "finish",
-        [shape((span, 2 * half), BF16), shape((8, 128), F32)],
-        args,
-        specs=specs,
+        [shape((span, lanes), BF16), shape((8, 128), F32)],
+        (reach, read, own, got, *bases),
         out_specs=[IN_HBM, WHOLE],
-        after=after,
-        alias={len(args) - 1: 0} if offset else None,
-        scratch=[pltpu.VMEM((span, half), BF16), pltpu.SemaphoreType.DMA((half // chunk,))],
+        scratch=[pltpu.VMEM((span, lanes), BF16), pltpu.SemaphoreType.DMA((lanes // chunk,))],
         moved=1,
     )
 
@@ -581,7 +568,7 @@
     wide = min(1024, lanes)
     rows = own_rows.shape[0]
     for k, ref in enumerate((own_ref, got_ref)):
-        both = ref[STATE_SIZE:, :].astype(F32)
+        both = ref[...].astype(F32)
         gated_ref[:, window((place ^ k) * half, half)] = both[0:8] + both[8:16]
     left_ref[0:rows, :] = own_rows[...]
     left_ref[rows : 2 * rows, :] = got_rows[...]
@@ -598,7 +585,7 @@
         offsets = [a + k * stride for k in range(factor) for a in offsets]
     owner = owner_ref[...]
     tail = total_ref[2 * rows : 2 * rows + DRAFTS, :]
-    for k in range(head_count):
+    for k in list(range(1, head_count)) + [0]:
         first = (head ^ k) * per_head
         for slot in range(per_head):
             at = slice(slot * DRAFTS, (slot + 1) * DRAFTS)
@@ -611,7 +598,7 @@
             outs[k][at, :] = drawn.astype(outs[k].dtype)
 
 
-def project(stages, owner, own_rows, got_rows, own, got, gain, weight, head_count, after):
+def project(stages, owner, own_rows, got_rows, own, got, gain, weight, head_count):
     lanes, cols = weight.shape
     rows = 2 * own_rows.shape[0]
     return call(
@@ -619,7 +606,6 @@
         "project",
         [shape((rows // head_count, cols), BF16 if k else F32) for k in range(head_count)],
         (owner, own_rows, got_rows, own, got, gain, weight),
-        after=after,
         scratch=[
             pltpu.VMEM((DRAFTS, lanes), F32),
             pltpu.VMEM((rows + 16, lanes), BF16),
@@ -629,102 +615,74 @@
     )
 
 
-def states_kernel(stage, scattered, offset, *refs):
-    owner_ref, resident_ref, prompt_ref, tail_ref, vwrite_ref = refs[:5]
+def states_kernel(stages, scattered, pieces, *refs):
+    owner_ref, resident_ref, tail_ref, vwrite_ref = refs[:4]
+    prompt_refs, refs = refs[4 : 4 + pieces], refs[4 + pieces :]
+    share_refs, (new_ref, slice_ref, verify_ref, turned_ref, held_ref, sems) = refs[:-6], refs[-6:]
     here = lax.axis_index("seq")
-    side = place_of(stage) ^ offset
-    if offset:
-        other_ref, _, new_ref, slice_ref, turned_ref, held_ref, sems = refs[5:]
-    else:
-        share_refs, (new_ref, turned_ref, verify_ref, held_ref, sems) = refs[5:-5], refs[-5:]
-        verify_ref[...] = sum(ref[...].astype(F32) for ref in share_refs).astype(BF16)
-    half = prompt_ref.shape[1]
-    wide = 2 * half // (vwrite_ref.shape[1] // STATE_SIZE)
-    blocks = [0]
-    for factor, stride in scattered:
-        blocks = [a | (k * stride) for k in range(factor) for a in blocks]
-    width = half // len(blocks)
-    chunk = half // sems.shape[0]
+    verify_ref[...] = sum(ref[...].astype(F32) for ref in share_refs).astype(BF16)
+    core, line, last = stages
+    lanes = resident_ref.shape[0]
+    wide = lanes // (vwrite_ref.shape[1] // STATE_SIZE)
+    part = lanes // pieces
+    width = part // (last[0] if len(scattered) > 1 else 1)
+    chunk = lanes // sems.shape[0]
     is_owner = owner_ref[0:1, :STATE_SIZE] == here
     row = lax.broadcasted_iota(jnp.int32, (32, STATE_SIZE), 0)
     ones = jnp.where((row >= 24) & (row < 27), 1.0, 0.0)
     copies = []
-    for part in range(sems.shape[0]):
-        rows = slice(part * chunk, (part + 1) * chunk)
-        for lane in range(part * chunk, (part + 1) * chunk, width):
-            spot, size, rest = 0, half, lane
-            for factor, stride in scattered:
-                size = size // factor
-                spot |= rest // size * stride
-                rest %= size
-            apart = (spot ^ here) & sum((factor - 1) * stride for factor, stride in scattered)
+    for step in range(sems.shape[0]):
+        rows = slice(step * chunk, (step + 1) * chunk)
+        for lane in range(step * chunk, (step + 1) * chunk, width):
+            spot = lane // part
+            piece = (spot // line[0] ^ place_of(core)) * line[0] + (spot % line[0] ^ place_of(line))
             position = jnp.int32(0)
-            for place, value in enumerate(blocks):
-                position = jnp.where(apart == value, place, position)
-            found = prompt_ref[:, window(position * width, width)]
+            if len(scattered) > 1:
+                position = lane % part // width ^ place_of(last)
+            at = window(position * width, width)
+            found = prompt_refs[0][:, at]
+            for k in range(1, pieces):
+                found = jnp.where(piece == k, prompt_refs[k][:, at], found)
             turned_ref[lane : lane + width, :] = found.astype(F32).T
-        groups = [start // wide for start in (part * chunk, half + part * chunk)]
-        low, high = (vwrite_ref[:, g * STATE_SIZE : (g + 1) * STATE_SIZE] for g in groups)
-        writes = jnp.where(side == 0, low, high).astype(F32)
+        group = step * chunk // wide
+        writes = vwrite_ref[:, group * STATE_SIZE : (group + 1) * STATE_SIZE].astype(F32)
         writes = jnp.concatenate([writes, writes, writes, jnp.zeros_like(writes)], axis=0)
         right = jnp.concatenate([writes, ones], axis=1).astype(BF16)
-        at = window(side * half + part * chunk, chunk)
-        left = tail_ref[:, at].astype(F32).T.astype(BF16)
+        left = tail_ref[:, rows].astype(F32).T.astype(BF16)
         both = dot(left, right)
-        start = jnp.where(is_owner, turned_ref[rows, :], resident_ref[at, :].astype(F32))
+        start = jnp.where(is_owner, turned_ref[rows, :], resident_ref[rows, :].astype(F32))
         held_ref[rows, :] = (start * both[:, STATE_SIZE:] + both[:, :STATE_SIZE]).astype(BF16)
-        copies.append(pltpu.make_async_copy(held_ref.at[rows, :], new_ref.at[at, :], sems.at[part]))
+        copies.append(pltpu.make_async_copy(held_ref.at[rows, :], new_ref.at[rows, :], sems.at[step]))
         copies[-1].start()
-    if offset:
-        per_slice = slice_ref.shape[1] // STATE_SIZE
-        heads = slice_ref.shape[0] // 2
-        for k in range(per_slice):
-            row = pl.ds(here * per_slice + k, heads, stride=HEAD_DIM)
-            got, own = turned_ref[row, :], other_ref[row, :]
-            low, high = jnp.where(side == 0, got, own), jnp.where(side == 0, own, got)
-            at = slice(k * STATE_SIZE, (k + 1) * STATE_SIZE)
-            slice_ref[:, at] = jnp.concatenate([low, high], axis=0).astype(BF16)
+    per_slice = slice_ref.shape[1] // STATE_SIZE
+    heads = slice_ref.shape[0]
+    for k in range(per_slice):
+        picked = turned_ref[pl.ds(here * per_slice + k, heads, stride=HEAD_DIM), :]
+        slice_ref[:, k * STATE_SIZE : (k + 1) * STATE_SIZE] = picked.astype(BF16)
     for copy in copies:
         copy.wait()
 
 
-def states(stage, scattered, owner, resident, prompts, tail, vwrite, shares, seq_count):
+def states(stages, scattered, owner, resident, prompts, tail, vwrite, shares, seq_count):
     lanes = resident.shape[0]
-    half = lanes // 2
-    chunk = min(512, half)
-    args = [owner, resident, prompts[0], tail, vwrite, *shares]
-    scratch = [pltpu.VMEM((half, STATE_SIZE), BF16), pltpu.SemaphoreType.DMA((half // chunk,))]
-    new, turned, verify = call(
-        functools.partial(states_kernel, stage, scattered, 0),
-        "states",
-        [
-            shape((lanes, STATE_SIZE), BF16),
-            shape((half, STATE_SIZE), F32),
-            shape(shares[0].shape, BF16),
-        ],
-        args,
-        out_specs=[IN_HBM, WHOLE, WHOLE],
-        scratch=scratch,
-        flops=lanes * STATE_SIZE * 64,
-        moved=lanes * STATE_SIZE * 3,
-    )
-    args = [owner, resident, prompts[1], tail, vwrite, turned, new]
-    new, sliced = call(
-        functools.partial(states_kernel, stage, scattered, 1),
+    chunk = min(512, lanes // 2)
+    return call(
+        functools.partial(states_kernel, stages, scattered, len(prompts)),
         "states",
         [
             shape((lanes, STATE_SIZE), BF16),
             shape((lanes // HEAD_DIM, HEAD_DIM // seq_count * STATE_SIZE), BF16),
+            shape(shares[0].shape, BF16),
         ],
-        args,
-        specs=[WHOLE] * 6 + [IN_HBM],
-        out_specs=[IN_HBM, WHOLE],
-        alias={6: 0},
-        scratch=[pltpu.VMEM((half, STATE_SIZE), F32)] + scratch,
-        flops=lanes * STATE_SIZE * 64,
-        moved=lanes * STATE_SIZE * 3,
-    )
-    return new, verify, sliced
+        (owner, resident, tail, vwrite, *prompts, *shares),
+        out_specs=[IN_HBM, WHOLE, WHOLE],
+        scratch=[
+            pltpu.VMEM((lanes, STATE_SIZE), F32),
+            pltpu.VMEM((lanes, STATE_SIZE), BF16),
+            pltpu.SemaphoreType.DMA((lanes // chunk,)),
+        ],
+        flops=2 * lanes * STATE_SIZE * 64,
+    )
 
 
 def on_device(
@@ -880,49 +838,52 @@
     hidden = join(hiddens, 0, [outs[-1]])
     hiddens = exchange([hidden] * line[0], line)
     filled = fill([outs[-1]])
-    prompts = exchange([prompt] * line[0], line)
     outs = call(
         functools.partial(down_kernel, line, last, len(pieces), line[0], False, range(line[0]), False),
         "down_line",
         [shape((DOWN_ROWS, line_width), BF16)] * line[0],
         [*turned(pieces), *line_parts],
-        after=filled + prompts[1:] + hiddens[1:],
+        after=filled + hiddens[1:],
         flops=line_width * UP_ROWS * 8,
     )
     pieces = exchange(outs, line)
-    filled = fill([outs[-1]])
+    hidden = join(hiddens, 0, [outs[-1]])
+    hiddens = [hidden, swap(hidden, "seq", core, 1)]
+    filled = fill([outs[-1]]) + hiddens[1:]
     scattered = [line, last] if split_last else [line]
-    hidden = join(hiddens, 0, [outs[-1]])
-    prompt = join(prompts, 1, [outs[-1]])
-    prompts = exchange([prompt] * last[0], last) if split_last else [prompt]
+    if split_last:
+        prompt = hand_on(prompt, [outs[-1]])
+        prompt = join(exchange([prompt] * last[0], last), 1)
+        filled.append(prompt)
+
     def down_core(target, after):
         return call(
             functools.partial(down_kernel, core, line, line[0], 2, True, (target,), False),
             "down_core",
-            [shape((DOWN_ROWS, half), BF16)],
+            [shape((STATE_SIZE, half), BF16)] + [shape((16, half), BF16)] * target,
             turned(pieces) + core_parts,
             after=after,
             moved=1,
-        )[0]
-
-    sent = down_core(1, filled + [prompts[k] for k in (1, last[0] - 1) if split_last])
-    entering = [down_core(0, [sent]), swap(sent, "seq", core, 1)]
+        )
+
+    sent, gated = down_core(1, filled)
+    received_gated, received = swap(gated, "seq", core, 1), swap(sent, "seq", core, 1)
     while len(bases) < groups:
         fill([])
 
-    prefill_out, token = finish(core, 0, reach, reads, entering[0], bases, None, entering[:1])
     shares = project(
-        stages, owner, hidden, swap(hidden, "seq", core, 1), *entering, gain, fetched[0], head_count, [token]
-    )
-    prefill_out, token = finish(
-        core, 1, reach, reads, entering[1], bases, prefill_out, [shares[0], token]
-    )
+        stages, owner, *hiddens, gated, received_gated, gain, fetched[0], head_count
+    )
+    (entering,) = down_core(0, shares[:1])
+    prefill_out, token = finish(core, reach, reads, entering, received, bases)
     shares = [shares[0]] + [swap(shares[k], "head", (head_count, 1), k) for k in range(1, head_count)]
 
-    prompt = join(prompts, 1, [token, *shares[1:]])
-    prompts = exchange([prompt] * 2, core)
-    new_state, verify_out, state_slice = states(
-        core, scattered, owner, resident, prompts, tail, vwrite, shares, seq_count
+    prompts = exchange([prompt] * line[0], line)
+    first = swap(hand_on(prompt, shares[:1]), "seq", core, 1)
+    late = [hand_on(piece, [token, *shares[1:]]) for piece in prompts[1:]]
+    prompts += [first] + [swap(piece, "seq", core, 1) for piece in late]
+    new_state, state_slice, verify_out = states(
+        stages, scattered, owner, resident, prompts, tail, vwrite, shares, seq_count
     )
     return (
         prefill_out,

time: 62.7 us -> 63 us (level)
  Pallas kernels: 23.5 us -> 21.2 us
  starting transfers between devices: 23.7 us -> 26 us
    pallas_call x24, Pallas kernels: 23.5 us -> 21.2 us  [call(): pl.pallas_call(ordered(kernel, first), name=name, grid=grid, out_shape=ou...]
    ppermute x22 -> x24, starting transfers between devices: 23.7 us -> 26 us  [swap(): lax.ppermute(value, axis, [(k, k ^ offset * stride) for k in range(count)])]
    ppermute x22 -> x24, waiting for transfers between devices: 14.4 us -> 14.8 us  [swap(): lax.ppermute(value, axis, [(k, k ^ offset * stride) for k in range(count)])]
  transfers between devices with their start and end apart: 22 -> 24, of which waited for: 9 -> 12; matrix products, arithmetic and copies ran while one was open for 0% -> 0% of each run, Pallas kernels for 28% -> 23%
where the time goes in v3:
time: 63 us; the launch traced here: 62.8 us
  starting transfers between devices  26 us (41%)
  Pallas kernels  21.2 us (34%)
  waiting for transfers between devices  14.8 us (23%)
  between operations  0.86 us (1%)
    ppermute x24, starting transfers between devices, swap(): lax.ppermute(value, axis, [(k, k ^ offset * stride) for k in range(count)])  26 us
    pallas_call x24, Pallas kernels, call(): pl.pallas_call(ordered(kernel, first), name=name, grid=grid, out_shape=ou...  21.2 us
    ppermute x24, waiting for transfers between devices, swap(): lax.ppermute(value, axis, [(k, k ^ offset * stride) for k in range(count)])  14.8 us
  transfers between devices with their start and end apart: 24, of which 12 were waited for; matrix products, arithmetic and copies ran while one was open for 0% of the time, Pallas kernels for 23%

profile of v3, /device:TPU:0, one launch (start us, length us, event | category | flops | bytes accessed | tf_op | source)
XLA Modules:
  0.0 62.8 jit_solution(13078090219114498858)
XLA Ops:
  0.6 2.9 %open_block.1 = (bf16[128,2048]{1,0:T(8,128)(2,1)S(1)}, f32[4,256,16]{2,1,0:T(8,128)S(1)}, f32[64,256]{1,0:T(8,128)S(1)}, f32[64,256]{1,0:T(8,128)S(1)}, bf16[25...) custom-call(f32[64,256]{1,0:T(8,128)} %bitcast.8, ...), custom_call_target="tpu_custom_call" | custom-call | flops 268435456 | bytes 8911232 | tf_op jit(solution)/shard_map/open_block/pallas_call | solution.py:95
  6.8 3.0 %collective-permute-start.4 = (bf16[160,1024]{1,0:T(8,128)(2,1)S(1)}, bf16[160,1024]{1,0:T(8,128)(2,1)S(1)}, u32[]{:S(2)}, u32[]{:S(2)}) collective-permute-start(bf16[160,1024]{1,0:T(8,128)(2,1)S(1)} %get-tuple-element.81.refs_0_), channel_id=1, source_target_pairs={{0,4},{2,6},{4,0},{6,2},{8,12},{10,14},{12,8},{14,10},{16,20},{18,... | collective-permute-start | bytes 983048 | tf_op jit(solution)/shard_map/ppermute | solution.py:44
  9.8 3.6 %collective-permute-start.3 = (bf16[8,4096]{1,0:T(8,128)(2,1)S(1)}, bf16[8,4096]{1,0:T(8,128)(2,1)S(1)}, u32[]{:S(2)}, u32[]{:S(2)}) collective-permute-start(bf16[8,4096]{1,0:T(8,128)(2,1)S(1)} %hand_on.4.refs_1_), channel_id=1, source_target_pairs={{0,24},{2,26},{4,28},{6,30},{8,16},{10,18},{12,20},{14,22},{16,8},... | collective-permute-start | bytes 196616 | tf_op jit(solution)/shard_map/ppermute | solution.py:44
  13.4 3.6 %intra.4 = (f32[256,1024]{1,0:T(8,128)S(1)}, bf16[4096,512]{1,0:T(8,128)(2,1)S(1)}) custom-call(bf16[160,1024]{1,0:T(8,128)(2,1)S(1)} %get-tuple-element.81.refs_0_, f32[4,256,16]{2,1,0:T(8,128)S(1)} %get-tuple-element.82.refs_1_, f32[64,256]{1,0:T(8,128)S(1)} %get-tuple-element.63.refs_4_.refs_2_, f32[64,256]{1,0:T(8,128)S(1)} %get-tuple-element.83.refs_3_, ...), custom_call_target="tpu_custom_call" | custom-call | flops 134217728 | bytes 1572864 | tf_op jit(solution)/shard_map/intra/pallas_call | solution.py:95
  17.0 1.9 %collective-permute-done.2.refs_1_.refs_3_ = bf16[8,4096]{1,0:T(8,128)(2,1)S(1)} collective-permute-done((bf16[8,4096]{1,0:T(8,128)(2,1)S(1)}, bf16[8,4096]{1,0:T(8,128)(2,1)S(1)}, u32[]{:S(2)}, u32[]{:S(2)}) %collective-permute-start.2) | collective-permute-done | bytes 65568 | tf_op jit(solution)/shard_map/ppermute | solution.py:44
  19.1 1.7 %collective-permute-start.6 = (bf16[160,256]{1,0:T(8,128)(2,1)S(1)}, bf16[160,256]{1,0:T(8,128)(2,1)S(1)}, u32[]{:S(2)}, u32[]{:S(2)}) collective-permute-start(bf16[160,256]{1,0:T(8,128)(2,1)S(1)} %get-tuple-element.89), channel_id=1, source_target_pairs={{0,16},{2,18},{4,20},{6,22},{8,24},{10,26},{12,28},{14,30},{16,0},... | collective-permute-start | bytes 245768 | tf_op jit(solution)/shard_map/ppermute | solution.py:44
  20.7 1.7 %collective-permute-start.7 = (bf16[160,256]{1,0:T(8,128)(2,1)S(1)}, bf16[160,256]{1,0:T(8,128)(2,1)S(1)}, u32[]{:S(2)}, u32[]{:S(2)}) collective-permute-start(bf16[160,256]{1,0:T(8,128)(2,1)S(1)} %get-tuple-element.90), channel_id=1, source_target_pairs={{0,8},{2,10},{4,12},{6,14},{8,0},{10,2},{12,4},{14,6},{16,24},{18,... | collective-permute-start | bytes 245768 | tf_op jit(solution)/shard_map/ppermute | solution.py:44
  23.5 1.6 %intra.5.refs_0_.refs_5_ = f32[256,1024]{1,0:T(8,128)S(1)} custom-call(bf16[160,256]{1,0:T(8,128)(2,1)S(1)} %get-tuple-element.87.refs_0_, f32[4,256,16]{2,1,0:T(8,128)S(1)} %get-tuple-element.82.refs_1_, f32[64,256]{1,0:T(8,128)S(1)} %get-tuple-element.63.refs_4_.refs_2_, f32[64,256]{1,0:T(8,128)S(1)} %get-tuple-element.83.refs_3_, ...), custom_call_target="tpu_custom_call" | custom-call | flops 134217728 | bytes 1572864 | tf_op jit(solution)/shard_map/intra/pallas_call | solution.py:95
  25.2 1.9 %collective-permute-done.6.refs_3_ = bf16[160,256]{1,0:T(8,128)(2,1)S(1)} collective-permute-done((bf16[160,256]{1,0:T(8,128)(2,1)S(1)}, bf16[160,256]{1,0:T(8,128)(2,1)S(1)}, u32[]{:S(2)}, u32[]{:S(2)}) %collective-permute-start.6) | collective-permute-done | bytes 81952 | tf_op jit(solution)/shard_map/ppermute | solution.py:44
  27.2 1.7 %collective-permute-done.5.refs_2_ = bf16[160,256]{1,0:T(8,128)(2,1)S(1)} collective-permute-done((bf16[160,256]{1,0:T(8,128)(2,1)S(1)}, bf16[160,256]{1,0:T(8,128)(2,1)S(1)}, u32[]{:S(2)}, u32[]{:S(2)}) %collective-permute-start.5) | collective-permute-done | bytes 81952 | tf_op jit(solution)/shard_map/ppermute | solution.py:44
  29.2 1.3 %collective-permute-start.9 = (bf16[32,4096]{1,0:T(8,128)(2,1)S(1)}, bf16[32,4096]{1,0:T(8,128)(2,1)S(1)}, u32[]{:S(2)}, u32[]{:S(2)}) collective-permute-start(bf16[32,4096]{1,0:T(8,128)(2,1)S(1)} %join.3.refs_1_), channel_id=1, source_target_pairs={{0,4},{2,6},{4,0},{6,2},{8,12},{10,14},{12,8},{14,10},{16,20},{18,... | collective-permute-start | bytes 786440 | tf_op jit(solution)/shard_map/ppermute | solution.py:44
  30.5 1.9 %collective-permute-start.11 = (bf16[144,256]{1,0:T(8,128)(2,1)S(1)}, bf16[144,256]{1,0:T(8,128)(2,1)S(1)}, u32[]{:S(2)}, u32[]{:S(2)}) collective-permute-start(bf16[144,256]{1,0:T(8,128)(2,1)S(1)} %get-tuple-element.93), channel_id=1, source_target_pairs={{0,16},{2,18},{4,20},{6,22},{8,24},{10,26},{12,28},{14,30},{16,0},... | collective-permute-start | bytes 221192 | tf_op jit(solution)/shard_map/ppermute | solution.py:44
  33.4 1.5 %collective-permute-start.10 = (bf16[144,256]{1,0:T(8,128)(2,1)S(1)}, bf16[144,256]{1,0:T(8,128)(2,1)S(1)}, u32[]{:S(2)}, u32[]{:S(2)}) collective-permute-start(bf16[144,256]{1,0:T(8,128)(2,1)S(1)} %get-tuple-element.91.refs_0_), channel_id=1, source_target_pairs={{0,24},{2,26},{4,28},{6,30},{8,16},{10,18},{12,20},{14,22},{16,8},... | collective-permute-start | bytes 221192 | tf_op jit(solution)/shard_map/ppermute | solution.py:44
  34.9 1.6 %intra.6.refs_0_.refs_6_ = f32[256,1024]{1,0:T(8,128)S(1)} custom-call(bf16[144,256]{1,0:T(8,128)(2,1)S(1)} %get-tuple-element.91.refs_0_, f32[4,256,16]{2,1,0:T(8,128)S(1)} %get-tuple-element.82.refs_1_, f32[64,256]{1,0:T(8,128)S(1)} %get-tuple-element.63.refs_4_.refs_2_, f32[64,256]{1,0:T(8,128)S(1)} %get-tuple-element.83.refs_3_, ...), custom_call_target="tpu_custom_call" | custom-call | flops 134217728 | bytes 1572864 | tf_op jit(solution)/shard_map/intra/pallas_call | solution.py:95
  37.6 1.9 %collective-permute-done.10.refs_3_ = bf16[144,256]{1,0:T(8,128)(2,1)S(1)} collective-permute-done((bf16[144,256]{1,0:T(8,128)(2,1)S(1)}, bf16[144,256]{1,0:T(8,128)(2,1)S(1)}, u32[]{:S(2)}, u32[]{:S(2)}) %collective-permute-start.10) | collective-permute-done | bytes 73760 | tf_op jit(solution)/shard_map/ppermute | solution.py:44
  40.6 1.7 %collective-permute-start.16 = (bf16[128,256]{1,0:T(8,128)(2,1)S(1)}, bf16[128,256]{1,0:T(8,128)(2,1)S(1)}, u32[]{:S(2)}, u32[]{:S(2)}) collective-permute-start(bf16[128,256]{1,0:T(8,128)(2,1)S(1)} %hand_on.5.refs_0_), channel_id=1, source_target_pairs={{0,24},{2,26},{4,28},{6,30},{8,16},{10,18},{12,20},{14,22},{16,8},... | collective-permute-start | bytes 196616 | tf_op jit(solution)/shard_map/ppermute | solution.py:44
  42.4 2.6 %collective-permute-start.14 = (bf16[128,256]{1,0:T(8,128)(2,1)S(1)}, bf16[128,256]{1,0:T(8,128)(2,1)S(1)}, u32[]{:S(2)}, u32[]{:S(2)}) collective-permute-start(bf16[128,256]{1,0:T(8,128)(2,1)S(1)} %hand_on.5.refs_0_), channel_id=1, source_target_pairs={{0,8},{2,10},{4,12},{6,14},{8,0},{10,2},{12,4},{14,6},{16,24},{18,... | collective-permute-start | bytes 196616 | tf_op jit(solution)/shard_map/ppermute | solution.py:44
  45.0 1.6 %intra.7.refs_0_.refs_7_ = f32[256,1024]{1,0:T(8,128)S(1)} custom-call(bf16[144,1024]{1,0:T(8,128)(2,1)S(1)} %get-tuple-element.95.refs_0_, f32[4,256,16]{2,1,0:T(8,128)S(1)} %get-tuple-element.82.refs_1_, f32[64,256]{1,0:T(8,128)S(1)} %get-tuple-element.63.refs_4_.refs_2_, f32[64,256]{1,0:T(8,128)S(1)} %get-tuple-element.83.refs_3_, ...), custom_call_target="tpu_custom_call" | custom-call | flops 134217728 | bytes 1572864 | tf_op jit(solution)/shard_map/intra/pallas_call | solution.py:95
  47.4 2.0 %collective-permute-done.15.refs_2_ = bf16[128,256]{1,0:T(8,128)(2,1)S(1)} collective-permute-done((bf16[128,256]{1,0:T(8,128)(2,1)S(1)}, bf16[128,256]{1,0:T(8,128)(2,1)S(1)}, u32[]{:S(2)}, u32[]{:S(2)}) %collective-permute-start.15) | collective-permute-done | bytes 65568 | tf_op jit(solution)/shard_map/ppermute | solution.py:44
  49.9 1.5 %collective-permute-start.20 = (bf16[128,1024]{1,0:T(8,128)(2,1)S(1)}, bf16[128,1024]{1,0:T(8,128)(2,1)S(1)}, u32[]{:S(2)}, u32[]{:S(2)}) collective-permute-start(bf16[128,1024]{1,0:T(8,128)(2,1)S(1)} %join.5.refs_2_.refs_1_.refs_4_), channel_id=1, source_target_pairs={{0,4},{2,6},{4,0},{6,2},{8,12},{10,14},{12,8},{14,10},{16,20},{18,... | collective-permute-start | bytes 786440 | tf_op jit(solution)/shard_map/ppermute | solution.py:44
  53.7 1.6 %collective-permute-start.22 = (bf16[64,512]{1,0:T(8,128)(2,1)S(1)}, bf16[64,512]{1,0:T(8,128)(2,1)S(1)}, u32[]{:S(2)}, u32[]{:S(2)}) collective-permute-start(bf16[64,512]{1,0:T(8,128)(2,1)S(1)} %get-tuple-element.106), channel_id=1, source_target_pairs={{0,1},{1,0},{2,3},{3,2},{4,5},{5,4},{6,7},{7,6},{8,9},{9,8},{10,11... | collective-permute-start | bytes 196616 | tf_op jit(solution)/shard_map/ppermute | solution.py:44
  55.7 2.0 %finish.1 = (bf16[256,4096]{1,0:T(8,128)(2,1)}, f32[8,128]{1,0:T(8,128)S(1)}) custom-call(bf16[256,128]{1,0:T(8,128)(2,1)S(1)} %get-tuple-element.57.refs_0_, bf16[256,512]{1,0:T(8,128)(2,1)S(1)} %get-tuple-element.58.refs_7_.refs_1_, bf16[128,2048]{1,0:T(8,128)(2,1)S(1)} %down_core.3.refs_2_, bf16[128,2048]{1,0:T(8,128)(2,1)S(1)} %collective-permute-done.19.refs_3_, ...), custom_call_target="tpu_custom_call" | custom-call | bytes 1 | tf_op jit(solution)/shard_map/finish/pallas_call | solution.py:95
  58.8 1.5 %collective-permute-done.23.refs_7_ = bf16[128,1024]{1,0:T(8,128)(2,1)S(1)} collective-permute-done((bf16[128,1024]{1,0:T(8,128)(2,1)S(1)}, bf16[128,1024]{1,0:T(8,128)(2,1)S(1)}, u32[]{:S(2)}, u32[]{:S(2)}) %collective-permute-start.23) | collective-permute-done | bytes 262176 | tf_op jit(solution)/shard_map/ppermute | solution.py:44
  60.3 2.6 %states.1 = (bf16[4096,128]{1,0:T(8,128)(2,1)}, bf16[64,512]{1,0:T(8,128)(2,1)}, bf16[64,512]{1,0:T(8,128)(2,1)}) custom-call(s32[8,512]{1,0:T(8,128)S(1)} %get-tuple-element.59.refs_3_.refs_0_, bf16[4096,128]{1,0:T(8,128)(2,1)S(1)} %get-tuple-element.75.refs_1_, bf16[32,4096]{1,0:T(8,128)(2,1)S(1)} %get-tuple-element.103.refs_2_, ...), custom_call_target="tpu_custom_call" | custom-call | flops 67108864 | bytes 3760128 | tf_op jit(solution)/shard_map/states/pallas_call | solution.py:95
  (48 shorter events, 12.9 us)
Async XLA Ops:
  3.5 2.9 %collective-permute-start = (bf16[128,2048]{1,0:T(8,128)(2,1)S(1)}, bf16[128,2048]{1,0:T(8,128)(2,1)S(1)}, u32[]{:S(2)}, u32[]{:S(2)}) collective-permute-start(bf16[128,2048]{1,0:T(8,128)(2,1)S(1)} %get-tuple-element.60.refs_0_), channel_id=1, source_target_pairs={{0,2},{2,0},{4,6},{6,4},{8,10},{10,8},{12,14},{14,12},{16,18},{18,... | collective-permute-start | bytes 1572872 | tf_op jit(solution)/shard_map/ppermute | solution.py:44
  5.0 1.4 %collective-permute-start.1 = (bf16[32,2048]{1,0:T(8,128)(2,1)S(1)}, bf16[32,2048]{1,0:T(8,128)(2,1)S(1)}, u32[]{:S(2)}, u32[]{:S(2)}) collective-permute-start(bf16[32,2048]{1,0:T(8,128)(2,1)S(1)} %get-tuple-element.71.refs_0_), channel_id=1, source_target_pairs={{0,2},{2,0},{4,6},{6,4},{8,10},{10,8},{12,14},{14,12},{16,18},{18,... | collective-permute-start | bytes 393224 | tf_op jit(solution)/shard_map/ppermute | solution.py:44
  6.8 12.2 %collective-permute-start.4 = (bf16[160,1024]{1,0:T(8,128)(2,1)S(1)}, bf16[160,1024]{1,0:T(8,128)(2,1)S(1)}, u32[]{:S(2)}, u32[]{:S(2)}) collective-permute-start(bf16[160,1024]{1,0:T(8,128)(2,1)S(1)} %get-tuple-element.81.refs_0_), channel_id=1, source_target_pairs={{0,4},{2,6},{4,0},{6,2},{8,12},{10,14},{12,8},{14,10},{16,20},{18,... | collective-permute-start | bytes 983048 | tf_op jit(solution)/shard_map/ppermute | solution.py:44
  9.8 7.2 %collective-permute-start.3 = (bf16[8,4096]{1,0:T(8,128)(2,1)S(1)}, bf16[8,4096]{1,0:T(8,128)(2,1)S(1)}, u32[]{:S(2)}, u32[]{:S(2)}) collective-permute-start(bf16[8,4096]{1,0:T(8,128)(2,1)S(1)} %hand_on.4.refs_1_), channel_id=1, source_target_pairs={{0,24},{2,26},{4,28},{6,30},{8,16},{10,18},{12,20},{14,22},{16,8},... | collective-permute-start | bytes 196616 | tf_op jit(solution)/shard_map/ppermute | solution.py:44
  13.4 5.5 %collective-permute-start.2 = (bf16[8,4096]{1,0:T(8,128)(2,1)S(1)}, bf16[8,4096]{1,0:T(8,128)(2,1)S(1)}, u32[]{:S(2)}, u32[]{:S(2)}) collective-permute-start(bf16[8,4096]{1,0:T(8,128)(2,1)S(1)} %hand_on.4.refs_1_), channel_id=1, source_target_pairs={{0,16},{2,18},{4,20},{6,22},{8,24},{10,26},{12,28},{14,30},{16,0},... | collective-permute-start | bytes 196616 | tf_op jit(solution)/shard_map/ppermute | solution.py:44
  19.1 8.0 %collective-permute-start.6 = (bf16[160,256]{1,0:T(8,128)(2,1)S(1)}, bf16[160,256]{1,0:T(8,128)(2,1)S(1)}, u32[]{:S(2)}, u32[]{:S(2)}) collective-permute-start(bf16[160,256]{1,0:T(8,128)(2,1)S(1)} %get-tuple-element.89), channel_id=1, source_target_pairs={{0,16},{2,18},{4,20},{6,22},{8,24},{10,26},{12,28},{14,30},{16,0},... | collective-permute-start | bytes 245768 | tf_op jit(solution)/shard_map/ppermute | solution.py:44
  20.7 6.4 %collective-permute-start.7 = (bf16[160,256]{1,0:T(8,128)(2,1)S(1)}, bf16[160,256]{1,0:T(8,128)(2,1)S(1)}, u32[]{:S(2)}, u32[]{:S(2)}) collective-permute-start(bf16[160,256]{1,0:T(8,128)(2,1)S(1)} %get-tuple-element.90), channel_id=1, source_target_pairs={{0,8},{2,10},{4,12},{6,14},{8,0},{10,2},{12,4},{14,6},{16,24},{18,... | collective-permute-start | bytes 245768 | tf_op jit(solution)/shard_map/ppermute | solution.py:44
  22.4 6.4 %collective-permute-start.5 = (bf16[160,256]{1,0:T(8,128)(2,1)S(1)}, bf16[160,256]{1,0:T(8,128)(2,1)S(1)}, u32[]{:S(2)}, u32[]{:S(2)}) collective-permute-start(bf16[160,256]{1,0:T(8,128)(2,1)S(1)} %get-tuple-element.87.refs_0_), channel_id=1, source_target_pairs={{0,24},{2,26},{4,28},{6,30},{8,16},{10,18},{12,20},{14,22},{16,8},... | collective-permute-start | bytes 245768 | tf_op jit(solution)/shard_map/ppermute | solution.py:44
  23.5 5.6 %collective-permute-start.8 = (bf16[8,4096]{1,0:T(8,128)(2,1)S(1)}, bf16[8,4096]{1,0:T(8,128)(2,1)S(1)}, u32[]{:S(2)}, u32[]{:S(2)}) collective-permute-start(bf16[8,4096]{1,0:T(8,128)(2,1)S(1)} %hand_on.4.refs_1_), channel_id=1, source_target_pairs={{0,8},{2,10},{4,12},{6,14},{8,0},{10,2},{12,4},{14,6},{16,24},{18,... | collective-permute-start | bytes 196616 | tf_op jit(solution)/shard_map/ppermute | solution.py:44
  29.2 10.3 %collective-permute-start.9 = (bf16[32,4096]{1,0:T(8,128)(2,1)S(1)}, bf16[32,4096]{1,0:T(8,128)(2,1)S(1)}, u32[]{:S(2)}, u32[]{:S(2)}) collective-permute-start(bf16[32,4096]{1,0:T(8,128)(2,1)S(1)} %join.3.refs_1_), channel_id=1, source_target_pairs={{0,4},{2,6},{4,0},{6,2},{8,12},{10,14},{12,8},{14,10},{16,20},{18,... | collective-permute-start | bytes 786440 | tf_op jit(solution)/shard_map/ppermute | solution.py:44
  30.5 6.8 %collective-permute-start.11 = (bf16[144,256]{1,0:T(8,128)(2,1)S(1)}, bf16[144,256]{1,0:T(8,128)(2,1)S(1)}, u32[]{:S(2)}, u32[]{:S(2)}) collective-permute-start(bf16[144,256]{1,0:T(8,128)(2,1)S(1)} %get-tuple-element.93), channel_id=1, source_target_pairs={{0,16},{2,18},{4,20},{6,22},{8,24},{10,26},{12,28},{14,30},{16,0},... | collective-permute-start | bytes 221192 | tf_op jit(solution)/shard_map/ppermute | solution.py:44
  32.4 5.2 %collective-permute-start.12 = (bf16[144,256]{1,0:T(8,128)(2,1)S(1)}, bf16[144,256]{1,0:T(8,128)(2,1)S(1)}, u32[]{:S(2)}, u32[]{:S(2)}) collective-permute-start(bf16[144,256]{1,0:T(8,128)(2,1)S(1)} %get-tuple-element.94), channel_id=1, source_target_pairs={{0,8},{2,10},{4,12},{6,14},{8,0},{10,2},{12,4},{14,6},{16,24},{18,... | collective-permute-start | bytes 221192 | tf_op jit(solution)/shard_map/ppermute | solution.py:44
  33.4 6.2 %collective-permute-start.10 = (bf16[144,256]{1,0:T(8,128)(2,1)S(1)}, bf16[144,256]{1,0:T(8,128)(2,1)S(1)}, u32[]{:S(2)}, u32[]{:S(2)}) collective-permute-start(bf16[144,256]{1,0:T(8,128)(2,1)S(1)} %get-tuple-element.91.refs_0_), channel_id=1, source_target_pairs={{0,24},{2,26},{4,28},{6,30},{8,16},{10,18},{12,20},{14,22},{16,8},... | collective-permute-start | bytes 221192 | tf_op jit(solution)/shard_map/ppermute | solution.py:44
  39.9 9.5 %collective-permute-start.13 = (bf16[64,4096]{1,0:T(8,128)(2,1)S(1)}, bf16[64,4096]{1,0:T(8,128)(2,1)S(1)}, u32[]{:S(2)}, u32[]{:S(2)}) collective-permute-start(bf16[64,4096]{1,0:T(8,128)(2,1)S(1)} %join.4.refs_1_), channel_id=1, source_target_pairs={{0,2},{2,0},{4,6},{6,4},{8,10},{10,8},{12,14},{14,12},{16,18},{18,... | collective-permute-start | bytes 1572872 | tf_op jit(solution)/shard_map/ppermute | solution.py:44
  40.0 9.4 %collective-permute-start.17 = (bf16[144,1024]{1,0:T(8,128)(2,1)S(1)}, bf16[144,1024]{1,0:T(8,128)(2,1)S(1)}, u32[]{:S(2)}, u32[]{:S(2)}) collective-permute-start(bf16[144,1024]{1,0:T(8,128)(2,1)S(1)} %get-tuple-element.95.refs_0_), channel_id=1, source_target_pairs={{0,4},{2,6},{4,0},{6,2},{8,12},{10,14},{12,8},{14,10},{16,20},{18,... | collective-permute-start | bytes 884744 | tf_op jit(solution)/shard_map/ppermute | solution.py:44
  40.6 6.8 %collective-permute-start.16 = (bf16[128,256]{1,0:T(8,128)(2,1)S(1)}, bf16[128,256]{1,0:T(8,128)(2,1)S(1)}, u32[]{:S(2)}, u32[]{:S(2)}) collective-permute-start(bf16[128,256]{1,0:T(8,128)(2,1)S(1)} %hand_on.5.refs_0_), channel_id=1, source_target_pairs={{0,24},{2,26},{4,28},{6,30},{8,16},{10,18},{12,20},{14,22},{16,8},... | collective-permute-start | bytes 196616 | tf_op jit(solution)/shard_map/ppermute | solution.py:44
  42.4 7.0 %collective-permute-start.15 = (bf16[128,256]{1,0:T(8,128)(2,1)S(1)}, bf16[128,256]{1,0:T(8,128)(2,1)S(1)}, u32[]{:S(2)}, u32[]{:S(2)}) collective-permute-start(bf16[128,256]{1,0:T(8,128)(2,1)S(1)} %hand_on.5.refs_0_), channel_id=1, source_target_pairs={{0,16},{2,18},{4,20},{6,22},{8,24},{10,26},{12,28},{14,30},{16,0},... | collective-permute-start | bytes 196616 | tf_op jit(solution)/shard_map/ppermute | solution.py:44
  42.4 7.0 %collective-permute-start.14 = (bf16[128,256]{1,0:T(8,128)(2,1)S(1)}, bf16[128,256]{1,0:T(8,128)(2,1)S(1)}, u32[]{:S(2)}, u32[]{:S(2)}) collective-permute-start(bf16[128,256]{1,0:T(8,128)(2,1)S(1)} %hand_on.5.refs_0_), channel_id=1, source_target_pairs={{0,8},{2,10},{4,12},{6,14},{8,0},{10,2},{12,4},{14,6},{16,24},{18,... | collective-permute-start | bytes 196616 | tf_op jit(solution)/shard_map/ppermute | solution.py:44
  49.9 5.9 %collective-permute-start.19 = (bf16[128,2048]{1,0:T(8,128)(2,1)S(1)}, bf16[128,2048]{1,0:T(8,128)(2,1)S(1)}, u32[]{:S(2)}, u32[]{:S(2)}) collective-permute-start(bf16[128,2048]{1,0:T(8,128)(2,1)S(1)} %get-tuple-element.101), channel_id=1, source_target_pairs={{0,2},{2,0},{4,6},{6,4},{8,10},{10,8},{12,14},{14,12},{16,18},{18,... | collective-permute-start | bytes 1572872 | tf_op jit(solution)/shard_map/ppermute | solution.py:44
  49.9 8.7 %collective-permute-start.20 = (bf16[128,1024]{1,0:T(8,128)(2,1)S(1)}, bf16[128,1024]{1,0:T(8,128)(2,1)S(1)}, u32[]{:S(2)}, u32[]{:S(2)}) collective-permute-start(bf16[128,1024]{1,0:T(8,128)(2,1)S(1)} %join.5.refs_2_.refs_1_.refs_4_), channel_id=1, source_target_pairs={{0,4},{2,6},{4,0},{6,2},{8,12},{10,14},{12,8},{14,10},{16,20},{18,... | collective-permute-start | bytes 786440 | tf_op jit(solution)/shard_map/ppermute | solution.py:44
  51.5 1.3 %collective-permute-start.18 = (bf16[16,2048]{1,0:T(8,128)(2,1)S(1)}, bf16[16,2048]{1,0:T(8,128)(2,1)S(1)}, u32[]{:S(2)}, u32[]{:S(2)}) collective-permute-start(bf16[16,2048]{1,0:T(8,128)(2,1)S(1)} %get-tuple-element.98.refs_3_), channel_id=1, source_target_pairs={{0,2},{2,0},{4,6},{6,4},{8,10},{10,8},{12,14},{14,12},{16,18},{18,... | collective-permute-start | bytes 196616 | tf_op jit(solution)/shard_map/ppermute | solution.py:44
  53.7 5.0 %collective-permute-start.22 = (bf16[64,512]{1,0:T(8,128)(2,1)S(1)}, bf16[64,512]{1,0:T(8,128)(2,1)S(1)}, u32[]{:S(2)}, u32[]{:S(2)}) collective-permute-start(bf16[64,512]{1,0:T(8,128)(2,1)S(1)} %get-tuple-element.106), channel_id=1, source_target_pairs={{0,1},{1,0},{2,3},{3,2},{4,5},{5,4},{6,7},{7,6},{8,9},{9,8},{10,11... | collective-permute-start | bytes 196616 | tf_op jit(solution)/shard_map/ppermute | solution.py:44
  55.2 3.5 %collective-permute-start.21 = (bf16[128,1024]{1,0:T(8,128)(2,1)S(1)}, bf16[128,1024]{1,0:T(8,128)(2,1)S(1)}, u32[]{:S(2)}, u32[]{:S(2)}) collective-permute-start(bf16[128,1024]{1,0:T(8,128)(2,1)S(1)} %hand_on.6), channel_id=1, source_target_pairs={{0,2},{2,0},{4,6},{6,4},{8,10},{10,8},{12,14},{14,12},{16,18},{18,... | collective-permute-start | bytes 786440 | tf_op jit(solution)/shard_map/ppermute | solution.py:44
  58.7 1.6 %collective-permute-start.23 = (bf16[128,1024]{1,0:T(8,128)(2,1)S(1)}, bf16[128,1024]{1,0:T(8,128)(2,1)S(1)}, u32[]{:S(2)}, u32[]{:S(2)}) collective-permute-start(bf16[128,1024]{1,0:T(8,128)(2,1)S(1)} %hand_on.7), channel_id=1, source_target_pairs={{0,2},{2,0},{4,6},{6,4},{8,10},{10,8},{12,14},{14,12},{16,18},{18,... | collective-permute-start | bytes 786440 | tf_op jit(solution)/shard_map/ppermute | solution.py:44

commit v4 on v3

--- a/solution.py
+++ b/solution.py
@@ -16,7 +16,7 @@
 UP_ROWS = STATE_SIZE + EXTRA
 READ_AT = STATE_SIZE + 16
 LOG_AT = STATE_SIZE + 24
-DOWN_ROWS = STATE_SIZE + 16
+DOWN_ROWS = STATE_SIZE + 8
 
 F32 = jnp.float32
 BF16 = jnp.bfloat16
@@ -120,21 +120,30 @@
     outs, later = outs[:9], list(outs[9:])
     sent_ref, run_ref, runt_ref, stept_ref, reach_ref, end_ref, pick_ref, kept_out, owner_out = outs
     sems, held = scratch[0], [*scratch[1:], *later]
-    fetches = [
-        pltpu.make_async_copy(source, target, sems.at[k])
-        for k, (source, target) in enumerate(zip(sources, held))
-    ]
-    for fetch in fetches:
-        fetch.start()
+    here = lax.axis_index("seq")
+    place = place_of(stage)
     early = count - passed
-    for fetch in fetches[:early]:
-        fetch.wait()
+    half = sent_ref.shape[1]
+
+    def fetch(k, at=None):
+        if at is None:
+            return pltpu.make_async_copy(sources[k], held[k], sems.at[k])
+        sem = sems.at[k if at == 1 else count]
+        lanes = window((place ^ at) * half, half)
+        return pltpu.make_async_copy(sources[k].at[:, lanes], held[k].at[:, lanes], sem)
+
+    first = [fetch(k) for k in range(early + 1)] + [fetch(early + 1, 1)]
+    rest = [fetch(early + 1, 0)] + [fetch(k) for k in range(early + 2, count)]
+    for copy in first:
+        copy.start()
+    for copy in first[:early]:
+        copy.wait()
+    for copy in rest:
+        copy.start()
     turned_ref, rate_ref, owner_ref, ids_ref, kept_ref, write_ref, x_ref = held[:7]
     heads, span = turned_ref.shape
     groups = write_ref.shape[1] // STATE_SIZE
     per_group = heads // groups
-    here = lax.axis_index("seq")
-    place = place_of(stage)
 
     step_rows = turned_ref[...]
     stept_ref[...] = step_rows
@@ -151,8 +160,8 @@
     to_end = jnp.exp(running[span - 1 : span, :] - running) * step
     end_ref[...] = jnp.concatenate(split(to_end, 2), axis=1).astype(BF16)
 
-    for fetch in fetches[early : early + 2]:
-        fetch.wait()
+    for copy in first[early:]:
+        copy.wait()
     fill_message(place ^ 1, end_ref, x_ref, write_ref, sent_ref)
 
     wide_run = running
@@ -175,8 +184,8 @@
     pick_ref[...] = pick
     kept_out[...] = jnp.zeros(kept_out.shape, jnp.int32) + kept_ref[request]
     owner_out[...] = jnp.zeros(owner_out.shape, jnp.int32) + owner_ref[0]
-    for fetch in fetches[early + 2 :]:
-        fetch.wait()
+    for copy in rest:
+        copy.wait()
 
 
 def draft_kernel(
@@ -370,7 +379,7 @@
     mine = sum(extra_of(part, whole) for part in parts)
     reads = mine[16:24, :STATE_SIZE].astype(BF16)
     gated = mine[0:8] + mine[8:16] * dot(reads, final)
-    gated = jnp.concatenate(split(gated, 2), axis=0).astype(BF16)
+    gated = gated.astype(BF16)
     for k in list(range(1, len(outs))) + [0]:
         scale = weights_of(logs, place, place ^ k)
         outs[k][:STATE_SIZE, :] = sum(w * s for w, s in zip(scale, states)).astype(BF16)
@@ -538,6 +547,16 @@
     return call(copy, "hand_on", [shape(value.shape, value.dtype)], [value], after=after)[0]
 
 
+def gather_in(values):
+    def copy(*refs):
+        for k in range(len(values)):
+            refs[len(values) + k][...] = refs[k][...]
+
+    return call(
+        copy, "gather_in", [shape(v.shape, v.dtype) for v in values], values, flops=10**10, moved=1
+    )
+
+
 def join_kernel(axis, *refs):
     out_ref = refs[-1]
     for k, ref in enumerate(refs[:-1]):
@@ -568,8 +587,7 @@
     wide = min(1024, lanes)
     rows = own_rows.shape[0]
     for k, ref in enumerate((own_ref, got_ref)):
-        both = ref[...].astype(F32)
-        gated_ref[:, window((place ^ k) * half, half)] = both[0:8] + both[8:16]
+        gated_ref[:, window((place ^ k) * half, half)] = ref[...].astype(F32)
     left_ref[0:rows, :] = own_rows[...]
     left_ref[rows : 2 * rows, :] = got_rows[...]
     for lane0 in range(0, lanes, wide):
@@ -615,21 +633,49 @@
     )
 
 
+def prepare_kernel(owner_ref, resident_ref, tail_ref, vwrite_ref, base_ref, factor_ref):
+    here = lax.axis_index("seq")
+    lanes = resident_ref.shape[0]
+    wide = lanes // (vwrite_ref.shape[1] // STATE_SIZE)
+    chunk = min(512, wide)
+    is_owner = owner_ref[0:1, :STATE_SIZE] == here
+    row = lax.broadcasted_iota(jnp.int32, (32, STATE_SIZE), 0)
+    ones = jnp.where((row >= 24) & (row < 27), 1.0, 0.0)
+    for start in range(0, lanes, chunk):
+        rows, group = slice(start, start + chunk), start // wide
+        writes = vwrite_ref[:, group * STATE_SIZE : (group + 1) * STATE_SIZE].astype(F32)
+        writes = jnp.concatenate([writes, writes, writes, jnp.zeros_like(writes)], axis=0)
+        right = jnp.concatenate([writes, ones], axis=1).astype(BF16)
+        left = tail_ref[:, rows].astype(F32).T.astype(BF16)
+        both = dot(left, right)
+        added, decay = both[:, :STATE_SIZE], both[:, STATE_SIZE:]
+        kept = decay * resident_ref[rows, :].astype(F32)
+        base_ref[rows, :] = added + jnp.where(is_owner, 0.0, kept)
+        factor_ref[rows, :] = jnp.where(is_owner, decay, 0.0)
+
+
+def prepare(owner, resident, tail, vwrite, after):
+    return call(
+        prepare_kernel,
+        "prepare_states",
+        [shape(resident.shape, F32)] * 2,
+        (owner, resident, tail, vwrite),
+        after=after,
+        moved=1,
+    )
+
+
 def states_kernel(stages, scattered, pieces, *refs):
-    owner_ref, resident_ref, tail_ref, vwrite_ref = refs[:4]
-    prompt_refs, refs = refs[4 : 4 + pieces], refs[4 + pieces :]
+    base_ref, factor_ref = refs[:2]
+    prompt_refs, refs = refs[2 : 2 + pieces], refs[2 + pieces :]
     share_refs, (new_ref, slice_ref, verify_ref, turned_ref, held_ref, sems) = refs[:-6], refs[-6:]
     here = lax.axis_index("seq")
     verify_ref[...] = sum(ref[...].astype(F32) for ref in share_refs).astype(BF16)
     core, line, last = stages
-    lanes = resident_ref.shape[0]
-    wide = lanes // (vwrite_ref.shape[1] // STATE_SIZE)
+    lanes = base_ref.shape[0]
     part = lanes // pieces
     width = part // (last[0] if len(scattered) > 1 else 1)
     chunk = lanes // sems.shape[0]
-    is_owner = owner_ref[0:1, :STATE_SIZE] == here
-    row = lax.broadcasted_iota(jnp.int32, (32, STATE_SIZE), 0)
-    ones = jnp.where((row >= 24) & (row < 27), 1.0, 0.0)
     copies = []
     for step in range(sems.shape[0]):
         rows = slice(step * chunk, (step + 1) * chunk)
@@ -644,14 +690,8 @@
             for k in range(1, pieces):
                 found = jnp.where(piece == k, prompt_refs[k][:, at], found)
             turned_ref[lane : lane + width, :] = found.astype(F32).T
-        group = step * chunk // wide
-        writes = vwrite_ref[:, group * STATE_SIZE : (group + 1) * STATE_SIZE].astype(F32)
-        writes = jnp.concatenate([writes, writes, writes, jnp.zeros_like(writes)], axis=0)
-        right = jnp.concatenate([writes, ones], axis=1).astype(BF16)
-        left = tail_ref[:, rows].astype(F32).T.astype(BF16)
-        both = dot(left, right)
-        start = jnp.where(is_owner, turned_ref[rows, :], resident_ref[rows, :].astype(F32))
-        held_ref[rows, :] = (start * both[:, STATE_SIZE:] + both[:, :STATE_SIZE]).astype(BF16)
+        new = factor_ref[rows, :] * turned_ref[rows, :] + base_ref[rows, :]
+        held_ref[rows, :] = new.astype(BF16)
         copies.append(pltpu.make_async_copy(held_ref.at[rows, :], new_ref.at[rows, :], sems.at[step]))
         copies[-1].start()
     per_slice = slice_ref.shape[1] // STATE_SIZE
@@ -663,8 +703,8 @@
         copy.wait()
 
 
-def states(stages, scattered, owner, resident, prompts, tail, vwrite, shares, seq_count):
-    lanes = resident.shape[0]
+def states(stages, scattered, prepared, prompts, shares, seq_count):
+    lanes = prepared[0].shape[0]
     chunk = min(512, lanes // 2)
     return call(
         functools.partial(states_kernel, stages, scattered, len(prompts)),
@@ -674,7 +714,7 @@
             shape((lanes // HEAD_DIM, HEAD_DIM // seq_count * STATE_SIZE), BF16),
             shape(shares[0].shape, BF16),
         ],
-        (owner, resident, tail, vwrite, *prompts, *shares),
+        (*prepared, *prompts, *shares),
         out_specs=[IN_HBM, WHOLE, WHOLE],
         scratch=[
             pltpu.VMEM((lanes, STATE_SIZE), F32),
@@ -744,7 +784,7 @@
         + [shape(value.shape, value.dtype) for value in inputs[-passed:]],
         inputs,
         specs=[IN_HBM] * len(inputs),
-        scratch=[pltpu.SemaphoreType.DMA((len(inputs),))]
+        scratch=[pltpu.SemaphoreType.DMA((len(inputs) + 1,))]
         + [
             (pltpu.SMEM if value.dtype == jnp.int32 else pltpu.VMEM)(value.shape, value.dtype)
             for value in inputs[:-passed]
@@ -782,7 +822,6 @@
         flops=span * lanes * STATE_SIZE,
     )
     core_parts = [own, own_extra, received, received_extra]
-    hidden = resident_hidden(resident, vread, q1, q2, gain, [own])
 
     bases, fetched = [], []
 
@@ -808,11 +847,11 @@
         "up_line",
         [shape((UP_ROWS, line_width), BF16)] * line[0],
         core_parts,
-        after=[hidden],
         flops=half * UP_ROWS * 4,
     )
     line_parts = exchange(outs, line)
-    hiddens = exchange([hand_on(hidden, [outs[-1]])] * last[0], last)
+    hidden = resident_hidden(resident, vread, q1, q2, gain, [outs[-1]])
+    hiddens = exchange([hidden] * last[0], last)
     filled = fill([outs[-1]])
     outs = call(
         functools.partial(up_kernel, line, last, line[0], False),
@@ -835,6 +874,8 @@
     )
 
     pieces = exchange(outs, last) if split_last else outs
+    if split_last:
+        pieces = pieces[:1] + list(gather_in(pieces[:0:-1]))[::-1]
     hidden = join(hiddens, 0, [outs[-1]])
     hiddens = exchange([hidden] * line[0], line)
     filled = fill([outs[-1]])
@@ -849,7 +890,9 @@
     pieces = exchange(outs, line)
     hidden = join(hiddens, 0, [outs[-1]])
     hiddens = [hidden, swap(hidden, "seq", core, 1)]
-    filled = fill([outs[-1]]) + hiddens[1:]
+    filled = fill([outs[-1]])
+    prepared = prepare(owner, resident, tail, vwrite, filled)
+    filled = [*prepared, *hiddens[1:]]
     scattered = [line, last] if split_last else [line]
     if split_last:
         prompt = hand_on(prompt, [outs[-1]])
@@ -860,7 +903,7 @@
         return call(
             functools.partial(down_kernel, core, line, line[0], 2, True, (target,), False),
             "down_core",
-            [shape((STATE_SIZE, half), BF16)] + [shape((16, half), BF16)] * target,
+            [shape((STATE_SIZE, half), BF16)] + [shape((DRAFTS, half), BF16)] * target,
             turned(pieces) + core_parts,
             after=after,
             moved=1,
@@ -883,7 +926,7 @@
     late = [hand_on(piece, [token, *shares[1:]]) for piece in prompts[1:]]
     prompts += [first] + [swap(piece, "seq", core, 1) for piece in late]
     new_state, state_slice, verify_out = states(
-        stages, scattered, owner, resident, prompts, tail, vwrite, shares, seq_count
+        stages, scattered, prepared, prompts, shares, seq_count
     )
     return (
         prefill_out,

time: 63 us -> 65.3 us (1.037)
  starting transfers between devices: 26 us -> 27.2 us
    ppermute x24, starting transfers between devices: 26 us -> 27.2 us  [swap(): lax.ppermute(value, axis, [(k, k ^ offset * stride) for k in range(count)])]
    pallas_call x24 -> x25, Pallas kernels: 21.2 us -> 21.6 us  [call(): pl.pallas_call(ordered(kernel, first), name=name, grid=grid, out_shape=ou...]
  transfers between devices with their start and end apart: 24 -> 24, of which waited for: 12 -> 11; matrix products, arithmetic and copies ran while one was open for 0% -> 0% of each run, Pallas kernels for 23% -> 23%
where the time goes in v4:
time: 65.3 us; the launch traced here: 65.1 us
  starting transfers between devices  27.2 us (42%)
  Pallas kernels  21.6 us (33%)
  waiting for transfers between devices  15.2 us (23%)
  between operations  1.03 us (2%)
    ppermute x24, starting transfers between devices, swap(): lax.ppermute(value, axis, [(k, k ^ offset * stride) for k in range(count)])  27.2 us
    pallas_call x25, Pallas kernels, call(): pl.pallas_call(ordered(kernel, first), name=name, grid=grid, out_shape=ou...  21.6 us
    ppermute x24, waiting for transfers between devices, swap(): lax.ppermute(value, axis, [(k, k ^ offset * stride) for k in range(count)])  15.2 us
  transfers between devices with their start and end apart: 24, of which 11 were waited for; matrix products, arithmetic and copies ran while one was open for 0% of the time, Pallas kernels for 23%

profile of v4, /device:TPU:0, one launch (start us, length us, event | category | flops | bytes accessed | tf_op | source)
XLA Modules:
  0.0 65.1 jit_solution(11447622281492578747)
XLA Ops:
  0.6 3.0 %open_block.1 = (bf16[128,2048]{1,0:T(8,128)(2,1)S(1)}, f32[4,256,16]{2,1,0:T(8,128)S(1)}, f32[64,256]{1,0:T(8,128)S(1)}, f32[64,256]{1,0:T(8,128)S(1)}, bf16[25...) custom-call(f32[64,256]{1,0:T(8,128)} %bitcast.8, ...), custom_call_target="tpu_custom_call" | custom-call | flops 268435456 | bytes 8911232 | tf_op jit(solution)/shard_map/open_block/pallas_call | solution.py:95
  6.8 2.8 %collective-permute-start.4 = (bf16[160,1024]{1,0:T(8,128)(2,1)S(1)}, bf16[160,1024]{1,0:T(8,128)(2,1)S(1)}, u32[]{:S(2)}, u32[]{:S(2)}) collective-permute-start(bf16[160,1024]{1,0:T(8,128)(2,1)S(1)} %get-tuple-element.81.refs_0_), channel_id=1, source_target_pairs={{0,4},{2,6},{4,0},{6,2},{8,12},{10,14},{12,8},{14,10},{16,20},{18,... | collective-permute-start | bytes 983048 | tf_op jit(solution)/shard_map/ppermute | solution.py:44
  10.0 2.6 %collective-permute-start.2 = (bf16[8,4096]{1,0:T(8,128)(2,1)S(1)}, bf16[8,4096]{1,0:T(8,128)(2,1)S(1)}, u32[]{:S(2)}, u32[]{:S(2)}) collective-permute-start(bf16[8,4096]{1,0:T(8,128)(2,1)S(1)} %resident_hidden.1.refs_1_), channel_id=1, source_target_pairs={{0,16},{2,18},{4,20},{6,22},{8,24},{10,26},{12,28},{14,30},{16,0},... | collective-permute-start | bytes 196616 | tf_op jit(solution)/shard_map/ppermute | solution.py:44
  12.6 1.3 %collective-permute-start.3 = (bf16[8,4096]{1,0:T(8,128)(2,1)S(1)}, bf16[8,4096]{1,0:T(8,128)(2,1)S(1)}, u32[]{:S(2)}, u32[]{:S(2)}) collective-permute-start(bf16[8,4096]{1,0:T(8,128)(2,1)S(1)} %resident_hidden.1.refs_1_), channel_id=1, source_target_pairs={{0,24},{2,26},{4,28},{6,30},{8,16},{10,18},{12,20},{14,22},{16,8},... | collective-permute-start | bytes 196616 | tf_op jit(solution)/shard_map/ppermute | solution.py:44
  14.0 3.6 %intra.4 = (f32[256,1024]{1,0:T(8,128)S(1)}, bf16[4096,512]{1,0:T(8,128)(2,1)S(1)}) custom-call(bf16[160,1024]{1,0:T(8,128)(2,1)S(1)} %get-tuple-element.81.refs_0_, f32[4,256,16]{2,1,0:T(8,128)S(1)} %get-tuple-element.82.refs_1_, f32[64,256]{1,0:T(8,128)S(1)} %get-tuple-element.68.refs_4_.refs_2_, f32[64,256]{1,0:T(8,128)S(1)} %get-tuple-element.83.refs_3_, ...), custom_call_target="tpu_custom_call" | custom-call | flops 134217728 | bytes 1572864 | tf_op jit(solution)/shard_map/intra/pallas_call | solution.py:95
  18.9 2.9 %collective-permute-start.5 = (bf16[160,256]{1,0:T(8,128)(2,1)S(1)}, bf16[160,256]{1,0:T(8,128)(2,1)S(1)}, u32[]{:S(2)}, u32[]{:S(2)}) collective-permute-start(bf16[160,256]{1,0:T(8,128)(2,1)S(1)} %get-tuple-element.92.refs_0_), channel_id=1, source_target_pairs={{0,24},{2,26},{4,28},{6,30},{8,16},{10,18},{12,20},{14,22},{16,8},... | collective-permute-start | bytes 245768 | tf_op jit(solution)/shard_map/ppermute | solution.py:44
  22.1 1.3 %collective-permute-start.7 = (bf16[160,256]{1,0:T(8,128)(2,1)S(1)}, bf16[160,256]{1,0:T(8,128)(2,1)S(1)}, u32[]{:S(2)}, u32[]{:S(2)}) collective-permute-start(bf16[160,256]{1,0:T(8,128)(2,1)S(1)} %get-tuple-element.95), channel_id=1, source_target_pairs={{0,8},{2,10},{4,12},{6,14},{8,0},{10,2},{12,4},{14,6},{16,24},{18,... | collective-permute-start | bytes 245768 | tf_op jit(solution)/shard_map/ppermute | solution.py:44
  24.2 1.6 %intra.5.refs_0_.refs_5_ = f32[256,1024]{1,0:T(8,128)S(1)} custom-call(bf16[160,256]{1,0:T(8,128)(2,1)S(1)} %get-tuple-element.92.refs_0_, f32[4,256,16]{2,1,0:T(8,128)S(1)} %get-tuple-element.82.refs_1_, f32[64,256]{1,0:T(8,128)S(1)} %get-tuple-element.68.refs_4_.refs_2_, f32[64,256]{1,0:T(8,128)S(1)} %get-tuple-element.83.refs_3_, ...), custom_call_target="tpu_custom_call" | custom-call | flops 134217728 | bytes 1572864 | tf_op jit(solution)/shard_map/intra/pallas_call | solution.py:95
  25.8 3.6 %collective-permute-done.6.refs_3_ = bf16[160,256]{1,0:T(8,128)(2,1)S(1)} collective-permute-done((bf16[160,256]{1,0:T(8,128)(2,1)S(1)}, bf16[160,256]{1,0:T(8,128)(2,1)S(1)}, u32[]{:S(2)}, u32[]{:S(2)}) %collective-permute-start.6) | collective-permute-done | bytes 81952 | tf_op jit(solution)/shard_map/ppermute | solution.py:44
  29.8 3.2 %collective-permute-start.10 = (bf16[136,256]{1,0:T(8,128)(2,1)S(1)}, bf16[136,256]{1,0:T(8,128)(2,1)S(1)}, u32[]{:S(2)}, u32[]{:S(2)}) collective-permute-start(bf16[136,256]{1,0:T(8,128)(2,1)S(1)} %get-tuple-element.96.refs_0_), channel_id=1, source_target_pairs={{0,24},{2,26},{4,28},{6,30},{8,16},{10,18},{12,20},{14,22},{16,8},... | collective-permute-start | bytes 208904 | tf_op jit(solution)/shard_map/ppermute | solution.py:44
  33.0 1.2 %collective-permute-start.12 = (bf16[136,256]{1,0:T(8,128)(2,1)S(1)}, bf16[136,256]{1,0:T(8,128)(2,1)S(1)}, u32[]{:S(2)}, u32[]{:S(2)}) collective-permute-start(bf16[136,256]{1,0:T(8,128)(2,1)S(1)} %get-tuple-element.99), channel_id=1, source_target_pairs={{0,8},{2,10},{4,12},{6,14},{8,0},{10,2},{12,4},{14,6},{16,24},{18,... | collective-permute-start | bytes 208904 | tf_op jit(solution)/shard_map/ppermute | solution.py:44
  34.2 1.1 %collective-permute-start.9 = (bf16[32,4096]{1,0:T(8,128)(2,1)S(1)}, bf16[32,4096]{1,0:T(8,128)(2,1)S(1)}, u32[]{:S(2)}, u32[]{:S(2)}) collective-permute-start(bf16[32,4096]{1,0:T(8,128)(2,1)S(1)} %join.3.refs_1_), channel_id=1, source_target_pairs={{0,4},{2,6},{4,0},{6,2},{8,12},{10,14},{12,8},{14,10},{16,20},{18,... | collective-permute-start | bytes 786440 | tf_op jit(solution)/shard_map/ppermute | solution.py:44
  35.3 1.6 %intra.6.refs_0_.refs_6_ = f32[256,1024]{1,0:T(8,128)S(1)} custom-call(bf16[136,256]{1,0:T(8,128)(2,1)S(1)} %get-tuple-element.96.refs_0_, f32[4,256,16]{2,1,0:T(8,128)S(1)} %get-tuple-element.82.refs_1_, f32[64,256]{1,0:T(8,128)S(1)} %get-tuple-element.68.refs_4_.refs_2_, f32[64,256]{1,0:T(8,128)S(1)} %get-tuple-element.83.refs_3_, ...), custom_call_target="tpu_custom_call" | custom-call | flops 134217728 | bytes 1572864 | tf_op jit(solution)/shard_map/intra/pallas_call | solution.py:95
  37.0 1.8 %collective-permute-done.11.refs_1_ = bf16[136,256]{1,0:T(8,128)(2,1)S(1)} collective-permute-done((bf16[136,256]{1,0:T(8,128)(2,1)S(1)}, bf16[136,256]{1,0:T(8,128)(2,1)S(1)}, u32[]{:S(2)}, u32[]{:S(2)}) %collective-permute-start.11) | collective-permute-done | bytes 69664 | tf_op jit(solution)/shard_map/ppermute | solution.py:44
  38.8 2.5 %collective-permute-done.9.refs_1_.refs_2_ = bf16[32,4096]{1,0:T(8,128)(2,1)S(1)} collective-permute-done((bf16[32,4096]{1,0:T(8,128)(2,1)S(1)}, bf16[32,4096]{1,0:T(8,128)(2,1)S(1)}, u32[]{:S(2)}, u32[]{:S(2)}) %collective-permute-start.9) | collective-permute-done | bytes 262176 | tf_op jit(solution)/shard_map/ppermute | solution.py:44
  43.1 2.6 %collective-permute-start.15 = (bf16[128,256]{1,0:T(8,128)(2,1)S(1)}, bf16[128,256]{1,0:T(8,128)(2,1)S(1)}, u32[]{:S(2)}, u32[]{:S(2)}) collective-permute-start(bf16[128,256]{1,0:T(8,128)(2,1)S(1)} %hand_on.3.refs_0_), channel_id=1, source_target_pairs={{0,16},{2,18},{4,20},{6,22},{8,24},{10,26},{12,28},{14,30},{16,0},... | collective-permute-start | bytes 196616 | tf_op jit(solution)/shard_map/ppermute | solution.py:44
  45.7 1.4 %collective-permute-start.16 = (bf16[128,256]{1,0:T(8,128)(2,1)S(1)}, bf16[128,256]{1,0:T(8,128)(2,1)S(1)}, u32[]{:S(2)}, u32[]{:S(2)}) collective-permute-start(bf16[128,256]{1,0:T(8,128)(2,1)S(1)} %hand_on.3.refs_0_), channel_id=1, source_target_pairs={{0,24},{2,26},{4,28},{6,30},{8,16},{10,18},{12,20},{14,22},{16,8},... | collective-permute-start | bytes 196616 | tf_op jit(solution)/shard_map/ppermute | solution.py:44
  47.1 1.6 %intra.7.refs_0_.refs_7_ = f32[256,1024]{1,0:T(8,128)S(1)} custom-call(bf16[136,1024]{1,0:T(8,128)(2,1)S(1)} %get-tuple-element.103.refs_0_, f32[4,256,16]{2,1,0:T(8,128)S(1)} %get-tuple-element.82.refs_1_, f32[64,256]{1,0:T(8,128)S(1)} %get-tuple-element.68.refs_4_.refs_2_, f32[64,256]{1,0:T(8,128)S(1)} %get-tuple-element.83.refs_3_, ...), custom_call_target="tpu_custom_call" | custom-call | flops 134217728 | bytes 1572864 | tf_op jit(solution)/shard_map/intra/pallas_call | solution.py:95
  49.5 1.4 %collective-permute-done.15.refs_2_ = bf16[128,256]{1,0:T(8,128)(2,1)S(1)} collective-permute-done((bf16[128,256]{1,0:T(8,128)(2,1)S(1)}, bf16[128,256]{1,0:T(8,128)(2,1)S(1)}, u32[]{:S(2)}, u32[]{:S(2)}) %collective-permute-start.15) | collective-permute-done | bytes 65568 | tf_op jit(solution)/shard_map/ppermute | solution.py:44
  52.4 1.8 %collective-permute-start.20 = (bf16[128,1024]{1,0:T(8,128)(2,1)S(1)}, bf16[128,1024]{1,0:T(8,128)(2,1)S(1)}, u32[]{:S(2)}, u32[]{:S(2)}) collective-permute-start(bf16[128,1024]{1,0:T(8,128)(2,1)S(1)} %join.5.refs_3_.refs_1_.refs_2_), channel_id=1, source_target_pairs={{0,4},{2,6},{4,0},{6,2},{8,12},{10,14},{12,8},{14,10},{16,20},{18,... | collective-permute-start | bytes 786440 | tf_op jit(solution)/shard_map/ppermute | solution.py:44
  56.3 1.6 %collective-permute-start.22 = (bf16[64,512]{1,0:T(8,128)(2,1)S(1)}, bf16[64,512]{1,0:T(8,128)(2,1)S(1)}, u32[]{:S(2)}, u32[]{:S(2)}) collective-permute-start(bf16[64,512]{1,0:T(8,128)(2,1)S(1)} %get-tuple-element.116), channel_id=1, source_target_pairs={{0,1},{1,0},{2,3},{3,2},{4,5},{5,4},{6,7},{7,6},{8,9},{9,8},{10,11... | collective-permute-start | bytes 196616 | tf_op jit(solution)/shard_map/ppermute | solution.py:44
  58.4 2.0 %finish.1 = (bf16[256,4096]{1,0:T(8,128)(2,1)}, f32[8,128]{1,0:T(8,128)S(1)}) custom-call(bf16[256,128]{1,0:T(8,128)(2,1)S(1)} %get-tuple-element.62.refs_0_, bf16[256,512]{1,0:T(8,128)(2,1)S(1)} %get-tuple-element.63.refs_7_.refs_1_, bf16[128,2048]{1,0:T(8,128)(2,1)S(1)} %down_core.3.refs_2_, bf16[128,2048]{1,0:T(8,128)(2,1)S(1)} %collective-permute-done.19.refs_3_, ...), custom_call_target="tpu_custom_call" | custom-call | bytes 1 | tf_op jit(solution)/shard_map/finish/pallas_call | solution.py:95
  61.2 1.5 %collective-permute-done.23.refs_5_ = bf16[128,1024]{1,0:T(8,128)(2,1)S(1)} collective-permute-done((bf16[128,1024]{1,0:T(8,128)(2,1)S(1)}, bf16[128,1024]{1,0:T(8,128)(2,1)S(1)}, u32[]{:S(2)}, u32[]{:S(2)}) %collective-permute-start.23) | collective-permute-done | bytes 262176 | tf_op jit(solution)/shard_map/ppermute | solution.py:44
  62.8 2.2 %states.1 = (bf16[4096,128]{1,0:T(8,128)(2,1)}, bf16[64,512]{1,0:T(8,128)(2,1)}, bf16[64,512]{1,0:T(8,128)(2,1)}) custom-call(f32[4096,128]{1,0:T(8,128)S(1)} %get-tuple-element.106.refs_0_, f32[4096,128]{1,0:T(8,128)S(1)} %get-tuple-element.107.refs_1_, bf16[128,1024]{1,0:T(8,128)(2,1)S(1)} %join.5.refs_3_.refs_1_.refs_2_, ...), custom_call_target="tpu_custom_call" | custom-call | flops 67108864 | bytes 6619136 | tf_op jit(solution)/shard_map/states/pallas_call | solution.py:95
  (49 shorter events, 13.7 us)
Async XLA Ops:
  3.6 2.9 %collective-permute-start = (bf16[128,2048]{1,0:T(8,128)(2,1)S(1)}, bf16[128,2048]{1,0:T(8,128)(2,1)S(1)}, u32[]{:S(2)}, u32[]{:S(2)}) collective-permute-start(bf16[128,2048]{1,0:T(8,128)(2,1)S(1)} %get-tuple-element.65.refs_0_), channel_id=1, source_target_pairs={{0,2},{2,0},{4,6},{6,4},{8,10},{10,8},{12,14},{14,12},{16,18},{18,... | collective-permute-start | bytes 1572872 | tf_op jit(solution)/shard_map/ppermute | solution.py:44
  5.1 1.4 %collective-permute-start.1 = (bf16[32,2048]{1,0:T(8,128)(2,1)S(1)}, bf16[32,2048]{1,0:T(8,128)(2,1)S(1)}, u32[]{:S(2)}, u32[]{:S(2)}) collective-permute-start(bf16[32,2048]{1,0:T(8,128)(2,1)S(1)} %get-tuple-element.76.refs_0_), channel_id=1, source_target_pairs={{0,2},{2,0},{4,6},{6,4},{8,10},{10,8},{12,14},{14,12},{16,18},{18,... | collective-permute-start | bytes 393224 | tf_op jit(solution)/shard_map/ppermute | solution.py:44
  6.8 12.0 %collective-permute-start.4 = (bf16[160,1024]{1,0:T(8,128)(2,1)S(1)}, bf16[160,1024]{1,0:T(8,128)(2,1)S(1)}, u32[]{:S(2)}, u32[]{:S(2)}) collective-permute-start(bf16[160,1024]{1,0:T(8,128)(2,1)S(1)} %get-tuple-element.81.refs_0_), channel_id=1, source_target_pairs={{0,4},{2,6},{4,0},{6,2},{8,12},{10,14},{12,8},{14,10},{16,20},{18,... | collective-permute-start | bytes 983048 | tf_op jit(solution)/shard_map/ppermute | solution.py:44
  10.0 7.7 %collective-permute-start.2 = (bf16[8,4096]{1,0:T(8,128)(2,1)S(1)}, bf16[8,4096]{1,0:T(8,128)(2,1)S(1)}, u32[]{:S(2)}, u32[]{:S(2)}) collective-permute-start(bf16[8,4096]{1,0:T(8,128)(2,1)S(1)} %resident_hidden.1.refs_1_), channel_id=1, source_target_pairs={{0,16},{2,18},{4,20},{6,22},{8,24},{10,26},{12,28},{14,30},{16,0},... | collective-permute-start | bytes 196616 | tf_op jit(solution)/shard_map/ppermute | solution.py:44
  12.6 6.1 %collective-permute-start.3 = (bf16[8,4096]{1,0:T(8,128)(2,1)S(1)}, bf16[8,4096]{1,0:T(8,128)(2,1)S(1)}, u32[]{:S(2)}, u32[]{:S(2)}) collective-permute-start(bf16[8,4096]{1,0:T(8,128)(2,1)S(1)} %resident_hidden.1.refs_1_), channel_id=1, source_target_pairs={{0,24},{2,26},{4,28},{6,30},{8,16},{10,18},{12,20},{14,22},{16,8},... | collective-permute-start | bytes 196616 | tf_op jit(solution)/shard_map/ppermute | solution.py:44
  18.9 6.9 %collective-permute-start.5 = (bf16[160,256]{1,0:T(8,128)(2,1)S(1)}, bf16[160,256]{1,0:T(8,128)(2,1)S(1)}, u32[]{:S(2)}, u32[]{:S(2)}) collective-permute-start(bf16[160,256]{1,0:T(8,128)(2,1)S(1)} %get-tuple-element.92.refs_0_), channel_id=1, source_target_pairs={{0,24},{2,26},{4,28},{6,30},{8,16},{10,18},{12,20},{14,22},{16,8},... | collective-permute-start | bytes 245768 | tf_op jit(solution)/shard_map/ppermute | solution.py:44
  21.8 7.6 %collective-permute-start.6 = (bf16[160,256]{1,0:T(8,128)(2,1)S(1)}, bf16[160,256]{1,0:T(8,128)(2,1)S(1)}, u32[]{:S(2)}, u32[]{:S(2)}) collective-permute-start(bf16[160,256]{1,0:T(8,128)(2,1)S(1)} %get-tuple-element.94), channel_id=1, source_target_pairs={{0,16},{2,18},{4,20},{6,22},{8,24},{10,26},{12,28},{14,30},{16,0},... | collective-permute-start | bytes 245768 | tf_op jit(solution)/shard_map/ppermute | solution.py:44
  22.1 7.3 %collective-permute-start.7 = (bf16[160,256]{1,0:T(8,128)(2,1)S(1)}, bf16[160,256]{1,0:T(8,128)(2,1)S(1)}, u32[]{:S(2)}, u32[]{:S(2)}) collective-permute-start(bf16[160,256]{1,0:T(8,128)(2,1)S(1)} %get-tuple-element.95), channel_id=1, source_target_pairs={{0,8},{2,10},{4,12},{6,14},{8,0},{10,2},{12,4},{14,6},{16,24},{18,... | collective-permute-start | bytes 245768 | tf_op jit(solution)/shard_map/ppermute | solution.py:44
  23.4 10.8 %collective-permute-start.8 = (bf16[8,4096]{1,0:T(8,128)(2,1)S(1)}, bf16[8,4096]{1,0:T(8,128)(2,1)S(1)}, u32[]{:S(2)}, u32[]{:S(2)}) collective-permute-start(bf16[8,4096]{1,0:T(8,128)(2,1)S(1)} %resident_hidden.1.refs_1_), channel_id=1, source_target_pairs={{0,8},{2,10},{4,12},{6,14},{8,0},{10,2},{12,4},{14,6},{16,24},{18,... | collective-permute-start | bytes 196616 | tf_op jit(solution)/shard_map/ppermute | solution.py:44
  29.8 7.2 %collective-permute-start.10 = (bf16[136,256]{1,0:T(8,128)(2,1)S(1)}, bf16[136,256]{1,0:T(8,128)(2,1)S(1)}, u32[]{:S(2)}, u32[]{:S(2)}) collective-permute-start(bf16[136,256]{1,0:T(8,128)(2,1)S(1)} %get-tuple-element.96.refs_0_), channel_id=1, source_target_pairs={{0,24},{2,26},{4,28},{6,30},{8,16},{10,18},{12,20},{14,22},{16,8},... | collective-permute-start | bytes 208904 | tf_op jit(solution)/shard_map/ppermute | solution.py:44
  33.0 5.8 %collective-permute-start.11 = (bf16[136,256]{1,0:T(8,128)(2,1)S(1)}, bf16[136,256]{1,0:T(8,128)(2,1)S(1)}, u32[]{:S(2)}, u32[]{:S(2)}) collective-permute-start(bf16[136,256]{1,0:T(8,128)(2,1)S(1)} %get-tuple-element.98), channel_id=1, source_target_pairs={{0,16},{2,18},{4,20},{6,22},{8,24},{10,26},{12,28},{14,30},{16,0},... | collective-permute-start | bytes 208904 | tf_op jit(solution)/shard_map/ppermute | solution.py:44
  33.0 5.8 %collective-permute-start.12 = (bf16[136,256]{1,0:T(8,128)(2,1)S(1)}, bf16[136,256]{1,0:T(8,128)(2,1)S(1)}, u32[]{:S(2)}, u32[]{:S(2)}) collective-permute-start(bf16[136,256]{1,0:T(8,128)(2,1)S(1)} %get-tuple-element.99), channel_id=1, source_target_pairs={{0,8},{2,10},{4,12},{6,14},{8,0},{10,2},{12,4},{14,6},{16,24},{18,... | collective-permute-start | bytes 208904 | tf_op jit(solution)/shard_map/ppermute | solution.py:44
  34.2 7.1 %collective-permute-start.9 = (bf16[32,4096]{1,0:T(8,128)(2,1)S(1)}, bf16[32,4096]{1,0:T(8,128)(2,1)S(1)}, u32[]{:S(2)}, u32[]{:S(2)}) collective-permute-start(bf16[32,4096]{1,0:T(8,128)(2,1)S(1)} %join.3.refs_1_), channel_id=1, source_target_pairs={{0,4},{2,6},{4,0},{6,2},{8,12},{10,14},{12,8},{14,10},{16,20},{18,... | collective-permute-start | bytes 786440 | tf_op jit(solution)/shard_map/ppermute | solution.py:44
  41.7 10.2 %collective-permute-start.13 = (bf16[64,4096]{1,0:T(8,128)(2,1)S(1)}, bf16[64,4096]{1,0:T(8,128)(2,1)S(1)}, u32[]{:S(2)}, u32[]{:S(2)}) collective-permute-start(bf16[64,4096]{1,0:T(8,128)(2,1)S(1)} %join.4.refs_1_), channel_id=1, source_target_pairs={{0,2},{2,0},{4,6},{6,4},{8,10},{10,8},{12,14},{14,12},{16,18},{18,... | collective-permute-start | bytes 1572872 | tf_op jit(solution)/shard_map/ppermute | solution.py:44
  41.8 10.1 %collective-permute-start.17 = (bf16[136,1024]{1,0:T(8,128)(2,1)S(1)}, bf16[136,1024]{1,0:T(8,128)(2,1)S(1)}, u32[]{:S(2)}, u32[]{:S(2)}) collective-permute-start(bf16[136,1024]{1,0:T(8,128)(2,1)S(1)} %get-tuple-element.103.refs_0_), channel_id=1, source_target_pairs={{0,4},{2,6},{4,0},{6,2},{8,12},{10,14},{12,8},{14,10},{16,20},{18,... | collective-permute-start | bytes 835592 | tf_op jit(solution)/shard_map/ppermute | solution.py:44
  42.7 6.8 %collective-permute-start.14 = (bf16[128,256]{1,0:T(8,128)(2,1)S(1)}, bf16[128,256]{1,0:T(8,128)(2,1)S(1)}, u32[]{:S(2)}, u32[]{:S(2)}) collective-permute-start(bf16[128,256]{1,0:T(8,128)(2,1)S(1)} %hand_on.3.refs_0_), channel_id=1, source_target_pairs={{0,8},{2,10},{4,12},{6,14},{8,0},{10,2},{12,4},{14,6},{16,24},{18,... | collective-permute-start | bytes 196616 | tf_op jit(solution)/shard_map/ppermute | solution.py:44
  43.1 7.9 %collective-permute-start.15 = (bf16[128,256]{1,0:T(8,128)(2,1)S(1)}, bf16[128,256]{1,0:T(8,128)(2,1)S(1)}, u32[]{:S(2)}, u32[]{:S(2)}) collective-permute-start(bf16[128,256]{1,0:T(8,128)(2,1)S(1)} %hand_on.3.refs_0_), channel_id=1, source_target_pairs={{0,16},{2,18},{4,20},{6,22},{8,24},{10,26},{12,28},{14,30},{16,0},... | collective-permute-start | bytes 196616 | tf_op jit(solution)/shard_map/ppermute | solution.py:44
  45.7 6.2 %collective-permute-start.16 = (bf16[128,256]{1,0:T(8,128)(2,1)S(1)}, bf16[128,256]{1,0:T(8,128)(2,1)S(1)}, u32[]{:S(2)}, u32[]{:S(2)}) collective-permute-start(bf16[128,256]{1,0:T(8,128)(2,1)S(1)} %hand_on.3.refs_0_), channel_id=1, source_target_pairs={{0,24},{2,26},{4,28},{6,30},{8,16},{10,18},{12,20},{14,22},{16,8},... | collective-permute-start | bytes 196616 | tf_op jit(solution)/shard_map/ppermute | solution.py:44
  52.3 6.0 %collective-permute-start.19 = (bf16[128,2048]{1,0:T(8,128)(2,1)S(1)}, bf16[128,2048]{1,0:T(8,128)(2,1)S(1)}, u32[]{:S(2)}, u32[]{:S(2)}) collective-permute-start(bf16[128,2048]{1,0:T(8,128)(2,1)S(1)} %get-tuple-element.113), channel_id=1, source_target_pairs={{0,2},{2,0},{4,6},{6,4},{8,10},{10,8},{12,14},{14,12},{16,18},{18,... | collective-permute-start | bytes 1572872 | tf_op jit(solution)/shard_map/ppermute | solution.py:44
  52.4 8.7 %collective-permute-start.20 = (bf16[128,1024]{1,0:T(8,128)(2,1)S(1)}, bf16[128,1024]{1,0:T(8,128)(2,1)S(1)}, u32[]{:S(2)}, u32[]{:S(2)}) collective-permute-start(bf16[128,1024]{1,0:T(8,128)(2,1)S(1)} %join.5.refs_3_.refs_1_.refs_2_), channel_id=1, source_target_pairs={{0,4},{2,6},{4,0},{6,2},{8,12},{10,14},{12,8},{14,10},{16,20},{18,... | collective-permute-start | bytes 786440 | tf_op jit(solution)/shard_map/ppermute | solution.py:44
  54.2 1.2 %collective-permute-start.18 = (bf16[8,2048]{1,0:T(8,128)(2,1)S(1)}, bf16[8,2048]{1,0:T(8,128)(2,1)S(1)}, u32[]{:S(2)}, u32[]{:S(2)}) collective-permute-start(bf16[8,2048]{1,0:T(8,128)(2,1)S(1)} %get-tuple-element.110.refs_3_), channel_id=1, source_target_pairs={{0,2},{2,0},{4,6},{6,4},{8,10},{10,8},{12,14},{14,12},{16,18},{18,... | collective-permute-start | bytes 98312 | tf_op jit(solution)/shard_map/ppermute | solution.py:44
  56.3 4.8 %collective-permute-start.22 = (bf16[64,512]{1,0:T(8,128)(2,1)S(1)}, bf16[64,512]{1,0:T(8,128)(2,1)S(1)}, u32[]{:S(2)}, u32[]{:S(2)}) collective-permute-start(bf16[64,512]{1,0:T(8,128)(2,1)S(1)} %get-tuple-element.116), channel_id=1, source_target_pairs={{0,1},{1,0},{2,3},{3,2},{4,5},{5,4},{6,7},{7,6},{8,9},{9,8},{10,11... | collective-permute-start | bytes 196616 | tf_op jit(solution)/shard_map/ppermute | solution.py:44
  57.9 3.3 %collective-permute-start.21 = (bf16[128,1024]{1,0:T(8,128)(2,1)S(1)}, bf16[128,1024]{1,0:T(8,128)(2,1)S(1)}, u32[]{:S(2)}, u32[]{:S(2)}) collective-permute-start(bf16[128,1024]{1,0:T(8,128)(2,1)S(1)} %hand_on.4), channel_id=1, source_target_pairs={{0,2},{2,0},{4,6},{6,4},{8,10},{10,8},{12,14},{14,12},{16,18},{18,... | collective-permute-start | bytes 786440 | tf_op jit(solution)/shard_map/ppermute | solution.py:44
  61.2 1.6 %collective-permute-start.23 = (bf16[128,1024]{1,0:T(8,128)(2,1)S(1)}, bf16[128,1024]{1,0:T(8,128)(2,1)S(1)}, u32[]{:S(2)}, u32[]{:S(2)}) collective-permute-start(bf16[128,1024]{1,0:T(8,128)(2,1)S(1)} %hand_on.5), channel_id=1, source_target_pairs={{0,2},{2,0},{4,6},{6,4},{8,10},{10,8},{12,14},{14,12},{16,18},{18,... | collective-permute-start | bytes 786440 | tf_op jit(solution)/shard_map/ppermute | solution.py:44

commit v5 on v4

--- a/solution.py
+++ b/solution.py
@@ -547,13 +547,14 @@
     return call(copy, "hand_on", [shape(value.shape, value.dtype)], [value], after=after)[0]
 
 
-def gather_in(values):
+def gather_in(values, after=()):
     def copy(*refs):
         for k in range(len(values)):
             refs[len(values) + k][...] = refs[k][...]
 
     return call(
-        copy, "gather_in", [shape(v.shape, v.dtype) for v in values], values, flops=10**10, moved=1
+        copy, "gather_in", [shape(v.shape, v.dtype) for v in values], values, after=after,
+        flops=10**10, moved=1,
     )
 
 
@@ -684,7 +685,8 @@
             piece = (spot // line[0] ^ place_of(core)) * line[0] + (spot % line[0] ^ place_of(line))
             position = jnp.int32(0)
             if len(scattered) > 1:
-                position = lane % part // width ^ place_of(last)
+                apart = lane % part // width ^ place_of(last)
+                position = jnp.where(apart == 0, 0, last[0] - apart)
             at = window(position * width, width)
             found = prompt_refs[0][:, at]
             for k in range(1, pieces):
@@ -827,7 +829,7 @@
 
     def fill(after):
         if len(bases) < groups:
-            wanted = [] if bases else [out_weight]
+            wanted = [out_weight] if len(bases) == min(1, groups - 1) else []
             base, *found = intra(
                 len(bases), run, runt, stept, skip_lanes, x, writes, reads, after, wanted
             )
@@ -858,11 +860,14 @@
         "up_last",
         [shape((UP_ROWS, last_width), BF16)] * (last[0] if split_last else 1),
         line_parts,
-        after=filled + hiddens[2:],
+        after=filled + hiddens[:0:-1],
         flops=line_width * UP_ROWS * 4,
     )
     last_parts = exchange(outs if split_last else outs * last[0], last)
+    hidden = join(hiddens, 0, [outs[-1]])
+    hiddens = exchange([hidden] * line[0], line)
     filled = fill([outs[-1]])
+    last_parts = last_parts[:1] + list(gather_in(last_parts[:0:-1], filled))[::-1]
     *outs, prompt = call(
         functools.partial(top_kernel, last, last[0]),
         "top",
@@ -874,21 +879,19 @@
     )
 
     pieces = exchange(outs, last) if split_last else outs
+    hidden = join(hiddens, 0, [outs[-1]])
+    filled = fill([outs[-1], hidden])
     if split_last:
-        pieces = pieces[:1] + list(gather_in(pieces[:0:-1]))[::-1]
-    hidden = join(hiddens, 0, [outs[-1]])
-    hiddens = exchange([hidden] * line[0], line)
-    filled = fill([outs[-1]])
+        pieces = pieces[:1] + list(gather_in(pieces[:0:-1], filled))[::-1]
     outs = call(
         functools.partial(down_kernel, line, last, len(pieces), line[0], False, range(line[0]), False),
         "down_line",
         [shape((DOWN_ROWS, line_width), BF16)] * line[0],
         [*turned(pieces), *line_parts],
-        after=filled + hiddens[1:],
+        after=filled,
         flops=line_width * UP_ROWS * 8,
     )
     pieces = exchange(outs, line)
-    hidden = join(hiddens, 0, [outs[-1]])
     hiddens = [hidden, swap(hidden, "seq", core, 1)]
     filled = fill([outs[-1]])
     prepared = prepare(owner, resident, tail, vwrite, filled)
@@ -896,7 +899,8 @@
     scattered = [line, last] if split_last else [line]
     if split_last:
         prompt = hand_on(prompt, [outs[-1]])
-        prompt = join(exchange([prompt] * last[0], last), 1)
+        parts = exchange([prompt] * last[0], last)
+        prompt = join(turned(parts), 1)
         filled.append(prompt)
 
     def down_core(target, after):
@@ -911,6 +915,7 @@
 
     sent, gated = down_core(1, filled)
     received_gated, received = swap(gated, "seq", core, 1), swap(sent, "seq", core, 1)
+    (received_gated,) = gather_in([received_gated])
     while len(bases) < groups:
         fill([])
 

time: 65.3 us -> 61.6 us (0.943)
  waiting for transfers between devices: 15.2 us -> 12.5 us
  starting transfers between devices: 27.2 us -> 26.2 us
    ppermute x24, waiting for transfers between devices: 15.2 us -> 12.5 us  [swap(): lax.ppermute(value, axis, [(k, k ^ offset * stride) for k in range(count)])]
    ppermute x24, starting transfers between devices: 27.2 us -> 26.2 us  [swap(): lax.ppermute(value, axis, [(k, k ^ offset * stride) for k in range(count)])]
    pallas_call x25 -> x27, Pallas kernels: 21.6 us -> 21.6 us  [call(): pl.pallas_call(ordered(kernel, first), name=name, grid=grid, out_shape=ou...]
  transfers between devices with their start and end apart: 24 -> 24, of which waited for: 11 -> 9; matrix products, arithmetic and copies ran while one was open for 0% -> 0% of each run, Pallas kernels for 23% -> 26%
where the time goes in v5:
time: 61.6 us; the launch traced here: 61.4 us
  starting transfers between devices  26.2 us (43%)
  Pallas kernels  21.6 us (35%)
  waiting for transfers between devices  12.5 us (20%)
  between operations  1.02 us (2%)
    ppermute x24, starting transfers between devices, swap(): lax.ppermute(value, axis, [(k, k ^ offset * stride) for k in range(count)])  26.2 us
    pallas_call x27, Pallas kernels, call(): pl.pallas_call(ordered(kernel, first), name=name, grid=grid, out_shape=ou...  21.6 us
    ppermute x24, waiting for transfers between devices, swap(): lax.ppermute(value, axis, [(k, k ^ offset * stride) for k in range(count)])  12.5 us
  transfers between devices with their start and end apart: 24, of which 9 were waited for; matrix products, arithmetic and copies ran while one was open for 0% of the time, Pallas kernels for 26%

profile of v5, /device:TPU:0, one launch (start us, length us, event | category | flops | bytes accessed | tf_op | source)
XLA Modules:
  0.0 61.4 jit_solution(18179843274135003500)
XLA Ops:
  0.6 3.0 %open_block.1 = (bf16[128,2048]{1,0:T(8,128)(2,1)S(1)}, f32[4,256,16]{2,1,0:T(8,128)S(1)}, f32[64,256]{1,0:T(8,128)S(1)}, f32[64,256]{1,0:T(8,128)S(1)}, bf16[25...) custom-call(f32[64,256]{1,0:T(8,128)} %bitcast.8, ...), custom_call_target="tpu_custom_call" | custom-call | flops 268435456 | bytes 8911232 | tf_op jit(solution)/shard_map/open_block/pallas_call | solution.py:95
  6.8 2.8 %collective-permute-start.5 = (bf16[160,1024]{1,0:T(8,128)(2,1)S(1)}, bf16[160,1024]{1,0:T(8,128)(2,1)S(1)}, u32[]{:S(2)}, u32[]{:S(2)}) collective-permute-start(bf16[160,1024]{1,0:T(8,128)(2,1)S(1)} %get-tuple-element.84.refs_0_), channel_id=1, source_target_pairs={{0,4},{2,6},{4,0},{6,2},{8,12},{10,14},{12,8},{14,10},{16,20},{18,... | collective-permute-start | bytes 983048 | tf_op jit(solution)/shard_map/ppermute | solution.py:44
  10.0 3.6 %collective-permute-start.2 = (bf16[8,4096]{1,0:T(8,128)(2,1)S(1)}, bf16[8,4096]{1,0:T(8,128)(2,1)S(1)}, u32[]{:S(2)}, u32[]{:S(2)}) collective-permute-start(bf16[8,4096]{1,0:T(8,128)(2,1)S(1)} %resident_hidden.1.refs_1_), channel_id=1, source_target_pairs={{0,24},{2,26},{4,28},{6,30},{8,16},{10,18},{12,20},{14,22},{16,8},... | collective-permute-start | bytes 196616 | tf_op jit(solution)/shard_map/ppermute | solution.py:44
  14.4 1.6 %intra.4.refs_0_.refs_4_ = f32[256,1024]{1,0:T(8,128)S(1)} custom-call(bf16[160,1024]{1,0:T(8,128)(2,1)S(1)} %get-tuple-element.84.refs_0_, f32[4,256,16]{2,1,0:T(8,128)S(1)} %get-tuple-element.85.refs_1_.refs_2_, f32[64,256]{1,0:T(8,128)S(1)} %get-tuple-element.71.refs_4_.refs_2_.refs_3_, f32[64,256]{1,0:T(8,128)S(1)} %get-tuple-element.86.refs_3_.refs_4_, ...), custom_call_target="tpu_custom_call" | custom-call | flops 134217728 | bytes 1572864 | tf_op jit(solution)/shard_map/intra/pallas_call | solution.py:95
  16.4 3.1 %collective-permute-done.3.refs_2_.refs_3_ = bf16[8,4096]{1,0:T(8,128)(2,1)S(1)} collective-permute-done((bf16[8,4096]{1,0:T(8,128)(2,1)S(1)}, bf16[8,4096]{1,0:T(8,128)(2,1)S(1)}, u32[]{:S(2)}, u32[]{:S(2)}) %collective-permute-start.3) | collective-permute-done | bytes 65568 | tf_op jit(solution)/shard_map/ppermute | solution.py:44
  19.7 2.6 %collective-permute-start.6 = (bf16[160,256]{1,0:T(8,128)(2,1)S(1)}, bf16[160,256]{1,0:T(8,128)(2,1)S(1)}, u32[]{:S(2)}, u32[]{:S(2)}) collective-permute-start(bf16[160,256]{1,0:T(8,128)(2,1)S(1)} %get-tuple-element.94.refs_0_), channel_id=1, source_target_pairs={{0,24},{2,26},{4,28},{6,30},{8,16},{10,18},{12,20},{14,22},{16,8},... | collective-permute-start | bytes 245768 | tf_op jit(solution)/shard_map/ppermute | solution.py:44
  22.3 1.8 %collective-permute-start.8 = (bf16[160,256]{1,0:T(8,128)(2,1)S(1)}, bf16[160,256]{1,0:T(8,128)(2,1)S(1)}, u32[]{:S(2)}, u32[]{:S(2)}) collective-permute-start(bf16[160,256]{1,0:T(8,128)(2,1)S(1)} %get-tuple-element.98), channel_id=1, source_target_pairs={{0,8},{2,10},{4,12},{6,14},{8,0},{10,2},{12,4},{14,6},{16,24},{18,... | collective-permute-start | bytes 245768 | tf_op jit(solution)/shard_map/ppermute | solution.py:44
  24.7 3.6 %intra.5 = (f32[256,1024]{1,0:T(8,128)S(1)}, bf16[4096,512]{1,0:T(8,128)(2,1)S(1)}) custom-call(bf16[160,256]{1,0:T(8,128)(2,1)S(1)} %get-tuple-element.94.refs_0_, f32[4,256,16]{2,1,0:T(8,128)S(1)} %get-tuple-element.85.refs_1_.refs_2_, f32[64,256]{1,0:T(8,128)S(1)} %get-tuple-element.71.refs_4_.refs_2_.refs_3_, ...), custom_call_target="tpu_custom_call" | custom-call | flops 134217728 | bytes 1572864 | tf_op jit(solution)/shard_map/intra/pallas_call | solution.py:95
  28.3 1.6 %collective-permute-done.7.refs_2_ = bf16[160,256]{1,0:T(8,128)(2,1)S(1)} collective-permute-done((bf16[160,256]{1,0:T(8,128)(2,1)S(1)}, bf16[160,256]{1,0:T(8,128)(2,1)S(1)}, u32[]{:S(2)}, u32[]{:S(2)}) %collective-permute-start.7) | collective-permute-done | bytes 81952 | tf_op jit(solution)/shard_map/ppermute | solution.py:44
  30.3 1.8 %collective-permute-start.11 = (bf16[136,256]{1,0:T(8,128)(2,1)S(1)}, bf16[136,256]{1,0:T(8,128)(2,1)S(1)}, u32[]{:S(2)}, u32[]{:S(2)}) collective-permute-start(bf16[136,256]{1,0:T(8,128)(2,1)S(1)} %get-tuple-element.102.refs_0_), channel_id=1, source_target_pairs={{0,24},{2,26},{4,28},{6,30},{8,16},{10,18},{12,20},{14,22},{16,8},... | collective-permute-start | bytes 208904 | tf_op jit(solution)/shard_map/ppermute | solution.py:44
  32.1 2.6 %collective-permute-start.13 = (bf16[136,256]{1,0:T(8,128)(2,1)S(1)}, bf16[136,256]{1,0:T(8,128)(2,1)S(1)}, u32[]{:S(2)}, u32[]{:S(2)}) collective-permute-start(bf16[136,256]{1,0:T(8,128)(2,1)S(1)} %get-tuple-element.105), channel_id=1, source_target_pairs={{0,8},{2,10},{4,12},{6,14},{8,0},{10,2},{12,4},{14,6},{16,24},{18,... | collective-permute-start | bytes 208904 | tf_op jit(solution)/shard_map/ppermute | solution.py:44
  34.8 1.6 %intra.6.refs_0_.refs_6_ = f32[256,1024]{1,0:T(8,128)S(1)} custom-call(bf16[136,256]{1,0:T(8,128)(2,1)S(1)} %get-tuple-element.102.refs_0_, bf16[64,4096]{1,0:T(8,128)(2,1)S(1)} %join.4.refs_1_, f32[4,256,16]{2,1,0:T(8,128)S(1)} %get-tuple-element.85.refs_1_.refs_2_, f32[64,256]{1,0:T(8,128)S(1)} %get-tuple-element.71.refs_4_.refs_2_.refs_3_, ...), custom_call_target="tpu_custom_call" | custom-call | flops 134217728 | bytes 1572864 | tf_op jit(solution)/shard_map/intra/pallas_call | solution.py:95
  36.9 1.7 %collective-permute-done.12.refs_2_ = bf16[136,256]{1,0:T(8,128)(2,1)S(1)} collective-permute-done((bf16[136,256]{1,0:T(8,128)(2,1)S(1)}, bf16[136,256]{1,0:T(8,128)(2,1)S(1)}, u32[]{:S(2)}, u32[]{:S(2)}) %collective-permute-start.12) | collective-permute-done | bytes 69664 | tf_op jit(solution)/shard_map/ppermute | solution.py:44
  38.9 1.0 %collective-permute-start.17 = (bf16[136,1024]{1,0:T(8,128)(2,1)S(1)}, bf16[136,1024]{1,0:T(8,128)(2,1)S(1)}, u32[]{:S(2)}, u32[]{:S(2)}) collective-permute-start(bf16[136,1024]{1,0:T(8,128)(2,1)S(1)} %get-tuple-element.109.refs_0_), channel_id=1, source_target_pairs={{0,4},{2,6},{4,0},{6,2},{8,12},{10,14},{12,8},{14,10},{16,20},{18,... | collective-permute-start | bytes 835592 | tf_op jit(solution)/shard_map/ppermute | solution.py:44
  39.9 2.2 %collective-permute-start.14 = (bf16[128,256]{1,0:T(8,128)(2,1)S(1)}, bf16[128,256]{1,0:T(8,128)(2,1)S(1)}, u32[]{:S(2)}, u32[]{:S(2)}) collective-permute-start(bf16[128,256]{1,0:T(8,128)(2,1)S(1)} %hand_on.3.refs_0_), channel_id=1, source_target_pairs={{0,24},{2,26},{4,28},{6,30},{8,16},{10,18},{12,20},{14,22},{16,8},... | collective-permute-start | bytes 196616 | tf_op jit(solution)/shard_map/ppermute | solution.py:44
  42.0 2.2 %collective-permute-start.16 = (bf16[128,256]{1,0:T(8,128)(2,1)S(1)}, bf16[128,256]{1,0:T(8,128)(2,1)S(1)}, u32[]{:S(2)}, u32[]{:S(2)}) collective-permute-start(bf16[128,256]{1,0:T(8,128)(2,1)S(1)} %hand_on.3.refs_0_), channel_id=1, source_target_pairs={{0,8},{2,10},{4,12},{6,14},{8,0},{10,2},{12,4},{14,6},{16,24},{18,... | collective-permute-start | bytes 196616 | tf_op jit(solution)/shard_map/ppermute | solution.py:44
  44.3 1.6 %intra.7.refs_0_.refs_7_ = f32[256,1024]{1,0:T(8,128)S(1)} custom-call(bf16[136,1024]{1,0:T(8,128)(2,1)S(1)} %get-tuple-element.109.refs_0_, f32[4,256,16]{2,1,0:T(8,128)S(1)} %get-tuple-element.85.refs_1_.refs_2_, f32[64,256]{1,0:T(8,128)S(1)} %get-tuple-element.71.refs_4_.refs_2_.refs_3_, f32[64,256]{1,0:T(8,128)S(1)} %get-tuple-element.86.refs_3_.refs_4_, ...), custom_call_target="tpu_custom_call" | custom-call | flops 134217728 | bytes 1572864 | tf_op jit(solution)/shard_map/intra/pallas_call | solution.py:95
  46.7 1.5 %collective-permute-done.15.refs_2_ = bf16[128,256]{1,0:T(8,128)(2,1)S(1)} collective-permute-done((bf16[128,256]{1,0:T(8,128)(2,1)S(1)}, bf16[128,256]{1,0:T(8,128)(2,1)S(1)}, u32[]{:S(2)}, u32[]{:S(2)}) %collective-permute-start.15) | collective-permute-done | bytes 65568 | tf_op jit(solution)/shard_map/ppermute | solution.py:44
  48.7 1.3 %collective-permute-start.20 = (bf16[128,1024]{1,0:T(8,128)(2,1)S(1)}, bf16[128,1024]{1,0:T(8,128)(2,1)S(1)}, u32[]{:S(2)}, u32[]{:S(2)}) collective-permute-start(bf16[128,1024]{1,0:T(8,128)(2,1)S(1)} %join.5.refs_3_.refs_1_.refs_2_), channel_id=1, source_target_pairs={{0,4},{2,6},{4,0},{6,2},{8,12},{10,14},{12,8},{14,10},{16,20},{18,... | collective-permute-start | bytes 786440 | tf_op jit(solution)/shard_map/ppermute | solution.py:44
  51.1 1.7 %collective-permute-start.22 = (bf16[64,512]{1,0:T(8,128)(2,1)S(1)}, bf16[64,512]{1,0:T(8,128)(2,1)S(1)}, u32[]{:S(2)}, u32[]{:S(2)}) collective-permute-start(bf16[64,512]{1,0:T(8,128)(2,1)S(1)} %get-tuple-element.122), channel_id=1, source_target_pairs={{0,1},{1,0},{2,3},{3,2},{4,5},{5,4},{6,7},{7,6},{8,9},{9,8},{10,11... | collective-permute-start | bytes 196616 | tf_op jit(solution)/shard_map/ppermute | solution.py:44
  53.4 2.0 %finish.1 = (bf16[256,4096]{1,0:T(8,128)(2,1)}, f32[8,128]{1,0:T(8,128)S(1)}) custom-call(bf16[256,128]{1,0:T(8,128)(2,1)S(1)} %get-tuple-element.65.refs_0_, bf16[256,512]{1,0:T(8,128)(2,1)S(1)} %get-tuple-element.66.refs_7_.refs_8_.refs_1_, bf16[128,2048]{1,0:T(8,128)(2,1)S(1)} %down_core.3.refs_2_, bf16[128,2048]{1,0:T(8,128)(2,1)S(1)} %collective-permute-done.19.refs_3_, ...), custom_call_target="tpu_custom_call" | custom-call | bytes 1 | tf_op jit(solution)/shard_map/finish/pallas_call | solution.py:95
  55.4 2.0 %collective-permute-done.20.refs_2_.refs_3_ = bf16[128,1024]{1,0:T(8,128)(2,1)S(1)} collective-permute-done((bf16[128,1024]{1,0:T(8,128)(2,1)S(1)}, bf16[128,1024]{1,0:T(8,128)(2,1)S(1)}, u32[]{:S(2)}, u32[]{:S(2)}) %collective-permute-start.20) | collective-permute-done | bytes 262176 | tf_op jit(solution)/shard_map/ppermute | solution.py:44
  57.5 1.5 %collective-permute-done.23.refs_5_ = bf16[128,1024]{1,0:T(8,128)(2,1)S(1)} collective-permute-done((bf16[128,1024]{1,0:T(8,128)(2,1)S(1)}, bf16[128,1024]{1,0:T(8,128)(2,1)S(1)}, u32[]{:S(2)}, u32[]{:S(2)}) %collective-permute-start.23) | collective-permute-done | bytes 262176 | tf_op jit(solution)/shard_map/ppermute | solution.py:44
  59.0 2.2 %states.1 = (bf16[4096,128]{1,0:T(8,128)(2,1)}, bf16[64,512]{1,0:T(8,128)(2,1)}, bf16[64,512]{1,0:T(8,128)(2,1)}) custom-call(f32[4096,128]{1,0:T(8,128)S(1)} %get-tuple-element.112.refs_0_, f32[4096,128]{1,0:T(8,128)S(1)} %get-tuple-element.113.refs_1_, bf16[128,1024]{1,0:T(8,128)(2,1)S(1)} %join.5.refs_3_.refs_1_.refs_2_, ...), custom_call_target="tpu_custom_call" | custom-call | flops 67108864 | bytes 6619136 | tf_op jit(solution)/shard_map/states/pallas_call | solution.py:95
  (51 shorter events, 9.7 us)
Async XLA Ops:
  3.6 2.9 %collective-permute-start = (bf16[128,2048]{1,0:T(8,128)(2,1)S(1)}, bf16[128,2048]{1,0:T(8,128)(2,1)S(1)}, u32[]{:S(2)}, u32[]{:S(2)}) collective-permute-start(bf16[128,2048]{1,0:T(8,128)(2,1)S(1)} %get-tuple-element.68.refs_0_), channel_id=1, source_target_pairs={{0,2},{2,0},{4,6},{6,4},{8,10},{10,8},{12,14},{14,12},{16,18},{18,... | collective-permute-start | bytes 1572872 | tf_op jit(solution)/shard_map/ppermute | solution.py:44
  5.1 1.4 %collective-permute-start.1 = (bf16[32,2048]{1,0:T(8,128)(2,1)S(1)}, bf16[32,2048]{1,0:T(8,128)(2,1)S(1)}, u32[]{:S(2)}, u32[]{:S(2)}) collective-permute-start(bf16[32,2048]{1,0:T(8,128)(2,1)S(1)} %get-tuple-element.79.refs_0_), channel_id=1, source_target_pairs={{0,2},{2,0},{4,6},{6,4},{8,10},{10,8},{12,14},{14,12},{16,18},{18,... | collective-permute-start | bytes 393224 | tf_op jit(solution)/shard_map/ppermute | solution.py:44
  6.8 12.7 %collective-permute-start.5 = (bf16[160,1024]{1,0:T(8,128)(2,1)S(1)}, bf16[160,1024]{1,0:T(8,128)(2,1)S(1)}, u32[]{:S(2)}, u32[]{:S(2)}) collective-permute-start(bf16[160,1024]{1,0:T(8,128)(2,1)S(1)} %get-tuple-element.84.refs_0_), channel_id=1, source_target_pairs={{0,4},{2,6},{4,0},{6,2},{8,12},{10,14},{12,8},{14,10},{16,20},{18,... | collective-permute-start | bytes 983048 | tf_op jit(solution)/shard_map/ppermute | solution.py:44
  10.0 6.4 %collective-permute-start.2 = (bf16[8,4096]{1,0:T(8,128)(2,1)S(1)}, bf16[8,4096]{1,0:T(8,128)(2,1)S(1)}, u32[]{:S(2)}, u32[]{:S(2)}) collective-permute-start(bf16[8,4096]{1,0:T(8,128)(2,1)S(1)} %resident_hidden.1.refs_1_), channel_id=1, source_target_pairs={{0,24},{2,26},{4,28},{6,30},{8,16},{10,18},{12,20},{14,22},{16,8},... | collective-permute-start | bytes 196616 | tf_op jit(solution)/shard_map/ppermute | solution.py:44
  13.7 5.8 %collective-permute-start.3 = (bf16[8,4096]{1,0:T(8,128)(2,1)S(1)}, bf16[8,4096]{1,0:T(8,128)(2,1)S(1)}, u32[]{:S(2)}, u32[]{:S(2)}) collective-permute-start(bf16[8,4096]{1,0:T(8,128)(2,1)S(1)} %resident_hidden.1.refs_1_), channel_id=1, source_target_pairs={{0,16},{2,18},{4,20},{6,22},{8,24},{10,26},{12,28},{14,30},{16,0},... | collective-permute-start | bytes 196616 | tf_op jit(solution)/shard_map/ppermute | solution.py:44
  13.7 5.8 %collective-permute-start.4 = (bf16[8,4096]{1,0:T(8,128)(2,1)S(1)}, bf16[8,4096]{1,0:T(8,128)(2,1)S(1)}, u32[]{:S(2)}, u32[]{:S(2)}) collective-permute-start(bf16[8,4096]{1,0:T(8,128)(2,1)S(1)} %resident_hidden.1.refs_1_), channel_id=1, source_target_pairs={{0,8},{2,10},{4,12},{6,14},{8,0},{10,2},{12,4},{14,6},{16,24},{18,... | collective-permute-start | bytes 196616 | tf_op jit(solution)/shard_map/ppermute | solution.py:44
  19.7 8.7 %collective-permute-start.6 = (bf16[160,256]{1,0:T(8,128)(2,1)S(1)}, bf16[160,256]{1,0:T(8,128)(2,1)S(1)}, u32[]{:S(2)}, u32[]{:S(2)}) collective-permute-start(bf16[160,256]{1,0:T(8,128)(2,1)S(1)} %get-tuple-element.94.refs_0_), channel_id=1, source_target_pairs={{0,24},{2,26},{4,28},{6,30},{8,16},{10,18},{12,20},{14,22},{16,8},... | collective-permute-start | bytes 245768 | tf_op jit(solution)/shard_map/ppermute | solution.py:44
  22.3 7.7 %collective-permute-start.7 = (bf16[160,256]{1,0:T(8,128)(2,1)S(1)}, bf16[160,256]{1,0:T(8,128)(2,1)S(1)}, u32[]{:S(2)}, u32[]{:S(2)}) collective-permute-start(bf16[160,256]{1,0:T(8,128)(2,1)S(1)} %get-tuple-element.97), channel_id=1, source_target_pairs={{0,16},{2,18},{4,20},{6,22},{8,24},{10,26},{12,28},{14,30},{16,0},... | collective-permute-start | bytes 245768 | tf_op jit(solution)/shard_map/ppermute | solution.py:44
  22.3 7.7 %collective-permute-start.8 = (bf16[160,256]{1,0:T(8,128)(2,1)S(1)}, bf16[160,256]{1,0:T(8,128)(2,1)S(1)}, u32[]{:S(2)}, u32[]{:S(2)}) collective-permute-start(bf16[160,256]{1,0:T(8,128)(2,1)S(1)} %get-tuple-element.98), channel_id=1, source_target_pairs={{0,8},{2,10},{4,12},{6,14},{8,0},{10,2},{12,4},{14,6},{16,24},{18,... | collective-permute-start | bytes 245768 | tf_op jit(solution)/shard_map/ppermute | solution.py:44
  24.1 10.6 %collective-permute-start.9 = (bf16[32,4096]{1,0:T(8,128)(2,1)S(1)}, bf16[32,4096]{1,0:T(8,128)(2,1)S(1)}, u32[]{:S(2)}, u32[]{:S(2)}) collective-permute-start(bf16[32,4096]{1,0:T(8,128)(2,1)S(1)} %join.3.refs_1_), channel_id=1, source_target_pairs={{0,4},{2,6},{4,0},{6,2},{8,12},{10,14},{12,8},{14,10},{16,20},{18,... | collective-permute-start | bytes 786440 | tf_op jit(solution)/shard_map/ppermute | solution.py:44
  30.3 6.6 %collective-permute-start.11 = (bf16[136,256]{1,0:T(8,128)(2,1)S(1)}, bf16[136,256]{1,0:T(8,128)(2,1)S(1)}, u32[]{:S(2)}, u32[]{:S(2)}) collective-permute-start(bf16[136,256]{1,0:T(8,128)(2,1)S(1)} %get-tuple-element.102.refs_0_), channel_id=1, source_target_pairs={{0,24},{2,26},{4,28},{6,30},{8,16},{10,18},{12,20},{14,22},{16,8},... | collective-permute-start | bytes 208904 | tf_op jit(solution)/shard_map/ppermute | solution.py:44
  32.1 6.4 %collective-permute-start.12 = (bf16[136,256]{1,0:T(8,128)(2,1)S(1)}, bf16[136,256]{1,0:T(8,128)(2,1)S(1)}, u32[]{:S(2)}, u32[]{:S(2)}) collective-permute-start(bf16[136,256]{1,0:T(8,128)(2,1)S(1)} %get-tuple-element.104), channel_id=1, source_target_pairs={{0,16},{2,18},{4,20},{6,22},{8,24},{10,26},{12,28},{14,30},{16,0},... | collective-permute-start | bytes 208904 | tf_op jit(solution)/shard_map/ppermute | solution.py:44
  32.1 6.4 %collective-permute-start.13 = (bf16[136,256]{1,0:T(8,128)(2,1)S(1)}, bf16[136,256]{1,0:T(8,128)(2,1)S(1)}, u32[]{:S(2)}, u32[]{:S(2)}) collective-permute-start(bf16[136,256]{1,0:T(8,128)(2,1)S(1)} %get-tuple-element.105), channel_id=1, source_target_pairs={{0,8},{2,10},{4,12},{6,14},{8,0},{10,2},{12,4},{14,6},{16,24},{18,... | collective-permute-start | bytes 208904 | tf_op jit(solution)/shard_map/ppermute | solution.py:44
  34.8 13.4 %collective-permute-start.10 = (bf16[64,4096]{1,0:T(8,128)(2,1)S(1)}, bf16[64,4096]{1,0:T(8,128)(2,1)S(1)}, u32[]{:S(2)}, u32[]{:S(2)}) collective-permute-start(bf16[64,4096]{1,0:T(8,128)(2,1)S(1)} %join.4.refs_1_), channel_id=1, source_target_pairs={{0,2},{2,0},{4,6},{6,4},{8,10},{10,8},{12,14},{14,12},{16,18},{18,... | collective-permute-start | bytes 1572872 | tf_op jit(solution)/shard_map/ppermute | solution.py:44
  38.9 9.3 %collective-permute-start.17 = (bf16[136,1024]{1,0:T(8,128)(2,1)S(1)}, bf16[136,1024]{1,0:T(8,128)(2,1)S(1)}, u32[]{:S(2)}, u32[]{:S(2)}) collective-permute-start(bf16[136,1024]{1,0:T(8,128)(2,1)S(1)} %get-tuple-element.109.refs_0_), channel_id=1, source_target_pairs={{0,4},{2,6},{4,0},{6,2},{8,12},{10,14},{12,8},{14,10},{16,20},{18,... | collective-permute-start | bytes 835592 | tf_op jit(solution)/shard_map/ppermute | solution.py:44
  39.9 6.8 %collective-permute-start.14 = (bf16[128,256]{1,0:T(8,128)(2,1)S(1)}, bf16[128,256]{1,0:T(8,128)(2,1)S(1)}, u32[]{:S(2)}, u32[]{:S(2)}) collective-permute-start(bf16[128,256]{1,0:T(8,128)(2,1)S(1)} %hand_on.3.refs_0_), channel_id=1, source_target_pairs={{0,24},{2,26},{4,28},{6,30},{8,16},{10,18},{12,20},{14,22},{16,8},... | collective-permute-start | bytes 196616 | tf_op jit(solution)/shard_map/ppermute | solution.py:44
  42.0 6.1 %collective-permute-start.15 = (bf16[128,256]{1,0:T(8,128)(2,1)S(1)}, bf16[128,256]{1,0:T(8,128)(2,1)S(1)}, u32[]{:S(2)}, u32[]{:S(2)}) collective-permute-start(bf16[128,256]{1,0:T(8,128)(2,1)S(1)} %hand_on.3.refs_0_), channel_id=1, source_target_pairs={{0,16},{2,18},{4,20},{6,22},{8,24},{10,26},{12,28},{14,30},{16,0},... | collective-permute-start | bytes 196616 | tf_op jit(solution)/shard_map/ppermute | solution.py:44
  42.0 6.1 %collective-permute-start.16 = (bf16[128,256]{1,0:T(8,128)(2,1)S(1)}, bf16[128,256]{1,0:T(8,128)(2,1)S(1)}, u32[]{:S(2)}, u32[]{:S(2)}) collective-permute-start(bf16[128,256]{1,0:T(8,128)(2,1)S(1)} %hand_on.3.refs_0_), channel_id=1, source_target_pairs={{0,8},{2,10},{4,12},{6,14},{8,0},{10,2},{12,4},{14,6},{16,24},{18,... | collective-permute-start | bytes 196616 | tf_op jit(solution)/shard_map/ppermute | solution.py:44
  48.6 1.6 %collective-permute-start.18 = (bf16[8,2048]{1,0:T(8,128)(2,1)S(1)}, bf16[8,2048]{1,0:T(8,128)(2,1)S(1)}, u32[]{:S(2)}, u32[]{:S(2)}) collective-permute-start(bf16[8,2048]{1,0:T(8,128)(2,1)S(1)} %get-tuple-element.116.refs_3_), channel_id=1, source_target_pairs={{0,2},{2,0},{4,6},{6,4},{8,10},{10,8},{12,14},{14,12},{16,18},{18,... | collective-permute-start | bytes 98312 | tf_op jit(solution)/shard_map/ppermute | solution.py:44
  48.7 8.7 %collective-permute-start.20 = (bf16[128,1024]{1,0:T(8,128)(2,1)S(1)}, bf16[128,1024]{1,0:T(8,128)(2,1)S(1)}, u32[]{:S(2)}, u32[]{:S(2)}) collective-permute-start(bf16[128,1024]{1,0:T(8,128)(2,1)S(1)} %join.5.refs_3_.refs_1_.refs_2_), channel_id=1, source_target_pairs={{0,4},{2,6},{4,0},{6,2},{8,12},{10,14},{12,8},{14,10},{16,20},{18,... | collective-permute-start | bytes 786440 | tf_op jit(solution)/shard_map/ppermute | solution.py:44
  50.0 3.4 %collective-permute-start.19 = (bf16[128,2048]{1,0:T(8,128)(2,1)S(1)}, bf16[128,2048]{1,0:T(8,128)(2,1)S(1)}, u32[]{:S(2)}, u32[]{:S(2)}) collective-permute-start(bf16[128,2048]{1,0:T(8,128)(2,1)S(1)} %get-tuple-element.119), channel_id=1, source_target_pairs={{0,2},{2,0},{4,6},{6,4},{8,10},{10,8},{12,14},{14,12},{16,18},{18,... | collective-permute-start | bytes 1572872 | tf_op jit(solution)/shard_map/ppermute | solution.py:44
  51.1 6.3 %collective-permute-start.22 = (bf16[64,512]{1,0:T(8,128)(2,1)S(1)}, bf16[64,512]{1,0:T(8,128)(2,1)S(1)}, u32[]{:S(2)}, u32[]{:S(2)}) collective-permute-start(bf16[64,512]{1,0:T(8,128)(2,1)S(1)} %get-tuple-element.122), channel_id=1, source_target_pairs={{0,1},{1,0},{2,3},{3,2},{4,5},{5,4},{6,7},{7,6},{8,9},{9,8},{10,11... | collective-permute-start | bytes 196616 | tf_op jit(solution)/shard_map/ppermute | solution.py:44
  52.9 4.6 %collective-permute-start.21 = (bf16[128,1024]{1,0:T(8,128)(2,1)S(1)}, bf16[128,1024]{1,0:T(8,128)(2,1)S(1)}, u32[]{:S(2)}, u32[]{:S(2)}) collective-permute-start(bf16[128,1024]{1,0:T(8,128)(2,1)S(1)} %hand_on.4), channel_id=1, source_target_pairs={{0,2},{2,0},{4,6},{6,4},{8,10},{10,8},{12,14},{14,12},{16,18},{18,... | collective-permute-start | bytes 786440 | tf_op jit(solution)/shard_map/ppermute | solution.py:44
  57.4 1.6 %collective-permute-start.23 = (bf16[128,1024]{1,0:T(8,128)(2,1)S(1)}, bf16[128,1024]{1,0:T(8,128)(2,1)S(1)}, u32[]{:S(2)}, u32[]{:S(2)}) collective-permute-start(bf16[128,1024]{1,0:T(8,128)(2,1)S(1)} %hand_on.5), channel_id=1, source_target_pairs={{0,2},{2,0},{4,6},{6,4},{8,10},{10,8},{12,14},{14,12},{16,18},{18,... | collective-permute-start | bytes 786440 | tf_op jit(solution)/shard_map/ppermute | solution.py:44

commit v6 on v5

--- a/solution.py
+++ b/solution.py
@@ -666,64 +666,109 @@
     )
 
 
-def states_kernel(stages, scattered, pieces, *refs):
+def states_kernel(stages, scattered, pieces, offsets, ending, *refs):
     base_ref, factor_ref = refs[:2]
-    prompt_refs, refs = refs[2 : 2 + pieces], refs[2 + pieces :]
-    share_refs, (new_ref, slice_ref, verify_ref, turned_ref, held_ref, sems) = refs[:-6], refs[-6:]
+    count = len(offsets)
+    prompt_refs, refs = refs[2 : 2 + count], refs[2 + count :]
+    new_ref, *slice_refs, turned_ref, held_ref, sems = refs[-4 - count :] if not ending else refs[-6:]
     here = lax.axis_index("seq")
-    verify_ref[...] = sum(ref[...].astype(F32) for ref in share_refs).astype(BF16)
     core, line, last = stages
     lanes = base_ref.shape[0]
     part = lanes // pieces
     width = part // (last[0] if len(scattered) > 1 else 1)
-    chunk = lanes // sems.shape[0]
-    copies = []
-    for step in range(sems.shape[0]):
-        rows = slice(step * chunk, (step + 1) * chunk)
-        for lane in range(step * chunk, (step + 1) * chunk, width):
-            spot = lane // part
-            piece = (spot // line[0] ^ place_of(core)) * line[0] + (spot % line[0] ^ place_of(line))
-            position = jnp.int32(0)
-            if len(scattered) > 1:
-                apart = lane % part // width ^ place_of(last)
-                position = jnp.where(apart == 0, 0, last[0] - apart)
-            at = window(position * width, width)
-            found = prompt_refs[0][:, at]
+
+    def piece_at(spot):
+        return (spot // line[0] ^ place_of(core)) * line[0] + (spot % line[0] ^ place_of(line))
+
+    def spot_of(offset):
+        return (offset // line[0] ^ place_of(core)) * line[0] + (offset % line[0] ^ place_of(line))
+
+    copies, found = [], []
+    chunk = part // 2 if part >= 512 else part
+    per_slice = HEAD_DIM // (core[0] * line[0] * last[0])
+    for index, (offset, prompt_ref) in enumerate(zip(offsets, prompt_refs)):
+        start = spot_of(offset) * part
+        for at in range(0, part, chunk):
+            inner = index * part + at
+            for lane in range(at, at + chunk, width):
+                position = jnp.int32(0)
+                if len(scattered) > 1:
+                    apart = lane // width ^ place_of(last)
+                    position = jnp.where(apart == 0, 0, last[0] - apart)
+                block = prompt_ref[:, window(position * width, width)].astype(F32).T
+                turned_ref[index * part + lane : index * part + lane + width, :] = block
+            rows = window(start + at, chunk)
+            mine = slice(inner, inner + chunk)
+            new = factor_ref[rows, :] * turned_ref[mine, :] + base_ref[rows, :]
+            held_ref[mine, :] = new.astype(BF16)
+            copies.append(
+                pltpu.make_async_copy(
+                    held_ref.at[mine, :], new_ref.at[rows, :], sems.at[len(copies)]
+                )
+            )
+            copies[-1].start()
+        heads = part // HEAD_DIM
+        picked = [
+            turned_ref[pl.ds(index * part + here * per_slice + k, heads, stride=HEAD_DIM), :]
+            for k in range(per_slice)
+        ]
+        found.append(jnp.concatenate(picked, axis=1))
+    if ending:
+        others, shares = refs[: pieces - count], refs[pieces - count : -7]
+        slice_ref, verify_ref = slice_refs
+        verify_ref[...] = sum(ref[...].astype(F32) for ref in shares).astype(BF16)
+        every = dict(zip(offsets, found))
+        rest = [k for k in range(pieces) if k not in offsets]
+        every.update(zip(rest, (ref[...] for ref in others)))
+        rows = []
+        for spot in range(pieces):
+            chosen = every[0]
             for k in range(1, pieces):
-                found = jnp.where(piece == k, prompt_refs[k][:, at], found)
-            turned_ref[lane : lane + width, :] = found.astype(F32).T
-        new = factor_ref[rows, :] * turned_ref[rows, :] + base_ref[rows, :]
-        held_ref[rows, :] = new.astype(BF16)
-        copies.append(pltpu.make_async_copy(held_ref.at[rows, :], new_ref.at[rows, :], sems.at[step]))
-        copies[-1].start()
-    per_slice = slice_ref.shape[1] // STATE_SIZE
-    heads = slice_ref.shape[0]
-    for k in range(per_slice):
-        picked = turned_ref[pl.ds(here * per_slice + k, heads, stride=HEAD_DIM), :]
-        slice_ref[:, k * STATE_SIZE : (k + 1) * STATE_SIZE] = picked.astype(BF16)
+                chosen = jnp.where(piece_at(spot) == k, every[k], chosen)
+            rows.append(chosen)
+        slice_ref[...] = jnp.concatenate(rows, axis=0).astype(BF16)
+    else:
+        for ref, value in zip(slice_refs, found):
+            ref[...] = value
     for copy in copies:
         copy.wait()
 
 
-def states(stages, scattered, prepared, prompts, shares, seq_count):
+def states(stages, scattered, prepared, pieces, offsets, prompts, new, slices, shares, after=()):
     lanes = prepared[0].shape[0]
-    chunk = min(512, lanes // 2)
+    part = lanes // pieces
+    count = len(offsets)
+    cols = HEAD_DIM // (stages[2][0] * stages[2][1]) * STATE_SIZE
+    ending = bool(shares)
+    args = [*prepared, *prompts]
+    if ending:
+        args += [slices[k] for k in range(pieces) if k not in offsets] + shares
+    specs = [WHOLE] * len(args)
+    alias = None
+    if new is not None:
+        alias = {len(args): 0}
+        args.append(new)
+        specs.append(IN_HBM)
+    outs = [shape((lanes, STATE_SIZE), BF16)]
+    if ending:
+        outs += [shape((lanes // HEAD_DIM, cols), BF16), shape(shares[0].shape, BF16)]
+    else:
+        outs += [shape((part // HEAD_DIM, cols), F32)] * count
     return call(
-        functools.partial(states_kernel, stages, scattered, len(prompts)),
+        functools.partial(states_kernel, stages, scattered, pieces, offsets, ending),
         "states",
-        [
-            shape((lanes, STATE_SIZE), BF16),
-            shape((lanes // HEAD_DIM, HEAD_DIM // seq_count * STATE_SIZE), BF16),
-            shape(shares[0].shape, BF16),
+        outs,
+        args,
+        specs=specs,
+        out_specs=[IN_HBM] + [WHOLE] * (len(outs) - 1),
+        after=after,
+        alias=alias,
+        scratch=[
+            pltpu.VMEM((count * part, STATE_SIZE), F32),
+            pltpu.VMEM((count * part, STATE_SIZE), BF16),
+            pltpu.SemaphoreType.DMA((2 * count,)),
         ],
-        (*prepared, *prompts, *shares),
-        out_specs=[IN_HBM, WHOLE, WHOLE],
-        scratch=[
-            pltpu.VMEM((lanes, STATE_SIZE), F32),
-            pltpu.VMEM((lanes, STATE_SIZE), BF16),
-            pltpu.SemaphoreType.DMA((lanes // chunk,)),
-        ],
-        flops=2 * lanes * STATE_SIZE * 64,
+        moved=1,
     )
 
 
@@ -927,11 +972,17 @@
     shares = [shares[0]] + [swap(shares[k], "head", (head_count, 1), k) for k in range(1, head_count)]
 
     prompts = exchange([prompt] * line[0], line)
-    first = swap(hand_on(prompt, shares[:1]), "seq", core, 1)
-    late = [hand_on(piece, [token, *shares[1:]]) for piece in prompts[1:]]
-    prompts += [first] + [swap(piece, "seq", core, 1) for piece in late]
+    pieces = 2 * line[0]
+    crossed = swap(hand_on(prompt, shares[:1]), "seq", core, 1)
+    late = gather_in(prompts[1:], [token, *shares[1:]])
+    slices = {}
+    new_state, slices[0], slices[line[0]] = states(
+        stages, scattered, prepared, pieces, (0, line[0]), (prompt, crossed), None, None, (), late[:1]
+    )
+    offsets = (*range(1, line[0]), *range(line[0] + 1, pieces))
+    prompts = prompts[1:] + [swap(piece, "seq", core, 1) for piece in late]
     new_state, state_slice, verify_out = states(
-        stages, scattered, prepared, prompts, shares, seq_count
+        stages, scattered, prepared, pieces, offsets, prompts, new_state, slices, shares
     )
     return (
         prefill_out,

time: 61.6 us -> 61 us (level)
  waiting for transfers between devices: 12.5 us -> 11.5 us
    ppermute x24, waiting for transfers between devices: 12.5 us -> 11.5 us  [swap(): lax.ppermute(value, axis, [(k, k ^ offset * stride) for k in range(count)])]
    pallas_call x27 -> x28, Pallas kernels: 21.6 us -> 22.1 us  [call(): pl.pallas_call(ordered(kernel, first), name=name, grid=grid, out_shape=ou...]
  transfers between devices with their start and end apart: 24 -> 24, of which waited for: 9 -> 9; matrix products, arithmetic and copies ran while one was open for 0% -> 0% of each run, Pallas kernels for 26% -> 27%
where the time goes in v6:
time: 61 us; the launch traced here: 60.8 us
  starting transfers between devices  26.2 us (43%)
  Pallas kernels  22.1 us (36%)
  waiting for transfers between devices  11.5 us (19%)
  between operations  1.03 us (2%)
    ppermute x24, starting transfers between devices, swap(): lax.ppermute(value, axis, [(k, k ^ offset * stride) for k in range(count)])  26.2 us
    pallas_call x28, Pallas kernels, call(): pl.pallas_call(ordered(kernel, first), name=name, grid=grid, out_shape=ou...  22.1 us
    ppermute x24, waiting for transfers between devices, swap(): lax.ppermute(value, axis, [(k, k ^ offset * stride) for k in range(count)])  11.5 us
  transfers between devices with their start and end apart: 24, of which 9 were waited for; matrix products, arithmetic and copies ran while one was open for 0% of the time, Pallas kernels for 27%

profile of v6, /device:TPU:0, one launch (start us, length us, event | category | flops | bytes accessed | tf_op | source)
XLA Modules:
  0.0 60.8 jit_solution(9172436206681051757)
XLA Ops:
  0.6 3.0 %open_block.1 = (bf16[128,2048]{1,0:T(8,128)(2,1)S(1)}, f32[4,256,16]{2,1,0:T(8,128)S(1)}, f32[64,256]{1,0:T(8,128)S(1)}, f32[64,256]{1,0:T(8,128)S(1)}, bf16[25...) custom-call(f32[64,256]{1,0:T(8,128)} %bitcast.9, ...), custom_call_target="tpu_custom_call" | custom-call | flops 268435456 | bytes 8911232 | tf_op jit(solution)/shard_map/open_block/pallas_call | solution.py:95
  6.8 2.8 %collective-permute-start.5 = (bf16[160,1024]{1,0:T(8,128)(2,1)S(1)}, bf16[160,1024]{1,0:T(8,128)(2,1)S(1)}, u32[]{:S(2)}, u32[]{:S(2)}) collective-permute-start(bf16[160,1024]{1,0:T(8,128)(2,1)S(1)} %get-tuple-element.87.refs_0_), channel_id=1, source_target_pairs={{0,4},{2,6},{4,0},{6,2},{8,12},{10,14},{12,8},{14,10},{16,20},{18,... | collective-permute-start | bytes 983048 | tf_op jit(solution)/shard_map/ppermute | solution.py:44
  10.0 3.6 %collective-permute-start.2 = (bf16[8,4096]{1,0:T(8,128)(2,1)S(1)}, bf16[8,4096]{1,0:T(8,128)(2,1)S(1)}, u32[]{:S(2)}, u32[]{:S(2)}) collective-permute-start(bf16[8,4096]{1,0:T(8,128)(2,1)S(1)} %resident_hidden.1.refs_1_), channel_id=1, source_target_pairs={{0,24},{2,26},{4,28},{6,30},{8,16},{10,18},{12,20},{14,22},{16,8},... | collective-permute-start | bytes 196616 | tf_op jit(solution)/shard_map/ppermute | solution.py:44
  14.4 1.6 %intra.4.refs_0_.refs_4_ = f32[256,1024]{1,0:T(8,128)S(1)} custom-call(bf16[160,1024]{1,0:T(8,128)(2,1)S(1)} %get-tuple-element.87.refs_0_, f32[4,256,16]{2,1,0:T(8,128)S(1)} %get-tuple-element.88.refs_1_.refs_2_, f32[64,256]{1,0:T(8,128)S(1)} %get-tuple-element.74.refs_4_.refs_2_.refs_3_, f32[64,256]{1,0:T(8,128)S(1)} %get-tuple-element.89.refs_3_.refs_4_, ...), custom_call_target="tpu_custom_call" | custom-call | flops 134217728 | bytes 1572864 | tf_op jit(solution)/shard_map/intra/pallas_call | solution.py:95
  16.4 3.1 %collective-permute-done.3.refs_2_.refs_3_ = bf16[8,4096]{1,0:T(8,128)(2,1)S(1)} collective-permute-done((bf16[8,4096]{1,0:T(8,128)(2,1)S(1)}, bf16[8,4096]{1,0:T(8,128)(2,1)S(1)}, u32[]{:S(2)}, u32[]{:S(2)}) %collective-permute-start.3) | collective-permute-done | bytes 65568 | tf_op jit(solution)/shard_map/ppermute | solution.py:44
  19.7 2.6 %collective-permute-start.6 = (bf16[160,256]{1,0:T(8,128)(2,1)S(1)}, bf16[160,256]{1,0:T(8,128)(2,1)S(1)}, u32[]{:S(2)}, u32[]{:S(2)}) collective-permute-start(bf16[160,256]{1,0:T(8,128)(2,1)S(1)} %get-tuple-element.97.refs_0_), channel_id=1, source_target_pairs={{0,24},{2,26},{4,28},{6,30},{8,16},{10,18},{12,20},{14,22},{16,8},... | collective-permute-start | bytes 245768 | tf_op jit(solution)/shard_map/ppermute | solution.py:44
  22.3 1.8 %collective-permute-start.8 = (bf16[160,256]{1,0:T(8,128)(2,1)S(1)}, bf16[160,256]{1,0:T(8,128)(2,1)S(1)}, u32[]{:S(2)}, u32[]{:S(2)}) collective-permute-start(bf16[160,256]{1,0:T(8,128)(2,1)S(1)} %get-tuple-element.101), channel_id=1, source_target_pairs={{0,8},{2,10},{4,12},{6,14},{8,0},{10,2},{12,4},{14,6},{16,24},{18,... | collective-permute-start | bytes 245768 | tf_op jit(solution)/shard_map/ppermute | solution.py:44
  24.7 3.6 %intra.5 = (f32[256,1024]{1,0:T(8,128)S(1)}, bf16[4096,512]{1,0:T(8,128)(2,1)S(1)}) custom-call(bf16[160,256]{1,0:T(8,128)(2,1)S(1)} %get-tuple-element.97.refs_0_, f32[4,256,16]{2,1,0:T(8,128)S(1)} %get-tuple-element.88.refs_1_.refs_2_, f32[64,256]{1,0:T(8,128)S(1)} %get-tuple-element.74.refs_4_.refs_2_.refs_3_, ...), custom_call_target="tpu_custom_call" | custom-call | flops 134217728 | bytes 1572864 | tf_op jit(solution)/shard_map/intra/pallas_call | solution.py:95
  28.3 1.6 %collective-permute-done.7.refs_2_ = bf16[160,256]{1,0:T(8,128)(2,1)S(1)} collective-permute-done((bf16[160,256]{1,0:T(8,128)(2,1)S(1)}, bf16[160,256]{1,0:T(8,128)(2,1)S(1)}, u32[]{:S(2)}, u32[]{:S(2)}) %collective-permute-start.7) | collective-permute-done | bytes 81952 | tf_op jit(solution)/shard_map/ppermute | solution.py:44
  30.3 1.8 %collective-permute-start.11 = (bf16[136,256]{1,0:T(8,128)(2,1)S(1)}, bf16[136,256]{1,0:T(8,128)(2,1)S(1)}, u32[]{:S(2)}, u32[]{:S(2)}) collective-permute-start(bf16[136,256]{1,0:T(8,128)(2,1)S(1)} %get-tuple-element.105.refs_0_), channel_id=1, source_target_pairs={{0,24},{2,26},{4,28},{6,30},{8,16},{10,18},{12,20},{14,22},{16,8},... | collective-permute-start | bytes 208904 | tf_op jit(solution)/shard_map/ppermute | solution.py:44
  32.1 2.6 %collective-permute-start.13 = (bf16[136,256]{1,0:T(8,128)(2,1)S(1)}, bf16[136,256]{1,0:T(8,128)(2,1)S(1)}, u32[]{:S(2)}, u32[]{:S(2)}) collective-permute-start(bf16[136,256]{1,0:T(8,128)(2,1)S(1)} %get-tuple-element.108), channel_id=1, source_target_pairs={{0,8},{2,10},{4,12},{6,14},{8,0},{10,2},{12,4},{14,6},{16,24},{18,... | collective-permute-start | bytes 208904 | tf_op jit(solution)/shard_map/ppermute | solution.py:44
  34.8 1.6 %intra.6.refs_0_.refs_6_ = f32[256,1024]{1,0:T(8,128)S(1)} custom-call(bf16[136,256]{1,0:T(8,128)(2,1)S(1)} %get-tuple-element.105.refs_0_, bf16[64,4096]{1,0:T(8,128)(2,1)S(1)} %join.4.refs_1_, f32[4,256,16]{2,1,0:T(8,128)S(1)} %get-tuple-element.88.refs_1_.refs_2_, f32[64,256]{1,0:T(8,128)S(1)} %get-tuple-element.74.refs_4_.refs_2_.refs_3_, ...), custom_call_target="tpu_custom_call" | custom-call | flops 134217728 | bytes 1572864 | tf_op jit(solution)/shard_map/intra/pallas_call | solution.py:95
  36.9 1.7 %collective-permute-done.12.refs_2_ = bf16[136,256]{1,0:T(8,128)(2,1)S(1)} collective-permute-done((bf16[136,256]{1,0:T(8,128)(2,1)S(1)}, bf16[136,256]{1,0:T(8,128)(2,1)S(1)}, u32[]{:S(2)}, u32[]{:S(2)}) %collective-permute-start.12) | collective-permute-done | bytes 69664 | tf_op jit(solution)/shard_map/ppermute | solution.py:44
  38.9 1.0 %collective-permute-start.17 = (bf16[136,1024]{1,0:T(8,128)(2,1)S(1)}, bf16[136,1024]{1,0:T(8,128)(2,1)S(1)}, u32[]{:S(2)}, u32[]{:S(2)}) collective-permute-start(bf16[136,1024]{1,0:T(8,128)(2,1)S(1)} %get-tuple-element.112.refs_0_), channel_id=1, source_target_pairs={{0,4},{2,6},{4,0},{6,2},{8,12},{10,14},{12,8},{14,10},{16,20},{18,... | collective-permute-start | bytes 835592 | tf_op jit(solution)/shard_map/ppermute | solution.py:44
  39.9 2.2 %collective-permute-start.14 = (bf16[128,256]{1,0:T(8,128)(2,1)S(1)}, bf16[128,256]{1,0:T(8,128)(2,1)S(1)}, u32[]{:S(2)}, u32[]{:S(2)}) collective-permute-start(bf16[128,256]{1,0:T(8,128)(2,1)S(1)} %hand_on.2.refs_0_), channel_id=1, source_target_pairs={{0,24},{2,26},{4,28},{6,30},{8,16},{10,18},{12,20},{14,22},{16,8},... | collective-permute-start | bytes 196616 | tf_op jit(solution)/shard_map/ppermute | solution.py:44
  42.0 2.2 %collective-permute-start.16 = (bf16[128,256]{1,0:T(8,128)(2,1)S(1)}, bf16[128,256]{1,0:T(8,128)(2,1)S(1)}, u32[]{:S(2)}, u32[]{:S(2)}) collective-permute-start(bf16[128,256]{1,0:T(8,128)(2,1)S(1)} %hand_on.2.refs_0_), channel_id=1, source_target_pairs={{0,8},{2,10},{4,12},{6,14},{8,0},{10,2},{12,4},{14,6},{16,24},{18,... | collective-permute-start | bytes 196616 | tf_op jit(solution)/shard_map/ppermute | solution.py:44
  44.3 1.6 %intra.7.refs_0_.refs_7_ = f32[256,1024]{1,0:T(8,128)S(1)} custom-call(bf16[136,1024]{1,0:T(8,128)(2,1)S(1)} %get-tuple-element.112.refs_0_, f32[4,256,16]{2,1,0:T(8,128)S(1)} %get-tuple-element.88.refs_1_.refs_2_, f32[64,256]{1,0:T(8,128)S(1)} %get-tuple-element.74.refs_4_.refs_2_.refs_3_, f32[64,256]{1,0:T(8,128)S(1)} %get-tuple-element.89.refs_3_.refs_4_, ...), custom_call_target="tpu_custom_call" | custom-call | flops 134217728 | bytes 1572864 | tf_op jit(solution)/shard_map/intra/pallas_call | solution.py:95
  46.7 1.5 %collective-permute-done.15.refs_2_ = bf16[128,256]{1,0:T(8,128)(2,1)S(1)} collective-permute-done((bf16[128,256]{1,0:T(8,128)(2,1)S(1)}, bf16[128,256]{1,0:T(8,128)(2,1)S(1)}, u32[]{:S(2)}, u32[]{:S(2)}) %collective-permute-start.15) | collective-permute-done | bytes 65568 | tf_op jit(solution)/shard_map/ppermute | solution.py:44
  48.7 1.3 %collective-permute-start.20 = (bf16[128,1024]{1,0:T(8,128)(2,1)S(1)}, bf16[128,1024]{1,0:T(8,128)(2,1)S(1)}, u32[]{:S(2)}, u32[]{:S(2)}) collective-permute-start(bf16[128,1024]{1,0:T(8,128)(2,1)S(1)} %join.5.refs_3_.refs_1_), channel_id=1, source_target_pairs={{0,4},{2,6},{4,0},{6,2},{8,12},{10,14},{12,8},{14,10},{16,20},{18,... | collective-permute-start | bytes 786440 | tf_op jit(solution)/shard_map/ppermute | solution.py:44
  51.1 1.7 %collective-permute-start.21 = (bf16[64,512]{1,0:T(8,128)(2,1)S(1)}, bf16[64,512]{1,0:T(8,128)(2,1)S(1)}, u32[]{:S(2)}, u32[]{:S(2)}) collective-permute-start(bf16[64,512]{1,0:T(8,128)(2,1)S(1)} %get-tuple-element.125), channel_id=1, source_target_pairs={{0,1},{1,0},{2,3},{3,2},{4,5},{5,4},{6,7},{7,6},{8,9},{9,8},{10,11... | collective-permute-start | bytes 196616 | tf_op jit(solution)/shard_map/ppermute | solution.py:44
  53.4 2.0 %finish.1 = (bf16[256,4096]{1,0:T(8,128)(2,1)}, f32[8,128]{1,0:T(8,128)S(1)}) custom-call(bf16[256,128]{1,0:T(8,128)(2,1)S(1)} %get-tuple-element.68.refs_0_, bf16[256,512]{1,0:T(8,128)(2,1)S(1)} %get-tuple-element.69.refs_7_.refs_8_.refs_1_, bf16[128,2048]{1,0:T(8,128)(2,1)S(1)} %down_core.3.refs_2_, bf16[128,2048]{1,0:T(8,128)(2,1)S(1)} %collective-permute-done.19.refs_3_, ...), custom_call_target="tpu_custom_call" | custom-call | bytes 1 | tf_op jit(solution)/shard_map/finish/pallas_call | solution.py:95
  55.4 2.0 %collective-permute-done.20.refs_2_ = bf16[128,1024]{1,0:T(8,128)(2,1)S(1)} collective-permute-done((bf16[128,1024]{1,0:T(8,128)(2,1)S(1)}, bf16[128,1024]{1,0:T(8,128)(2,1)S(1)}, u32[]{:S(2)}, u32[]{:S(2)}) %collective-permute-start.20) | collective-permute-done | bytes 262176 | tf_op jit(solution)/shard_map/ppermute | solution.py:44
  57.5 1.0 %states.2 = (bf16[4096,128]{1,0:T(8,128)(2,1)}, f32[16,512]{1,0:T(8,128)S(1)}, f32[16,512]{1,0:T(8,128)S(1)}) custom-call(bf16[128,1024]{1,0:T(8,128)(2,1)S(1)} %gather_in.7.refs_0_, f32[4096,128]{1,0:T(8,128)S(1)} %get-tuple-element.115.refs_0_.refs_1_, f32[4096,128]{1,0:T(8,128)S(1)} %get-tuple-element.116.refs_1_.refs_2_, ...), custom_call_target="tpu_custom_call" | custom-call | bytes 1 | tf_op jit(solution)/shard_map/states/pallas_call | solution.py:95
  59.0 1.6 %states.3 = (bf16[4096,128]{1,0:T(8,128)(2,1)}, bf16[64,512]{1,0:T(8,128)(2,1)}, bf16[64,512]{1,0:T(8,128)(2,1)}) custom-call(f32[4096,128]{1,0:T(8,128)S(1)} %get-tuple-element.115.refs_0_.refs_1_, f32[4096,128]{1,0:T(8,128)S(1)} %get-tuple-element.116.refs_1_.refs_2_, ...), custom_call_target="tpu_custom_call", output_to_operand_aliasing={{0}: (8, {})} | custom-call | bytes 1 | tf_op jit(solution)/shard_map/states/pallas_call | solution.py:95
  (52 shorter events, 10.2 us)
Async XLA Ops:
  3.6 2.9 %collective-permute-start = (bf16[128,2048]{1,0:T(8,128)(2,1)S(1)}, bf16[128,2048]{1,0:T(8,128)(2,1)S(1)}, u32[]{:S(2)}, u32[]{:S(2)}) collective-permute-start(bf16[128,2048]{1,0:T(8,128)(2,1)S(1)} %get-tuple-element.71.refs_0_), channel_id=1, source_target_pairs={{0,2},{2,0},{4,6},{6,4},{8,10},{10,8},{12,14},{14,12},{16,18},{18,... | collective-permute-start | bytes 1572872 | tf_op jit(solution)/shard_map/ppermute | solution.py:44
  5.1 1.4 %collective-permute-start.1 = (bf16[32,2048]{1,0:T(8,128)(2,1)S(1)}, bf16[32,2048]{1,0:T(8,128)(2,1)S(1)}, u32[]{:S(2)}, u32[]{:S(2)}) collective-permute-start(bf16[32,2048]{1,0:T(8,128)(2,1)S(1)} %get-tuple-element.82.refs_0_), channel_id=1, source_target_pairs={{0,2},{2,0},{4,6},{6,4},{8,10},{10,8},{12,14},{14,12},{16,18},{18,... | collective-permute-start | bytes 393224 | tf_op jit(solution)/shard_map/ppermute | solution.py:44
  6.8 12.7 %collective-permute-start.5 = (bf16[160,1024]{1,0:T(8,128)(2,1)S(1)}, bf16[160,1024]{1,0:T(8,128)(2,1)S(1)}, u32[]{:S(2)}, u32[]{:S(2)}) collective-permute-start(bf16[160,1024]{1,0:T(8,128)(2,1)S(1)} %get-tuple-element.87.refs_0_), channel_id=1, source_target_pairs={{0,4},{2,6},{4,0},{6,2},{8,12},{10,14},{12,8},{14,10},{16,20},{18,... | collective-permute-start | bytes 983048 | tf_op jit(solution)/shard_map/ppermute | solution.py:44
  10.0 6.4 %collective-permute-start.2 = (bf16[8,4096]{1,0:T(8,128)(2,1)S(1)}, bf16[8,4096]{1,0:T(8,128)(2,1)S(1)}, u32[]{:S(2)}, u32[]{:S(2)}) collective-permute-start(bf16[8,4096]{1,0:T(8,128)(2,1)S(1)} %resident_hidden.1.refs_1_), channel_id=1, source_target_pairs={{0,24},{2,26},{4,28},{6,30},{8,16},{10,18},{12,20},{14,22},{16,8},... | collective-permute-start | bytes 196616 | tf_op jit(solution)/shard_map/ppermute | solution.py:44
  13.7 5.8 %collective-permute-start.3 = (bf16[8,4096]{1,0:T(8,128)(2,1)S(1)}, bf16[8,4096]{1,0:T(8,128)(2,1)S(1)}, u32[]{:S(2)}, u32[]{:S(2)}) collective-permute-start(bf16[8,4096]{1,0:T(8,128)(2,1)S(1)} %resident_hidden.1.refs_1_), channel_id=1, source_target_pairs={{0,16},{2,18},{4,20},{6,22},{8,24},{10,26},{12,28},{14,30},{16,0},... | collective-permute-start | bytes 196616 | tf_op jit(solution)/shard_map/ppermute | solution.py:44
  13.7 5.8 %collective-permute-start.4 = (bf16[8,4096]{1,0:T(8,128)(2,1)S(1)}, bf16[8,4096]{1,0:T(8,128)(2,1)S(1)}, u32[]{:S(2)}, u32[]{:S(2)}) collective-permute-start(bf16[8,4096]{1,0:T(8,128)(2,1)S(1)} %resident_hidden.1.refs_1_), channel_id=1, source_target_pairs={{0,8},{2,10},{4,12},{6,14},{8,0},{10,2},{12,4},{14,6},{16,24},{18,... | collective-permute-start | bytes 196616 | tf_op jit(solution)/shard_map/ppermute | solution.py:44
  19.7 8.7 %collective-permute-start.6 = (bf16[160,256]{1,0:T(8,128)(2,1)S(1)}, bf16[160,256]{1,0:T(8,128)(2,1)S(1)}, u32[]{:S(2)}, u32[]{:S(2)}) collective-permute-start(bf16[160,256]{1,0:T(8,128)(2,1)S(1)} %get-tuple-element.97.refs_0_), channel_id=1, source_target_pairs={{0,24},{2,26},{4,28},{6,30},{8,16},{10,18},{12,20},{14,22},{16,8},... | collective-permute-start | bytes 245768 | tf_op jit(solution)/shard_map/ppermute | solution.py:44
  22.3 7.7 %collective-permute-start.7 = (bf16[160,256]{1,0:T(8,128)(2,1)S(1)}, bf16[160,256]{1,0:T(8,128)(2,1)S(1)}, u32[]{:S(2)}, u32[]{:S(2)}) collective-permute-start(bf16[160,256]{1,0:T(8,128)(2,1)S(1)} %get-tuple-element.100), channel_id=1, source_target_pairs={{0,16},{2,18},{4,20},{6,22},{8,24},{10,26},{12,28},{14,30},{16,0},... | collective-permute-start | bytes 245768 | tf_op jit(solution)/shard_map/ppermute | solution.py:44
  22.3 7.7 %collective-permute-start.8 = (bf16[160,256]{1,0:T(8,128)(2,1)S(1)}, bf16[160,256]{1,0:T(8,128)(2,1)S(1)}, u32[]{:S(2)}, u32[]{:S(2)}) collective-permute-start(bf16[160,256]{1,0:T(8,128)(2,1)S(1)} %get-tuple-element.101), channel_id=1, source_target_pairs={{0,8},{2,10},{4,12},{6,14},{8,0},{10,2},{12,4},{14,6},{16,24},{18,... | collective-permute-start | bytes 245768 | tf_op jit(solution)/shard_map/ppermute | solution.py:44
  24.1 10.6 %collective-permute-start.9 = (bf16[32,4096]{1,0:T(8,128)(2,1)S(1)}, bf16[32,4096]{1,0:T(8,128)(2,1)S(1)}, u32[]{:S(2)}, u32[]{:S(2)}) collective-permute-start(bf16[32,4096]{1,0:T(8,128)(2,1)S(1)} %join.3.refs_1_), channel_id=1, source_target_pairs={{0,4},{2,6},{4,0},{6,2},{8,12},{10,14},{12,8},{14,10},{16,20},{18,... | collective-permute-start | bytes 786440 | tf_op jit(solution)/shard_map/ppermute | solution.py:44
  30.3 6.6 %collective-permute-start.11 = (bf16[136,256]{1,0:T(8,128)(2,1)S(1)}, bf16[136,256]{1,0:T(8,128)(2,1)S(1)}, u32[]{:S(2)}, u32[]{:S(2)}) collective-permute-start(bf16[136,256]{1,0:T(8,128)(2,1)S(1)} %get-tuple-element.105.refs_0_), channel_id=1, source_target_pairs={{0,24},{2,26},{4,28},{6,30},{8,16},{10,18},{12,20},{14,22},{16,8},... | collective-permute-start | bytes 208904 | tf_op jit(solution)/shard_map/ppermute | solution.py:44
  32.1 6.4 %collective-permute-start.12 = (bf16[136,256]{1,0:T(8,128)(2,1)S(1)}, bf16[136,256]{1,0:T(8,128)(2,1)S(1)}, u32[]{:S(2)}, u32[]{:S(2)}) collective-permute-start(bf16[136,256]{1,0:T(8,128)(2,1)S(1)} %get-tuple-element.107), channel_id=1, source_target_pairs={{0,16},{2,18},{4,20},{6,22},{8,24},{10,26},{12,28},{14,30},{16,0},... | collective-permute-start | bytes 208904 | tf_op jit(solution)/shard_map/ppermute | solution.py:44
  32.1 6.4 %collective-permute-start.13 = (bf16[136,256]{1,0:T(8,128)(2,1)S(1)}, bf16[136,256]{1,0:T(8,128)(2,1)S(1)}, u32[]{:S(2)}, u32[]{:S(2)}) collective-permute-start(bf16[136,256]{1,0:T(8,128)(2,1)S(1)} %get-tuple-element.108), channel_id=1, source_target_pairs={{0,8},{2,10},{4,12},{6,14},{8,0},{10,2},{12,4},{14,6},{16,24},{18,... | collective-permute-start | bytes 208904 | tf_op jit(solution)/shard_map/ppermute | solution.py:44
  34.8 13.4 %collective-permute-start.10 = (bf16[64,4096]{1,0:T(8,128)(2,1)S(1)}, bf16[64,4096]{1,0:T(8,128)(2,1)S(1)}, u32[]{:S(2)}, u32[]{:S(2)}) collective-permute-start(bf16[64,4096]{1,0:T(8,128)(2,1)S(1)} %join.4.refs_1_), channel_id=1, source_target_pairs={{0,2},{2,0},{4,6},{6,4},{8,10},{10,8},{12,14},{14,12},{16,18},{18,... | collective-permute-start | bytes 1572872 | tf_op jit(solution)/shard_map/ppermute | solution.py:44
  38.9 9.3 %collective-permute-start.17 = (bf16[136,1024]{1,0:T(8,128)(2,1)S(1)}, bf16[136,1024]{1,0:T(8,128)(2,1)S(1)}, u32[]{:S(2)}, u32[]{:S(2)}) collective-permute-start(bf16[136,1024]{1,0:T(8,128)(2,1)S(1)} %get-tuple-element.112.refs_0_), channel_id=1, source_target_pairs={{0,4},{2,6},{4,0},{6,2},{8,12},{10,14},{12,8},{14,10},{16,20},{18,... | collective-permute-start | bytes 835592 | tf_op jit(solution)/shard_map/ppermute | solution.py:44
  39.9 6.8 %collective-permute-start.14 = (bf16[128,256]{1,0:T(8,128)(2,1)S(1)}, bf16[128,256]{1,0:T(8,128)(2,1)S(1)}, u32[]{:S(2)}, u32[]{:S(2)}) collective-permute-start(bf16[128,256]{1,0:T(8,128)(2,1)S(1)} %hand_on.2.refs_0_), channel_id=1, source_target_pairs={{0,24},{2,26},{4,28},{6,30},{8,16},{10,18},{12,20},{14,22},{16,8},... | collective-permute-start | bytes 196616 | tf_op jit(solution)/shard_map/ppermute | solution.py:44
  42.0 6.1 %collective-permute-start.15 = (bf16[128,256]{1,0:T(8,128)(2,1)S(1)}, bf16[128,256]{1,0:T(8,128)(2,1)S(1)}, u32[]{:S(2)}, u32[]{:S(2)}) collective-permute-start(bf16[128,256]{1,0:T(8,128)(2,1)S(1)} %hand_on.2.refs_0_), channel_id=1, source_target_pairs={{0,16},{2,18},{4,20},{6,22},{8,24},{10,26},{12,28},{14,30},{16,0},... | collective-permute-start | bytes 196616 | tf_op jit(solution)/shard_map/ppermute | solution.py:44
  42.0 6.1 %collective-permute-start.16 = (bf16[128,256]{1,0:T(8,128)(2,1)S(1)}, bf16[128,256]{1,0:T(8,128)(2,1)S(1)}, u32[]{:S(2)}, u32[]{:S(2)}) collective-permute-start(bf16[128,256]{1,0:T(8,128)(2,1)S(1)} %hand_on.2.refs_0_), channel_id=1, source_target_pairs={{0,8},{2,10},{4,12},{6,14},{8,0},{10,2},{12,4},{14,6},{16,24},{18,... | collective-permute-start | bytes 196616 | tf_op jit(solution)/shard_map/ppermute | solution.py:44
  48.6 1.6 %collective-permute-start.18 = (bf16[8,2048]{1,0:T(8,128)(2,1)S(1)}, bf16[8,2048]{1,0:T(8,128)(2,1)S(1)}, u32[]{:S(2)}, u32[]{:S(2)}) collective-permute-start(bf16[8,2048]{1,0:T(8,128)(2,1)S(1)} %get-tuple-element.119.refs_3_), channel_id=1, source_target_pairs={{0,2},{2,0},{4,6},{6,4},{8,10},{10,8},{12,14},{14,12},{16,18},{18,... | collective-permute-start | bytes 98312 | tf_op jit(solution)/shard_map/ppermute | solution.py:44
  48.7 8.7 %collective-permute-start.20 = (bf16[128,1024]{1,0:T(8,128)(2,1)S(1)}, bf16[128,1024]{1,0:T(8,128)(2,1)S(1)}, u32[]{:S(2)}, u32[]{:S(2)}) collective-permute-start(bf16[128,1024]{1,0:T(8,128)(2,1)S(1)} %join.5.refs_3_.refs_1_), channel_id=1, source_target_pairs={{0,4},{2,6},{4,0},{6,2},{8,12},{10,14},{12,8},{14,10},{16,20},{18,... | collective-permute-start | bytes 786440 | tf_op jit(solution)/shard_map/ppermute | solution.py:44
  50.0 3.4 %collective-permute-start.19 = (bf16[128,2048]{1,0:T(8,128)(2,1)S(1)}, bf16[128,2048]{1,0:T(8,128)(2,1)S(1)}, u32[]{:S(2)}, u32[]{:S(2)}) collective-permute-start(bf16[128,2048]{1,0:T(8,128)(2,1)S(1)} %get-tuple-element.122), channel_id=1, source_target_pairs={{0,2},{2,0},{4,6},{6,4},{8,10},{10,8},{12,14},{14,12},{16,18},{18,... | collective-permute-start | bytes 1572872 | tf_op jit(solution)/shard_map/ppermute | solution.py:44
  51.1 6.3 %collective-permute-start.21 = (bf16[64,512]{1,0:T(8,128)(2,1)S(1)}, bf16[64,512]{1,0:T(8,128)(2,1)S(1)}, u32[]{:S(2)}, u32[]{:S(2)}) collective-permute-start(bf16[64,512]{1,0:T(8,128)(2,1)S(1)} %get-tuple-element.125), channel_id=1, source_target_pairs={{0,1},{1,0},{2,3},{3,2},{4,5},{5,4},{6,7},{7,6},{8,9},{9,8},{10,11... | collective-permute-start | bytes 196616 | tf_op jit(solution)/shard_map/ppermute | solution.py:44
  52.9 4.7 %collective-permute-start.23 = (bf16[128,1024]{1,0:T(8,128)(2,1)S(1)}, bf16[128,1024]{1,0:T(8,128)(2,1)S(1)}, u32[]{:S(2)}, u32[]{:S(2)}) collective-permute-start(bf16[128,1024]{1,0:T(8,128)(2,1)S(1)} %hand_on.3), channel_id=1, source_target_pairs={{0,2},{2,0},{4,6},{6,4},{8,10},{10,8},{12,14},{14,12},{16,18},{18,... | collective-permute-start | bytes 786440 | tf_op jit(solution)/shard_map/ppermute | solution.py:44
  57.4 1.6 %collective-permute-start.22 = (bf16[128,1024]{1,0:T(8,128)(2,1)S(1)}, bf16[128,1024]{1,0:T(8,128)(2,1)S(1)}, u32[]{:S(2)}, u32[]{:S(2)}) collective-permute-start(bf16[128,1024]{1,0:T(8,128)(2,1)S(1)} %gather_in.7.refs_0_), channel_id=1, source_target_pairs={{0,2},{2,0},{4,6},{6,4},{8,10},{10,8},{12,14},{14,12},{16,18},{18,... | collective-permute-start | bytes 786440 | tf_op jit(solution)/shard_map/ppermute | solution.py:44

commit v7 on v6

--- a/solution.py
+++ b/solution.py
@@ -559,21 +559,21 @@
 
 
 def join_kernel(axis, *refs):
-    out_ref = refs[-1]
-    for k, ref in enumerate(refs[:-1]):
-        size = ref.shape[axis]
-        at = slice(k * size, (k + 1) * size)
+    out_ref, start = refs[-1], 0
+    for ref in refs[:-1]:
+        at = slice(start, start + ref.shape[axis])
+        start = at.stop
         if axis == 0:
             out_ref[at, :] = ref[...]
         else:
             out_ref[:, at] = ref[...]
 
 
-def join(parts, axis, after=()):
+def join(parts, axis, after=(), flops=0):
     dims = list(parts[0].shape)
-    dims[axis] *= len(parts)
+    dims[axis] = sum(part.shape[axis] for part in parts)
     return call(
-        functools.partial(join_kernel, axis), "join", [shape(tuple(dims), parts[0].dtype)], parts, after=after, moved=1
+        functools.partial(join_kernel, axis), "join", [shape(tuple(dims), parts[0].dtype)], parts, after=after, moved=1, flops=flops
     )[0]
 
 
@@ -926,6 +926,7 @@
     pieces = exchange(outs, last) if split_last else outs
     hidden = join(hiddens, 0, [outs[-1]])
     filled = fill([outs[-1], hidden])
+    ahead = exchange([prompt] * line[0], line)
     if split_last:
         pieces = pieces[:1] + list(gather_in(pieces[:0:-1], filled))[::-1]
     outs = call(
@@ -933,7 +934,7 @@
         "down_line",
         [shape((DOWN_ROWS, line_width), BF16)] * line[0],
         [*turned(pieces), *line_parts],
-        after=filled,
+        after=filled + ahead[1:],
         flops=line_width * UP_ROWS * 8,
     )
     pieces = exchange(outs, line)
@@ -945,8 +946,8 @@
     if split_last:
         prompt = hand_on(prompt, [outs[-1]])
         parts = exchange([prompt] * last[0], last)
-        prompt = join(turned(parts), 1)
-        filled.append(prompt)
+        others = join(turned(parts)[1:], 1)
+        filled.append(others)
 
     def down_core(target, after):
         return call(
@@ -971,16 +972,21 @@
     prefill_out, token = finish(core, reach, reads, entering, received, bases)
     shares = [shares[0]] + [swap(shares[k], "head", (head_count, 1), k) for k in range(1, head_count)]
 
-    prompts = exchange([prompt] * line[0], line)
     pieces = 2 * line[0]
-    crossed = swap(hand_on(prompt, shares[:1]), "seq", core, 1)
-    late = gather_in(prompts[1:], [token, *shares[1:]])
+    late = ahead[1:]
+    if split_last:
+        behind = exchange([others] * line[0], line)
+        prompt = join([prompt, others], 1, shares[:1])
+        late = [
+            join(pair, 1, [token, *shares[1:]], flops=10**10) for pair in zip(late, behind[1:])
+        ]
+    crossed = swap(prompt, "seq", core, 1)
     slices = {}
     new_state, slices[0], slices[line[0]] = states(
         stages, scattered, prepared, pieces, (0, line[0]), (prompt, crossed), None, None, (), late[:1]
     )
     offsets = (*range(1, line[0]), *range(line[0] + 1, pieces))
-    prompts = prompts[1:] + [swap(piece, "seq", core, 1) for piece in late]
+    prompts = late + [swap(piece, "seq", core, 1) for piece in late]
     new_state, state_slice, verify_out = states(
         stages, scattered, prepared, pieces, offsets, prompts, new_state, slices, shares
     )

time: 61 us -> 59.6 us (0.977)
  waiting for transfers between devices: 11.5 us -> 9.96 us
    ppermute x24 -> x25, waiting for transfers between devices: 11.5 us -> 9.96 us  [swap(): lax.ppermute(value, axis, [(k, k ^ offset * stride) for k in range(count)])]
    ppermute x24 -> x25, starting transfers between devices: 26.2 us -> 26.2 us  [swap(): lax.ppermute(value, axis, [(k, k ^ offset * stride) for k in range(count)])]
  transfers between devices with their start and end apart: 24 -> 25, of which waited for: 9 -> 9; matrix products, arithmetic and copies ran while one was open for 0% -> 0% of each run, Pallas kernels for 27% -> 28%
where the time goes in v7:
time: 59.6 us; the launch traced here: 59.4 us
  starting transfers between devices  26.2 us (44%)
  Pallas kernels  22.3 us (37%)
  waiting for transfers between devices  9.96 us (17%)
  between operations  1.04 us (2%)
    ppermute x25, starting transfers between devices, swap(): lax.ppermute(value, axis, [(k, k ^ offset * stride) for k in range(count)])  26.2 us
    pallas_call x28, Pallas kernels, call(): pl.pallas_call(ordered(kernel, first), name=name, grid=grid, out_shape=ou...  22.3 us
    ppermute x25, waiting for transfers between devices, swap(): lax.ppermute(value, axis, [(k, k ^ offset * stride) for k in range(count)])  9.96 us
  transfers between devices with their start and end apart: 25, of which 9 were waited for; matrix products, arithmetic and copies ran while one was open for 0% of the time, Pallas kernels for 28%

profile of v7, /device:TPU:0, one launch (start us, length us, event | category | flops | bytes accessed | tf_op | source)
XLA Modules:
  0.0 59.4 jit_solution(15157373925401382907)
XLA Ops:
  0.6 3.0 %open_block.1 = (bf16[128,2048]{1,0:T(8,128)(2,1)S(1)}, f32[4,256,16]{2,1,0:T(8,128)S(1)}, f32[64,256]{1,0:T(8,128)S(1)}, f32[64,256]{1,0:T(8,128)S(1)}, bf16[25...) custom-call(f32[64,256]{1,0:T(8,128)} %bitcast.9, ...), custom_call_target="tpu_custom_call" | custom-call | flops 268435456 | bytes 8911232 | tf_op jit(solution)/shard_map/open_block/pallas_call | solution.py:95
  4.1 1.0 %draft_rows.1 = (bf16[32,2048]{1,0:T(8,128)(2,1)S(1)}, bf16[32,2048]{1,0:T(8,128)(2,1)S(1)}, f32[1,4096]{1,0:T(1,128)S(1)}, f32[8,4096]{1,0:T(8,128)S(1)}, f32[8...) custom-call(bf16[128,2048]{1,0:T(8,128)(2,1)S(1)} %get-tuple-element.7, ...), custom_call_target="tpu_custom_call" | custom-call | flops 3276800 | bytes 1205248 | tf_op jit(solution)/shard_map/draft_rows/pallas_call | solution.py:95
  6.8 2.8 %collective-permute-start.5 = (bf16[160,1024]{1,0:T(8,128)(2,1)S(1)}, bf16[160,1024]{1,0:T(8,128)(2,1)S(1)}, u32[]{:S(2)}, u32[]{:S(2)}) collective-permute-start(bf16[160,1024]{1,0:T(8,128)(2,1)S(1)} %get-tuple-element.87.refs_0_), channel_id=1, source_target_pairs={{0,4},{2,6},{4,0},{6,2},{8,12},{10,14},{12,8},{14,10},{16,20},{18,... | collective-permute-start | bytes 983048 | tf_op jit(solution)/shard_map/ppermute | solution.py:44
  10.0 3.6 %collective-permute-start.2 = (bf16[8,4096]{1,0:T(8,128)(2,1)S(1)}, bf16[8,4096]{1,0:T(8,128)(2,1)S(1)}, u32[]{:S(2)}, u32[]{:S(2)}) collective-permute-start(bf16[8,4096]{1,0:T(8,128)(2,1)S(1)} %resident_hidden.1.refs_1_), channel_id=1, source_target_pairs={{0,24},{2,26},{4,28},{6,30},{8,16},{10,18},{12,20},{14,22},{16,8},... | collective-permute-start | bytes 196616 | tf_op jit(solution)/shard_map/ppermute | solution.py:44
  14.4 1.6 %intra.4.refs_0_.refs_4_ = f32[256,1024]{1,0:T(8,128)S(1)} custom-call(bf16[160,1024]{1,0:T(8,128)(2,1)S(1)} %get-tuple-element.87.refs_0_, f32[4,256,16]{2,1,0:T(8,128)S(1)} %get-tuple-element.88.refs_1_.refs_2_, f32[64,256]{1,0:T(8,128)S(1)} %get-tuple-element.74.refs_4_.refs_2_.refs_3_, f32[64,256]{1,0:T(8,128)S(1)} %get-tuple-element.89.refs_3_.refs_4_, ...), custom_call_target="tpu_custom_call" | custom-call | flops 134217728 | bytes 1572864 | tf_op jit(solution)/shard_map/intra/pallas_call | solution.py:95
  16.4 3.1 %collective-permute-done.3.refs_2_.refs_3_ = bf16[8,4096]{1,0:T(8,128)(2,1)S(1)} collective-permute-done((bf16[8,4096]{1,0:T(8,128)(2,1)S(1)}, bf16[8,4096]{1,0:T(8,128)(2,1)S(1)}, u32[]{:S(2)}, u32[]{:S(2)}) %collective-permute-start.3) | collective-permute-done | bytes 65568 | tf_op jit(solution)/shard_map/ppermute | solution.py:44
  19.7 2.6 %collective-permute-start.6 = (bf16[160,256]{1,0:T(8,128)(2,1)S(1)}, bf16[160,256]{1,0:T(8,128)(2,1)S(1)}, u32[]{:S(2)}, u32[]{:S(2)}) collective-permute-start(bf16[160,256]{1,0:T(8,128)(2,1)S(1)} %get-tuple-element.97.refs_0_), channel_id=1, source_target_pairs={{0,24},{2,26},{4,28},{6,30},{8,16},{10,18},{12,20},{14,22},{16,8},... | collective-permute-start | bytes 245768 | tf_op jit(solution)/shard_map/ppermute | solution.py:44
  22.3 1.8 %collective-permute-start.8 = (bf16[160,256]{1,0:T(8,128)(2,1)S(1)}, bf16[160,256]{1,0:T(8,128)(2,1)S(1)}, u32[]{:S(2)}, u32[]{:S(2)}) collective-permute-start(bf16[160,256]{1,0:T(8,128)(2,1)S(1)} %get-tuple-element.101), channel_id=1, source_target_pairs={{0,8},{2,10},{4,12},{6,14},{8,0},{10,2},{12,4},{14,6},{16,24},{18,... | collective-permute-start | bytes 245768 | tf_op jit(solution)/shard_map/ppermute | solution.py:44
  24.7 3.6 %intra.5 = (f32[256,1024]{1,0:T(8,128)S(1)}, bf16[4096,512]{1,0:T(8,128)(2,1)S(1)}) custom-call(bf16[160,256]{1,0:T(8,128)(2,1)S(1)} %get-tuple-element.97.refs_0_, f32[4,256,16]{2,1,0:T(8,128)S(1)} %get-tuple-element.88.refs_1_.refs_2_, f32[64,256]{1,0:T(8,128)S(1)} %get-tuple-element.74.refs_4_.refs_2_.refs_3_, ...), custom_call_target="tpu_custom_call" | custom-call | flops 134217728 | bytes 1572864 | tf_op jit(solution)/shard_map/intra/pallas_call | solution.py:95
  28.3 1.6 %collective-permute-done.7.refs_2_ = bf16[160,256]{1,0:T(8,128)(2,1)S(1)} collective-permute-done((bf16[160,256]{1,0:T(8,128)(2,1)S(1)}, bf16[160,256]{1,0:T(8,128)(2,1)S(1)}, u32[]{:S(2)}, u32[]{:S(2)}) %collective-permute-start.7) | collective-permute-done | bytes 81952 | tf_op jit(solution)/shard_map/ppermute | solution.py:44
  30.3 1.8 %collective-permute-start.12 = (bf16[136,256]{1,0:T(8,128)(2,1)S(1)}, bf16[136,256]{1,0:T(8,128)(2,1)S(1)}, u32[]{:S(2)}, u32[]{:S(2)}) collective-permute-start(bf16[136,256]{1,0:T(8,128)(2,1)S(1)} %get-tuple-element.105.refs_0_), channel_id=1, source_target_pairs={{0,24},{2,26},{4,28},{6,30},{8,16},{10,18},{12,20},{14,22},{16,8},... | collective-permute-start | bytes 208904 | tf_op jit(solution)/shard_map/ppermute | solution.py:44
  32.1 2.6 %collective-permute-start.14 = (bf16[136,256]{1,0:T(8,128)(2,1)S(1)}, bf16[136,256]{1,0:T(8,128)(2,1)S(1)}, u32[]{:S(2)}, u32[]{:S(2)}) collective-permute-start(bf16[136,256]{1,0:T(8,128)(2,1)S(1)} %get-tuple-element.109), channel_id=1, source_target_pairs={{0,8},{2,10},{4,12},{6,14},{8,0},{10,2},{12,4},{14,6},{16,24},{18,... | collective-permute-start | bytes 208904 | tf_op jit(solution)/shard_map/ppermute | solution.py:44
  35.4 1.6 %intra.6.refs_0_.refs_6_ = f32[256,1024]{1,0:T(8,128)S(1)} custom-call(bf16[136,256]{1,0:T(8,128)(2,1)S(1)} %get-tuple-element.105.refs_0_, bf16[64,4096]{1,0:T(8,128)(2,1)S(1)} %join.6.refs_1_, f32[4,256,16]{2,1,0:T(8,128)S(1)} %get-tuple-element.88.refs_1_.refs_2_, f32[64,256]{1,0:T(8,128)S(1)} %get-tuple-element.74.refs_4_.refs_2_.refs_3_, ...), custom_call_target="tpu_custom_call" | custom-call | flops 134217728 | bytes 1572864 | tf_op jit(solution)/shard_map/intra/pallas_call | solution.py:95
  37.0 1.5 %collective-permute-done.13.refs_2_ = bf16[136,256]{1,0:T(8,128)(2,1)S(1)} collective-permute-done((bf16[136,256]{1,0:T(8,128)(2,1)S(1)}, bf16[136,256]{1,0:T(8,128)(2,1)S(1)}, u32[]{:S(2)}, u32[]{:S(2)}) %collective-permute-start.13) | collective-permute-done | bytes 69664 | tf_op jit(solution)/shard_map/ppermute | solution.py:44
  39.9 2.5 %collective-permute-start.15 = (bf16[128,256]{1,0:T(8,128)(2,1)S(1)}, bf16[128,256]{1,0:T(8,128)(2,1)S(1)}, u32[]{:S(2)}, u32[]{:S(2)}) collective-permute-start(bf16[128,256]{1,0:T(8,128)(2,1)S(1)} %hand_on.1.refs_1_), channel_id=1, source_target_pairs={{0,24},{2,26},{4,28},{6,30},{8,16},{10,18},{12,20},{14,22},{16,8},... | collective-permute-start | bytes 196616 | tf_op jit(solution)/shard_map/ppermute | solution.py:44
  42.4 1.9 %collective-permute-start.17 = (bf16[128,256]{1,0:T(8,128)(2,1)S(1)}, bf16[128,256]{1,0:T(8,128)(2,1)S(1)}, u32[]{:S(2)}, u32[]{:S(2)}) collective-permute-start(bf16[128,256]{1,0:T(8,128)(2,1)S(1)} %hand_on.1.refs_1_), channel_id=1, source_target_pairs={{0,8},{2,10},{4,12},{6,14},{8,0},{10,2},{12,4},{14,6},{16,24},{18,... | collective-permute-start | bytes 196616 | tf_op jit(solution)/shard_map/ppermute | solution.py:44
  44.3 1.6 %intra.7.refs_0_.refs_7_ = f32[256,1024]{1,0:T(8,128)S(1)} custom-call(bf16[136,1024]{1,0:T(8,128)(2,1)S(1)} %get-tuple-element.113.refs_0_, f32[4,256,16]{2,1,0:T(8,128)S(1)} %get-tuple-element.88.refs_1_.refs_2_, f32[64,256]{1,0:T(8,128)S(1)} %get-tuple-element.74.refs_4_.refs_2_.refs_3_, f32[64,256]{1,0:T(8,128)S(1)} %get-tuple-element.89.refs_3_.refs_4_, ...), custom_call_target="tpu_custom_call" | custom-call | flops 134217728 | bytes 1572864 | tf_op jit(solution)/shard_map/intra/pallas_call | solution.py:95
  46.7 1.4 %collective-permute-done.16.refs_1_ = bf16[128,256]{1,0:T(8,128)(2,1)S(1)} collective-permute-done((bf16[128,256]{1,0:T(8,128)(2,1)S(1)}, bf16[128,256]{1,0:T(8,128)(2,1)S(1)}, u32[]{:S(2)}, u32[]{:S(2)}) %collective-permute-start.16) | collective-permute-done | bytes 65568 | tf_op jit(solution)/shard_map/ppermute | solution.py:44
  48.7 1.3 %collective-permute-start.22 = (bf16[128,768]{1,0:T(8,128)(2,1)S(1)}, bf16[128,768]{1,0:T(8,128)(2,1)S(1)}, u32[]{:S(2)}, u32[]{:S(2)}) collective-permute-start(bf16[128,768]{1,0:T(8,128)(2,1)S(1)} %join.7.refs_3_.refs_2_), channel_id=1, source_target_pairs={{0,4},{2,6},{4,0},{6,2},{8,12},{10,14},{12,8},{14,10},{16,20},{18,... | collective-permute-start | bytes 589832 | tf_op jit(solution)/shard_map/ppermute | solution.py:44
  50.2 1.1 %project.1 = (f32[64,512]{1,0:T(8,128)S(1)}, bf16[64,512]{1,0:T(8,128)(2,1)S(1)}) custom-call(s32[8,512]{1,0:T(8,128)S(1)} %get-tuple-element.70.refs_3_.refs_1_.refs_0_, bf16[64,4096]{1,0:T(8,128)(2,1)S(1)} %join.6.refs_1_, bf16[64,4096]{1,0:T(8,128)(2,1)S(1)} %collective-permute-done.10.refs_2_, bf16[8,2048]{1,0:T(8,128)(2,1)S(1)} %get-tuple-element.119.refs_3_, ...), custom_call_target="tpu_custom_call" | custom-call | bytes 1 | tf_op jit(solution)/shard_map/project/pallas_call | solution.py:95
  51.3 1.6 %collective-permute-start.21 = (bf16[64,512]{1,0:T(8,128)(2,1)S(1)}, bf16[64,512]{1,0:T(8,128)(2,1)S(1)}, u32[]{:S(2)}, u32[]{:S(2)}) collective-permute-start(bf16[64,512]{1,0:T(8,128)(2,1)S(1)} %get-tuple-element.125), channel_id=1, source_target_pairs={{0,1},{1,0},{2,3},{3,2},{4,5},{5,4},{6,7},{7,6},{8,9},{9,8},{10,11... | collective-permute-start | bytes 196616 | tf_op jit(solution)/shard_map/ppermute | solution.py:44
  53.4 2.0 %finish.1 = (bf16[256,4096]{1,0:T(8,128)(2,1)}, f32[8,128]{1,0:T(8,128)S(1)}) custom-call(bf16[256,128]{1,0:T(8,128)(2,1)S(1)} %get-tuple-element.68.refs_0_, bf16[256,512]{1,0:T(8,128)(2,1)S(1)} %get-tuple-element.69.refs_7_.refs_8_.refs_1_, bf16[128,2048]{1,0:T(8,128)(2,1)S(1)} %down_core.3.refs_2_, bf16[128,2048]{1,0:T(8,128)(2,1)S(1)} %collective-permute-done.20.refs_3_, ...), custom_call_target="tpu_custom_call" | custom-call | bytes 1 | tf_op jit(solution)/shard_map/finish/pallas_call | solution.py:95
  56.1 1.0 %states.2 = (bf16[4096,128]{1,0:T(8,128)(2,1)}, f32[16,512]{1,0:T(8,128)S(1)}, f32[16,512]{1,0:T(8,128)S(1)}) custom-call(bf16[128,1024]{1,0:T(8,128)(2,1)S(1)} %join.8.refs_0_.refs_2_, f32[4096,128]{1,0:T(8,128)S(1)} %get-tuple-element.116.refs_0_.refs_1_, f32[4096,128]{1,0:T(8,128)S(1)} %get-tuple-element.117.refs_1_.refs_2_, ...), custom_call_target="tpu_custom_call" | custom-call | bytes 1 | tf_op jit(solution)/shard_map/states/pallas_call | solution.py:95
  57.6 1.6 %states.3 = (bf16[4096,128]{1,0:T(8,128)(2,1)}, bf16[64,512]{1,0:T(8,128)(2,1)}, bf16[64,512]{1,0:T(8,128)(2,1)}) custom-call(f32[4096,128]{1,0:T(8,128)S(1)} %get-tuple-element.116.refs_0_.refs_1_, f32[4096,128]{1,0:T(8,128)S(1)} %get-tuple-element.117.refs_1_.refs_2_, bf16[128,1024]{1,0:T(8,128)(2,1)S(1)} %join.8.refs_0_.refs_2_, ...), custom_call_target="tpu_custom_call", output_to_operand_aliasing={{0}: (8, {})} | custom-call | bytes 1 | tf_op jit(solution)/shard_map/states/pallas_call | solution.py:95
  (54 shorter events, 10.0 us)
Async XLA Ops:
  3.6 2.9 %collective-permute-start = (bf16[128,2048]{1,0:T(8,128)(2,1)S(1)}, bf16[128,2048]{1,0:T(8,128)(2,1)S(1)}, u32[]{:S(2)}, u32[]{:S(2)}) collective-permute-start(bf16[128,2048]{1,0:T(8,128)(2,1)S(1)} %get-tuple-element.71.refs_0_), channel_id=1, source_target_pairs={{0,2},{2,0},{4,6},{6,4},{8,10},{10,8},{12,14},{14,12},{16,18},{18,... | collective-permute-start | bytes 1572872 | tf_op jit(solution)/shard_map/ppermute | solution.py:44
  6.8 12.7 %collective-permute-start.5 = (bf16[160,1024]{1,0:T(8,128)(2,1)S(1)}, bf16[160,1024]{1,0:T(8,128)(2,1)S(1)}, u32[]{:S(2)}, u32[]{:S(2)}) collective-permute-start(bf16[160,1024]{1,0:T(8,128)(2,1)S(1)} %get-tuple-element.87.refs_0_), channel_id=1, source_target_pairs={{0,4},{2,6},{4,0},{6,2},{8,12},{10,14},{12,8},{14,10},{16,20},{18,... | collective-permute-start | bytes 983048 | tf_op jit(solution)/shard_map/ppermute | solution.py:44
  10.0 6.4 %collective-permute-start.2 = (bf16[8,4096]{1,0:T(8,128)(2,1)S(1)}, bf16[8,4096]{1,0:T(8,128)(2,1)S(1)}, u32[]{:S(2)}, u32[]{:S(2)}) collective-permute-start(bf16[8,4096]{1,0:T(8,128)(2,1)S(1)} %resident_hidden.1.refs_1_), channel_id=1, source_target_pairs={{0,24},{2,26},{4,28},{6,30},{8,16},{10,18},{12,20},{14,22},{16,8},... | collective-permute-start | bytes 196616 | tf_op jit(solution)/shard_map/ppermute | solution.py:44
  13.7 5.8 %collective-permute-start.3 = (bf16[8,4096]{1,0:T(8,128)(2,1)S(1)}, bf16[8,4096]{1,0:T(8,128)(2,1)S(1)}, u32[]{:S(2)}, u32[]{:S(2)}) collective-permute-start(bf16[8,4096]{1,0:T(8,128)(2,1)S(1)} %resident_hidden.1.refs_1_), channel_id=1, source_target_pairs={{0,16},{2,18},{4,20},{6,22},{8,24},{10,26},{12,28},{14,30},{16,0},... | collective-permute-start | bytes 196616 | tf_op jit(solution)/shard_map/ppermute | solution.py:44
  13.7 5.8 %collective-permute-start.4 = (bf16[8,4096]{1,0:T(8,128)(2,1)S(1)}, bf16[8,4096]{1,0:T(8,128)(2,1)S(1)}, u32[]{:S(2)}, u32[]{:S(2)}) collective-permute-start(bf16[8,4096]{1,0:T(8,128)(2,1)S(1)} %resident_hidden.1.refs_1_), channel_id=1, source_target_pairs={{0,8},{2,10},{4,12},{6,14},{8,0},{10,2},{12,4},{14,6},{16,24},{18,... | collective-permute-start | bytes 196616 | tf_op jit(solution)/shard_map/ppermute | solution.py:44
  19.7 8.7 %collective-permute-start.6 = (bf16[160,256]{1,0:T(8,128)(2,1)S(1)}, bf16[160,256]{1,0:T(8,128)(2,1)S(1)}, u32[]{:S(2)}, u32[]{:S(2)}) collective-permute-start(bf16[160,256]{1,0:T(8,128)(2,1)S(1)} %get-tuple-element.97.refs_0_), channel_id=1, source_target_pairs={{0,24},{2,26},{4,28},{6,30},{8,16},{10,18},{12,20},{14,22},{16,8},... | collective-permute-start | bytes 245768 | tf_op jit(solution)/shard_map/ppermute | solution.py:44
  22.3 7.7 %collective-permute-start.7 = (bf16[160,256]{1,0:T(8,128)(2,1)S(1)}, bf16[160,256]{1,0:T(8,128)(2,1)S(1)}, u32[]{:S(2)}, u32[]{:S(2)}) collective-permute-start(bf16[160,256]{1,0:T(8,128)(2,1)S(1)} %get-tuple-element.100), channel_id=1, source_target_pairs={{0,16},{2,18},{4,20},{6,22},{8,24},{10,26},{12,28},{14,30},{16,0},... | collective-permute-start | bytes 245768 | tf_op jit(solution)/shard_map/ppermute | solution.py:44
  22.3 7.7 %collective-permute-start.8 = (bf16[160,256]{1,0:T(8,128)(2,1)S(1)}, bf16[160,256]{1,0:T(8,128)(2,1)S(1)}, u32[]{:S(2)}, u32[]{:S(2)}) collective-permute-start(bf16[160,256]{1,0:T(8,128)(2,1)S(1)} %get-tuple-element.101), channel_id=1, source_target_pairs={{0,8},{2,10},{4,12},{6,14},{8,0},{10,2},{12,4},{14,6},{16,24},{18,... | collective-permute-start | bytes 245768 | tf_op jit(solution)/shard_map/ppermute | solution.py:44
  24.1 11.1 %collective-permute-start.9 = (bf16[32,4096]{1,0:T(8,128)(2,1)S(1)}, bf16[32,4096]{1,0:T(8,128)(2,1)S(1)}, u32[]{:S(2)}, u32[]{:S(2)}) collective-permute-start(bf16[32,4096]{1,0:T(8,128)(2,1)S(1)} %join.5.refs_1_), channel_id=1, source_target_pairs={{0,4},{2,6},{4,0},{6,2},{8,12},{10,14},{12,8},{14,10},{16,20},{18,... | collective-permute-start | bytes 786440 | tf_op jit(solution)/shard_map/ppermute | solution.py:44
  30.3 6.7 %collective-permute-start.12 = (bf16[136,256]{1,0:T(8,128)(2,1)S(1)}, bf16[136,256]{1,0:T(8,128)(2,1)S(1)}, u32[]{:S(2)}, u32[]{:S(2)}) collective-permute-start(bf16[136,256]{1,0:T(8,128)(2,1)S(1)} %get-tuple-element.105.refs_0_), channel_id=1, source_target_pairs={{0,24},{2,26},{4,28},{6,30},{8,16},{10,18},{12,20},{14,22},{16,8},... | collective-permute-start | bytes 208904 | tf_op jit(solution)/shard_map/ppermute | solution.py:44
  32.1 6.4 %collective-permute-start.13 = (bf16[136,256]{1,0:T(8,128)(2,1)S(1)}, bf16[136,256]{1,0:T(8,128)(2,1)S(1)}, u32[]{:S(2)}, u32[]{:S(2)}) collective-permute-start(bf16[136,256]{1,0:T(8,128)(2,1)S(1)} %get-tuple-element.108), channel_id=1, source_target_pairs={{0,16},{2,18},{4,20},{6,22},{8,24},{10,26},{12,28},{14,30},{16,0},... | collective-permute-start | bytes 208904 | tf_op jit(solution)/shard_map/ppermute | solution.py:44
  32.1 6.4 %collective-permute-start.14 = (bf16[136,256]{1,0:T(8,128)(2,1)S(1)}, bf16[136,256]{1,0:T(8,128)(2,1)S(1)}, u32[]{:S(2)}, u32[]{:S(2)}) collective-permute-start(bf16[136,256]{1,0:T(8,128)(2,1)S(1)} %get-tuple-element.109), channel_id=1, source_target_pairs={{0,8},{2,10},{4,12},{6,14},{8,0},{10,2},{12,4},{14,6},{16,24},{18,... | collective-permute-start | bytes 208904 | tf_op jit(solution)/shard_map/ppermute | solution.py:44
  34.7 4.3 %collective-permute-start.11 = (bf16[128,256]{1,0:T(8,128)(2,1)S(1)}, bf16[128,256]{1,0:T(8,128)(2,1)S(1)}, u32[]{:S(2)}, u32[]{:S(2)}) collective-permute-start(bf16[128,256]{1,0:T(8,128)(2,1)S(1)} %get-tuple-element.106.refs_1_), channel_id=1, source_target_pairs={{0,4},{2,6},{4,0},{6,2},{8,12},{10,14},{12,8},{14,10},{16,20},{18,... | collective-permute-start | bytes 196616 | tf_op jit(solution)/shard_map/ppermute | solution.py:44
  35.3 12.9 %collective-permute-start.10 = (bf16[64,4096]{1,0:T(8,128)(2,1)S(1)}, bf16[64,4096]{1,0:T(8,128)(2,1)S(1)}, u32[]{:S(2)}, u32[]{:S(2)}) collective-permute-start(bf16[64,4096]{1,0:T(8,128)(2,1)S(1)} %join.6.refs_1_), channel_id=1, source_target_pairs={{0,2},{2,0},{4,6},{6,4},{8,10},{10,8},{12,14},{14,12},{16,18},{18,... | collective-permute-start | bytes 1572872 | tf_op jit(solution)/shard_map/ppermute | solution.py:44
  39.3 8.9 %collective-permute-start.18 = (bf16[136,1024]{1,0:T(8,128)(2,1)S(1)}, bf16[136,1024]{1,0:T(8,128)(2,1)S(1)}, u32[]{:S(2)}, u32[]{:S(2)}) collective-permute-start(bf16[136,1024]{1,0:T(8,128)(2,1)S(1)} %get-tuple-element.113.refs_0_), channel_id=1, source_target_pairs={{0,4},{2,6},{4,0},{6,2},{8,12},{10,14},{12,8},{14,10},{16,20},{18,... | collective-permute-start | bytes 835592 | tf_op jit(solution)/shard_map/ppermute | solution.py:44
  39.9 6.8 %collective-permute-start.15 = (bf16[128,256]{1,0:T(8,128)(2,1)S(1)}, bf16[128,256]{1,0:T(8,128)(2,1)S(1)}, u32[]{:S(2)}, u32[]{:S(2)}) collective-permute-start(bf16[128,256]{1,0:T(8,128)(2,1)S(1)} %hand_on.1.refs_1_), channel_id=1, source_target_pairs={{0,24},{2,26},{4,28},{6,30},{8,16},{10,18},{12,20},{14,22},{16,8},... | collective-permute-start | bytes 196616 | tf_op jit(solution)/shard_map/ppermute | solution.py:44
  42.4 5.7 %collective-permute-start.16 = (bf16[128,256]{1,0:T(8,128)(2,1)S(1)}, bf16[128,256]{1,0:T(8,128)(2,1)S(1)}, u32[]{:S(2)}, u32[]{:S(2)}) collective-permute-start(bf16[128,256]{1,0:T(8,128)(2,1)S(1)} %hand_on.1.refs_1_), channel_id=1, source_target_pairs={{0,16},{2,18},{4,20},{6,22},{8,24},{10,26},{12,28},{14,30},{16,0},... | collective-permute-start | bytes 196616 | tf_op jit(solution)/shard_map/ppermute | solution.py:44
  42.4 5.7 %collective-permute-start.17 = (bf16[128,256]{1,0:T(8,128)(2,1)S(1)}, bf16[128,256]{1,0:T(8,128)(2,1)S(1)}, u32[]{:S(2)}, u32[]{:S(2)}) collective-permute-start(bf16[128,256]{1,0:T(8,128)(2,1)S(1)} %hand_on.1.refs_1_), channel_id=1, source_target_pairs={{0,8},{2,10},{4,12},{6,14},{8,0},{10,2},{12,4},{14,6},{16,24},{18,... | collective-permute-start | bytes 196616 | tf_op jit(solution)/shard_map/ppermute | solution.py:44
  48.6 1.6 %collective-permute-start.19 = (bf16[8,2048]{1,0:T(8,128)(2,1)S(1)}, bf16[8,2048]{1,0:T(8,128)(2,1)S(1)}, u32[]{:S(2)}, u32[]{:S(2)}) collective-permute-start(bf16[8,2048]{1,0:T(8,128)(2,1)S(1)} %get-tuple-element.119.refs_3_), channel_id=1, source_target_pairs={{0,2},{2,0},{4,6},{6,4},{8,10},{10,8},{12,14},{14,12},{16,18},{18,... | collective-permute-start | bytes 98312 | tf_op jit(solution)/shard_map/ppermute | solution.py:44
  48.7 7.3 %collective-permute-start.22 = (bf16[128,768]{1,0:T(8,128)(2,1)S(1)}, bf16[128,768]{1,0:T(8,128)(2,1)S(1)}, u32[]{:S(2)}, u32[]{:S(2)}) collective-permute-start(bf16[128,768]{1,0:T(8,128)(2,1)S(1)} %join.7.refs_3_.refs_2_), channel_id=1, source_target_pairs={{0,4},{2,6},{4,0},{6,2},{8,12},{10,14},{12,8},{14,10},{16,20},{18,... | collective-permute-start | bytes 589832 | tf_op jit(solution)/shard_map/ppermute | solution.py:44
  50.0 3.4 %collective-permute-start.20 = (bf16[128,2048]{1,0:T(8,128)(2,1)S(1)}, bf16[128,2048]{1,0:T(8,128)(2,1)S(1)}, u32[]{:S(2)}, u32[]{:S(2)}) collective-permute-start(bf16[128,2048]{1,0:T(8,128)(2,1)S(1)} %get-tuple-element.122), channel_id=1, source_target_pairs={{0,2},{2,0},{4,6},{6,4},{8,10},{10,8},{12,14},{14,12},{16,18},{18,... | collective-permute-start | bytes 1572872 | tf_op jit(solution)/shard_map/ppermute | solution.py:44
  51.3 4.7 %collective-permute-start.21 = (bf16[64,512]{1,0:T(8,128)(2,1)S(1)}, bf16[64,512]{1,0:T(8,128)(2,1)S(1)}, u32[]{:S(2)}, u32[]{:S(2)}) collective-permute-start(bf16[64,512]{1,0:T(8,128)(2,1)S(1)} %get-tuple-element.125), channel_id=1, source_target_pairs={{0,1},{1,0},{2,3},{3,2},{4,5},{5,4},{6,7},{7,6},{8,9},{9,8},{10,11... | collective-permute-start | bytes 196616 | tf_op jit(solution)/shard_map/ppermute | solution.py:44
  52.9 3.2 %collective-permute-start.24 = (bf16[128,1024]{1,0:T(8,128)(2,1)S(1)}, bf16[128,1024]{1,0:T(8,128)(2,1)S(1)}, u32[]{:S(2)}, u32[]{:S(2)}) collective-permute-start(bf16[128,1024]{1,0:T(8,128)(2,1)S(1)} %join.9.refs_3_), channel_id=1, source_target_pairs={{0,2},{2,0},{4,6},{6,4},{8,10},{10,8},{12,14},{14,12},{16,18},{18,... | collective-permute-start | bytes 786440 | tf_op jit(solution)/shard_map/ppermute | solution.py:44
  56.0 1.6 %collective-permute-start.23 = (bf16[128,1024]{1,0:T(8,128)(2,1)S(1)}, bf16[128,1024]{1,0:T(8,128)(2,1)S(1)}, u32[]{:S(2)}, u32[]{:S(2)}) collective-permute-start(bf16[128,1024]{1,0:T(8,128)(2,1)S(1)} %join.8.refs_0_.refs_2_), channel_id=1, source_target_pairs={{0,2},{2,0},{4,6},{6,4},{8,10},{10,8},{12,14},{14,12},{16,18},{18,... | collective-permute-start | bytes 786440 | tf_op jit(solution)/shard_map/ppermute | solution.py:44
  (1 other events, 1.4 us)

commit v8 on v7

--- a/solution.py
+++ b/solution.py
@@ -684,7 +684,7 @@
         return (offset // line[0] ^ place_of(core)) * line[0] + (offset % line[0] ^ place_of(line))
 
     copies, found = [], []
-    chunk = part // 2 if part >= 512 else part
+    chunk = part // 4 if part >= 1024 else part
     per_slice = HEAD_DIM // (core[0] * line[0] * last[0])
     for index, (offset, prompt_ref) in enumerate(zip(offsets, prompt_refs)):
         start = spot_of(offset) * part
@@ -766,7 +766,7 @@
         scratch=[
             pltpu.VMEM((count * part, STATE_SIZE), F32),
             pltpu.VMEM((count * part, STATE_SIZE), BF16),
-            pltpu.SemaphoreType.DMA((2 * count,)),
+            pltpu.SemaphoreType.DMA((4 * count,)),
         ],
         moved=1,
     )
@@ -981,12 +981,13 @@
             join(pair, 1, [token, *shares[1:]], flops=10**10) for pair in zip(late, behind[1:])
         ]
     crossed = swap(prompt, "seq", core, 1)
-    slices = {}
-    new_state, slices[0], slices[line[0]] = states(
-        stages, scattered, prepared, pieces, (0, line[0]), (prompt, crossed), None, None, (), late[:1]
-    )
-    offsets = (*range(1, line[0]), *range(line[0] + 1, pieces))
-    prompts = late + [swap(piece, "seq", core, 1) for piece in late]
+    early = (0, line[0], *range(1, line[0]))
+    new_state, *found = states(
+        stages, scattered, prepared, pieces, early, (prompt, crossed, *late), None, None, ()
+    )
+    slices = dict(zip(early, found))
+    offsets = tuple(range(line[0] + 1, pieces))
+    prompts = [swap(piece, "seq", core, 1) for piece in late]
     new_state, state_slice, verify_out = states(
         stages, scattered, prepared, pieces, offsets, prompts, new_state, slices, shares
     )

time: 59.6 us -> 59.5 us (level)
  transfers between devices with their start and end apart: 25 -> 25, of which waited for: 9 -> 9; matrix products, arithmetic and copies ran while one was open for 0% -> 0% of each run, Pallas kernels for 28% -> 29%
where the time goes in v8:
time: 59.5 us; the launch traced here: 59.3 us
  starting transfers between devices  26.2 us (44%)
  Pallas kernels  22.3 us (37%)
  waiting for transfers between devices  9.74 us (16%)
  between operations  1.04 us (2%)
    ppermute x25, starting transfers between devices, swap(): lax.ppermute(value, axis, [(k, k ^ offset * stride) for k in range(count)])  26.2 us
    pallas_call x28, Pallas kernels, call(): pl.pallas_call(ordered(kernel, first), name=name, grid=grid, out_shape=ou...  22.3 us
    ppermute x25, waiting for transfers between devices, swap(): lax.ppermute(value, axis, [(k, k ^ offset * stride) for k in range(count)])  9.74 us
  transfers between devices with their start and end apart: 25, of which 9 were waited for; matrix products, arithmetic and copies ran while one was open for 0% of the time, Pallas kernels for 29%

profile of v8, /device:TPU:0, one launch (start us, length us, event | category | flops | bytes accessed | tf_op | source)
XLA Modules:
  0.0 59.3 jit_solution(3738685489029757418)
XLA Ops:
  0.6 3.0 %open_block.1 = (bf16[128,2048]{1,0:T(8,128)(2,1)S(1)}, f32[4,256,16]{2,1,0:T(8,128)S(1)}, f32[64,256]{1,0:T(8,128)S(1)}, f32[64,256]{1,0:T(8,128)S(1)}, bf16[25...) custom-call(f32[64,256]{1,0:T(8,128)} %bitcast.9, ...), custom_call_target="tpu_custom_call" | custom-call | flops 268435456 | bytes 8911232 | tf_op jit(solution)/shard_map/open_block/pallas_call | solution.py:95
  4.1 1.0 %draft_rows.1 = (bf16[32,2048]{1,0:T(8,128)(2,1)S(1)}, bf16[32,2048]{1,0:T(8,128)(2,1)S(1)}, f32[1,4096]{1,0:T(1,128)S(1)}, f32[8,4096]{1,0:T(8,128)S(1)}, f32[8...) custom-call(bf16[128,2048]{1,0:T(8,128)(2,1)S(1)} %get-tuple-element.7, ...), custom_call_target="tpu_custom_call" | custom-call | flops 3276800 | bytes 1205248 | tf_op jit(solution)/shard_map/draft_rows/pallas_call | solution.py:95
  6.8 2.8 %collective-permute-start.5 = (bf16[160,1024]{1,0:T(8,128)(2,1)S(1)}, bf16[160,1024]{1,0:T(8,128)(2,1)S(1)}, u32[]{:S(2)}, u32[]{:S(2)}) collective-permute-start(bf16[160,1024]{1,0:T(8,128)(2,1)S(1)} %get-tuple-element.88.refs_0_), channel_id=1, source_target_pairs={{0,4},{2,6},{4,0},{6,2},{8,12},{10,14},{12,8},{14,10},{16,20},{18,... | collective-permute-start | bytes 983048 | tf_op jit(solution)/shard_map/ppermute | solution.py:44
  10.0 3.6 %collective-permute-start.2 = (bf16[8,4096]{1,0:T(8,128)(2,1)S(1)}, bf16[8,4096]{1,0:T(8,128)(2,1)S(1)}, u32[]{:S(2)}, u32[]{:S(2)}) collective-permute-start(bf16[8,4096]{1,0:T(8,128)(2,1)S(1)} %resident_hidden.1.refs_1_), channel_id=1, source_target_pairs={{0,24},{2,26},{4,28},{6,30},{8,16},{10,18},{12,20},{14,22},{16,8},... | collective-permute-start | bytes 196616 | tf_op jit(solution)/shard_map/ppermute | solution.py:44
  14.4 1.6 %intra.4.refs_0_.refs_4_ = f32[256,1024]{1,0:T(8,128)S(1)} custom-call(bf16[160,1024]{1,0:T(8,128)(2,1)S(1)} %get-tuple-element.88.refs_0_, f32[4,256,16]{2,1,0:T(8,128)S(1)} %get-tuple-element.89.refs_1_.refs_2_, f32[64,256]{1,0:T(8,128)S(1)} %get-tuple-element.75.refs_4_.refs_2_.refs_3_, f32[64,256]{1,0:T(8,128)S(1)} %get-tuple-element.90.refs_3_.refs_4_, ...), custom_call_target="tpu_custom_call" | custom-call | flops 134217728 | bytes 1572864 | tf_op jit(solution)/shard_map/intra/pallas_call | solution.py:95
  16.4 3.1 %collective-permute-done.3.refs_2_.refs_3_ = bf16[8,4096]{1,0:T(8,128)(2,1)S(1)} collective-permute-done((bf16[8,4096]{1,0:T(8,128)(2,1)S(1)}, bf16[8,4096]{1,0:T(8,128)(2,1)S(1)}, u32[]{:S(2)}, u32[]{:S(2)}) %collective-permute-start.3) | collective-permute-done | bytes 65568 | tf_op jit(solution)/shard_map/ppermute | solution.py:44
  19.7 2.6 %collective-permute-start.6 = (bf16[160,256]{1,0:T(8,128)(2,1)S(1)}, bf16[160,256]{1,0:T(8,128)(2,1)S(1)}, u32[]{:S(2)}, u32[]{:S(2)}) collective-permute-start(bf16[160,256]{1,0:T(8,128)(2,1)S(1)} %get-tuple-element.98.refs_0_), channel_id=1, source_target_pairs={{0,24},{2,26},{4,28},{6,30},{8,16},{10,18},{12,20},{14,22},{16,8},... | collective-permute-start | bytes 245768 | tf_op jit(solution)/shard_map/ppermute | solution.py:44
  22.3 1.8 %collective-permute-start.8 = (bf16[160,256]{1,0:T(8,128)(2,1)S(1)}, bf16[160,256]{1,0:T(8,128)(2,1)S(1)}, u32[]{:S(2)}, u32[]{:S(2)}) collective-permute-start(bf16[160,256]{1,0:T(8,128)(2,1)S(1)} %get-tuple-element.102), channel_id=1, source_target_pairs={{0,8},{2,10},{4,12},{6,14},{8,0},{10,2},{12,4},{14,6},{16,24},{18,... | collective-permute-start | bytes 245768 | tf_op jit(solution)/shard_map/ppermute | solution.py:44
  24.7 3.6 %intra.5 = (f32[256,1024]{1,0:T(8,128)S(1)}, bf16[4096,512]{1,0:T(8,128)(2,1)S(1)}) custom-call(bf16[160,256]{1,0:T(8,128)(2,1)S(1)} %get-tuple-element.98.refs_0_, f32[4,256,16]{2,1,0:T(8,128)S(1)} %get-tuple-element.89.refs_1_.refs_2_, f32[64,256]{1,0:T(8,128)S(1)} %get-tuple-element.75.refs_4_.refs_2_.refs_3_, ...), custom_call_target="tpu_custom_call" | custom-call | flops 134217728 | bytes 1572864 | tf_op jit(solution)/shard_map/intra/pallas_call | solution.py:95
  28.3 1.6 %collective-permute-done.7.refs_2_ = bf16[160,256]{1,0:T(8,128)(2,1)S(1)} collective-permute-done((bf16[160,256]{1,0:T(8,128)(2,1)S(1)}, bf16[160,256]{1,0:T(8,128)(2,1)S(1)}, u32[]{:S(2)}, u32[]{:S(2)}) %collective-permute-start.7) | collective-permute-done | bytes 81952 | tf_op jit(solution)/shard_map/ppermute | solution.py:44
  30.3 1.8 %collective-permute-start.12 = (bf16[136,256]{1,0:T(8,128)(2,1)S(1)}, bf16[136,256]{1,0:T(8,128)(2,1)S(1)}, u32[]{:S(2)}, u32[]{:S(2)}) collective-permute-start(bf16[136,256]{1,0:T(8,128)(2,1)S(1)} %get-tuple-element.106.refs_0_), channel_id=1, source_target_pairs={{0,24},{2,26},{4,28},{6,30},{8,16},{10,18},{12,20},{14,22},{16,8},... | collective-permute-start | bytes 208904 | tf_op jit(solution)/shard_map/ppermute | solution.py:44
  32.1 2.6 %collective-permute-start.14 = (bf16[136,256]{1,0:T(8,128)(2,1)S(1)}, bf16[136,256]{1,0:T(8,128)(2,1)S(1)}, u32[]{:S(2)}, u32[]{:S(2)}) collective-permute-start(bf16[136,256]{1,0:T(8,128)(2,1)S(1)} %get-tuple-element.110), channel_id=1, source_target_pairs={{0,8},{2,10},{4,12},{6,14},{8,0},{10,2},{12,4},{14,6},{16,24},{18,... | collective-permute-start | bytes 208904 | tf_op jit(solution)/shard_map/ppermute | solution.py:44
  35.4 1.6 %intra.6.refs_0_.refs_6_ = f32[256,1024]{1,0:T(8,128)S(1)} custom-call(bf16[136,256]{1,0:T(8,128)(2,1)S(1)} %get-tuple-element.106.refs_0_, bf16[64,4096]{1,0:T(8,128)(2,1)S(1)} %join.6.refs_1_, f32[4,256,16]{2,1,0:T(8,128)S(1)} %get-tuple-element.89.refs_1_.refs_2_, f32[64,256]{1,0:T(8,128)S(1)} %get-tuple-element.75.refs_4_.refs_2_.refs_3_, ...), custom_call_target="tpu_custom_call" | custom-call | flops 134217728 | bytes 1572864 | tf_op jit(solution)/shard_map/intra/pallas_call | solution.py:95
  37.0 1.5 %collective-permute-done.13.refs_2_ = bf16[136,256]{1,0:T(8,128)(2,1)S(1)} collective-permute-done((bf16[136,256]{1,0:T(8,128)(2,1)S(1)}, bf16[136,256]{1,0:T(8,128)(2,1)S(1)}, u32[]{:S(2)}, u32[]{:S(2)}) %collective-permute-start.13) | collective-permute-done | bytes 69664 | tf_op jit(solution)/shard_map/ppermute | solution.py:44
  39.9 2.5 %collective-permute-start.15 = (bf16[128,256]{1,0:T(8,128)(2,1)S(1)}, bf16[128,256]{1,0:T(8,128)(2,1)S(1)}, u32[]{:S(2)}, u32[]{:S(2)}) collective-permute-start(bf16[128,256]{1,0:T(8,128)(2,1)S(1)} %hand_on.1.refs_1_), channel_id=1, source_target_pairs={{0,24},{2,26},{4,28},{6,30},{8,16},{10,18},{12,20},{14,22},{16,8},... | collective-permute-start | bytes 196616 | tf_op jit(solution)/shard_map/ppermute | solution.py:44
  42.4 1.9 %collective-permute-start.17 = (bf16[128,256]{1,0:T(8,128)(2,1)S(1)}, bf16[128,256]{1,0:T(8,128)(2,1)S(1)}, u32[]{:S(2)}, u32[]{:S(2)}) collective-permute-start(bf16[128,256]{1,0:T(8,128)(2,1)S(1)} %hand_on.1.refs_1_), channel_id=1, source_target_pairs={{0,8},{2,10},{4,12},{6,14},{8,0},{10,2},{12,4},{14,6},{16,24},{18,... | collective-permute-start | bytes 196616 | tf_op jit(solution)/shard_map/ppermute | solution.py:44
  44.3 1.6 %intra.7.refs_0_.refs_7_ = f32[256,1024]{1,0:T(8,128)S(1)} custom-call(bf16[136,1024]{1,0:T(8,128)(2,1)S(1)} %get-tuple-element.114.refs_0_, f32[4,256,16]{2,1,0:T(8,128)S(1)} %get-tuple-element.89.refs_1_.refs_2_, f32[64,256]{1,0:T(8,128)S(1)} %get-tuple-element.75.refs_4_.refs_2_.refs_3_, f32[64,256]{1,0:T(8,128)S(1)} %get-tuple-element.90.refs_3_.refs_4_, ...), custom_call_target="tpu_custom_call" | custom-call | flops 134217728 | bytes 1572864 | tf_op jit(solution)/shard_map/intra/pallas_call | solution.py:95
  46.7 1.4 %collective-permute-done.16.refs_1_ = bf16[128,256]{1,0:T(8,128)(2,1)S(1)} collective-permute-done((bf16[128,256]{1,0:T(8,128)(2,1)S(1)}, bf16[128,256]{1,0:T(8,128)(2,1)S(1)}, u32[]{:S(2)}, u32[]{:S(2)}) %collective-permute-start.16) | collective-permute-done | bytes 65568 | tf_op jit(solution)/shard_map/ppermute | solution.py:44
  48.7 1.3 %collective-permute-start.22 = (bf16[128,768]{1,0:T(8,128)(2,1)S(1)}, bf16[128,768]{1,0:T(8,128)(2,1)S(1)}, u32[]{:S(2)}, u32[]{:S(2)}) collective-permute-start(bf16[128,768]{1,0:T(8,128)(2,1)S(1)} %join.7.refs_3_.refs_2_), channel_id=1, source_target_pairs={{0,4},{2,6},{4,0},{6,2},{8,12},{10,14},{12,8},{14,10},{16,20},{18,... | collective-permute-start | bytes 589832 | tf_op jit(solution)/shard_map/ppermute | solution.py:44
  50.2 1.1 %project.1 = (f32[64,512]{1,0:T(8,128)S(1)}, bf16[64,512]{1,0:T(8,128)(2,1)S(1)}) custom-call(s32[8,512]{1,0:T(8,128)S(1)} %get-tuple-element.71.refs_3_.refs_1_.refs_0_, bf16[64,4096]{1,0:T(8,128)(2,1)S(1)} %join.6.refs_1_, bf16[64,4096]{1,0:T(8,128)(2,1)S(1)} %collective-permute-done.10.refs_2_, bf16[8,2048]{1,0:T(8,128)(2,1)S(1)} %get-tuple-element.120.refs_3_, ...), custom_call_target="tpu_custom_call" | custom-call | bytes 1 | tf_op jit(solution)/shard_map/project/pallas_call | solution.py:95
  51.3 1.6 %collective-permute-start.21 = (bf16[64,512]{1,0:T(8,128)(2,1)S(1)}, bf16[64,512]{1,0:T(8,128)(2,1)S(1)}, u32[]{:S(2)}, u32[]{:S(2)}) collective-permute-start(bf16[64,512]{1,0:T(8,128)(2,1)S(1)} %get-tuple-element.126), channel_id=1, source_target_pairs={{0,1},{1,0},{2,3},{3,2},{4,5},{5,4},{6,7},{7,6},{8,9},{9,8},{10,11... | collective-permute-start | bytes 196616 | tf_op jit(solution)/shard_map/ppermute | solution.py:44
  53.4 2.0 %finish.1 = (bf16[256,4096]{1,0:T(8,128)(2,1)}, f32[8,128]{1,0:T(8,128)S(1)}) custom-call(bf16[256,128]{1,0:T(8,128)(2,1)S(1)} %get-tuple-element.69.refs_0_, bf16[256,512]{1,0:T(8,128)(2,1)S(1)} %get-tuple-element.70.refs_7_.refs_8_.refs_1_, bf16[128,2048]{1,0:T(8,128)(2,1)S(1)} %down_core.3.refs_2_, bf16[128,2048]{1,0:T(8,128)(2,1)S(1)} %collective-permute-done.20.refs_3_, ...), custom_call_target="tpu_custom_call" | custom-call | bytes 1 | tf_op jit(solution)/shard_map/finish/pallas_call | solution.py:95
  56.1 1.2 %states.2 = (bf16[4096,128]{1,0:T(8,128)(2,1)}, f32[16,512]{1,0:T(8,128)S(1)}, f32[16,512]{1,0:T(8,128)S(1)}, f32[16,512]{1,0:T(8,128)S(1)}) custom-call(f32[4096,128]{1,0:T(8,128)S(1)} %get-tuple-element.117.refs_0_, f32[4096,128]{1,0:T(8,128)S(1)} %get-tuple-element.118.refs_1_, bf16[128,1024]{1,0:T(8,128)(2,1)S(1)} %join.9.refs_2_, ...), custom_call_target="tpu_custom_call" | custom-call | bytes 1 | tf_op jit(solution)/shard_map/states/pallas_call | solution.py:95
  57.6 1.5 %states.3 = (bf16[4096,128]{1,0:T(8,128)(2,1)}, bf16[64,512]{1,0:T(8,128)(2,1)}, bf16[64,512]{1,0:T(8,128)(2,1)}) custom-call(f32[4096,128]{1,0:T(8,128)S(1)} %get-tuple-element.117.refs_0_, f32[4096,128]{1,0:T(8,128)S(1)} %get-tuple-element.118.refs_1_, bf16[128,1024]{1,0:T(8,128)(2,1)S(1)} %collective-permute-done.23.refs_2_, ...), custom_call_target="tpu_custom_call", output_to_operand_aliasing={{0}: (8, {})} | custom-call | bytes 1 | tf_op jit(solution)/shard_map/states/pallas_call | solution.py:95
  (54 shorter events, 9.8 us)
Async XLA Ops:
  3.6 2.9 %collective-permute-start = (bf16[128,2048]{1,0:T(8,128)(2,1)S(1)}, bf16[128,2048]{1,0:T(8,128)(2,1)S(1)}, u32[]{:S(2)}, u32[]{:S(2)}) collective-permute-start(bf16[128,2048]{1,0:T(8,128)(2,1)S(1)} %get-tuple-element.72.refs_0_), channel_id=1, source_target_pairs={{0,2},{2,0},{4,6},{6,4},{8,10},{10,8},{12,14},{14,12},{16,18},{18,... | collective-permute-start | bytes 1572872 | tf_op jit(solution)/shard_map/ppermute | solution.py:44
  6.8 12.7 %collective-permute-start.5 = (bf16[160,1024]{1,0:T(8,128)(2,1)S(1)}, bf16[160,1024]{1,0:T(8,128)(2,1)S(1)}, u32[]{:S(2)}, u32[]{:S(2)}) collective-permute-start(bf16[160,1024]{1,0:T(8,128)(2,1)S(1)} %get-tuple-element.88.refs_0_), channel_id=1, source_target_pairs={{0,4},{2,6},{4,0},{6,2},{8,12},{10,14},{12,8},{14,10},{16,20},{18,... | collective-permute-start | bytes 983048 | tf_op jit(solution)/shard_map/ppermute | solution.py:44
  10.0 6.4 %collective-permute-start.2 = (bf16[8,4096]{1,0:T(8,128)(2,1)S(1)}, bf16[8,4096]{1,0:T(8,128)(2,1)S(1)}, u32[]{:S(2)}, u32[]{:S(2)}) collective-permute-start(bf16[8,4096]{1,0:T(8,128)(2,1)S(1)} %resident_hidden.1.refs_1_), channel_id=1, source_target_pairs={{0,24},{2,26},{4,28},{6,30},{8,16},{10,18},{12,20},{14,22},{16,8},... | collective-permute-start | bytes 196616 | tf_op jit(solution)/shard_map/ppermute | solution.py:44
  13.7 5.8 %collective-permute-start.3 = (bf16[8,4096]{1,0:T(8,128)(2,1)S(1)}, bf16[8,4096]{1,0:T(8,128)(2,1)S(1)}, u32[]{:S(2)}, u32[]{:S(2)}) collective-permute-start(bf16[8,4096]{1,0:T(8,128)(2,1)S(1)} %resident_hidden.1.refs_1_), channel_id=1, source_target_pairs={{0,16},{2,18},{4,20},{6,22},{8,24},{10,26},{12,28},{14,30},{16,0},... | collective-permute-start | bytes 196616 | tf_op jit(solution)/shard_map/ppermute | solution.py:44
  13.7 5.8 %collective-permute-start.4 = (bf16[8,4096]{1,0:T(8,128)(2,1)S(1)}, bf16[8,4096]{1,0:T(8,128)(2,1)S(1)}, u32[]{:S(2)}, u32[]{:S(2)}) collective-permute-start(bf16[8,4096]{1,0:T(8,128)(2,1)S(1)} %resident_hidden.1.refs_1_), channel_id=1, source_target_pairs={{0,8},{2,10},{4,12},{6,14},{8,0},{10,2},{12,4},{14,6},{16,24},{18,... | collective-permute-start | bytes 196616 | tf_op jit(solution)/shard_map/ppermute | solution.py:44
  19.7 8.7 %collective-permute-start.6 = (bf16[160,256]{1,0:T(8,128)(2,1)S(1)}, bf16[160,256]{1,0:T(8,128)(2,1)S(1)}, u32[]{:S(2)}, u32[]{:S(2)}) collective-permute-start(bf16[160,256]{1,0:T(8,128)(2,1)S(1)} %get-tuple-element.98.refs_0_), channel_id=1, source_target_pairs={{0,24},{2,26},{4,28},{6,30},{8,16},{10,18},{12,20},{14,22},{16,8},... | collective-permute-start | bytes 245768 | tf_op jit(solution)/shard_map/ppermute | solution.py:44
  22.3 7.7 %collective-permute-start.7 = (bf16[160,256]{1,0:T(8,128)(2,1)S(1)}, bf16[160,256]{1,0:T(8,128)(2,1)S(1)}, u32[]{:S(2)}, u32[]{:S(2)}) collective-permute-start(bf16[160,256]{1,0:T(8,128)(2,1)S(1)} %get-tuple-element.101), channel_id=1, source_target_pairs={{0,16},{2,18},{4,20},{6,22},{8,24},{10,26},{12,28},{14,30},{16,0},... | collective-permute-start | bytes 245768 | tf_op jit(solution)/shard_map/ppermute | solution.py:44
  22.3 7.7 %collective-permute-start.8 = (bf16[160,256]{1,0:T(8,128)(2,1)S(1)}, bf16[160,256]{1,0:T(8,128)(2,1)S(1)}, u32[]{:S(2)}, u32[]{:S(2)}) collective-permute-start(bf16[160,256]{1,0:T(8,128)(2,1)S(1)} %get-tuple-element.102), channel_id=1, source_target_pairs={{0,8},{2,10},{4,12},{6,14},{8,0},{10,2},{12,4},{14,6},{16,24},{18,... | collective-permute-start | bytes 245768 | tf_op jit(solution)/shard_map/ppermute | solution.py:44
  24.1 11.1 %collective-permute-start.9 = (bf16[32,4096]{1,0:T(8,128)(2,1)S(1)}, bf16[32,4096]{1,0:T(8,128)(2,1)S(1)}, u32[]{:S(2)}, u32[]{:S(2)}) collective-permute-start(bf16[32,4096]{1,0:T(8,128)(2,1)S(1)} %join.5.refs_1_), channel_id=1, source_target_pairs={{0,4},{2,6},{4,0},{6,2},{8,12},{10,14},{12,8},{14,10},{16,20},{18,... | collective-permute-start | bytes 786440 | tf_op jit(solution)/shard_map/ppermute | solution.py:44
  30.3 6.7 %collective-permute-start.12 = (bf16[136,256]{1,0:T(8,128)(2,1)S(1)}, bf16[136,256]{1,0:T(8,128)(2,1)S(1)}, u32[]{:S(2)}, u32[]{:S(2)}) collective-permute-start(bf16[136,256]{1,0:T(8,128)(2,1)S(1)} %get-tuple-element.106.refs_0_), channel_id=1, source_target_pairs={{0,24},{2,26},{4,28},{6,30},{8,16},{10,18},{12,20},{14,22},{16,8},... | collective-permute-start | bytes 208904 | tf_op jit(solution)/shard_map/ppermute | solution.py:44
  32.1 6.4 %collective-permute-start.13 = (bf16[136,256]{1,0:T(8,128)(2,1)S(1)}, bf16[136,256]{1,0:T(8,128)(2,1)S(1)}, u32[]{:S(2)}, u32[]{:S(2)}) collective-permute-start(bf16[136,256]{1,0:T(8,128)(2,1)S(1)} %get-tuple-element.109), channel_id=1, source_target_pairs={{0,16},{2,18},{4,20},{6,22},{8,24},{10,26},{12,28},{14,30},{16,0},... | collective-permute-start | bytes 208904 | tf_op jit(solution)/shard_map/ppermute | solution.py:44
  32.1 6.4 %collective-permute-start.14 = (bf16[136,256]{1,0:T(8,128)(2,1)S(1)}, bf16[136,256]{1,0:T(8,128)(2,1)S(1)}, u32[]{:S(2)}, u32[]{:S(2)}) collective-permute-start(bf16[136,256]{1,0:T(8,128)(2,1)S(1)} %get-tuple-element.110), channel_id=1, source_target_pairs={{0,8},{2,10},{4,12},{6,14},{8,0},{10,2},{12,4},{14,6},{16,24},{18,... | collective-permute-start | bytes 208904 | tf_op jit(solution)/shard_map/ppermute | solution.py:44
  34.7 4.3 %collective-permute-start.11 = (bf16[128,256]{1,0:T(8,128)(2,1)S(1)}, bf16[128,256]{1,0:T(8,128)(2,1)S(1)}, u32[]{:S(2)}, u32[]{:S(2)}) collective-permute-start(bf16[128,256]{1,0:T(8,128)(2,1)S(1)} %get-tuple-element.107.refs_1_), channel_id=1, source_target_pairs={{0,4},{2,6},{4,0},{6,2},{8,12},{10,14},{12,8},{14,10},{16,20},{18,... | collective-permute-start | bytes 196616 | tf_op jit(solution)/shard_map/ppermute | solution.py:44
  35.3 12.9 %collective-permute-start.10 = (bf16[64,4096]{1,0:T(8,128)(2,1)S(1)}, bf16[64,4096]{1,0:T(8,128)(2,1)S(1)}, u32[]{:S(2)}, u32[]{:S(2)}) collective-permute-start(bf16[64,4096]{1,0:T(8,128)(2,1)S(1)} %join.6.refs_1_), channel_id=1, source_target_pairs={{0,2},{2,0},{4,6},{6,4},{8,10},{10,8},{12,14},{14,12},{16,18},{18,... | collective-permute-start | bytes 1572872 | tf_op jit(solution)/shard_map/ppermute | solution.py:44
  39.3 8.9 %collective-permute-start.18 = (bf16[136,1024]{1,0:T(8,128)(2,1)S(1)}, bf16[136,1024]{1,0:T(8,128)(2,1)S(1)}, u32[]{:S(2)}, u32[]{:S(2)}) collective-permute-start(bf16[136,1024]{1,0:T(8,128)(2,1)S(1)} %get-tuple-element.114.refs_0_), channel_id=1, source_target_pairs={{0,4},{2,6},{4,0},{6,2},{8,12},{10,14},{12,8},{14,10},{16,20},{18,... | collective-permute-start | bytes 835592 | tf_op jit(solution)/shard_map/ppermute | solution.py:44
  39.9 6.8 %collective-permute-start.15 = (bf16[128,256]{1,0:T(8,128)(2,1)S(1)}, bf16[128,256]{1,0:T(8,128)(2,1)S(1)}, u32[]{:S(2)}, u32[]{:S(2)}) collective-permute-start(bf16[128,256]{1,0:T(8,128)(2,1)S(1)} %hand_on.1.refs_1_), channel_id=1, source_target_pairs={{0,24},{2,26},{4,28},{6,30},{8,16},{10,18},{12,20},{14,22},{16,8},... | collective-permute-start | bytes 196616 | tf_op jit(solution)/shard_map/ppermute | solution.py:44
  42.4 5.7 %collective-permute-start.16 = (bf16[128,256]{1,0:T(8,128)(2,1)S(1)}, bf16[128,256]{1,0:T(8,128)(2,1)S(1)}, u32[]{:S(2)}, u32[]{:S(2)}) collective-permute-start(bf16[128,256]{1,0:T(8,128)(2,1)S(1)} %hand_on.1.refs_1_), channel_id=1, source_target_pairs={{0,16},{2,18},{4,20},{6,22},{8,24},{10,26},{12,28},{14,30},{16,0},... | collective-permute-start | bytes 196616 | tf_op jit(solution)/shard_map/ppermute | solution.py:44
  42.4 5.7 %collective-permute-start.17 = (bf16[128,256]{1,0:T(8,128)(2,1)S(1)}, bf16[128,256]{1,0:T(8,128)(2,1)S(1)}, u32[]{:S(2)}, u32[]{:S(2)}) collective-permute-start(bf16[128,256]{1,0:T(8,128)(2,1)S(1)} %hand_on.1.refs_1_), channel_id=1, source_target_pairs={{0,8},{2,10},{4,12},{6,14},{8,0},{10,2},{12,4},{14,6},{16,24},{18,... | collective-permute-start | bytes 196616 | tf_op jit(solution)/shard_map/ppermute | solution.py:44
  48.6 1.6 %collective-permute-start.19 = (bf16[8,2048]{1,0:T(8,128)(2,1)S(1)}, bf16[8,2048]{1,0:T(8,128)(2,1)S(1)}, u32[]{:S(2)}, u32[]{:S(2)}) collective-permute-start(bf16[8,2048]{1,0:T(8,128)(2,1)S(1)} %get-tuple-element.120.refs_3_), channel_id=1, source_target_pairs={{0,2},{2,0},{4,6},{6,4},{8,10},{10,8},{12,14},{14,12},{16,18},{18,... | collective-permute-start | bytes 98312 | tf_op jit(solution)/shard_map/ppermute | solution.py:44
  48.7 7.3 %collective-permute-start.22 = (bf16[128,768]{1,0:T(8,128)(2,1)S(1)}, bf16[128,768]{1,0:T(8,128)(2,1)S(1)}, u32[]{:S(2)}, u32[]{:S(2)}) collective-permute-start(bf16[128,768]{1,0:T(8,128)(2,1)S(1)} %join.7.refs_3_.refs_2_), channel_id=1, source_target_pairs={{0,4},{2,6},{4,0},{6,2},{8,12},{10,14},{12,8},{14,10},{16,20},{18,... | collective-permute-start | bytes 589832 | tf_op jit(solution)/shard_map/ppermute | solution.py:44
  50.0 3.4 %collective-permute-start.20 = (bf16[128,2048]{1,0:T(8,128)(2,1)S(1)}, bf16[128,2048]{1,0:T(8,128)(2,1)S(1)}, u32[]{:S(2)}, u32[]{:S(2)}) collective-permute-start(bf16[128,2048]{1,0:T(8,128)(2,1)S(1)} %get-tuple-element.123), channel_id=1, source_target_pairs={{0,2},{2,0},{4,6},{6,4},{8,10},{10,8},{12,14},{14,12},{16,18},{18,... | collective-permute-start | bytes 1572872 | tf_op jit(solution)/shard_map/ppermute | solution.py:44
  51.3 4.7 %collective-permute-start.21 = (bf16[64,512]{1,0:T(8,128)(2,1)S(1)}, bf16[64,512]{1,0:T(8,128)(2,1)S(1)}, u32[]{:S(2)}, u32[]{:S(2)}) collective-permute-start(bf16[64,512]{1,0:T(8,128)(2,1)S(1)} %get-tuple-element.126), channel_id=1, source_target_pairs={{0,1},{1,0},{2,3},{3,2},{4,5},{5,4},{6,7},{7,6},{8,9},{9,8},{10,11... | collective-permute-start | bytes 196616 | tf_op jit(solution)/shard_map/ppermute | solution.py:44
  52.9 3.2 %collective-permute-start.24 = (bf16[128,1024]{1,0:T(8,128)(2,1)S(1)}, bf16[128,1024]{1,0:T(8,128)(2,1)S(1)}, u32[]{:S(2)}, u32[]{:S(2)}) collective-permute-start(bf16[128,1024]{1,0:T(8,128)(2,1)S(1)} %join.9.refs_2_), channel_id=1, source_target_pairs={{0,2},{2,0},{4,6},{6,4},{8,10},{10,8},{12,14},{14,12},{16,18},{18,... | collective-permute-start | bytes 786440 | tf_op jit(solution)/shard_map/ppermute | solution.py:44
  56.0 1.6 %collective-permute-start.23 = (bf16[128,1024]{1,0:T(8,128)(2,1)S(1)}, bf16[128,1024]{1,0:T(8,128)(2,1)S(1)}, u32[]{:S(2)}, u32[]{:S(2)}) collective-permute-start(bf16[128,1024]{1,0:T(8,128)(2,1)S(1)} %join.8.refs_4_), channel_id=1, source_target_pairs={{0,2},{2,0},{4,6},{6,4},{8,10},{10,8},{12,14},{14,12},{16,18},{18,... | collective-permute-start | bytes 786440 | tf_op jit(solution)/shard_map/ppermute | solution.py:44
  (1 other events, 1.4 us)
